TPU v7x, 32 devices: a whole 2x2x4 slice. The times are simulated.
32 devices in a mesh: grp: 4 (over z), shard: 8 (over y, x, core).
Axes of the slice: x: 2, y: 2, z: 4, core: 2. Of those that a mesh axis runs over, the one named last changes fastest.
Arguments:
- video: bfloat16 [2, 32, 393, 768], P(None, ('grp', 'shard')), may hold values from -6 to 6
- cotangent: bfloat16 [2, 32, 393, 768], P(None, ('grp', 'shard')), may hold values from -6 to 6
- live: int32 [2, 32], P(None, ('grp', 'shard')), may hold values 0 or 1
- time_entry: bfloat16 [768, 2304], P('shard'), may hold values from -0.21875 to 0.21875
- time_exit: bfloat16 [768, 768], P('shard'), may hold values from -0.4375 to 0.4375
- time_mixer: bfloat16 [768, 768], P('shard'), may hold values from -0.21875 to 0.21875
- space_entry: bfloat16 [768, 2304], P('shard'), may hold values from -0.21875 to 0.21875
- space_exit: bfloat16 [768, 768], P('shard'), may hold values from -0.875 to 0.875
- hidden_expand: bfloat16 [768, 3072], P('shard'), may hold values from -0.21875 to 0.21875
- hidden_reduce: bfloat16 [3072, 768], P('shard'), may hold values from -0.109375 to 0.109375
- bias_rows: bfloat16 [8, 768], P(None, 'shard'), may hold values from -3 to 3
- hidden_bias: bfloat16 [3072], P('shard'), may hold values from -3 to 3
- norm_gain: bfloat16 [3, 768], P(None, 'shard'), may hold values from 0.5 to 1.5
- norm_shift: bfloat16 [3, 768], P(None, 'shard'), may hold values from -3 to 3
Outputs:
- block_output: bfloat16 [2, 32, 393, 768], P(None, ('grp', 'shard'))
- input_grad: bfloat16 [2, 32, 393, 768], P(None, ('grp', 'shard'))
- grad_time_entry: float32 [768, 2304], P('shard')
- grad_time_exit: float32 [768, 768], P('shard')
- grad_time_mixer: float32 [768, 768], P('shard')
- grad_space_entry: float32 [768, 2304], P('shard')
- grad_space_exit: float32 [768, 768], P('shard')
- grad_hidden_expand: float32 [768, 3072], P('shard')
- grad_hidden_reduce: float32 [3072, 768], P('shard')
- grad_bias_rows: float32 [8, 768], P(None, 'shard')
- grad_hidden_bias: float32 [3072], P('shard')
- grad_norm_gain: float32 [3, 768], P(None, 'shard')
- grad_norm_shift: float32 [3, 768], P(None, 'shard')
Inputs may be any that keep to these rules, and one draw needn't show every extreme that they name: `live`: 1 where a slot of a micro-batch holds a clip, 0 where it is empty.
All inputs are finite; a program needn't handle non-finite values. No bound on the sum of `live` on one device may be relied on, other than what follows from the above.
Results may differ from a plain program's by a relative error of at most 0.017.
Values may be sent and summed in bfloat16 or wider, within the bound.
No kernel may reach another device: no remote copies, remote signals or barrier semaphores. Data moves between devices by JAX's collectives and lax.ppermute only.
A program may use at most 256 MiB of HBM per device.

v0:
```python
import jax
import jax.numpy as jnp
from jax import lax
from jax.sharding import PartitionSpec as P

HEADS = 12
FRAMES = 2
PLACES = 196


EPSILON = 1e-06


def times_plain(first_op, second_op):
    return jnp.dot(first_op, second_op, preferred_element_type=jnp.float32)


def times_first(first_op, second_op):
    return lax.dot_general(
        first_op, second_op, (((0,), (0,)), ((), ())), preferred_element_type=jnp.float32
    )


def times_second(first_op, second_op):
    return lax.dot_general(
        first_op, second_op, (((1,), (1,)), ((), ())), preferred_element_type=jnp.float32
    )


def lowered(tensor):
    return tensor.astype(jnp.bfloat16)


def column_sums(tensor):
    return jnp.sum(tensor.astype(jnp.float32), axis=0)


def exact_gelu(tensor):
    return jax.nn.gelu(tensor, approximate=False)


def norm_forward(activations, gain_row, shift_row):
    center = activations - jnp.mean(activations, axis=-1, keepdims=True)
    factor = lax.rsqrt(jnp.mean(center * center, axis=-1, keepdims=True) + EPSILON)
    unit_rows = center * factor
    return (unit_rows * gain_row + shift_row, unit_rows, factor)


def norm_backward(gradient, unit_rows, factor, gain_row):
    scaled = gradient * gain_row
    plain_mean = jnp.mean(scaled, axis=-1, keepdims=True)
    cross_mean = jnp.mean(scaled * unit_rows, axis=-1, keepdims=True)
    return (
        factor * (scaled - plain_mean - unit_rows * cross_mean),
        jnp.sum(gradient * unit_rows, axis=0),
        jnp.sum(gradient, axis=0),
    )


def attend_forward(queries, key_part, values):
    score_scale = queries.shape[-1] ** (-0.5)
    scores = (
        jnp.einsum("bhqd,bhkd->bhqk", queries, key_part, preferred_element_type=jnp.float32)
        * score_scale
    )
    row_peak = jnp.max(scores, axis=-1, keepdims=True)
    powered = jnp.exp(scores - row_peak)
    row_total = jnp.sum(powered, axis=-1, keepdims=True)
    soft_weights = lowered(powered / row_total)
    mixture = jnp.einsum(
        "bhqk,bhkd->bhqd", soft_weights, values, preferred_element_type=jnp.float32
    )
    return (mixture, row_peak + jnp.log(row_total))


def attend_backward(queries, key_part, values, log_total, grad_mixture):
    score_scale = queries.shape[-1] ** (-0.5)
    scores = (
        jnp.einsum("bhqd,bhkd->bhqk", queries, key_part, preferred_element_type=jnp.float32)
        * score_scale
    )
    soft_weights = jnp.exp(scores - log_total)
    grad_soft = jnp.einsum(
        "bhqd,bhkd->bhqk", grad_mixture, values, preferred_element_type=jnp.float32
    )
    grad_values = jnp.einsum(
        "bhqk,bhqd->bhkd", lowered(soft_weights), grad_mixture, preferred_element_type=jnp.float32
    )
    grad_scores = lowered(
        soft_weights * (grad_soft - jnp.sum(grad_soft * soft_weights, axis=-1, keepdims=True))
    )
    grad_queries = (
        jnp.einsum("bhqk,bhkd->bhqd", grad_scores, key_part, preferred_element_type=jnp.float32)
        * score_scale
    )
    grad_keys = (
        jnp.einsum("bhqk,bhqd->bhkd", grad_scores, queries, preferred_element_type=jnp.float32)
        * score_scale
    )
    return (grad_queries, grad_keys, grad_values)


def to_time(matrix):
    return matrix.reshape(FRAMES, PLACES, HEADS, -1).transpose(1, 2, 0, 3)


def from_time(matrix):
    return matrix.transpose(2, 0, 1, 3).reshape(FRAMES * PLACES, -1)


def heads_space(framed):
    return framed.reshape(FRAMES, 1 + PLACES, HEADS, -1).transpose(0, 2, 1, 3)


def to_space(matrix):
    columns = matrix.shape[-1]
    class_rows = jnp.broadcast_to(matrix[:1][None], (FRAMES, 1, columns))
    return heads_space(
        jnp.concatenate([class_rows, matrix[1:].reshape(FRAMES, PLACES, columns)], axis=1)
    )


def from_space(matrix):
    return matrix.transpose(0, 2, 1, 3).reshape(FRAMES, 1 + PLACES, -1)


def fold_space(framed):
    columns = framed.shape[-1]
    return jnp.concatenate(
        [jnp.sum(framed[:, :1], axis=0), framed[:, 1:].reshape(FRAMES * PLACES, columns)], axis=0
    )


def clip_step(operands):
    clip_rows, grad_out, weights = operands
    (
        time_entry,
        time_exit,
        time_mixer,
        space_entry,
        space_exit,
        hidden_expand,
        hidden_reduce,
        bias_rows,
        hidden_bias,
        norm_gain,
        norm_shift,
    ) = weights
    columns = clip_rows.shape[-1]
    inputs = clip_rows.astype(jnp.float32)
    biases = bias_rows.astype(jnp.float32)
    gain_rows = norm_gain.astype(jnp.float32)
    shifts = norm_shift.astype(jnp.float32)
    patches = inputs[1:]
    normed_time, unit_time, factor_time = norm_forward(patches, gain_rows[0], shifts[0])
    normed_time = lowered(normed_time)
    packed = times_plain(normed_time, time_entry)
    query_time = to_time(lowered(packed[:, :columns] + biases[0]))
    key_time = to_time(lowered(packed[:, columns : 2 * columns]))
    value_time = to_time(lowered(packed[:, 2 * columns :] + biases[1]))
    mixture, total_time = attend_forward(query_time, key_time, value_time)
    attended_time = lowered(from_time(mixture))
    exit_time = lowered(times_plain(attended_time, time_exit) + biases[2])
    after_time = patches + (times_plain(exit_time, time_mixer) + biases[3])
    whole_rows = jnp.concatenate([inputs[:1], after_time], axis=0)
    normed_space, unit_space, factor_space = norm_forward(whole_rows, gain_rows[1], shifts[1])
    normed_space = lowered(normed_space)
    packed = times_plain(normed_space, space_entry)
    query_space = to_space(lowered(packed[:, :columns] + biases[4]))
    key_space = to_space(lowered(packed[:, columns : 2 * columns]))
    value_space = to_space(lowered(packed[:, 2 * columns :] + biases[5]))
    mixture, total_space = attend_forward(query_space, key_space, value_space)
    attended_space = lowered(from_space(mixture)).reshape(-1, columns)
    branch_space = (times_plain(attended_space, space_exit) + biases[6]).reshape(
        FRAMES, 1 + PLACES, columns
    )
    update = jnp.concatenate(
        [
            jnp.mean(branch_space[:, 0], axis=0, keepdims=True),
            branch_space[:, 1:].reshape(FRAMES * PLACES, columns),
        ],
        axis=0,
    )
    after_space = whole_rows + update
    normed_hidden, unit_hidden, factor_hidden = norm_forward(after_space, gain_rows[2], shifts[2])
    normed_hidden = lowered(normed_hidden)
    inner_rows = times_plain(normed_hidden, hidden_expand) + hidden_bias.astype(jnp.float32)
    gelu_out, gelu_back = jax.vjp(exact_gelu, inner_rows)
    active = lowered(gelu_out)
    result = after_space + (times_plain(active, hidden_reduce) + biases[7])
    grad_low = lowered(grad_out)
    grad_reduce = times_first(active, grad_low)
    grad_inner = lowered(gelu_back(times_second(grad_low, hidden_reduce))[0])
    grad_expand = times_first(normed_hidden, grad_inner)
    grad_norm, gain_hidden, shift_hidden = norm_backward(
        times_second(grad_inner, hidden_expand), unit_hidden, factor_hidden, gain_rows[2]
    )
    grad_after = grad_out + grad_norm
    class_share = jnp.broadcast_to(grad_after[:1][None] / FRAMES, (FRAMES, 1, columns))
    grad_branch = lowered(
        jnp.concatenate([class_share, grad_after[1:].reshape(FRAMES, PLACES, columns)], axis=1)
    ).reshape(-1, columns)
    grad_space_exit = times_first(attended_space, grad_branch)
    grad_attended = heads_space(
        lowered(times_second(grad_branch, space_exit)).reshape(FRAMES, 1 + PLACES, columns)
    )
    grad_query, grad_key, grad_value = attend_backward(
        query_space, key_space, value_space, total_space, grad_attended
    )
    grad_query_space = lowered(fold_space(from_space(grad_query)))
    grad_value_space = lowered(fold_space(from_space(grad_value)))
    grad_packed = jnp.concatenate(
        [grad_query_space, lowered(fold_space(from_space(grad_key))), grad_value_space], axis=1
    )
    grad_space_entry = times_first(normed_space, grad_packed)
    grad_norm, gain_space, shift_space = norm_backward(
        times_second(grad_packed, space_entry), unit_space, factor_space, gain_rows[1]
    )
    grad_whole = grad_after + grad_norm
    grad_mixer_in = lowered(grad_whole[1:])
    grad_time_mixer = times_first(exit_time, grad_mixer_in)
    grad_exit = lowered(times_second(grad_mixer_in, time_mixer))
    grad_time_exit = times_first(attended_time, grad_exit)
    grad_attended = to_time(lowered(times_second(grad_exit, time_exit)))
    grad_query, grad_key, grad_value = attend_backward(
        query_time, key_time, value_time, total_time, grad_attended
    )
    grad_query_time = lowered(from_time(grad_query))
    grad_value_time = lowered(from_time(grad_value))
    grad_packed = jnp.concatenate(
        [grad_query_time, lowered(from_time(grad_key)), grad_value_time], axis=1
    )
    grad_time_entry = times_first(normed_time, grad_packed)
    grad_norm, gain_time, shift_time = norm_backward(
        times_second(grad_packed, time_entry), unit_time, factor_time, gain_rows[0]
    )
    grad_input = jnp.concatenate([grad_whole[:1], grad_whole[1:] + grad_norm], axis=0)
    grad_bias_rows = jnp.stack(
        [
            column_sums(grad_query_time),
            column_sums(grad_value_time),
            column_sums(grad_exit),
            column_sums(grad_mixer_in),
            column_sums(grad_query_space),
            column_sums(grad_value_space),
            column_sums(grad_branch),
            column_sums(grad_low),
        ]
    )
    gradients = (
        grad_time_entry,
        grad_time_exit,
        grad_time_mixer,
        grad_space_entry,
        grad_space_exit,
        grad_expand,
        grad_reduce,
        grad_bias_rows,
        column_sums(grad_inner),
        jnp.stack([gain_time, gain_space, gain_hidden]),
        jnp.stack([shift_time, shift_space, shift_hidden]),
    )
    return (lowered(result), lowered(grad_input), gradients)


def empty_step(operands):
    clip_rows, grad_out, weights = operands
    return (
        jnp.zeros_like(clip_rows),
        jnp.zeros_like(clip_rows),
        tuple((jnp.zeros(weight.shape, jnp.float32) for weight in weights)),
    )


def local(
    video,
    cotangent,
    live,
    time_entry,
    time_exit,
    time_mixer,
    space_entry,
    space_exit,
    hidden_expand,
    hidden_reduce,
    bias_rows,
    hidden_bias,
    norm_gain,
    norm_shift,
):
    outputs = []
    input_grads = []
    running = None
    for micro_index in range(video.shape[0]):
        gathered = (
            lax.all_gather(time_entry, "shard", axis=0, tiled=True),
            lax.all_gather(time_exit, "shard", axis=0, tiled=True),
            lax.all_gather(time_mixer, "shard", axis=0, tiled=True),
            lax.all_gather(space_entry, "shard", axis=0, tiled=True),
            lax.all_gather(space_exit, "shard", axis=0, tiled=True),
            lax.all_gather(hidden_expand, "shard", axis=0, tiled=True),
            lax.all_gather(hidden_reduce, "shard", axis=0, tiled=True),
            lax.all_gather(bias_rows, "shard", axis=1, tiled=True),
            lax.all_gather(hidden_bias, "shard", axis=0, tiled=True),
            lax.all_gather(norm_gain, "shard", axis=1, tiled=True),
            lax.all_gather(norm_shift, "shard", axis=1, tiled=True),
        )
        result, grad_input, gradients = lax.cond(
            live[micro_index, 0] > 0,
            clip_step,
            empty_step,
            (video[micro_index, 0], cotangent[micro_index, 0].astype(jnp.float32), tuple(gathered)),
        )
        outputs.append(result)
        input_grads.append(grad_input)
        time_part = (
            lax.psum_scatter(gradients[0], "shard", scatter_dimension=0, tiled=True),
            lax.psum_scatter(gradients[1], "shard", scatter_dimension=0, tiled=True),
            lax.psum_scatter(gradients[2], "shard", scatter_dimension=0, tiled=True),
            lax.psum_scatter(gradients[7], "shard", scatter_dimension=1, tiled=True),
            lax.psum_scatter(gradients[9], "shard", scatter_dimension=1, tiled=True),
            lax.psum_scatter(gradients[10], "shard", scatter_dimension=1, tiled=True),
        )
        space_part = (
            lax.psum_scatter(gradients[3], "shard", scatter_dimension=0, tiled=True),
            lax.psum_scatter(gradients[4], "shard", scatter_dimension=0, tiled=True),
        )
        hidden_part = (
            lax.psum_scatter(gradients[5], "shard", scatter_dimension=0, tiled=True),
            lax.psum_scatter(gradients[6], "shard", scatter_dimension=0, tiled=True),
            lax.psum_scatter(gradients[8], "shard", scatter_dimension=0, tiled=True),
        )
        pieces = (
            time_part[0],
            time_part[1],
            time_part[2],
            space_part[0],
            space_part[1],
            hidden_part[0],
            hidden_part[1],
            time_part[3],
            hidden_part[2],
            time_part[4],
            time_part[5],
        )
        running = (
            pieces
            if running is None
            else tuple((earlier + later for earlier, later in zip(running, pieces)))
        )
    totals = (
        lax.psum(running[0].astype(jnp.bfloat16), "grp").astype(jnp.float32),
        lax.psum(running[1].astype(jnp.bfloat16), "grp").astype(jnp.float32),
        lax.psum(running[2].astype(jnp.bfloat16), "grp").astype(jnp.float32),
        lax.psum(running[3].astype(jnp.bfloat16), "grp").astype(jnp.float32),
        lax.psum(running[4].astype(jnp.bfloat16), "grp").astype(jnp.float32),
        lax.psum(running[5].astype(jnp.bfloat16), "grp").astype(jnp.float32),
        lax.psum(running[6].astype(jnp.bfloat16), "grp").astype(jnp.float32),
        lax.psum(running[7].astype(jnp.bfloat16), "grp").astype(jnp.float32),
        lax.psum(running[8].astype(jnp.bfloat16), "grp").astype(jnp.float32),
        lax.psum(running[9].astype(jnp.bfloat16), "grp").astype(jnp.float32),
        lax.psum(running[10].astype(jnp.bfloat16), "grp").astype(jnp.float32),
    )
    return (
        jnp.stack(outputs)[:, None],
        jnp.stack(input_grads)[:, None],
        totals[0],
        totals[1],
        totals[2],
        totals[3],
        totals[4],
        totals[5],
        totals[6],
        totals[7],
        totals[8],
        totals[9],
        totals[10],
    )


def solution(mesh):
    placed = (
        P(None, ("grp", "shard"), None, None),
        P(None, ("grp", "shard"), None, None),
        P(None, ("grp", "shard")),
        P("shard", None),
        P("shard", None),
        P("shard", None),
        P("shard", None),
        P("shard", None),
        P("shard", None),
        P("shard", None),
        P(None, "shard"),
        P("shard"),
        P(None, "shard"),
        P(None, "shard"),
    )
    return jax.shard_map(
        local,
        mesh=mesh,
        in_specs=placed,
        out_specs=(
            P(None, ("grp", "shard"), None, None),
            P(None, ("grp", "shard"), None, None),
            P("shard", None),
            P("shard", None),
            P("shard", None),
            P("shard", None),
            P("shard", None),
            P("shard", None),
            P("shard", None),
            P(None, "shard"),
            P("shard"),
            P(None, "shard"),
            P(None, "shard"),
        ),
        check_vma=False,
    )
```

profile of v0, /device:TPU:0, one launch (start us, length us, event | category | flops | bytes accessed | tf_op | source)
XLA Modules:
  0.0 1499.6 jit_solution(1470953704916013711)
XLA Ops:
  12.0 10.4 all-gather.2
  22.5 8.9 all-gather.3
  31.4 7.9 all-gather
  39.5 8.9 all-gather.1
  50.3 12.4 all-gather.16.cloned.1.call-done
  62.7 26.0 %all-gather.20.cloned.1.call-done = bf16[768,768]{1,0:T(8,128)(2,1)} async-done(((bf16[96,768]{1,0:T(8,128)(2,1)}), bf16[768,768]{1,0:T(8,128)(2,1)}) %all-gather.20.cloned.1.call-update) | async-done | bytes 1179664 | tf_op jit(solution)/shard_map/all_gather | solution.py:300
  88.7 35.7 %all-gather.12.cloned.1.call-done = bf16[768,2304]{1,0:T(8,128)(2,1)} async-done(((bf16[96,2304]{1,0:T(8,128)(2,1)}), bf16[768,2304]{1,0:T(8,128)(2,1)}) %all-gather.12.cloned.1.call-update) | async-done | bytes 3538960 | tf_op jit(solution)/shard_map/all_gather | solution.py:296
  124.5 35.7 %all-gather.18.cloned.1.call-done = bf16[768,2304]{1,0:T(8,128)(2,1)} async-done(((bf16[96,2304]{1,0:T(8,128)(2,1)}), bf16[768,2304]{1,0:T(8,128)(2,1)}) %all-gather.18.cloned.1.call-update) | async-done | bytes 3538960 | tf_op jit(solution)/shard_map/all_gather | solution.py:299
  160.2 40.7 %all-gather.22.cloned.1.call-done = bf16[768,3072]{1,0:T(8,128)(2,1)} async-done(((bf16[96,3072]{1,0:T(8,128)(2,1)}), bf16[768,3072]{1,0:T(8,128)(2,1)}) %all-gather.22.cloned.1.call-update) | async-done | bytes 4718608 | tf_op jit(solution)/shard_map/all_gather | solution.py:301
  200.9 40.8 %all-gather.24.cloned.1.call-done = bf16[3072,768]{1,0:T(8,128)(2,1)} async-done(((bf16[384,768]{1,0:T(8,128)(2,1)}), bf16[3072,768]{1,0:T(8,128)(2,1)}) %all-gather.24.cloned.1.call-update) | async-done | bytes 4718608 | tf_op jit(solution)/shard_map/all_gather | solution.py:302
  241.7 22.8 %conditional.2 = (f32[768,2304]{1,0:T(8,128)S(1)}, f32[768,768]{1,0:T(8,128)}, f32[768,768]{1,0:T(8,128)}, f32[768,2304]{1,0:T(8,128)S(1)}, f32[768,768]{1,0:T(8...) conditional(s32[]{:T(128)} %bitcast.60, () %tuple.32, ...), branch_computations={%region_0.0_spmd, %region_1.0_spmd} | conditional | flops 24550756352 | bytes 628997312 | solution.py:308
  272.6 295.1 %conditional.3 = (f32[768,2304]{1,0:T(8,128)}, f32[768,768]{1,0:T(8,128)}, f32[768,768]{1,0:T(8,128)}, f32[768,2304]{1,0:T(8,128)}, f32[768,768]{1,0:T(8,128)}, ...) conditional(s32[]{:T(128)} %bitcast.70, () %tuple.34, ...), branch_computations={%region_39.0_spmd, %region_40.78_spmd} | conditional | flops 24550756352 | bytes 629083456 | solution.py:308
  287.0 6.0 fusion.120
  293.1 5.3 fusion.77
  300.6 7.9 fusion.72
  369.0 16.1 %multiply_convert_fusion.5 = (bf16[393,3072]{1,0:T(8,128)(2,1)}, f32[393,3072]{1,0:T(8,128)S(1)}, f32[393,3072]{1,0:T(8,128)}) fusion(f32[3072]{0:T(1024)S(1)} %convert_element_type.394, bf16[768,3072]{1,0:T(8,128)(2,1)} %get-tuple-element.89, f32[393,768]{1,0:T(8,128)S(1)} %get-tuple-element.391, f32[768]{0:T(1024)S(1)} %get-tuple-element.366, ...), kind=kOutput, calls=%fused_computation.189 | convolution fusion | flops 1935597312 | bytes 18020424 | tf_op jit(solution)/shard_map/cond/branch_1_fun/dot_general | solution.py:15
  385.3 6.4 convert_reduce_fusion.9
  408.3 4.7 multiply_reduce_fusion.15
  443.9 4.4 multiply_reduce_fusion.19
  455.7 5.3 copy.462
  463.7 5.8 convert_reduce_fusion.10
  469.5 4.7 copy.469
  476.7 12.2 multiply_reduce_fusion.17
  488.9 6.1 multiply_convert_fusion.9
  499.9 4.7 copy.467
  507.8 5.9 convert_reduce_fusion.11
  513.7 4.7 copy.465
  532.2 8.6 fusion.109
  540.9 5.5 fusion.107
  546.4 5.4 fusion.94
  562.4 5.0 fusion.92
  580.2 8.8 add.462
  589.0 8.8 add.465
  597.9 12.8 add.467
  610.7 11.2 add.468
  627.9 247.6 %reduce-scatter.19.cloned.1.call-done = f32[96,768]{1,0:T(8,128)} async-done(((f32[768,768]{1,0:T(8,128)}), f32[96,768]{1,0:T(8,128)}) %reduce-scatter.19.cloned.1.call-update) | async-done | bytes 294928 | tf_op jit(solution)/shard_map/reduce_scatter | solution.py:318
  877.2 44.6 %reduce-scatter.21.cloned.1.call-done = f32[96,768]{1,0:T(8,128)} async-done(((f32[768,768]{1,0:T(8,128)}), f32[96,768]{1,0:T(8,128)}) %reduce-scatter.21.cloned.1.call-update) | async-done | bytes 294928 | tf_op jit(solution)/shard_map/reduce_scatter | solution.py:319
  923.4 44.1 %reduce-scatter.25.cloned.1.call-done = f32[96,768]{1,0:T(8,128)} async-done(((f32[768,768]{1,0:T(8,128)}), f32[96,768]{1,0:T(8,128)}) %reduce-scatter.25.cloned.1.call-update) | async-done | bytes 294928 | tf_op jit(solution)/shard_map/reduce_scatter | solution.py:326
  969.1 67.8 %reduce-scatter.17.cloned.1.call-done = f32[96,2304]{1,0:T(8,128)} async-done(((f32[768,2304]{1,0:T(8,128)}), f32[96,2304]{1,0:T(8,128)}) %reduce-scatter.17.cloned.1.call-update) | async-done | bytes 884752 | tf_op jit(solution)/shard_map/reduce_scatter | solution.py:317
  1038.9 66.9 %reduce-scatter.23.cloned.1.call-done = f32[96,2304]{1,0:T(8,128)} async-done(((f32[768,2304]{1,0:T(8,128)}), f32[96,2304]{1,0:T(8,128)}) %reduce-scatter.23.cloned.1.call-update) | async-done | bytes 884752 | tf_op jit(solution)/shard_map/reduce_scatter | solution.py:325
  1107.8 78.4 %reduce-scatter.27.cloned.1.call-done = f32[96,3072]{1,0:T(8,128)} async-done(((f32[768,3072]{1,0:T(8,128)}), f32[96,3072]{1,0:T(8,128)}) %reduce-scatter.27.cloned.1.call-update) | async-done | bytes 1179664 | tf_op jit(solution)/shard_map/reduce_scatter | solution.py:329
  1188.4 78.1 %reduce-scatter.29.cloned.1.call-done = f32[384,768]{1,0:T(8,128)} async-done(((f32[3072,768]{1,0:T(8,128)}), f32[384,768]{1,0:T(8,128)}) %reduce-scatter.29.cloned.1.call-update) | async-done | bytes 1179664 | tf_op jit(solution)/shard_map/reduce_scatter | solution.py:330
  1271.2 23.1 %all-reduce = bf16[3072]{0:T(1024)(128)(2,1)S(1)} all-reduce(f32[3072]{0:T(1024)S(1)} %add.470), channel_id=21, replica_groups=mesh['grp'=4,'shard'=8] {'shard'}, use_global_device_ids=true, to_apply=%region_102.0.clone | all-reduce | flops 3072 | bytes 18432
  1294.5 7.3 maximum_bitcast_fusion.18
  1304.4 36.2 %reduce-scatter.35.cloned.1.call-done = f32[96,3]{1,0:T(8,128)} async-done(((f32[768,3]{1,0:T(8,128)}), f32[96,3]{1,0:T(8,128)}) %reduce-scatter.35.cloned.1.call-update) | async-done | bytes 1168
  1341.5 36.2 %reduce-scatter.31.cloned.1.call-done = f32[96,8]{1,0:T(8,128)} async-done(((f32[768,8]{1,0:T(8,128)}), f32[96,8]{1,0:T(8,128)}) %reduce-scatter.31.cloned.1.call-update) | async-done | bytes 3088
  1378.6 11.8 all-reduce.1
  1392.7 92.0 %all-reduce.5.cloned.1.call-done = (bf16[96,2304]{1,0:T(8,128)(2,1)}, bf16[96,768]{1,0:T(8,128)(2,1)}, bf16[96,768]{1,0:T(8,128)(2,1)}, bf16[96,2304]{1,0:T(8,12...) async-done(((bf16[96,2304]{1,0:T(8,128)(2,1)}, bf16[96,768]{1,0:T(8,128)(2,1)}, bf16[96,768]{1,0:T(8,128)(2,1)}, ...) | async-done | bytes 2506768 | tf_op jit(solution)/shard_map/psum | solution.py:352
  (445 shorter events, 247.2 us)
Async XLA Ops:
  7.2 15.3 %copy-start.145 = (bf16[384]{0:T(512)(128)(2,1)S(1)}, bf16[384]{0:T(512)(128)(2,1)}, u32[]{:S(2)}) copy-start(bf16[384]{0:T(512)(128)(2,1)} %param.29) | copy-start | bytes 2308
  7.2 24.2 %copy-start.143 = (bf16[3,96]{1,0:T(4,128)(2,1)S(1)}, bf16[3,96]{1,0:T(4,128)(2,1)}, u32[]{:S(2)}) copy-start(bf16[3,96]{1,0:T(4,128)(2,1)} %param.30) | copy-start | bytes 1732
  7.2 32.2 %copy-start.144 = (bf16[3,96]{1,0:T(4,128)(2,1)S(1)}, bf16[3,96]{1,0:T(4,128)(2,1)}, u32[]{:S(2)}) copy-start(bf16[3,96]{1,0:T(4,128)(2,1)} %param.31) | copy-start | bytes 1732
  7.2 41.2 %copy-start.142 = (s32[2,1]{0,1:T(1,128)S(1)}, s32[2,1]{0,1:T(1,128)}, u32[]{:S(2)}) copy-start(s32[2,1]{0,1:T(1,128)} %param.20) | copy-start | bytes 28
  7.2 234.5 %copy-start.43 = (bf16[2,1,393,768]{3,0,2,1:T(2,128)(2,1)S(1)}, bf16[2,1,393,768]{3,0,2,1:T(2,128)(2,1)}, u32[]{:S(2)}) copy-start(bf16[2,1,393,768]{3,0,2,1:T(2,128)(2,1)} %param.18) | copy-start | bytes 3621892
  7.2 43.1 %all-gather.14.cloned.1.call-start = ((), (), s32[]{:S(2)}) async-start(), calls=%async_computation.11 | async-start | bytes 1327104 | tf_op jit(solution)/shard_map/all_gather | solution.py:297
  8.0 54.8 %all-gather.16.cloned.1.call-start = ((), (), s32[]{:S(2)}) async-start(), calls=%async_computation.12 | async-start | bytes 1327104 | tf_op jit(solution)/shard_map/all_gather | solution.py:298
  8.7 80.0 %all-gather.20.cloned.1.call-start = ((), (), s32[]{:S(2)}) async-start(), calls=%async_computation.14 | async-start | bytes 1327104 | tf_op jit(solution)/shard_map/all_gather | solution.py:300
  9.5 115.0 %all-gather.12.cloned.1.call-start = ((), (), s32[]{:S(2)}) async-start(), calls=%async_computation.10 | async-start | bytes 3981312 | tf_op jit(solution)/shard_map/all_gather | solution.py:296
  10.0 150.2 %all-gather.18.cloned.1.call-start = ((), (), s32[]{:S(2)}) async-start(), calls=%async_computation.13 | async-start | bytes 3981312 | tf_op jit(solution)/shard_map/all_gather | solution.py:299
  10.6 190.3 %all-gather.22.cloned.1.call-start = ((), (), s32[]{:S(2)}) async-start(), calls=%async_computation.15 | async-start | bytes 5308416 | tf_op jit(solution)/shard_map/all_gather | solution.py:301
  11.2 230.5 %all-gather.24.cloned.1.call-start = ((), (), s32[]{:S(2)}) async-start(), calls=%async_computation.16 | async-start | bytes 5308416 | tf_op jit(solution)/shard_map/all_gather | solution.py:302
  11.9 863.6 %reduce-scatter.19.cloned.1.call-start = ((), (), s32[]{:S(2)}) async-start(), calls=%async_computation.18 | async-start | bytes 2654208 | tf_op jit(solution)/shard_map/reduce_scatter | solution.py:318
  22.5 219.3 %copy-start.114 = (bf16[768,8]{0,1:T(8,128)(2,1)}, bf16[768,8]{0,1:T(8,128)(2,1)S(1)}, u32[]{:S(2)}) copy-start(bf16[768,8]{0,1:T(8,128)(2,1)S(1)} %reshape.501) | copy-start | bytes 36868
  39.4 202.3 %copy-start.116 = (bf16[768,3]{0,1:T(4,128)(2,1)}, bf16[768,3]{0,1:T(4,128)(2,1)S(1)}, u32[]{:S(2)}) copy-start(bf16[768,3]{0,1:T(4,128)(2,1)S(1)} %reshape.497) | copy-start | bytes 13828
  48.4 193.3 %copy-start.118 = (bf16[768,3]{0,1:T(4,128)(2,1)}, bf16[768,3]{0,1:T(4,128)(2,1)S(1)}, u32[]{:S(2)}) copy-start(bf16[768,3]{0,1:T(4,128)(2,1)S(1)} %reshape.499) | copy-start | bytes 13828
  264.5 5.7 copy-start.3
  264.5 8.1 copy-start.4
  300.6 7.9 copy-start.95
  326.5 11.1 copy-start.26
  366.9 24.8 %slice-start.6 = ((s8[4718592]{0:T(1024)(128)(4,1)}), s8[4194304]{0:T(1024)(128)(4,1)S(1)}, s32[]{:S(2)}) async-start(s8[4718592]{0:T(1024)(128)(4,1)} %bitcast.376), calls=%async_computation.34 | async-start | bytes 8388608 | tf_op jit(solution)/shard_map/cond
  368.7 25.6 %copy-start.15 = (f32[393,768]{1,0:T(8,128)}, f32[393,768]{1,0:T(8,128)S(1)}, u32[]{:S(2)}) copy-start(f32[393,768]{1,0:T(8,128)S(1)} %get-tuple-element.391) | copy-start | bytes 3621892 | tf_op jit(solution)/shard_map/cond
  369.0 16.3 %slice-start.12 = ((s8[4718592]{0:T(1024)(128)(4,1)}), s8[4194304]{0:T(1024)(128)(4,1)S(1)}, s32[]{:S(2)}) async-start(s8[4718592]{0:T(1024)(128)(4,1)} %bitcast.382), calls=%async_computation.40 | async-start | bytes 8388608 | tf_op jit(solution)/shard_map/cond
  369.0 16.1 %copy-start.45 = (bf16[2,1,393,768]{3,0,2,1:T(2,128)(2,1)S(1)}, bf16[2,1,393,768]{3,0,2,1:T(2,128)(2,1)}, u32[]{:S(2)}) copy-start(bf16[2,1,393,768]{3,0,2,1:T(2,128)(2,1)} %get-tuple-element.305) | copy-start | bytes 3621892 | tf_op jit(solution)/shard_map/cond
  369.0 16.2 %slice-start.13 = ((s8[4718592]{0:T(1024)(128)(4,1)}), s8[524288]{0:T(1024)(128)(4,1)S(1)}, s32[]{:S(2)}) async-start(s8[4718592]{0:T(1024)(128)(4,1)} %bitcast.382), calls=%async_computation.41 | async-start | bytes 1048576 | tf_op jit(solution)/shard_map/cond
  369.0 22.7 %slice-start.7 = ((s8[4718592]{0:T(1024)(128)(4,1)}), s8[524288]{0:T(1024)(128)(4,1)S(1)}, s32[]{:S(2)}) async-start(s8[4718592]{0:T(1024)(128)(4,1)} %bitcast.376), calls=%async_computation.35 | async-start | bytes 1048576 | tf_op jit(solution)/shard_map/cond
  385.2 9.0 copy-start.68
  463.7 5.8 copy-start.32
  488.9 7.2 copy-start.93
  532.2 8.6 copy-start.85
  532.2 8.6 copy-start.99
  532.2 19.5 %slice-start.14 = ((s8[4718592]{0:T(1024)(128)(4,1)}), s8[4194304]{0:T(1024)(128)(4,1)S(1)}, s32[]{:S(2)}) async-start(s8[4718592]{0:T(1024)(128)(4,1)} %bitcast.384), calls=%async_computation.42 | async-start | bytes 8388608 | tf_op jit(solution)/shard_map/cond
  540.8 5.5 copy-start.110
  540.8 5.5 copy-start.140
  540.9 10.9 slice-start.15
  546.3 5.4 copy-start.16
  546.4 5.4 copy-start.136
  546.4 5.4 copy-start.156
  571.8 349.9 %reduce-scatter.21.cloned.1.call-start = ((), (), s32[]{:S(2)}) async-start(), calls=%async_computation.19 | async-start | bytes 2654208 | tf_op jit(solution)/shard_map/reduce_scatter | solution.py:319
  576.0 391.5 %reduce-scatter.25.cloned.1.call-start = ((), (), s32[]{:S(2)}) async-start(), calls=%async_computation.21 | async-start | bytes 2654208 | tf_op jit(solution)/shard_map/reduce_scatter | solution.py:326
  580.1 456.8 %reduce-scatter.17.cloned.1.call-start = ((), (), s32[]{:S(2)}) async-start(), calls=%async_computation.17 | async-start | bytes 7962624 | tf_op jit(solution)/shard_map/reduce_scatter | solution.py:317
  589.0 516.8 %reduce-scatter.23.cloned.1.call-start = ((), (), s32[]{:S(2)}) async-start(), calls=%async_computation.20 | async-start | bytes 7962624 | tf_op jit(solution)/shard_map/reduce_scatter | solution.py:325
  597.8 588.4 %reduce-scatter.27.cloned.1.call-start = ((), (), s32[]{:S(2)}) async-start(), calls=%async_computation.22 | async-start | bytes 10616832 | tf_op jit(solution)/shard_map/reduce_scatter | solution.py:329
  610.7 655.8 %reduce-scatter.29.cloned.1.call-start = ((), (), s32[]{:S(2)}) async-start(), calls=%async_computation.23 | async-start | bytes 10616832 | tf_op jit(solution)/shard_map/reduce_scatter | solution.py:330
  621.9 681.6 %reduce-scatter.33.cloned.1.call-start = ((), (), s32[]{:S(2)}) async-start(), calls=%async_computation.25 | async-start | bytes 442368
  624.3 716.3 %reduce-scatter.35.cloned.1.call-start = ((), (), s32[]{:S(2)}) async-start(), calls=%async_computation.26 | async-start | bytes 442368
  626.1 751.6 %reduce-scatter.31.cloned.1.call-start = ((), (), s32[]{:S(2)}) async-start(), calls=%async_computation.24 | async-start | bytes 442368
  627.8 856.9 %all-reduce.5.cloned.1.call-start = ((), (), s32[]{:S(2)}) async-start(), calls=%async_computation.27 | async-start | bytes 5013504 | tf_op jit(solution)/shard_map/psum | solution.py:352
  (70 other events, 166.4 us)
Sparse Core Ops, SparseCore 0:
  10.0 26.7 all-gather.13
  38.6 24.0 all-gather.15
  64.6 24.0 all-gather.19
  90.5 33.9 all-gather.11
  126.2 33.9 all-gather.17
  161.9 38.9 all-gather.21
  202.8 38.9 all-gather.23
  571.9 303.5 reduce-scatter.18
  879.2 42.4 reduce-scatter.20
  924.9 42.4 reduce-scatter.24
  971.4 65.4 reduce-scatter.16
  1040.3 65.4 reduce-scatter.22
  1109.7 76.4 reduce-scatter.26
  1190.0 76.4 reduce-scatter.28
  1269.7 33.8 reduce-scatter.32
  1306.8 33.8 reduce-scatter.34
  1343.8 33.8 reduce-scatter.30
  1381.9 102.7 all-reduce.4
where the time goes:
time: 1510 us; the launch traced here: 1500 us
  waiting for transfers between devices  990 us (66%)
  local copies, waits for them, and re-layouts  154 us (10%)
  matrix products  141 us (9%)
  other arithmetic  119 us (8%)
  blocking collectives  71 us (5%)
  between operations  17 us (1%)
    reduce_scatter x1, waiting for transfers between devices, local(): lax.psum_scatter(gradients[1], 'shard', scatter_dimension=0, tiled=True)  248 us
    psum x1, waiting for transfers between devices, local(): lax.psum(running[0].astype(jnp.bfloat16), 'grp').astype(jnp.float32)  92 us
    unnamed x21, waiting for transfers between devices  78.7 us
    reduce_scatter x1, waiting for transfers between devices, local(): lax.psum_scatter(gradients[5], 'shard', scatter_dimension=0, tiled=True)  78.4 us
    reduce_scatter x1, waiting for transfers between devices, local(): lax.psum_scatter(gradients[6], 'shard', scatter_dimension=0, tiled=True)  78.1 us
    reduce_scatter x1, waiting for transfers between devices, local(): lax.psum_scatter(gradients[0], 'shard', scatter_dimension=0, tiled=True)  67.8 us
    reduce_scatter x1, waiting for transfers between devices, local(): lax.psum_scatter(gradients[3], 'shard', scatter_dimension=0, tiled=True)  66.9 us
    add x11, other arithmetic, local(): earlier + later  56.6 us
  transfers between devices with their start and end apart: 18, of which 17 were waited for; matrix products, arithmetic and copies ran while one was open for 5% of the time, Pallas kernels for 0%

commit v1 on v0

v1 whole, which is shorter than its diff:
```python
import functools

import jax
import jax.numpy as jnp
from jax import lax
from jax.experimental import pallas as pl
from jax.experimental.pallas import tpu as pltpu
from jax.sharding import PartitionSpec as P

FRAMES = 2
PLACES = 196
HD = 64
EPSILON = 1e-06
BLOCK = 208
EDGE = 192
CLASS = PLACES - EDGE
CHUNK = 64
WIDE = 256
BF = jnp.bfloat16
F32 = jnp.float32
VMEM_LIMIT = 60 * 1024 * 1024


def nn(a, b):
    return lax.dot_general(a, b, (((1,), (0,)), ((), ())), preferred_element_type=F32)


def nt(a, b):
    return lax.dot_general(a, b, (((1,), (1,)), ((), ())), preferred_element_type=F32)


def tn(a, b):
    return lax.dot_general(a, b, (((0,), (0,)), ((), ())), preferred_element_type=F32)


def loop(count, body):
    def step(i, carry):
        body(i)
        return carry

    lax.fori_loop(0, count, step, 0)


def rows_of(i, size):
    return pl.ds(pl.multiple_of(i * size, size), size)


def cols_of(i, size, base=0):
    return pl.ds(pl.multiple_of(base + i * size, 128), size)


def unit(x):
    center = x - jnp.mean(x, axis=-1, keepdims=True)
    factor = lax.rsqrt(jnp.mean(center * center, axis=-1, keepdims=True) + EPSILON)
    return center * factor, factor


def norm_chunks(src, dst, gain, shift):
    def body(i):
        at = rows_of(i, CHUNK)
        w, _ = unit(src[at, :].astype(F32))
        dst[at, :] = (w * gain + shift).astype(BF)

    loop(src.shape[0] // CHUNK, body)


def fold(x):
    return jnp.sum(x.reshape(x.shape[0] // 8, 8, x.shape[1]), axis=0)


def norm_back_chunks(gn_ref, x_ref, gain, base_of, store):
    columns = x_ref.shape[1]

    def body(i, carry):
        gain_sum, shift_sum = carry
        at = rows_of(i, CHUNK)
        gn = gn_ref[at, :]
        w, factor = unit(x_ref[at, :].astype(F32))
        scaled = gn * gain
        plain = jnp.mean(scaled, axis=-1, keepdims=True)
        cross = jnp.mean(scaled * w, axis=-1, keepdims=True)
        store(at, base_of(at) + factor * (scaled - plain - w * cross))
        return gain_sum + fold(gn * w), shift_sum + fold(gn)

    zero = jnp.zeros((8, columns), F32)
    gain_sum, shift_sum = lax.fori_loop(0, x_ref.shape[0] // CHUNK, body, (zero, zero))
    return jnp.sum(gain_sum, axis=0, keepdims=True), jnp.sum(shift_sum, axis=0, keepdims=True)


def column_sums(ref, start, size):
    def body(i, total):
        return total + fold(ref[rows_of(i, CHUNK), start : start + size].astype(F32))

    total = lax.fori_loop(0, ref.shape[0] // CHUNK, body, jnp.zeros((8, size), F32))
    return jnp.sum(total, axis=0, keepdims=True)


def head_map(columns):
    feature = lax.broadcasted_iota(jnp.int32, (columns, 128), 0) // HD
    head = lax.broadcasted_iota(jnp.int32, (columns, 128), 1)
    return (feature == head).astype(BF)


def split_store(high, low, at, value):
    top = value.astype(BF)
    high[at, :] = top
    low[at, :] = (value - top.astype(F32)).astype(BF)


def row_in_block(i, size, columns):
    return (i * size + lax.broadcasted_iota(jnp.int32, (size, columns), 0)) % BLOCK


def load(loads, sems):
    copies = [pltpu.make_async_copy(s, d, sems.at[n]) for n, (s, d) in enumerate(loads)]
    for copy in copies:
        copy.start()
    return copies


def wait(copies):
    for copy in copies:
        copy.wait()


def time_forward(x_ref, small_ref, w_ref, nt_ref, qkv_ref, o_ref, e_ref, p_ref, y_ref, w, high, low, sems):
    columns = x_ref.shape[1]
    copies = load([(w_ref, w)], sems)
    norm_chunks(x_ref, nt_ref, small_ref[12:13, :], small_ref[15:16, :])
    wait(copies)
    zero_bias = jnp.zeros((1, columns), F32)
    for part, bias in enumerate((small_ref[0:1, :], zero_bias, small_ref[1:2, :])):
        for j in range(columns // WIDE):
            at = slice(j * WIDE, (j + 1) * WIDE)
            to = slice(part * columns + j * WIDE, part * columns + (j + 1) * WIDE)
            qkv_ref[:, to] = (nn(nt_ref[...], w[:, to]) + bias[:, at]).astype(BF)
    heads = head_map(columns)
    small = 16
    for clip in range(x_ref.shape[0] // (FRAMES * BLOCK)):
        first = clip * FRAMES * BLOCK

        def products(i, first=first):
            at = [pl.ds(pl.multiple_of(first + f * BLOCK + i * small, small), small) for f in range(FRAMES)]
            q = [qkv_ref[a, 0:columns].astype(F32) for a in at]
            k = [qkv_ref[a, columns : 2 * columns].astype(F32) for a in at]
            for f in range(FRAMES):
                for g in range(FRAMES):
                    to = pl.ds(pl.multiple_of((f * FRAMES + g) * BLOCK + i * small, small), small)
                    split_store(high, low, to, q[f] * k[g])

        loop(BLOCK // small, products)
        scores = (nn(high[...], heads) + nn(low[...], heads)) * HD ** (-0.5)
        s = [scores[n * BLOCK : (n + 1) * BLOCK, :] for n in range(4)]
        for f in range(FRAMES):
            peak = jnp.maximum(s[2 * f], s[2 * f + 1])
            powered = [jnp.exp(s[2 * f] - peak), jnp.exp(s[2 * f + 1] - peak)]
            total = powered[0] + powered[1]
            for g in range(FRAMES):
                to = slice(clip * 4 * BLOCK + (2 * f + g) * BLOCK, clip * 4 * BLOCK + (2 * f + g + 1) * BLOCK)
                p_ref[to, :] = powered[g] / total
        spread = p_ref[clip * 4 * BLOCK : (clip + 1) * 4 * BLOCK, :].astype(BF)
        for j in range(columns // WIDE):
            at = slice(j * WIDE, (j + 1) * WIDE)
            high[:, at] = nt(spread, heads[at, :]).astype(BF)

        def mixture(i, first=first):
            at = [pl.ds(pl.multiple_of(first + f * BLOCK + i * small, small), small) for f in range(FRAMES)]
            v = [qkv_ref[a, 2 * columns : 3 * columns].astype(F32) for a in at]
            for f in range(FRAMES):
                total = 0.0
                for g in range(FRAMES):
                    p = high[pl.ds(pl.multiple_of((f * FRAMES + g) * BLOCK + i * small, small), small), :]
                    total = total + p.astype(F32) * v[g]
                o_ref[at[f], :] = total.astype(BF)

        loop(BLOCK // small, mixture)
    for j in range(columns // WIDE):
        at = slice(j * WIDE, (j + 1) * WIDE)
        from_w = slice(3 * columns + j * WIDE, 3 * columns + (j + 1) * WIDE)
        e_ref[:, at] = (nn(o_ref[...], w[:, from_w]) + small_ref[2:3, at]).astype(BF)
    patch = row_in_block(0, x_ref.shape[0], WIDE) < PLACES
    for j in range(columns // WIDE):
        at = slice(j * WIDE, (j + 1) * WIDE)
        from_w = slice(4 * columns + j * WIDE, 4 * columns + (j + 1) * WIDE)
        branch = nn(e_ref[...], w[:, from_w]) + small_ref[3:4, at]
        y_ref[:, at] = x_ref[:, at].astype(F32) + jnp.where(patch, branch, 0.0)


def half_masks():
    lane = lax.broadcasted_iota(jnp.int32, (1, 128), 1)
    return (lane < HD).astype(BF), (lane >= HD).astype(BF)


def space_forward(y_ref, small_ref, w_ref, ns_ref, qkv_ref, p_ref, o_ref, z_ref, w, sems):
    columns = y_ref.shape[1]
    blocks = y_ref.shape[0] // BLOCK
    pairs = columns // 128
    copies = load([(w_ref, w)], sems)
    norm_chunks(y_ref, ns_ref, small_ref[13:14, :], small_ref[16:17, :])
    wait(copies)
    zero_bias = jnp.zeros((1, columns), F32)
    for part, bias in enumerate((small_ref[4:5, :], zero_bias, small_ref[5:6, :])):
        for j in range(columns // WIDE):
            at = slice(j * WIDE, (j + 1) * WIDE)
            to = slice(part * columns + j * WIDE, part * columns + (j + 1) * WIDE)
            qkv_ref[:, to] = (nn(ns_ref[...], w[:, to]) + bias[:, at]).astype(BF)
    masks = half_masks()
    first = lax.broadcasted_iota(jnp.int32, (BLOCK, 128), 1) < HD
    column = lax.broadcasted_iota(jnp.int32, (1, BLOCK), 1)
    hidden = jnp.where(column <= PLACES, 0.0, -1e30)

    def attend(n):
        block, pair = n // pairs, n % pairs
        at = rows_of(block, BLOCK)
        q = qkv_ref[at, cols_of(pair, 128)]
        k = qkv_ref[at, cols_of(pair, 128, columns)]
        v = qkv_ref[at, cols_of(pair, 128, 2 * columns)]
        outs = []
        for half in range(2):
            scores = nt(q * masks[half], k) * HD ** (-0.5) + hidden
            powered = jnp.exp(scores - jnp.max(scores, axis=-1, keepdims=True))
            weights = (powered * (1.0 / jnp.sum(powered, axis=-1, keepdims=True))).astype(BF)
            p_ref[2 * n + half] = weights
            outs.append(nn(weights, v))
        o_ref[at, cols_of(pair, 128)] = jnp.where(first, outs[0], outs[1]).astype(BF)

    loop(blocks * pairs, attend)
    is_class = lax.broadcasted_iota(jnp.int32, (BLOCK - EDGE, WIDE), 0) == CLASS
    for j in range(columns // WIDE):
        at = slice(j * WIDE, (j + 1) * WIDE)
        from_w = slice(3 * columns + j * WIDE, 3 * columns + (j + 1) * WIDE)
        branch = nn(o_ref[...], w[:, from_w]) + small_ref[6:7, at]
        z_ref[:, at] = y_ref[:, at] + branch
        for clip in range(blocks // FRAMES):
            edges = [slice((clip * FRAMES + f) * BLOCK + EDGE, (clip * FRAMES + f + 1) * BLOCK) for f in range(FRAMES)]
            mean = (branch[edges[0], :] + branch[edges[1], :]) * (1.0 / FRAMES)
            for edge in edges:
                z_ref[edge, at] = y_ref[edge, at] + jnp.where(is_class, mean, branch[edge, :])


def gelu_both(h):
    cdf = 0.5 * (1.0 + lax.erf(h * 0.5**0.5))
    density = jnp.exp(h * h * -0.5) * 0.3989422804014327
    return h * cdf, cdf + h * density


def feed(z_ref, g_ref, small_ref, hb_ref, we_ref, wr_ref, out_ref, gz_ref, sums_ref, ghb_ref, dwe_ref, dwr_ref, we, wr, nm, a, gh, gn, sems):
    columns = z_ref.shape[1]
    units = we.shape[1]
    copies = load([(we_ref, we), (wr_ref, wr)], sems)
    norm_chunks(z_ref, nm, small_ref[14:15, :], small_ref[17:18, :])
    wait(copies)

    def inner(j):
        at = cols_of(j, WIDE)
        h = nn(nm[...], we[:, at]) + hb_ref[0:1, at]
        active, slope = gelu_both(h)
        a[:, at] = active.astype(BF)
        gh[:, at] = (nt(g_ref[...], wr[rows_of(j, WIDE), :]) * slope).astype(BF)

    loop(units // WIDE, inner)

    def outer(j):
        at = cols_of(j, WIDE)
        dwr_ref[rows_of(j, WIDE), :] = tn(a[:, at], g_ref[...]).astype(BF)
        block = gh[:, at]
        dwe_ref[:, at] = tn(nm[...], block).astype(BF)
        ghb_ref[0:1, at] = jnp.sum(block.astype(F32), axis=0, keepdims=True)

    loop(units // WIDE, outer)
    for j in range(columns // WIDE):
        at = slice(j * WIDE, (j + 1) * WIDE)
        gn[:, at] = nt(gh[...], we[at, :])
        out_ref[:, at] = (z_ref[:, at] + (nn(a[...], wr[:, at]) + small_ref[7:8, at])).astype(BF)

    def store(rows, value):
        gz_ref[rows, :] = value

    gain_sum, shift_sum = norm_back_chunks(
        gn, z_ref, small_ref[14:15, :], lambda rows: g_ref[rows, :].astype(F32), store
    )
    sums_ref[0:1, :] = column_sums(g_ref, 0, columns)
    sums_ref[1:2, :] = gain_sum
    sums_ref[2:3, :] = shift_sum


def space_backward(gz_ref, y_ref, ns_ref, qkv_ref, p_ref, o_ref, small_ref, w_ref, gy_ref, sums_ref, dw_ref, w, gbs, go, gqkv, gn, sems):
    columns = y_ref.shape[1]
    rows = y_ref.shape[0]
    clips = rows // (BLOCK * FRAMES)
    pairs = columns // 128
    copies = load([(w_ref, w)], sems)

    def lower(i):
        at = rows_of(i, CHUNK)
        gbs[at, :] = gz_ref[at, :].astype(BF)

    loop(rows // CHUNK, lower)
    is_class = lax.broadcasted_iota(jnp.int32, (BLOCK - EDGE, columns), 0) == CLASS
    for clip in range(clips):
        edges = [slice((clip * FRAMES + f) * BLOCK + EDGE, (clip * FRAMES + f + 1) * BLOCK) for f in range(FRAMES)]
        share = gz_ref[edges[0], :] * (1.0 / FRAMES)
        for edge in edges:
            gbs[edge, :] = jnp.where(is_class, share, gz_ref[edge, :]).astype(BF)
    wait(copies)
    for j in range(columns // WIDE):
        at = slice(j * WIDE, (j + 1) * WIDE)
        go[:, at] = nt(gbs[...], w[at, 3 * columns : 4 * columns]).astype(BF)
        dw_ref[:, 3 * columns + j * WIDE : 3 * columns + (j + 1) * WIDE] = tn(o_ref[...], gbs[:, at]).astype(BF)
    masks = half_masks()
    first = lax.broadcasted_iota(jnp.int32, (BLOCK, 128), 1) < HD
    class_row = lax.broadcasted_iota(jnp.int32, (BLOCK, 128), 0) == PLACES

    def attend(n):
        clip, pair = n // pairs, n % pairs
        found = []
        for f in range(FRAMES):
            block = clip * FRAMES + f
            at = rows_of(block, BLOCK)
            q = qkv_ref[at, cols_of(pair, 128)]
            k = qkv_ref[at, cols_of(pair, 128, columns)]
            v = qkv_ref[at, cols_of(pair, 128, 2 * columns)]
            grad = go[at, cols_of(pair, 128)]
            parts = []
            for half in range(2):
                p = p_ref[2 * (block * pairs + pair) + half]
                gp = nt(grad * masks[half], v)
                weights = p.astype(F32)
                shared = jnp.sum(gp * weights, axis=-1, keepdims=True)
                gs = (weights * (gp - shared)).astype(BF)
                parts.append((nn(gs, k), tn(gs, q), tn(p, grad)))
            scale = HD ** (-0.5)
            found.append(
                [jnp.where(first, left, right) * s for left, right, s in zip(*parts, (scale, scale, 1.0))]
            )
        for part in range(3):
            one, two = found[0][part], found[1][part]
            one = jnp.where(class_row, one + two, one)
            two = jnp.where(class_row, 0.0, two)
            to = cols_of(pair, 128, part * columns)
            gqkv[rows_of(clip * FRAMES, BLOCK), to] = one.astype(BF)
            gqkv[rows_of(clip * FRAMES + 1, BLOCK), to] = two.astype(BF)

    loop(clips * pairs, attend)
    for j in range(3 * columns // WIDE):
        at = slice(j * WIDE, (j + 1) * WIDE)
        dw_ref[:, at] = tn(ns_ref[...], gqkv[:, at]).astype(BF)
    for j in range(columns // WIDE):
        at = slice(j * WIDE, (j + 1) * WIDE)
        gn[:, at] = nt(gqkv[...], w[at, 0 : 3 * columns])

    def store(at, value):
        gy_ref[at, :] = value

    gain_sum, shift_sum = norm_back_chunks(gn, y_ref, small_ref[13:14, :], lambda at: gz_ref[at, :], store)
    sums_ref[0:1, :] = column_sums(gqkv, 0, columns)
    sums_ref[1:2, :] = column_sums(gqkv, 2 * columns, columns)
    sums_ref[2:3, :] = column_sums(gbs, 0, columns)
    sums_ref[3:4, :] = gain_sum
    sums_ref[4:5, :] = shift_sum


def time_backward(gy_ref, x_ref, nt_ref, qkv_ref, p_ref, o_ref, e_ref, small_ref, w_ref, gx_ref, sums_ref, dw_ref, w, grt, get, go, gqkv, gn, high, low, sems):
    columns = x_ref.shape[1]
    rows = x_ref.shape[0]
    copies = load([(w_ref, w)], sems)

    def lower(i):
        at = rows_of(i, CHUNK)
        patch = row_in_block(i, CHUNK, columns) < PLACES
        grt[at, :] = jnp.where(patch, gy_ref[at, :], 0.0).astype(BF)

    loop(rows // CHUNK, lower)
    wait(copies)
    for j in range(columns // WIDE):
        at = slice(j * WIDE, (j + 1) * WIDE)
        get[:, at] = nt(grt[...], w[at, 4 * columns : 5 * columns]).astype(BF)
        dw_ref[:, 4 * columns + j * WIDE : 4 * columns + (j + 1) * WIDE] = tn(e_ref[...], grt[:, at]).astype(BF)
    for j in range(columns // WIDE):
        at = slice(j * WIDE, (j + 1) * WIDE)
        go[:, at] = nt(get[...], w[at, 3 * columns : 4 * columns]).astype(BF)
        dw_ref[:, 3 * columns + j * WIDE : 3 * columns + (j + 1) * WIDE] = tn(o_ref[...], get[:, at]).astype(BF)
    heads = head_map(columns)
    small = 16
    scale = HD ** (-0.5)
    for clip in range(rows // (FRAMES * BLOCK)):
        start = clip * FRAMES * BLOCK

        def products(i, start=start):
            at = [pl.ds(pl.multiple_of(start + f * BLOCK + i * small, small), small) for f in range(FRAMES)]
            grad = [go[a, :].astype(F32) for a in at]
            v = [qkv_ref[a, 2 * columns : 3 * columns].astype(F32) for a in at]
            for f in range(FRAMES):
                for g in range(FRAMES):
                    to = pl.ds(pl.multiple_of((f * FRAMES + g) * BLOCK + i * small, small), small)
                    split_store(high, low, to, grad[f] * v[g])

        loop(BLOCK // small, products)
        gp_all = nn(high[...], heads) + nn(low[...], heads)
        gp = [gp_all[n * BLOCK : (n + 1) * BLOCK, :] for n in range(4)]
        p_all = p_ref[clip * 4 * BLOCK : (clip + 1) * 4 * BLOCK, :]
        p = [p_all[n * BLOCK : (n + 1) * BLOCK, :] for n in range(4)]
        gs = []
        for f in range(FRAMES):
            shared = gp[2 * f] * p[2 * f] + gp[2 * f + 1] * p[2 * f + 1]
            for g in range(FRAMES):
                gs.append((p[2 * f + g] * (gp[2 * f + g] - shared)).astype(BF))
        gs = jnp.concatenate(gs, axis=0)
        spread = p_all.astype(BF)
        for j in range(columns // WIDE):
            at = slice(j * WIDE, (j + 1) * WIDE)
            high[:, at] = nt(spread, heads[at, :]).astype(BF)
            low[:, at] = nt(gs, heads[at, :]).astype(BF)

        def gather(i, start=start):
            at = [pl.ds(pl.multiple_of(start + f * BLOCK + i * small, small), small) for f in range(FRAMES)]
            to = [pl.ds(pl.multiple_of(n * BLOCK + i * small, small), small) for n in range(4)]
            q = [qkv_ref[a, 0:columns].astype(F32) for a in at]
            k = [qkv_ref[a, columns : 2 * columns].astype(F32) for a in at]
            grad = [go[a, :].astype(F32) for a in at]
            s = [low[t, :].astype(F32) for t in to]
            w8 = [high[t, :].astype(F32) for t in to]
            for f in range(FRAMES):
                gqkv[at[f], 0:columns] = ((s[2 * f] * k[0] + s[2 * f + 1] * k[1]) * scale).astype(BF)
                gqkv[at[f], columns : 2 * columns] = ((s[f] * q[0] + s[2 + f] * q[1]) * scale).astype(BF)
                gqkv[at[f], 2 * columns : 3 * columns] = (w8[f] * grad[0] + w8[2 + f] * grad[1]).astype(BF)

        loop(BLOCK // small, gather)
    for j in range(3 * columns // WIDE):
        at = slice(j * WIDE, (j + 1) * WIDE)
        dw_ref[:, at] = tn(nt_ref[...], gqkv[:, at]).astype(BF)
    for j in range(columns // WIDE):
        at = slice(j * WIDE, (j + 1) * WIDE)
        gn[:, at] = nt(gqkv[...], w[at, 0 : 3 * columns])

    def store(at, value):
        gx_ref[at, :] = value.astype(BF)

    gain_sum, shift_sum = norm_back_chunks(gn, x_ref, small_ref[12:13, :], lambda at: gy_ref[at, :], store)
    sums_ref[0:1, :] = column_sums(gqkv, 0, columns)
    sums_ref[1:2, :] = column_sums(gqkv, 2 * columns, columns)
    sums_ref[2:3, :] = column_sums(get, 0, columns)
    sums_ref[3:4, :] = column_sums(grt, 0, columns)
    sums_ref[4:5, :] = gain_sum
    sums_ref[5:6, :] = shift_sum


IN_VMEM = pl.BlockSpec(memory_space=pltpu.VMEM)
IN_ANY = pl.BlockSpec(memory_space=pl.ANY)


def call(body, operands, spaces, outs, scratch, flops, name):
    moved = sum(o.size * o.dtype.itemsize for o in operands) + sum(
        functools.reduce(lambda a, b: a * b, s) * jnp.dtype(d).itemsize for s, d in outs
    )
    return pl.pallas_call(
        body,
        out_shape=[jax.ShapeDtypeStruct(s, d) for s, d in outs],
        in_specs=[IN_ANY if space else IN_VMEM for space in spaces],
        out_specs=[IN_VMEM] * len(outs),
        scratch_shapes=scratch,
        compiler_params=pltpu.CompilerParams(vmem_limit_bytes=VMEM_LIMIT),
        cost_estimate=pl.CostEstimate(flops=flops, bytes_accessed=moved, transcendentals=0),
        name=name,
    )(*operands)


def pack_rows(tokens, once):
    clips, _, columns = tokens.shape
    frames = []
    for f in range(FRAMES):
        places = tokens[:, 1 + f * PLACES : 1 + (f + 1) * PLACES]
        head = tokens[:, :1] if f == 0 or not once else jnp.zeros_like(tokens[:, :1])
        frames.append(jnp.concatenate([places, head, jnp.zeros((clips, BLOCK - PLACES - 1, columns), tokens.dtype)], axis=1))
    return jnp.stack(frames, axis=1).reshape(clips * FRAMES * BLOCK, columns)


def unpack_rows(rows, clips):
    framed = rows.reshape(clips, FRAMES, BLOCK, rows.shape[-1])
    return jnp.concatenate(
        [framed[:, 0, PLACES : PLACES + 1]] + [framed[:, f, :PLACES] for f in range(FRAMES)], axis=1
    )


def layer(x, g, small, hb, wt, ws, we, wr):
    rows, columns = x.shape
    units = we.shape[1]
    blocks = rows // BLOCK
    pairs = columns // 128
    act = ((rows, columns), BF)
    act3 = ((rows, 3 * columns), BF)
    wide = ((rows, columns), F32)
    probs = ((rows * FRAMES, 128), F32)
    sums = ((8, columns), F32)
    square = 2 * rows * columns * columns
    dma = pltpu.SemaphoreType.DMA
    normed_t, qkv_t, o_t, e_t, p_t, y = call(
        time_forward, (x, small, wt), (0, 0, 1), [act, act3, act, act, probs, wide],
        [pltpu.VMEM(wt.shape, BF), pltpu.VMEM((4 * BLOCK, columns), BF), pltpu.VMEM((4 * BLOCK, columns), BF), dma((8,))],
        5 * square, "time_forward",
    )
    normed_s, qkv_s, p_s, o_s, z = call(
        space_forward, (y, small, ws), (0, 0, 1),
        [act, act3, ((2 * blocks * pairs, BLOCK, BLOCK), BF), act, wide],
        [pltpu.VMEM(ws.shape, BF), dma((8,))], 5 * square, "space_forward",
    )
    out, gz, sums_f, ghb, dwe, dwr = call(
        feed, (z, g, small, hb, we, wr), (0, 0, 0, 0, 1, 1),
        [act, wide, sums, ((8, units), F32), (we.shape, BF), (wr.shape, BF)],
        [pltpu.VMEM(we.shape, BF), pltpu.VMEM(wr.shape, BF), pltpu.VMEM((rows, columns), BF),
         pltpu.VMEM((rows, units), BF), pltpu.VMEM((rows, units), BF), pltpu.VMEM((rows, columns), F32), dma((8,))],
        24 * square, "feed",
    )
    gy, sums_s, dws = call(
        space_backward, (gz, y, normed_s, qkv_s, p_s, o_s, small, ws), (0, 0, 0, 0, 0, 0, 0, 1),
        [wide, sums, (ws.shape, BF)],
        [pltpu.VMEM(ws.shape, BF), pltpu.VMEM((rows, columns), BF), pltpu.VMEM((rows, columns), BF),
         pltpu.VMEM((rows, 3 * columns), BF), pltpu.VMEM((rows, columns), F32), dma((8,))],
        10 * square, "space_backward",
    )
    gx, sums_t, dwt = call(
        time_backward, (gy, x, normed_t, qkv_t, p_t, o_t, e_t, small, wt), (0,) * 8 + (1,),
        [act, sums, (wt.shape, BF)],
        [pltpu.VMEM(wt.shape, BF)] + [pltpu.VMEM((rows, columns), BF)] * 3
        + [pltpu.VMEM((rows, 3 * columns), BF), pltpu.VMEM((rows, columns), F32)]
        + [pltpu.VMEM((4 * BLOCK, columns), BF)] * 2 + [dma((8,))],
        10 * square, "time_backward",
    )
    return out, gx, dwt, dws, dwe, dwr, sums_t, sums_s, sums_f, ghb


def local(video, cotangent, live, time_entry, time_exit, time_mixer, space_entry, space_exit, hidden_expand, hidden_reduce, bias_rows, hidden_bias, norm_gain, norm_shift):
    clips, _, tokens, columns = video.shape
    shards = lax.axis_size("shard")
    mine = lax.axis_index("shard")
    part = columns // shards

    def gather(value):
        return lax.all_gather(value, "shard", axis=0, tiled=True)

    packed = jnp.concatenate([bias_rows, hidden_bias.reshape(-1, part), norm_gain, norm_shift], axis=0)
    n_hidden = hidden_bias.shape[0] // part
    spread = lax.all_gather(packed, "shard", axis=0)
    by_rows = jnp.concatenate(
        [
            spread[:, :8].transpose(1, 0, 2).reshape(8, columns),
            spread[:, 8 : 8 + n_hidden].reshape(-1, columns),
            spread[:, 8 + n_hidden :].transpose(1, 0, 2).reshape(6, columns),
        ],
        axis=0,
    ).astype(F32)
    units = hidden_bias.shape[0] * shards
    small = jnp.pad(by_rows, ((0, 6), (0, 0)))
    hb = jnp.pad(spread[:, 8 : 8 + n_hidden].reshape(1, units).astype(F32), ((0, 7), (0, 0)))
    wt = gather(jnp.concatenate([time_entry, time_exit, time_mixer], axis=1))
    ws = gather(jnp.concatenate([space_entry, space_exit], axis=1))
    we = gather(hidden_expand)
    wr = gather(hidden_reduce)
    flags = live.astype(BF)[:, :, None]
    x = pack_rows(video[:, 0], False)
    g = pack_rows(cotangent[:, 0] * flags, True)
    out, gx, dwt, dws, dwe, dwr, sums_t, sums_s, sums_f, ghb = layer(x, g, small, hb, wt, ws, we, wr)

    def reduce(value):
        kept = lax.psum_scatter(value, "shard", scatter_dimension=0, tiled=True)
        return lax.psum(kept, "grp").astype(F32)

    rt, rs, re, rr = reduce(dwt), reduce(dws), reduce(dwe), reduce(dwr)
    sums = jnp.concatenate([sums_t[0:4], sums_s[0:3], sums_f[0:1], ghb[0:1].reshape(-1, columns), sums_t[4:5], sums_s[3:4], sums_f[1:2], sums_t[5:6], sums_s[4:5], sums_f[2:3]], axis=0)
    sums = lax.psum(sums, ("grp", "shard"))
    cut = lax.dynamic_slice_in_dim(sums, mine * part, part, axis=1)
    rows_hidden = lax.dynamic_slice_in_dim(sums[8:12].reshape(-1), mine * hidden_bias.shape[0], hidden_bias.shape[0])
    return (
        (unpack_rows(out, clips) * flags)[:, None],
        unpack_rows(gx, clips)[:, None],
        rt[:, : 3 * columns],
        rt[:, 3 * columns : 4 * columns],
        rt[:, 4 * columns :],
        rs[:, : 3 * columns],
        rs[:, 3 * columns :],
        re,
        rr,
        cut[0:8],
        rows_hidden,
        cut[12:15],
        cut[15:18],
    )


def solution(mesh):
    clips = P(None, ("grp", "shard"), None, None)
    rows = P("shard", None)
    cols = P(None, "shard")
    return jax.shard_map(
        local,
        mesh=mesh,
        in_specs=(clips, clips, P(None, ("grp", "shard"))) + (rows,) * 7 + (cols, P("shard"), cols, cols),
        out_specs=(clips, clips) + (rows,) * 7 + (cols, P("shard"), cols, cols),
        check_vma=False,
    )
```

time: 1510 us -> 629 us (0.42)
  waiting for transfers between devices: 990 us -> 337 us
  Pallas kernels: 0 us -> 180 us
  matrix products: 141 us -> 0 us
  local copies, waits for them, and re-layouts: 154 us -> 16.5 us
  other arithmetic: 119 us -> 22 us
  blocking collectives: 71 us -> 54.9 us
    reduce_scatter x7 -> x4, waiting for transfers between devices: 628 us -> 195 us  [reduce(): kept = lax.psum_scatter(value, 'shard', scatter_dimension=0, tiled=True)]
    pallas_call x0 -> x5, Pallas kernels: none -> 180 us  [call(): pl.pallas_call(body, out_shape=[jax.ShapeDtypeStruct(s, d) for s, d in ou...]
    dot_general x33 -> x0, matrix products: 141 us -> none  [the longest x7 31 us: times_first(): lax.dot_general(first_op, second_op, (((0,), (0,)), ((), ())), preferred_...]
    all_gather x7 -> x4, waiting for transfers between devices: 191 us -> 90 us  [gather(): return lax.all_gather(value, 'shard', axis=0, tiled=True)]
    unnamed x21 -> x9, waiting for transfers between devices: 78.7 us -> 2.5 us
    add x14 -> x0, other arithmetic: 59.4 us -> none  [the longest x11 56.6 us: local(): earlier + later]
    psum x1, waiting for transfers between devices: 92 us -> 48.8 us  [reduce(): return lax.psum(kept, 'grp').astype(F32)]
    convert_element_type x15 -> x1, local copies, waits for them, and re-layouts: 34.5 us -> 0.09 us  [local(): spread[:, 8:8 + n_hidden].reshape(1, units).astype(F32)]
  transfers between devices with their start and end apart: 18 -> 9, of which waited for: 17 -> 9; matrix products, arithmetic and copies ran while one was open for 5% -> 5% of each run, Pallas kernels for 0% -> 14%
where the time goes in v1:
time: 629 us; the launch traced here: 625 us
  waiting for transfers between devices  337 us (54%)
  Pallas kernels  180 us (29%)
  blocking collectives  54.9 us (9%)
  other arithmetic  22 us (3%)
  local copies, waits for them, and re-layouts  16.5 us (3%)
  between operations  14.5 us (2%)
    reduce_scatter x4, waiting for transfers between devices, reduce(): kept = lax.psum_scatter(value, 'shard', scatter_dimension=0, tiled=True)  195 us
    pallas_call x5, Pallas kernels, call(): pl.pallas_call(body, out_shape=[jax.ShapeDtypeStruct(s, d) for s, d in ou...  180 us
    all_gather x4, waiting for transfers between devices, gather(): return lax.all_gather(value, 'shard', axis=0, tiled=True)  90 us
    psum x1, waiting for transfers between devices, reduce(): return lax.psum(kept, 'grp').astype(F32)  48.8 us
    psum x1, blocking collectives, local(): sums = lax.psum(sums, ('grp', 'shard'))  44.2 us
  transfers between devices with their start and end apart: 9, of which 9 were waited for; matrix products, arithmetic and copies ran while one was open for 5% of the time, Pallas kernels for 14%

profile of v1, /device:TPU:0, one launch (start us, length us, event | category | flops | bytes accessed | tf_op | source)
XLA Modules:
  0.0 625.2 jit_solution(160447443411361569)
XLA Ops:
  7.2 2.1 pad_maximum_fusion.2
  9.5 0.9 pad_maximum_fusion.5
  10.5 0.7 all-gather.11.cloned.1.call-update
  11.2 0.5 all-gather.13.cloned.1.call-update
  11.9 10.7 %all-gather.1 = bf16[8,18,96]{2,1,0:T(8,128)(2,1)S(1)} all-gather(bf16[1,18,96]{2,1,0:T(8,128)(2,1)S(1)} %maximum_bitcast_fusion.3), channel_id=2, replica_groups=mesh['grp'=4,'shard'=8] {'shard'}, dimensions={0}, use_global_device_ids=true | all-gather | bytes 31104 | tf_op jit(solution)/shard_map/all_gather | solution.py:543
  22.9 1.1 bitcast_multiply_fusion
  24.2 0.8 fusion.12
  25.0 0.8 fusion.13
  25.8 5.3 maximum_bitcast_fusion.1
  31.1 3.7 pad_maximum_fusion
  34.9 1.3 copy.37
  36.4 1.2 copy.40
  37.6 0.6 fusion.9.small_ref
  38.3 0.7 pad_convert_fusion.hb_ref
  38.9 18.2 %all-gather.7.cloned.1.call-done.w_ref = bf16[768,3840]{1,0:T(8,128)(2,1)} async-done(((bf16[96,3840]{1,0:T(8,128)(2,1)}), bf16[768,3840]{1,0:T(8,128)(2,1)}) %all-gather.7.cloned.1.call-update) | async-done | bytes 5898256 | tf_op jit(solution)/shard_map/all_gather | solution.py:539
  57.1 17.4 %time_forward.1 = (bf16[832,768]{1,0:T(8,128)(2,1)}, bf16[832,2304]{1,0:T(8,128)(2,1)}, bf16[832,768]{1,0:T(8,128)(2,1)}, bf16[832,768]{1,0:T(8,128)(2,1)}, f32[1664,128]{1,0:T(8,128)}, /*index=5*/f32[832,768]{1,0:T(8,128)}) custom-call(bf16[832,768]{1,0:T(8,128)(2,1)} %bitcast.37, f32[24,768]{1,0:T(8,128)} %fusion.9.small_ref, ...), custom_call_target="tpu_custom_call" | custom-call | flops 4907335680 | bytes 18325504 | tf_op jit(solution)/shard_map/time_forward/pallas_call | solution.py:456
  74.6 24.0 %all-gather.9.cloned.1.call-done.w_ref = bf16[768,3072]{1,0:T(8,128)(2,1)} async-done(((bf16[96,3072]{1,0:T(8,128)(2,1)}), bf16[768,3072]{1,0:T(8,128)(2,1)}) %all-gather.9.cloned.1.call-update) | async-done | bytes 4718608 | tf_op jit(solution)/shard_map/all_gather | solution.py:539
  98.5 33.9 %space_forward.1 = (bf16[832,768]{1,0:T(8,128)(2,1)}, bf16[832,2304]{1,0:T(8,128)(2,1)}, bf16[48,208,208]{2,1,0:T(8,128)(2,1)}, bf16[832,768]{1,0:T(8,128)(2,1)}, f32[832,768]{1,0:T(8,128)}) custom-call(f32[832,768]{1,0:T(8,128)} %get-tuple-element.36.y_ref, f32[24,768]{1,0:T(8,128)} %fusion.9.small_ref, bf16[768,3072]{1,0:T(8,128)(2,1)} %all-gather.9.cloned.1.call-done.w_ref), custom_call_target="tpu_custom_call" | custom-call | flops 4907335680 | bytes 20447232 | tf_op jit(solution)/shard_map/space_forward/pallas_call | solution.py:456
  132.4 7.1 %all-gather.11.cloned.1.call-done.we_ref = bf16[768,3072]{1,0:T(8,128)(2,1)} async-done(((bf16[96,3072]{1,0:T(8,128)(2,1)}), bf16[768,3072]{1,0:T(8,128)(2,1)}) %all-gather.11.cloned.1.call-update) | async-done | bytes 4718608 | tf_op jit(solution)/shard_map/all_gather | solution.py:539
  139.5 40.7 %all-gather.13.cloned.1.call-done.wr_ref = bf16[3072,768]{1,0:T(8,128)(2,1)} async-done(((bf16[384,768]{1,0:T(8,128)(2,1)}), bf16[3072,768]{1,0:T(8,128)(2,1)}) %all-gather.13.cloned.1.call-update) | async-done | bytes 4718608 | tf_op jit(solution)/shard_map/all_gather | solution.py:539
  180.2 48.3 %feed.1 = (bf16[832,768]{1,0:T(8,128)(2,1)}, f32[832,768]{1,0:T(8,128)}, f32[8,768]{1,0:T(8,128)}, f32[8,3072]{1,0:T(8,128)}, bf16[768,3072]{1,0:T(8,128)(2,1)}, /*index=5*/bf16[3072,768]{1,0:T(8,128)(2,1)}) custom-call(f32[832,768]{1,0:T(8,128)} %get-tuple-element.37.z_ref, bf16[832,768]{1,0:T(8,128)(2,1)} %bitcast.39, f32[24,768]{1,0:T(8,128)} %fusion.9.small_ref, ...), custom_call_target="tpu_custom_call" | custom-call | flops 23555211264 | bytes 26836992 | tf_op jit(solution)/shard_map/feed/pallas_call | solution.py:456
  228.5 44.9 %space_backward.1 = (f32[832,768]{1,0:T(8,128)}, f32[8,768]{1,0:T(8,128)}, bf16[768,3072]{1,0:T(8,128)(2,1)}) custom-call(f32[832,768]{1,0:T(8,128)} %get-tuple-element.39.gz_ref, f32[832,768]{1,0:T(8,128)} %get-tuple-element.36.y_ref, bf16[832,768]{1,0:T(8,128)(2,1)} %get-tuple-element.40.ns_ref, bf16[832,2304]{1,0:T(8,128)(2,1)} %get-tuple-element.41.qkv_ref, ...), custom_call_target="tpu_custom_call" | custom-call | flops 9814671360 | bytes 27746304 | tf_op jit(solution)/shard_map/space_backward/pallas_call | solution.py:456
  273.4 0.5 reduce-scatter.11.cloned.1.call-update
  274.0 0.7 reduce-scatter.9.cloned.1.call-update
  274.8 35.7 %time_backward.1 = (bf16[832,768]{1,0:T(8,128)(2,1)}, f32[8,768]{1,0:T(8,128)}, bf16[768,3840]{1,0:T(8,128)(2,1)}) custom-call(f32[832,768]{1,0:T(8,128)} %get-tuple-element.44.gy_ref, bf16[832,768]{1,0:T(8,128)(2,1)} %bitcast.38, bf16[832,768]{1,0:T(8,128)(2,1)} %get-tuple-element.45.nt_ref, bf16[832,2304]{1,0:T(8,128)(2,1)} %get-tuple-element.46.qkv_ref, ...), custom_call_target="tpu_custom_call" | custom-call | flops 9814671360 | bytes 25526272 | tf_op jit(solution)/shard_map/time_backward/pallas_call | solution.py:456
  310.5 16.9 %reduce-scatter.7.cloned.1.call-done = bf16[96,3072]{1,0:T(8,128)(2,1)} async-done(((bf16[768,3072]{1,0:T(8,128)(2,1)}), bf16[96,3072]{1,0:T(8,128)(2,1)}) %reduce-scatter.7.cloned.1.call-update) | async-done | bytes 589840 | tf_op jit(solution)/shard_map/reduce_scatter | solution.py:565
  327.4 57.6 %reduce-scatter.11.cloned.1.call-done = bf16[384,768]{1,0:T(8,128)(2,1)} async-done(((bf16[3072,768]{1,0:T(8,128)(2,1)}), bf16[384,768]{1,0:T(8,128)(2,1)}) %reduce-scatter.11.cloned.1.call-update) | async-done | bytes 589840 | tf_op jit(solution)/shard_map/reduce_scatter | solution.py:565
  385.1 57.4 %reduce-scatter.9.cloned.1.call-done = bf16[96,3072]{1,0:T(8,128)(2,1)} async-done(((bf16[768,3072]{1,0:T(8,128)(2,1)}), bf16[96,3072]{1,0:T(8,128)(2,1)}) %reduce-scatter.9.cloned.1.call-update) | async-done | bytes 589840 | tf_op jit(solution)/shard_map/reduce_scatter | solution.py:565
  442.5 63.6 %reduce-scatter.5.cloned.1.call-done = bf16[96,3840]{1,0:T(8,128)(2,1)} async-done(((bf16[768,3840]{1,0:T(8,128)(2,1)}), bf16[96,3840]{1,0:T(8,128)(2,1)}) %reduce-scatter.5.cloned.1.call-update) | async-done | bytes 737296 | tf_op jit(solution)/shard_map/reduce_scatter | solution.py:565
  506.1 0.7 copy-done.10
  506.8 0.9 slice_reduce_fusion
  507.7 0.9 fusion.16
  508.7 44.2 %psum.39 = f32[18,768]{1,0:T(8,128)S(1)} all-reduce(f32[18,768]{1,0:T(8,128)S(1)} %concatenate.50), channel_id=1, replica_groups=mesh['grp'=4,'shard'=8] {'grp','shard'}, use_global_device_ids=true, to_apply=%region_8.9 | all-reduce | flops 13824 | bytes 110592 | tf_op jit(solution)/shard_map/psum | solution.py:570
  553.0 0.5 copy.56
  553.5 0.5 copy.57
  554.9 0.5 copy.49
  555.4 0.7 dynamic_slice.7
  556.0 0.7 constant_dynamic-slice_fusion
  556.7 0.7 fusion.15
  557.4 2.6 maximum_bitcast_fusion
  560.0 2.8 maximum_multiply_fusion
  562.8 48.8 %all-reduce.5.cloned.1.call-done = (bf16[96,3840]{1,0:T(8,128)(2,1)}, bf16[96,3072]{1,0:T(8,128)(2,1)}, bf16[96,3072]{1,0:T(8,128)(2,1)}, bf16[384,768]{1,0:T(8,128)(2,1)}) async-done(((bf16[96,3840]{1,0:T(8,128)(2,1)}, bf16[96,3072]{1,0:T(8,128)(2,1)}, bf16[96,3072]{1,0:T(8,128)(2,1)}, bf16[384,768]{1,0:T(8,128)(2,1)}), (bf16[96,3840]{1,0:T(8,128)(2,1)}, bf16[96,3072]{1,0:T(8,128)(2,1)}, ...) | async-done | bytes 2506768 | tf_op jit(solution)/shard_map/psum | solution.py:566
  611.5 2.1 slice.153
  613.6 0.9 fusion.14
  614.5 1.0 slice.156
  615.5 0.7 slice.157
  616.2 1.1 convert_element_type.36
  617.3 1.1 convert_element_type.37
  (79 shorter events, 2.3 us)
Async XLA Ops:
  7.2 2.3 copy-start.8
  7.2 2.3 copy-start.9
  7.2 49.9 %all-gather.7.cloned.1.call-start = ((), (), s32[]{:S(2)}) async-start(), calls=%async_computation.4 | async-start | bytes 6635520 | tf_op jit(solution)/shard_map/all_gather | solution.py:539
  9.4 2.4 copy-start.13
  9.4 2.5 copy-start.12
  9.4 2.5 copy-start.14
  9.4 2.5 copy-start.15
  9.4 13.4 %copy-start.16 = (s32[2,1]{0,1:T(1,128)S(1)}, s32[2,1]{0,1:T(1,128)}, u32[]{:S(2)}) copy-start(s32[2,1]{0,1:T(1,128)} %param.16) | copy-start | bytes 28
  9.4 13.4 %copy-start.2 = (bf16[2,1,393,768]{3,0,2,1:T(2,128)(2,1)S(1)}, bf16[2,1,393,768]{3,0,2,1:T(2,128)(2,1)}, u32[]{:S(2)}) copy-start(bf16[2,1,393,768]{3,0,2,1:T(2,128)(2,1)} %param.15) | copy-start | bytes 3621892
  9.5 89.1 %all-gather.9.cloned.1.call-start = ((), (), s32[]{:S(2)}) async-start(), calls=%async_computation.5 | async-start | bytes 5308416 | tf_op jit(solution)/shard_map/all_gather | solution.py:539
  10.4 129.1 %all-gather.11.cloned.1.call-start = ((), (), s32[]{:S(2)}) async-start(), calls=%async_computation.6 | async-start | bytes 5308416 | tf_op jit(solution)/shard_map/all_gather | solution.py:539
  11.2 169.0 %all-gather.13.cloned.1.call-start = ((), (), s32[]{:S(2)}) async-start(), calls=%async_computation.7 | async-start | bytes 5308416 | tf_op jit(solution)/shard_map/all_gather | solution.py:539
  11.7 12.3 %copy-start.3 = (bf16[2,1,393,768]{3,0,2,1:T(2,128)(2,1)S(1)}, bf16[2,1,393,768]{3,0,2,1:T(2,128)(2,1)}, u32[]{:S(2)}) copy-start(bf16[2,1,393,768]{3,0,2,1:T(2,128)(2,1)} %param.14) | copy-start | bytes 3621892
  11.7 315.7 %reduce-scatter.7.cloned.1.call-start = ((), (), s32[]{:S(2)}) async-start(), calls=%async_computation.9 | async-start | bytes 5308416 | tf_op jit(solution)/shard_map/reduce_scatter | solution.py:565
  273.4 111.7 %reduce-scatter.11.cloned.1.call-start = ((), (), s32[]{:S(2)}) async-start(), calls=%async_computation.11 | async-start | bytes 5308416 | tf_op jit(solution)/shard_map/reduce_scatter | solution.py:565
  274.0 168.5 %reduce-scatter.9.cloned.1.call-start = ((), (), s32[]{:S(2)}) async-start(), calls=%async_computation.10 | async-start | bytes 5308416 | tf_op jit(solution)/shard_map/reduce_scatter | solution.py:565
  274.7 231.3 %reduce-scatter.5.cloned.1.call-start = ((), (), s32[]{:S(2)}) async-start(), calls=%async_computation.8 | async-start | bytes 6635520 | tf_op jit(solution)/shard_map/reduce_scatter | solution.py:565
  310.5 195.6 %copy-start.11 = (f32[8,768]{1,0:T(8,128)S(1)}, f32[8,768]{1,0:T(8,128)}, u32[]{:S(2)}) copy-start(f32[8,768]{1,0:T(8,128)} %get-tuple-element.55) | copy-start | bytes 73732
  310.5 301.0 %all-reduce.5.cloned.1.call-start = ((), (), s32[]{:S(2)}) async-start(), calls=%async_computation.12 | async-start | bytes 5013504 | tf_op jit(solution)/shard_map/psum | solution.py:566
  506.0 0.7 copy-start.10
  506.0 46.9 %copy-start.5 = (bf16[832,768]{1,0:T(8,128)(2,1)S(1)}, bf16[832,768]{1,0:T(8,128)(2,1)}, u32[]{:S(2)}) copy-start(bf16[832,768]{1,0:T(8,128)(2,1)} %get-tuple-element.50) | copy-start | bytes 3833860
  553.0 1.3 copy-start.4
  611.5 2.1 copy-start
  611.5 2.9 copy-start.1
  614.5 1.7 copy-start.7
  615.5 1.9 copy-start.6
Sparse Core Ops, SparseCore 0:
  10.5 46.5 all-gather.6
  59.6 38.8 all-gather.8
  100.4 39.0 all-gather.10
  141.3 38.8 all-gather.12
  273.5 53.8 reduce-scatter.6
  331.1 53.8 reduce-scatter.10
  388.5 53.8 reduce-scatter.8
  446.3 59.6 reduce-scatter.4
  508.9 102.6 all-reduce.4

commit v2 on v1

--- a/solution.py
+++ b/solution.py
@@ -1,4 +1,5 @@
 import functools
+import math
 
 import jax
 import jax.numpy as jnp
@@ -111,8 +112,8 @@
     return (i * size + lax.broadcasted_iota(jnp.int32, (size, columns), 0)) % BLOCK
 
 
-def load(loads, sems):
-    copies = [pltpu.make_async_copy(s, d, sems.at[n]) for n, (s, d) in enumerate(loads)]
+def start(pairs, sems):
+    copies = [pltpu.make_async_copy(s, d, sems.at[n]) for n, (s, d) in enumerate(pairs)]
     for copy in copies:
         copy.start()
     return copies
@@ -123,9 +124,69 @@
         copy.wait()
 
 
-def time_forward(x_ref, small_ref, w_ref, nt_ref, qkv_ref, o_ref, e_ref, p_ref, y_ref, w, high, low, sems):
+def piece_views(bufs):
+    rows = bufs[2].shape[0]
+    return [b.at[k * rows : (k + 1) * rows] for b in bufs for k in range(b.shape[0] // rows)]
+
+
+def rows_at(place, rows, share=1, k=0):
+    return pl.ds(pl.multiple_of((place * share + k) * rows, 16), rows)
+
+
+def load(bufs, place_ref, w, sems):
+    if len(bufs) == 1:
+        return start([(bufs[0], w)], sems)
+    views = piece_views(bufs)
+    rows = views[0].shape[0]
+    return start([(v, w.at[rows_at(place_ref[n], rows), :]) for n, v in enumerate(views)], sems)
+
+
+def load_feed(bufs, place_ref, we, wr, sems):
+    if len(bufs) == 2:
+        return start([(bufs[0], we), (bufs[1], wr)], sems)
+    views = piece_views(bufs)
+    rows, units = views[0].shape[0], we.shape[1]
+    columns = wr.shape[1]
+    share = units // columns
+    pairs = [(v.at[:, 0:units], we.at[rows_at(place_ref[n], rows), :]) for n, v in enumerate(views)]
+    for n, v in enumerate(views):
+        for k in range(share):
+            to = rows_at(place_ref[n], rows, share, k)
+            pairs.append((v.at[:, units + k * columns : units + (k + 1) * columns], wr.at[to, :]))
+    return start(pairs, sems)
+
+
+def store_pieces(dw, outs, place_ref, sems):
+    if len(outs) == 1:
+        return start([(dw, outs[0])], sems)
+    rows = outs[0].shape[1]
+    pairs = []
+    for side, out in enumerate(outs):
+        for m in range(out.shape[0]):
+            pairs.append((dw.at[rows_at(place_ref[8 + side * 4 + m], rows), :], out.at[m]))
+    return start(pairs, sems)
+
+
+def store_feed(dwe, dwr, outs, whole, place_ref, sems):
+    if whole:
+        return start([(dwe, outs[0]), (dwr, outs[1])], sems)
+    rows, units, columns = outs[0].shape[1], dwe.shape[1], dwr.shape[1]
+    share = units // columns
+    pairs = []
+    for side, out in enumerate(outs):
+        for m in range(out.shape[0]):
+            place = place_ref[8 + side * 4 + m]
+            pairs.append((dwe.at[rows_at(place, rows), :], out.at[m, :, 0:units]))
+            for k in range(share):
+                source = dwr.at[rows_at(place, rows, share, k), :]
+                pairs.append((source, out.at[m, :, units + k * columns : units + (k + 1) * columns]))
+    return start(pairs, sems)
+
+
+def time_forward(nb, place_ref, x_ref, small_ref, *refs):
+    bufs, (nt_ref, qkv_ref, o_ref, e_ref, p_ref, y_ref, w, high, low, sems) = refs[:nb], refs[nb:]
     columns = x_ref.shape[1]
-    copies = load([(w_ref, w)], sems)
+    copies = load(bufs, place_ref, w, sems)
     norm_chunks(x_ref, nt_ref, small_ref[12:13, :], small_ref[15:16, :])
     wait(copies)
     zero_bias = jnp.zeros((1, columns), F32)
@@ -191,11 +252,12 @@
     return (lane < HD).astype(BF), (lane >= HD).astype(BF)
 
 
-def space_forward(y_ref, small_ref, w_ref, ns_ref, qkv_ref, p_ref, o_ref, z_ref, w, sems):
+def space_forward(nb, place_ref, y_ref, small_ref, *refs):
+    bufs, (ns_ref, qkv_ref, p_ref, o_ref, z_ref, w, sems) = refs[:nb], refs[nb:]
     columns = y_ref.shape[1]
     blocks = y_ref.shape[0] // BLOCK
     pairs = columns // 128
-    copies = load([(w_ref, w)], sems)
+    copies = load(bufs, place_ref, w, sems)
     norm_chunks(y_ref, ns_ref, small_ref[13:14, :], small_ref[16:17, :])
     wait(copies)
     zero_bias = jnp.zeros((1, columns), F32)
@@ -244,10 +306,12 @@
     return h * cdf, cdf + h * density
 
 
-def feed(z_ref, g_ref, small_ref, hb_ref, we_ref, wr_ref, out_ref, gz_ref, sums_ref, ghb_ref, dwe_ref, dwr_ref, we, wr, nm, a, gh, gn, sems):
+def feed(nb, place_ref, z_ref, g_ref, small_ref, hb_ref, *refs):
+    bufs, (out_ref, gz_ref, sums_ref, ghb_ref, *outs) = refs[:nb], refs[nb : nb + 6]
+    we, wr, dwe_ref, dwr_ref, nm, a, gh, gn, sems, out_sems = refs[nb + 6 :]
     columns = z_ref.shape[1]
     units = we.shape[1]
-    copies = load([(we_ref, we), (wr_ref, wr)], sems)
+    copies = load_feed(bufs, place_ref, we, wr, sems)
     norm_chunks(z_ref, nm, small_ref[14:15, :], small_ref[17:18, :])
     wait(copies)
 
@@ -268,6 +332,7 @@
         ghb_ref[0:1, at] = jnp.sum(block.astype(F32), axis=0, keepdims=True)
 
     loop(units // WIDE, outer)
+    copies = store_feed(dwe_ref, dwr_ref, outs, nb == 2, place_ref, out_sems)
     for j in range(columns // WIDE):
         at = slice(j * WIDE, (j + 1) * WIDE)
         gn[:, at] = nt(gh[...], we[at, :])
@@ -282,14 +347,17 @@
     sums_ref[0:1, :] = column_sums(g_ref, 0, columns)
     sums_ref[1:2, :] = gain_sum
     sums_ref[2:3, :] = shift_sum
-
-
-def space_backward(gz_ref, y_ref, ns_ref, qkv_ref, p_ref, o_ref, small_ref, w_ref, gy_ref, sums_ref, dw_ref, w, gbs, go, gqkv, gn, sems):
+    wait(copies)
+
+
+def space_backward(nb, no, place_ref, gz_ref, y_ref, ns_ref, qkv_ref, p_ref, o_ref, small_ref, *refs):
+    bufs, (gy_ref, sums_ref, *outs) = refs[:nb], refs[nb : nb + 2 + no]
+    w, dw_ref, gbs, go, gqkv, gn, sems, out_sems = refs[nb + 2 + no :]
     columns = y_ref.shape[1]
     rows = y_ref.shape[0]
     clips = rows // (BLOCK * FRAMES)
     pairs = columns // 128
-    copies = load([(w_ref, w)], sems)
+    copies = load(bufs, place_ref, w, sems)
 
     def lower(i):
         at = rows_of(i, CHUNK)
@@ -345,6 +413,7 @@
     for j in range(3 * columns // WIDE):
         at = slice(j * WIDE, (j + 1) * WIDE)
         dw_ref[:, at] = tn(ns_ref[...], gqkv[:, at]).astype(BF)
+    copies = store_pieces(dw_ref, outs, place_ref, out_sems)
     for j in range(columns // WIDE):
         at = slice(j * WIDE, (j + 1) * WIDE)
         gn[:, at] = nt(gqkv[...], w[at, 0 : 3 * columns])
@@ -358,12 +427,15 @@
     sums_ref[2:3, :] = column_sums(gbs, 0, columns)
     sums_ref[3:4, :] = gain_sum
     sums_ref[4:5, :] = shift_sum
-
-
-def time_backward(gy_ref, x_ref, nt_ref, qkv_ref, p_ref, o_ref, e_ref, small_ref, w_ref, gx_ref, sums_ref, dw_ref, w, grt, get, go, gqkv, gn, high, low, sems):
+    wait(copies)
+
+
+def time_backward(nb, no, place_ref, gy_ref, x_ref, nt_ref, qkv_ref, p_ref, o_ref, e_ref, small_ref, *refs):
+    bufs, (gx_ref, sums_ref, *outs) = refs[:nb], refs[nb : nb + 2 + no]
+    w, dw_ref, grt, get, go, gqkv, gn, high, low, sems, out_sems = refs[nb + 2 + no :]
     columns = x_ref.shape[1]
     rows = x_ref.shape[0]
-    copies = load([(w_ref, w)], sems)
+    copies = load(bufs, place_ref, w, sems)
 
     def lower(i):
         at = rows_of(i, CHUNK)
@@ -429,6 +501,7 @@
     for j in range(3 * columns // WIDE):
         at = slice(j * WIDE, (j + 1) * WIDE)
         dw_ref[:, at] = tn(nt_ref[...], gqkv[:, at]).astype(BF)
+    copies = store_pieces(dw_ref, outs, place_ref, out_sems)
     for j in range(columns // WIDE):
         at = slice(j * WIDE, (j + 1) * WIDE)
         gn[:, at] = nt(gqkv[...], w[at, 0 : 3 * columns])
@@ -443,21 +516,24 @@
     sums_ref[3:4, :] = column_sums(grt, 0, columns)
     sums_ref[4:5, :] = gain_sum
     sums_ref[5:6, :] = shift_sum
-
-
-IN_VMEM = pl.BlockSpec(memory_space=pltpu.VMEM)
-IN_ANY = pl.BlockSpec(memory_space=pl.ANY)
-
-
-def call(body, operands, spaces, outs, scratch, flops, name):
-    moved = sum(o.size * o.dtype.itemsize for o in operands) + sum(
-        functools.reduce(lambda a, b: a * b, s) * jnp.dtype(d).itemsize for s, d in outs
-    )
+    wait(copies)
+
+
+SPACES = {
+    "v": pl.BlockSpec(memory_space=pltpu.VMEM),
+    "a": pl.BlockSpec(memory_space=pl.ANY),
+    "s": pl.BlockSpec(memory_space=pltpu.SMEM),
+}
+
+
+def call(body, operands, spaces, outs, out_spaces, scratch, flops, name):
+    moved = sum(o.size * o.dtype.itemsize for o in operands)
+    moved += sum(math.prod(s) * jnp.dtype(d).itemsize for s, d in outs)
     return pl.pallas_call(
         body,
         out_shape=[jax.ShapeDtypeStruct(s, d) for s, d in outs],
-        in_specs=[IN_ANY if space else IN_VMEM for space in spaces],
-        out_specs=[IN_VMEM] * len(outs),
+        in_specs=[SPACES[space] for space in spaces],
+        out_specs=[SPACES[space] for space in out_spaces],
         scratch_shapes=scratch,
         compiler_params=pltpu.CompilerParams(vmem_limit_bytes=VMEM_LIMIT),
         cost_estimate=pl.CostEstimate(flops=flops, bytes_accessed=moved, transcendentals=0),
@@ -482,94 +558,207 @@
     )
 
 
-def layer(x, g, small, hb, wt, ws, we, wr):
-    rows, columns = x.shape
-    units = we.shape[1]
-    blocks = rows // BLOCK
-    pairs = columns // 128
-    act = ((rows, columns), BF)
-    act3 = ((rows, 3 * columns), BF)
-    wide = ((rows, columns), F32)
-    probs = ((rows * FRAMES, 128), F32)
-    sums = ((8, columns), F32)
-    square = 2 * rows * columns * columns
-    dma = pltpu.SemaphoreType.DMA
-    normed_t, qkv_t, o_t, e_t, p_t, y = call(
-        time_forward, (x, small, wt), (0, 0, 1), [act, act3, act, act, probs, wide],
-        [pltpu.VMEM(wt.shape, BF), pltpu.VMEM((4 * BLOCK, columns), BF), pltpu.VMEM((4 * BLOCK, columns), BF), dma((8,))],
-        5 * square, "time_forward",
-    )
-    normed_s, qkv_s, p_s, o_s, z = call(
-        space_forward, (y, small, ws), (0, 0, 1),
-        [act, act3, ((2 * blocks * pairs, BLOCK, BLOCK), BF), act, wide],
-        [pltpu.VMEM(ws.shape, BF), dma((8,))], 5 * square, "space_forward",
-    )
-    out, gz, sums_f, ghb, dwe, dwr = call(
-        feed, (z, g, small, hb, we, wr), (0, 0, 0, 0, 1, 1),
-        [act, wide, sums, ((8, units), F32), (we.shape, BF), (wr.shape, BF)],
-        [pltpu.VMEM(we.shape, BF), pltpu.VMEM(wr.shape, BF), pltpu.VMEM((rows, columns), BF),
-         pltpu.VMEM((rows, units), BF), pltpu.VMEM((rows, units), BF), pltpu.VMEM((rows, columns), F32), dma((8,))],
-        24 * square, "feed",
-    )
-    gy, sums_s, dws = call(
-        space_backward, (gz, y, normed_s, qkv_s, p_s, o_s, small, ws), (0, 0, 0, 0, 0, 0, 0, 1),
-        [wide, sums, (ws.shape, BF)],
-        [pltpu.VMEM(ws.shape, BF), pltpu.VMEM((rows, columns), BF), pltpu.VMEM((rows, columns), BF),
-         pltpu.VMEM((rows, 3 * columns), BF), pltpu.VMEM((rows, columns), F32), dma((8,))],
-        10 * square, "space_backward",
-    )
-    gx, sums_t, dwt = call(
-        time_backward, (gy, x, normed_t, qkv_t, p_t, o_t, e_t, small, wt), (0,) * 8 + (1,),
-        [act, sums, (wt.shape, BF)],
-        [pltpu.VMEM(wt.shape, BF)] + [pltpu.VMEM((rows, columns), BF)] * 3
-        + [pltpu.VMEM((rows, 3 * columns), BF), pltpu.VMEM((rows, columns), F32)]
-        + [pltpu.VMEM((4 * BLOCK, columns), BF)] * 2 + [dma((8,))],
-        10 * square, "time_backward",
-    )
-    return out, gx, dwt, dws, dwe, dwr, sums_t, sums_s, sums_f, ghb
+class Layer:
+    def __init__(self, rows, columns, units, shards, pieced, place):
+        self.rows, self.columns, self.units = rows, columns, units
+        self.pieced, self.place = pieced, place
+        self.piece = columns // shards
+        self.act = ((rows, columns), BF)
+        self.act3 = ((rows, 3 * columns), BF)
+        self.wide = ((rows, columns), F32)
+        self.sums = ((8, columns), F32)
+        self.square = 2 * rows * columns * columns
+
+    def grads(self, width):
+        if self.pieced:
+            return [((4, self.piece, width), BF)] * 2
+        return [((self.columns, width), BF)]
+
+    def vmem(self, *shapes):
+        return [pltpu.VMEM(s, d) for s, d in shapes]
+
+    def sems(self, count):
+        return [pltpu.SemaphoreType.DMA((count,))]
+
+    def time_forward(self, x, small, bufs):
+        c, n = self.columns, len(bufs)
+        quad = ((4 * BLOCK, c), BF)
+        return call(
+            functools.partial(time_forward, n), (self.place, x, small, *bufs), "svv" + "a" * n,
+            [self.act, self.act3, self.act, self.act, ((self.rows * FRAMES, 128), F32), self.wide], "v" * 6,
+            self.vmem(((c, 5 * c), BF), quad, quad) + self.sems(8), 5 * self.square, "time_forward",
+        )
+
+    def space_forward(self, y, small, bufs):
+        c, n = self.columns, len(bufs)
+        probs = ((self.rows // BLOCK * (c // 128) * 2, BLOCK, BLOCK), BF)
+        return call(
+            functools.partial(space_forward, n), (self.place, y, small, *bufs), "svv" + "a" * n,
+            [self.act, self.act3, probs, self.act, self.wide], "v" * 5,
+            self.vmem(((c, 4 * c), BF)) + self.sems(8), 5 * self.square, "space_forward",
+        )
+
+    def feed(self, z, g, small, hb, bufs):
+        c, u, n = self.columns, self.units, len(bufs)
+        outs = self.grads(u + u) if self.pieced else [((c, u), BF), ((u, c), BF)]
+        return call(
+            functools.partial(feed, n), (self.place, z, g, small, hb, *bufs), "svvvv" + "a" * n,
+            [self.act, self.wide, self.sums, ((8, u), F32)] + outs, "vvvv" + "a" * len(outs),
+            self.vmem(((c, u), BF), ((u, c), BF), ((c, u), BF), ((u, c), BF), self.act, ((self.rows, u), BF), ((self.rows, u), BF), self.wide)
+            + self.sems(64) + self.sems(64), 24 * self.square, "feed",
+        )
+
+    def space_backward(self, gz, y, normed, qkv, p, o, small, bufs):
+        c, n = self.columns, len(bufs)
+        outs = self.grads(4 * c)
+        return call(
+            functools.partial(space_backward, n, len(outs)), (self.place, gz, y, normed, qkv, p, o, small, *bufs), "s" + "v" * 7 + "a" * n,
+            [self.wide, self.sums] + outs, "vv" + "a" * len(outs),
+            self.vmem(((c, 4 * c), BF), ((c, 4 * c), BF), self.act, self.act, self.act3, self.wide) + self.sems(8) + self.sems(8),
+            10 * self.square, "space_backward",
+        )
+
+    def time_backward(self, gy, x, normed, qkv, p, o, e, small, bufs):
+        c, n = self.columns, len(bufs)
+        outs = self.grads(5 * c)
+        quad = ((4 * BLOCK, c), BF)
+        return call(
+            functools.partial(time_backward, n, len(outs)), (self.place, gy, x, normed, qkv, p, o, e, small, *bufs), "s" + "v" * 8 + "a" * n,
+            [self.act, self.sums] + outs, "vv" + "a" * len(outs),
+            self.vmem(((c, 5 * c), BF), ((c, 5 * c), BF), self.act, self.act, self.act, self.act3, self.wide, quad, quad) + self.sems(8) + self.sems(8),
+            10 * self.square, "time_backward",
+        )
+
+
+BOTH = ("grp", "shard")
+
+
+def permute(value, target):
+    shards = lax.axis_size("shard")
+    pairs = [(z * shards + s, z * shards + target(s)) for z in range(lax.axis_size("grp")) for s in range(shards)]
+    return lax.ppermute(value, BOTH, pairs)
+
+
+def to_sibling(value):
+    return permute(value, lambda s: s ^ 1)
+
+
+def along_x(value):
+    return permute(value, lambda s: s ^ 2)
+
+
+def along_y(value):
+    return permute(value, lambda s: s ^ 4)
+
+
+def gather_start(own):
+    return jnp.concatenate([own, to_sibling(own)], axis=0)
+
+
+def gather_hop(both):
+    return permute(both, lambda s: s ^ (2 if s % 2 == 0 else 4))
+
+
+def gather_rest(both, hop):
+    second = permute(hop[: hop.shape[0] // 2], lambda s: s ^ (4 if s % 2 == 0 else 2))
+    return (both, hop, second, to_sibling(hop), to_sibling(second))
+
+
+def places(s):
+    near = jnp.where(s % 2 == 0, 2, 4)
+    far = 6 - near
+    gathered = [s, s ^ 1, s ^ near, s ^ near ^ 1, s ^ 6, s ^ 1 ^ far, s ^ far, s ^ 7]
+    kept = [s, s ^ 2, s ^ 4, s ^ 6]
+    return jnp.stack(gathered + kept + [k ^ 1 for k in kept]).astype(jnp.int32)
+
+
+def reduce_pieces(keep, give):
+    summed = keep + to_sibling(give)
+    own, west, north, far = summed[0], summed[1], summed[2], summed[3]
+    half = own.shape[0] // 2
+    got_x = along_x(jnp.stack([far[:half], west[:half]]))
+    got_y = along_y(jnp.stack([far[half:], north[half:]]))
+    last_x = along_x(west[half:] + got_y[0])
+    last_y = along_y(north[:half] + got_x[0])
+    wide = own.astype(F32)
+    low_half = wide[:half] + got_x[1].astype(F32) + last_y.astype(F32)
+    high_half = wide[half:] + got_y[1].astype(F32) + last_x.astype(F32)
+    return jnp.concatenate([low_half, high_half], axis=0).astype(BF)
 
 
 def local(video, cotangent, live, time_entry, time_exit, time_mixer, space_entry, space_exit, hidden_expand, hidden_reduce, bias_rows, hidden_bias, norm_gain, norm_shift):
     clips, _, tokens, columns = video.shape
-    shards = lax.axis_size("shard")
+    shards, groups = lax.axis_size("shard"), lax.axis_size("grp")
     mine = lax.axis_index("shard")
     part = columns // shards
-
-    def gather(value):
-        return lax.all_gather(value, "shard", axis=0, tiled=True)
+    units = hidden_bias.shape[0] * shards
+    share = units // columns
+    pieced = shards == 8
+
+    own_t = jnp.concatenate([time_entry, time_exit, time_mixer], axis=1)
+    own_s = jnp.concatenate([space_entry, space_exit], axis=1)
+    if pieced:
+        own_f = jnp.concatenate([hidden_expand] + [hidden_reduce[k * part : (k + 1) * part] for k in range(share)], axis=1)
+        both_t = gather_start(own_t)
+        hop_t = gather_hop(both_t)
+        both_s, both_f = gather_start(own_s), gather_start(own_f)
+        both_s, hop_t = lax.optimization_barrier((both_s, hop_t))
+        wt = gather_rest(both_t, hop_t)
+        hop_s = gather_hop(both_s)
+        both_f, hop_s = lax.optimization_barrier((both_f, hop_s))
+        ws = gather_rest(both_s, hop_s)
+        wf = gather_rest(both_f, gather_hop(both_f))
+        place = places(mine)
+    else:
+        wt, ws, we, wr = (lax.all_gather(v, "shard", axis=0, tiled=True) for v in (own_t, own_s, hidden_expand, hidden_reduce))
+        wt, ws, wf = (wt,), (ws,), (we, wr)
+        place = jnp.zeros((16,), jnp.int32)
 
     packed = jnp.concatenate([bias_rows, hidden_bias.reshape(-1, part), norm_gain, norm_shift], axis=0)
-    n_hidden = hidden_bias.shape[0] // part
     spread = lax.all_gather(packed, "shard", axis=0)
     by_rows = jnp.concatenate(
         [
             spread[:, :8].transpose(1, 0, 2).reshape(8, columns),
-            spread[:, 8 : 8 + n_hidden].reshape(-1, columns),
-            spread[:, 8 + n_hidden :].transpose(1, 0, 2).reshape(6, columns),
+            spread[:, 8 : 8 + share].reshape(-1, columns),
+            spread[:, 8 + share :].transpose(1, 0, 2).reshape(6, columns),
         ],
         axis=0,
     ).astype(F32)
-    units = hidden_bias.shape[0] * shards
     small = jnp.pad(by_rows, ((0, 6), (0, 0)))
-    hb = jnp.pad(spread[:, 8 : 8 + n_hidden].reshape(1, units).astype(F32), ((0, 7), (0, 0)))
-    wt = gather(jnp.concatenate([time_entry, time_exit, time_mixer], axis=1))
-    ws = gather(jnp.concatenate([space_entry, space_exit], axis=1))
-    we = gather(hidden_expand)
-    wr = gather(hidden_reduce)
+    hb = jnp.pad(spread[:, 8 : 8 + share].reshape(1, units).astype(F32), ((0, 7), (0, 0)))
     flags = live.astype(BF)[:, :, None]
     x = pack_rows(video[:, 0], False)
     g = pack_rows(cotangent[:, 0] * flags, True)
-    out, gx, dwt, dws, dwe, dwr, sums_t, sums_s, sums_f, ghb = layer(x, g, small, hb, wt, ws, we, wr)
-
-    def reduce(value):
-        kept = lax.psum_scatter(value, "shard", scatter_dimension=0, tiled=True)
-        return lax.psum(kept, "grp").astype(F32)
-
-    rt, rs, re, rr = reduce(dwt), reduce(dws), reduce(dwe), reduce(dwr)
-    sums = jnp.concatenate([sums_t[0:4], sums_s[0:3], sums_f[0:1], ghb[0:1].reshape(-1, columns), sums_t[4:5], sums_s[3:4], sums_f[1:2], sums_t[5:6], sums_s[4:5], sums_f[2:3]], axis=0)
+
+    net = Layer(x.shape[0], columns, units, shards, pieced, place)
+    normed_t, qkv_t, o_t, e_t, p_t, y = net.time_forward(x, small, wt)
+    normed_s, qkv_s, p_s, o_s, z = net.space_forward(y, small, ws)
+    out, gz, sums_f, ghb, *grad_f = net.feed(z, g, small, hb, wf)
+    gy, sums_s, *grad_s = net.space_backward(gz, y, normed_s, qkv_s, p_s, o_s, small, ws)
+    gx, sums_t, *grad_t = net.time_backward(gy, x, normed_t, qkv_t, p_t, o_t, e_t, small, wt)
+
+    if pieced:
+        kept_f = lax.psum(reduce_pieces(*grad_f), "grp")
+        kept_s, kept_f = lax.optimization_barrier((reduce_pieces(*grad_s), kept_f))
+        kept_s = lax.psum(kept_s, "grp")
+        kept_t, kept_s = lax.optimization_barrier((reduce_pieces(*grad_t), kept_s))
+        kept_t = lax.psum(kept_t, "grp")
+        rt, rs, rf = (v.astype(F32) for v in (kept_t, kept_s, kept_f))
+        re = rf[:, :units]
+        rr = jnp.concatenate([rf[:, units + k * columns : units + (k + 1) * columns] for k in range(share)], axis=0)
+    else:
+        rt, rs, re, rr = (
+            lax.psum(lax.psum_scatter(v, "shard", scatter_dimension=0, tiled=True), "grp").astype(F32)
+            for v in (*grad_t, *grad_s, *grad_f)
+        )
+    sums = jnp.concatenate(
+        [sums_t[0:4], sums_s[0:3], sums_f[0:1], ghb[0:1].reshape(-1, columns), sums_t[4:5], sums_s[3:4], sums_f[1:2], sums_t[5:6], sums_s[4:5], sums_f[2:3]],
+        axis=0,
+    )
     sums = lax.psum(sums, ("grp", "shard"))
     cut = lax.dynamic_slice_in_dim(sums, mine * part, part, axis=1)
-    rows_hidden = lax.dynamic_slice_in_dim(sums[8:12].reshape(-1), mine * hidden_bias.shape[0], hidden_bias.shape[0])
+    rows_hidden = lax.dynamic_slice_in_dim(sums[8 : 8 + share].reshape(-1), mine * hidden_bias.shape[0], hidden_bias.shape[0])
+    last = 8 + share
     return (
         (unpack_rows(out, clips) * flags)[:, None],
         unpack_rows(gx, clips)[:, None],
@@ -582,8 +771,8 @@
         rr,
         cut[0:8],
         rows_hidden,
-        cut[12:15],
-        cut[15:18],
+        cut[last : last + 3],
+        cut[last + 3 : last + 6],
     )
 
 

time: 629 us -> 602 us (0.957)
  waiting for transfers between devices: 337 us -> 232 us
  local copies, waits for them, and re-layouts: 16.5 us -> 44.9 us
  starting transfers between devices: 0.36 us -> 26.9 us
  other arithmetic: 22 us -> 45.8 us
    reduce_scatter x4 -> x0, waiting for transfers between devices: 195 us -> none  [reduce(): kept = lax.psum_scatter(value, 'shard', scatter_dimension=0, tiled=True)]
    ppermute x0 -> x30, waiting for transfers between devices: none -> 112 us  [permute(): return lax.ppermute(value, BOTH, pairs)]
    all_gather x4 -> x0, waiting for transfers between devices: 90 us -> none  [gather(): return lax.all_gather(value, 'shard', axis=0, tiled=True)]
    psum x1 -> x3, waiting for transfers between devices: 48.8 us -> 120 us  [the longest x1 45.6 us: local(): kept_f = lax.psum(reduce_pieces(*grad_f), 'grp')]
    ppermute x0 -> x30, starting transfers between devices: none -> 26.8 us  [permute(): return lax.ppermute(value, BOTH, pairs)]
    add x0 -> x6, other arithmetic: none -> 13.5 us  [the longest x3 9.37 us: reduce_pieces(): summed = keep + to_sibling(give)]
    slice x3 -> x12, local copies, waits for them, and re-layouts: 0.67 us -> 7.78 us  [the longest x3 5.49 us: gather_rest(): hop[:hop.shape[0] // 2]]
    another operation x0 -> x9, other arithmetic: none -> 6.85 us
  transfers between devices with their start and end apart: 9 -> 33, of which waited for: 9 -> 11; matrix products, arithmetic and copies ran while one was open for 5% -> 14% of each run, Pallas kernels for 14% -> 14%
where the time goes in v2:
time: 602 us; the launch traced here: 594 us
  waiting for transfers between devices  232 us (39%)
  Pallas kernels  174 us (29%)
  blocking collectives  54.9 us (9%)
  other arithmetic  45.8 us (8%)
  local copies, waits for them, and re-layouts  44.9 us (7%)
  starting transfers between devices  26.9 us (4%)
  between operations  14.9 us (2%)
    pallas_call x5, Pallas kernels, call(): pl.pallas_call(body, out_shape=[jax.ShapeDtypeStruct(s, d) for s, d in ou...  174 us
    ppermute x30, waiting for transfers between devices, permute(): return lax.ppermute(value, BOTH, pairs)  112 us
    psum x1, waiting for transfers between devices, local(): kept_f = lax.psum(reduce_pieces(*grad_f), 'grp')  45.6 us
    psum x1, blocking collectives, local(): sums = lax.psum(sums, ('grp', 'shard'))  40.7 us
    psum x1, waiting for transfers between devices, local(): kept_s = lax.psum(kept_s, 'grp')  39.4 us
    psum x1, waiting for transfers between devices, local(): kept_t = lax.psum(kept_t, 'grp')  35.3 us
    ppermute x30, starting transfers between devices, permute(): return lax.ppermute(value, BOTH, pairs)  26.8 us
    all_gather x1, blocking collectives, local(): spread = lax.all_gather(packed, 'shard', axis=0)  14.1 us
  transfers between devices with their start and end apart: 33, of which 11 were waited for; matrix products, arithmetic and copies ran while one was open for 14% of the time, Pallas kernels for 14%

profile of v2, /device:TPU:0, one launch (start us, length us, event | category | flops | bytes accessed | tf_op | source)
XLA Modules:
  0.0 594.0 jit_solution(7476145596717561994)
XLA Ops:
  10.1 1.6 collective-permute-done
  11.8 2.9 collective-permute-start.2
  15.1 17.1 %collective-permute-done.2.refs_1_ = bf16[192,3840]{1,0:T(8,128)(2,1)} collective-permute-done((bf16[192,3840]{1,0:T(8,128)(2,1)S(1)}, bf16[192,3840]{1,0:T(8,128)(2,1)}, u32[]{:S(2)}, u32[]{:S(2)}) %collective-permute-start.2) | collective-permute-done | bytes 1474592 | tf_op jit(solution)/shard_map/ppermute | solution.py:639
  32.2 2.0 collective-permute-start.7
  34.5 14.0 %collective-permute-done.7.refs_1_ = bf16[192,3072]{1,0:T(8,128)(2,1)} collective-permute-done((bf16[192,3072]{1,0:T(8,128)(2,1)S(1)}, bf16[192,3072]{1,0:T(8,128)(2,1)}, u32[]{:S(2)}, u32[]{:S(2)}) %collective-permute-start.7) | collective-permute-done | bytes 1179680 | tf_op jit(solution)/shard_map/ppermute | solution.py:639
  48.5 2.0 collective-permute-start.11
  55.0 2.0 slice.314
  57.0 1.5 collective-permute-start.3
  58.5 26.8 %collective-permute-done.11.refs_1_ = bf16[192,6144]{1,0:T(8,128)(2,1)} collective-permute-done((bf16[192,6144]{1,0:T(8,128)(2,1)S(1)}, bf16[192,6144]{1,0:T(8,128)(2,1)}, u32[]{:S(2)}, u32[]{:S(2)}) %collective-permute-start.11) | collective-permute-done | bytes 2359328 | tf_op jit(solution)/shard_map/ppermute | solution.py:639
  85.4 2.4 slice.402
  87.7 2.0 collective-permute-start.12
  89.8 5.8 maximum_bitcast_fusion.1
  95.7 4.9 pad_maximum_fusion.2
  101.8 14.1 %all-gather.1 = bf16[8,18,96]{2,1,0:T(8,128)(2,1)S(1)} all-gather(bf16[1,18,96]{2,1,0:T(8,128)(2,1)S(1)} %maximum_bitcast_fusion.3), channel_id=2, replica_groups=mesh['grp'=4,'shard'=8] {'shard'}, dimensions={0}, use_global_device_ids=true | all-gather | bytes 31104 | tf_op jit(solution)/shard_map/all_gather | solution.py:718
  121.8 17.6 %time_forward.1 = (bf16[832,768]{1,0:T(8,128)(2,1)}, bf16[832,2304]{1,0:T(8,128)(2,1)}, bf16[832,768]{1,0:T(8,128)(2,1)}, bf16[832,768]{1,0:T(8,128)(2,1)}, f32[1664,128]{1,0:T(8,128)}, /*index=5*/f32[832,768]{1,0:T(8,128)}) custom-call(s32[16]{0:T(128)} %stack.106.place_ref, bf16[832,768]{1,0:T(8,128)(2,1)} %bitcast.100, f32[24,768]{1,0:T(8,128)} %fusion.33.small_ref, ...), custom_call_target="tpu_custom_call" | custom-call | flops 4907335680 | bytes 18325568 | tf_op jit(solution)/shard_map/time_forward/pallas_call | solution.py:532
  139.4 33.5 %space_forward.1 = (bf16[832,768]{1,0:T(8,128)(2,1)}, bf16[832,2304]{1,0:T(8,128)(2,1)}, bf16[48,208,208]{2,1,0:T(8,128)(2,1)}, bf16[832,768]{1,0:T(8,128)(2,1)}, f32[832,768]{1,0:T(8,128)}) custom-call(s32[16]{0:T(128)} %stack.106.place_ref, f32[832,768]{1,0:T(8,128)} %get-tuple-element.47.y_ref, f32[24,768]{1,0:T(8,128)} %fusion.33.small_ref, ...), custom_call_target="tpu_custom_call" | custom-call | flops 4907335680 | bytes 20447296 | tf_op jit(solution)/shard_map/space_forward/pallas_call | solution.py:532
  172.9 46.6 %feed.1 = (bf16[832,768]{1,0:T(8,128)(2,1)}, f32[832,768]{1,0:T(8,128)}, f32[8,768]{1,0:T(8,128)}, f32[8,3072]{1,0:T(8,128)}, bf16[4,96,6144]{2,1,0:T(8,128)(2,1)}, /*index=5*/bf16[4,96,6144]{2,1,0:T(8,128)(2,1)}) custom-call(s32[16]{0:T(128)} %stack.106.place_ref, f32[832,768]{1,0:T(8,128)} %get-tuple-element.50.z_ref, bf16[832,768]{1,0:T(8,128)(2,1)} %bitcast.102, ...), custom_call_target="tpu_custom_call" | custom-call | flops 23555211264 | bytes 26837056 | tf_op jit(solution)/shard_map/feed/pallas_call | solution.py:532
  219.6 43.6 %space_backward.1 = (f32[832,768]{1,0:T(8,128)}, f32[8,768]{1,0:T(8,128)}, bf16[4,96,3072]{2,1,0:T(8,128)(2,1)}, bf16[4,96,3072]{2,1,0:T(8,128)(2,1)}) custom-call(s32[16]{0:T(128)} %stack.106.place_ref, f32[832,768]{1,0:T(8,128)} %get-tuple-element.53.gz_ref, f32[832,768]{1,0:T(8,128)} %get-tuple-element.47.y_ref, ...), custom_call_target="tpu_custom_call" | custom-call | flops 9814671360 | bytes 27746368 | tf_op jit(solution)/shard_map/space_backward/pallas_call | solution.py:532
  263.7 33.0 %time_backward.1 = (bf16[832,768]{1,0:T(8,128)(2,1)}, f32[8,768]{1,0:T(8,128)}, bf16[4,96,3840]{2,1,0:T(8,128)(2,1)}, bf16[4,96,3840]{2,1,0:T(8,128)(2,1)}) custom-call(s32[16]{0:T(128)} %stack.106.place_ref, f32[832,768]{1,0:T(8,128)} %get-tuple-element.58.gy_ref, bf16[832,768]{1,0:T(8,128)(2,1)} %bitcast.101, bf16[832,768]{1,0:T(8,128)(2,1)} %get-tuple-element.59.nt_ref, ...), custom_call_target="tpu_custom_call" | custom-call | flops 9814671360 | bytes 25526336 | tf_op jit(solution)/shard_map/time_backward/pallas_call | solution.py:532
  296.6 1.3 slice.379
  301.4 1.3 fusion.38
  304.5 1.4 fusion.46
  305.9 1.4 fusion.45
  307.3 1.4 fusion.44
  308.7 4.0 concatenate.85
  312.8 40.7 %psum.31 = f32[18,768]{1,0:T(8,128)} all-reduce(f32[18,768]{1,0:T(8,128)} %concatenate.85), channel_id=1, replica_groups=mesh['grp'=4,'shard'=8] {'grp','shard'}, use_global_device_ids=true, to_apply=%region_3.4 | all-reduce | flops 13824 | bytes 110592 | tf_op jit(solution)/shard_map/psum | solution.py:758
  353.5 1.4 constant_dynamic-slice_fusion
  354.9 2.4 fusion.37
  357.3 2.8 maximum_multiply_fusion
  360.2 2.5 add.133
  363.7 2.3 collective-permute-start.23
  368.8 1.6 copy-done.6
  370.4 2.7 add.122
  374.4 4.1 add.144
  381.3 2.0 collective-permute-start.18
  385.1 1.8 fusion.27
  388.1 19.8 %collective-permute-done.28 = bf16[2,48,6144]{2,1,0:T(8,128)(2,1)S(1)} collective-permute-done((bf16[2,48,6144]{2,1,0:T(8,128)(2,1)S(1)}, bf16[2,48,6144]{2,1,0:T(8,128)(2,1)S(1)}, u32[]{:S(2)}, u32[]{:S(2)}) %collective-permute-start.28) | collective-permute-done | bytes 1179680 | tf_op jit(solution)/shard_map/ppermute | solution.py:639
  407.9 1.4 collective-permute-done.26
  411.7 28.1 %collective-permute-done.27 = bf16[48,6144]{1,0:T(8,128)(2,1)S(1)} collective-permute-done((bf16[48,6144]{1,0:T(8,128)(2,1)S(1)}, bf16[48,6144]{1,0:T(8,128)(2,1)S(1)}, u32[]{:S(2)}, u32[]{:S(2)}) %collective-permute-start.27) | collective-permute-done | bytes 589856 | tf_op jit(solution)/shard_map/ppermute | solution.py:639
  442.2 2.1 fusion.25
  444.7 1.6 collective-permute-start.19
  446.3 3.0 collective-permute-done.24
  449.3 1.4 fusion.23
  451.5 45.6 %all-reduce.6.cloned.1.call-done = bf16[96,6144]{1,0:T(8,128)(2,1)} async-done(((bf16[96,6144]{1,0:T(8,128)(2,1)}), bf16[96,6144]{1,0:T(8,128)(2,1)}) %all-reduce.6.cloned.1.call-update) | async-done | bytes 1179664 | tf_op jit(solution)/shard_map/psum | solution.py:741
  499.5 39.4 %all-reduce.8.cloned.1.call-done = bf16[96,3072]{1,0:T(8,128)(2,1)} async-done(((bf16[96,3072]{1,0:T(8,128)(2,1)}), bf16[96,3072]{1,0:T(8,128)(2,1)}) %all-reduce.8.cloned.1.call-update) | async-done | bytes 589840 | tf_op jit(solution)/shard_map/psum | solution.py:743
  542.0 2.6 maximum_bitcast_fusion
  548.8 35.3 %all-reduce.10.cloned.1.call-done = bf16[96,3840]{1,0:T(8,128)(2,1)} async-done(((bf16[96,3840]{1,0:T(8,128)(2,1)}), bf16[96,3840]{1,0:T(8,128)(2,1)}) %all-reduce.10.cloned.1.call-update) | async-done | bytes 737296 | tf_op jit(solution)/shard_map/psum | solution.py:745
  584.1 2.1 slice.448
  (196 shorter events, 47.7 us)
Async XLA Ops:
  7.2 489.9 %all-reduce.6.cloned.1.call-start = ((), (), s32[]{:S(2)}) async-start(), calls=%async_computation | async-start | bytes 2359296 | tf_op jit(solution)/shard_map/psum | solution.py:741
  9.4 2.4 collective-permute-start
  10.0 5.0 collective-permute-start.1
  11.8 20.4 %collective-permute-start.2 = (bf16[192,3840]{1,0:T(8,128)(2,1)S(1)}, bf16[192,3840]{1,0:T(8,128)(2,1)}, u32[]{:S(2)}, u32[]{:S(2)}) collective-permute-start(bf16[192,3840]{1,0:T(8,128)(2,1)S(1)} %pad_maximum_fusion.1.refs_0_), channel_id=1, source_target_pairs={{0,2},{1,5},{2,0},{3,7},{4,6},{5,1},{6,4},{7,3},{8,10},{9,13},{10,... | collective-permute-start | bytes 4423688 | tf_op jit(solution)/shard_map/ppermute | solution.py:639
  14.8 19.4 %collective-permute-start.6 = (bf16[96,6144]{1,0:T(8,128)(2,1)S(1)}, bf16[96,6144]{1,0:T(8,128)(2,1)S(1)}, u32[]{:S(2)}, u32[]{:S(2)}) collective-permute-start(bf16[96,6144]{1,0:T(8,128)(2,1)S(1)} %slice_dynamic-update-slice_fusion), channel_id=1, source_target_pairs={{0,1},{1,0},{2,3},{3,2},{4,5},{5,4},{6,7},{7,6},{8,9},{9,8},{10,11... | collective-permute-start | bytes 3538952 | tf_op jit(solution)/shard_map/ppermute | solution.py:639
  15.0 19.4 %copy-start.16 = (bf16[192,3072]{1,0:T(8,128)(2,1)}, bf16[192,3072]{1,0:T(8,128)(2,1)S(1)}, u32[]{:S(2)}) copy-start(bf16[192,3072]{1,0:T(8,128)(2,1)S(1)} %pad_maximum_fusion.4.refs_0_) | copy-start | bytes 3538948
  15.0 35.5 %copy-start.30 = (s32[2,1]{0,1:T(1,128)S(1)}, s32[2,1]{0,1:T(1,128)}, u32[]{:S(2)}) copy-start(s32[2,1]{0,1:T(1,128)} %param.16) | copy-start | bytes 28
  15.0 36.1 %copy-start.14 = (bf16[2,1,393,768]{3,0,2,1:T(2,128)(2,1)S(1)}, bf16[2,1,393,768]{3,0,2,1:T(2,128)(2,1)}, u32[]{:S(2)}) copy-start(bf16[2,1,393,768]{3,0,2,1:T(2,128)(2,1)} %param.15) | copy-start | bytes 3621892
  32.2 16.3 %collective-permute-start.7 = (bf16[192,3072]{1,0:T(8,128)(2,1)S(1)}, bf16[192,3072]{1,0:T(8,128)(2,1)}, u32[]{:S(2)}, u32[]{:S(2)}) collective-permute-start(bf16[192,3072]{1,0:T(8,128)(2,1)S(1)} %pad_maximum_fusion.4.refs_0_), channel_id=1, source_target_pairs={{0,2},{1,5},{2,0},{3,7},{4,6},{5,1},{6,4},{7,3},{8,10},{9,13},{10,... | collective-permute-start | bytes 3538952 | tf_op jit(solution)/shard_map/ppermute | solution.py:639
  34.5 17.8 %copy-start.12 = (bf16[192,6144]{1,0:T(8,128)(2,1)}, bf16[192,6144]{1,0:T(8,128)(2,1)S(1)}, u32[]{:S(2)}) copy-start(bf16[192,6144]{1,0:T(8,128)(2,1)S(1)} %pad_maximum_fusion.refs_0_) | copy-start | bytes 7077892
  48.5 36.8 %collective-permute-start.11 = (bf16[192,6144]{1,0:T(8,128)(2,1)S(1)}, bf16[192,6144]{1,0:T(8,128)(2,1)}, u32[]{:S(2)}, u32[]{:S(2)}) collective-permute-start(bf16[192,6144]{1,0:T(8,128)(2,1)S(1)} %pad_maximum_fusion.refs_0_), channel_id=1, source_target_pairs={{0,2},{1,5},{2,0},{3,7},{4,6},{5,1},{6,4},{7,3},{8,10},{9,13},{10,... | collective-permute-start | bytes 7077896 | tf_op jit(solution)/shard_map/ppermute | solution.py:639
  52.3 64.1 %collective-permute-start.4 = (bf16[192,3840]{1,0:T(8,128)(2,1)}, bf16[192,3840]{1,0:T(8,128)(2,1)}, u32[]{:S(2)}, u32[]{:S(2)}) collective-permute-start(bf16[192,3840]{1,0:T(8,128)(2,1)} %collective-permute-done.2.refs_1_), channel_id=1, source_target_pairs={{0,1},{1,0},{2,3},{3,2},{4,5},{5,4},{6,7},{7,6},{8,9},{9,8},{10,11... | collective-permute-start | bytes 4423688 | tf_op jit(solution)/shard_map/ppermute | solution.py:639
  57.0 32.8 %slice-start = ((bf16[2,393,768]{2,0,1:T(2,128)(2,1)}), bf16[2,1,768]{2,0,1:T(2,128)(2,1)S(1)}, s32[]{:S(2)}) async-start(bf16[2,393,768]{2,0,1:T(2,128)(2,1)} %copy-done.1), calls=%async_computation.3 | async-start | bytes 6144 | tf_op jit(solution)/shard_map/slice | solution.py:549
  57.0 59.0 %collective-permute-start.3 = (bf16[96,3840]{1,0:T(8,128)(2,1)}, bf16[96,3840]{1,0:T(8,128)(2,1)}, u32[]{:S(2)}, u32[]{:S(2)}) collective-permute-start(bf16[96,3840]{1,0:T(8,128)(2,1)} %slice.314), channel_id=1, source_target_pairs={{0,4},{1,3},{2,6},{3,1},{4,0},{5,7},{6,2},{7,5},{8,12},{9,11},{10,... | collective-permute-start | bytes 2211848 | tf_op jit(solution)/shard_map/ppermute | solution.py:639
  87.7 29.9 %collective-permute-start.12 = (bf16[96,6144]{1,0:T(8,128)(2,1)}, bf16[96,6144]{1,0:T(8,128)(2,1)}, u32[]{:S(2)}, u32[]{:S(2)}) collective-permute-start(bf16[96,6144]{1,0:T(8,128)(2,1)} %slice.402), channel_id=1, source_target_pairs={{0,4},{1,3},{2,6},{3,1},{4,0},{5,7},{6,2},{7,5},{8,12},{9,11},{10,... | collective-permute-start | bytes 3538952 | tf_op jit(solution)/shard_map/ppermute | solution.py:639
  95.7 77.2 %collective-permute-start.13 = (bf16[192,6144]{1,0:T(8,128)(2,1)}, bf16[192,6144]{1,0:T(8,128)(2,1)}, u32[]{:S(2)}, u32[]{:S(2)}) collective-permute-start(bf16[192,6144]{1,0:T(8,128)(2,1)} %collective-permute-done.11.refs_1_), channel_id=1, source_target_pairs={{0,1},{1,0},{2,3},{3,2},{4,5},{5,4},{6,7},{7,6},{8,9},{9,8},{10,11... | collective-permute-start | bytes 7077896 | tf_op jit(solution)/shard_map/ppermute | solution.py:639
  95.7 6.1 %copy-start.26 = (bf16[8,96]{1,0:T(8,128)(2,1)S(1)}, bf16[8,96]{1,0:T(8,128)(2,1)}, u32[]{:S(2)}) copy-start(bf16[8,96]{1,0:T(8,128)(2,1)} %param.24) | copy-start | bytes 4612
  95.7 6.1 %copy-start.28 = (bf16[3,96]{1,0:T(4,128)(2,1)S(1)}, bf16[3,96]{1,0:T(4,128)(2,1)}, u32[]{:S(2)}) copy-start(bf16[3,96]{1,0:T(4,128)(2,1)} %param.27) | copy-start | bytes 1732
  95.7 6.1 %copy-start.29 = (bf16[3,96]{1,0:T(4,128)(2,1)S(1)}, bf16[3,96]{1,0:T(4,128)(2,1)}, u32[]{:S(2)}) copy-start(bf16[3,96]{1,0:T(4,128)(2,1)} %param.26) | copy-start | bytes 1732
  101.7 15.6 %collective-permute-start.8 = (bf16[96,3072]{1,0:T(8,128)(2,1)S(1)}, bf16[96,3072]{1,0:T(8,128)(2,1)}, u32[]{:S(2)}, u32[]{:S(2)}) collective-permute-start(bf16[96,3072]{1,0:T(8,128)(2,1)S(1)} %slice.319), channel_id=1, source_target_pairs={{0,4},{1,3},{2,6},{3,1},{4,0},{5,7},{6,2},{7,5},{8,12},{9,11},{10,... | collective-permute-start | bytes 1769480 | tf_op jit(solution)/shard_map/ppermute | solution.py:639
  116.0 5.8 collective-permute-start.5
  116.4 23.0 %collective-permute-start.9 = (bf16[192,3072]{1,0:T(8,128)(2,1)}, bf16[192,3072]{1,0:T(8,128)(2,1)}, u32[]{:S(2)}, u32[]{:S(2)}) collective-permute-start(bf16[192,3072]{1,0:T(8,128)(2,1)} %collective-permute-done.7.refs_1_), channel_id=1, source_target_pairs={{0,1},{1,0},{2,3},{3,2},{4,5},{5,4},{6,7},{7,6},{8,9},{9,8},{10,11... | collective-permute-start | bytes 3538952 | tf_op jit(solution)/shard_map/ppermute | solution.py:639
  117.3 22.1 %collective-permute-start.10 = (bf16[96,3072]{1,0:T(8,128)(2,1)}, bf16[96,3072]{1,0:T(8,128)(2,1)}, u32[]{:S(2)}, u32[]{:S(2)}) collective-permute-start(bf16[96,3072]{1,0:T(8,128)(2,1)} %collective-permute-done.8.refs_2_), channel_id=1, source_target_pairs={{0,1},{1,0},{2,3},{3,2},{4,5},{5,4},{6,7},{7,6},{8,9},{9,8},{10,11... | collective-permute-start | bytes 1769480 | tf_op jit(solution)/shard_map/ppermute | solution.py:639
  117.7 55.2 %collective-permute-start.14 = (bf16[96,6144]{1,0:T(8,128)(2,1)}, bf16[96,6144]{1,0:T(8,128)(2,1)}, u32[]{:S(2)}, u32[]{:S(2)}) collective-permute-start(bf16[96,6144]{1,0:T(8,128)(2,1)} %collective-permute-done.12.refs_2_), channel_id=1, source_target_pairs={{0,1},{1,0},{2,3},{3,2},{4,5},{5,4},{6,7},{7,6},{8,9},{9,8},{10,11... | collective-permute-start | bytes 3538952 | tf_op jit(solution)/shard_map/ppermute | solution.py:639
  263.2 96.9 %collective-permute-start.20 = (bf16[4,96,3072]{2,1,0:T(8,128)(2,1)}, bf16[4,96,3072]{2,1,0:T(8,128)(2,1)}, u32[]{:S(2)}, u32[]{:S(2)}) collective-permute-start(bf16[4,96,3072]{2,1,0:T(8,128)(2,1)} %get-tuple-element.68), channel_id=1, source_target_pairs={{0,1},{1,0},{2,3},{3,2},{4,5},{5,4},{6,7},{7,6},{8,9},{9,8},{10,11... | collective-permute-start | bytes 7077896 | tf_op jit(solution)/shard_map/ppermute | solution.py:639
  263.7 34.3 %copy-start.23 = (f32[8,768]{1,0:T(8,128)S(1)}, f32[8,768]{1,0:T(8,128)}, u32[]{:S(2)}) copy-start(f32[8,768]{1,0:T(8,128)} %get-tuple-element.76) | copy-start | bytes 73732
  300.1 74.3 %collective-permute-start.25 = (bf16[4,96,6144]{2,1,0:T(8,128)(2,1)}, bf16[4,96,6144]{2,1,0:T(8,128)(2,1)}, u32[]{:S(2)}, u32[]{:S(2)}) collective-permute-start(bf16[4,96,6144]{2,1,0:T(8,128)(2,1)} %get-tuple-element.70), channel_id=1, source_target_pairs={{0,1},{1,0},{2,3},{3,2},{4,5},{5,4},{6,7},{7,6},{8,9},{9,8},{10,11... | collective-permute-start | bytes 14155784 | tf_op jit(solution)/shard_map/ppermute | solution.py:639
  300.2 68.5 %collective-permute-start.15 = (bf16[4,96,3840]{2,1,0:T(8,128)(2,1)}, bf16[4,96,3840]{2,1,0:T(8,128)(2,1)S(1)}, u32[]{:S(2)}, u32[]{:S(2)}) collective-permute-start(bf16[4,96,3840]{2,1,0:T(8,128)(2,1)} %get-tuple-element.66), channel_id=1, source_target_pairs={{0,1},{1,0},{2,3},{3,2},{4,5},{5,4},{6,7},{7,6},{8,9},{9,8},{10,11... | collective-permute-start | bytes 8847368 | tf_op jit(solution)/shard_map/ppermute | solution.py:639
  363.7 20.5 %collective-permute-start.23 = (bf16[2,48,3072]{2,1,0:T(8,128)(2,1)}, bf16[2,48,3072]{2,1,0:T(8,128)(2,1)S(1)}, u32[]{:S(2)}, u32[]{:S(2)}) collective-permute-start(bf16[2,48,3072]{2,1,0:T(8,128)(2,1)} %pad_maximum_fusion.15), channel_id=1, source_target_pairs={{0,4},{1,5},{2,6},{3,7},{4,0},{5,1},{6,2},{7,3},{8,12},{9,13},{10,... | collective-permute-start | bytes 1769480 | tf_op jit(solution)/shard_map/ppermute | solution.py:639
  366.8 18.3 %collective-permute-start.21 = (bf16[2,48,3072]{2,1,0:T(8,128)(2,1)}, bf16[2,48,3072]{2,1,0:T(8,128)(2,1)}, u32[]{:S(2)}, u32[]{:S(2)}) collective-permute-start(bf16[2,48,3072]{2,1,0:T(8,128)(2,1)} %pad_maximum_fusion.14), channel_id=1, source_target_pairs={{0,2},{1,3},{2,0},{3,1},{4,6},{5,7},{6,4},{7,5},{8,10},{9,11},{10,... | collective-permute-start | bytes 1769480 | tf_op jit(solution)/shard_map/ppermute | solution.py:639
  378.9 29.0 %collective-permute-start.28 = (bf16[2,48,6144]{2,1,0:T(8,128)(2,1)S(1)}, bf16[2,48,6144]{2,1,0:T(8,128)(2,1)S(1)}, u32[]{:S(2)}, u32[]{:S(2)}) collective-permute-start(bf16[2,48,6144]{2,1,0:T(8,128)(2,1)S(1)} %pad_maximum_fusion.6), channel_id=1, source_target_pairs={{0,4},{1,5},{2,6},{3,7},{4,0},{5,1},{6,2},{7,3},{8,12},{9,13},{10,... | collective-permute-start | bytes 3538952 | tf_op jit(solution)/shard_map/ppermute | solution.py:639
  380.3 29.0 %collective-permute-start.26 = (bf16[2,48,6144]{2,1,0:T(8,128)(2,1)S(1)}, bf16[2,48,6144]{2,1,0:T(8,128)(2,1)S(1)}, u32[]{:S(2)}, u32[]{:S(2)}) collective-permute-start(bf16[2,48,6144]{2,1,0:T(8,128)(2,1)S(1)} %pad_maximum_fusion.5), channel_id=1, source_target_pairs={{0,2},{1,3},{2,0},{3,1},{4,6},{5,7},{6,4},{7,5},{8,10},{9,11},{10,... | collective-permute-start | bytes 3538952 | tf_op jit(solution)/shard_map/ppermute | solution.py:639
  381.3 60.9 %collective-permute-start.18 = (bf16[2,48,3840]{2,1,0:T(8,128)(2,1)}, bf16[2,48,3840]{2,1,0:T(8,128)(2,1)}, u32[]{:S(2)}, u32[]{:S(2)}) collective-permute-start(bf16[2,48,3840]{2,1,0:T(8,128)(2,1)} %pad_maximum_fusion.10), channel_id=1, source_target_pairs={{0,4},{1,5},{2,6},{3,7},{4,0},{5,1},{6,2},{7,3},{8,12},{9,13},{10,... | collective-permute-start | bytes 2211848 | tf_op jit(solution)/shard_map/ppermute | solution.py:639
  384.2 58.0 %collective-permute-start.16 = (bf16[2,48,3840]{2,1,0:T(8,128)(2,1)}, bf16[2,48,3840]{2,1,0:T(8,128)(2,1)}, u32[]{:S(2)}, u32[]{:S(2)}) collective-permute-start(bf16[2,48,3840]{2,1,0:T(8,128)(2,1)} %pad_maximum_fusion.9), channel_id=1, source_target_pairs={{0,2},{1,3},{2,0},{3,1},{4,6},{5,7},{6,4},{7,5},{8,10},{9,11},{10,... | collective-permute-start | bytes 2211848 | tf_op jit(solution)/shard_map/ppermute | solution.py:639
  386.9 59.4 %collective-permute-start.22 = (bf16[48,3072]{1,0:T(8,128)(2,1)}, bf16[48,3072]{1,0:T(8,128)(2,1)}, u32[]{:S(2)}, u32[]{:S(2)}) collective-permute-start(bf16[48,3072]{1,0:T(8,128)(2,1)} %get-tuple-element.93), channel_id=1, source_target_pairs={{0,4},{1,5},{2,6},{3,7},{4,0},{5,1},{6,2},{7,3},{8,12},{9,13},{10,... | collective-permute-start | bytes 884744 | tf_op jit(solution)/shard_map/ppermute | solution.py:639
  409.4 30.4 %collective-permute-start.27 = (bf16[48,6144]{1,0:T(8,128)(2,1)S(1)}, bf16[48,6144]{1,0:T(8,128)(2,1)S(1)}, u32[]{:S(2)}, u32[]{:S(2)}) collective-permute-start(bf16[48,6144]{1,0:T(8,128)(2,1)S(1)} %get-tuple-element.79), channel_id=1, source_target_pairs={{0,4},{1,5},{2,6},{3,7},{4,0},{5,1},{6,2},{7,3},{8,12},{9,13},{10,... | collective-permute-start | bytes 1769480 | tf_op jit(solution)/shard_map/ppermute | solution.py:639
  410.3 30.4 %collective-permute-start.29 = (bf16[48,6144]{1,0:T(8,128)(2,1)S(1)}, bf16[48,6144]{1,0:T(8,128)(2,1)S(1)}, u32[]{:S(2)}, u32[]{:S(2)}) collective-permute-start(bf16[48,6144]{1,0:T(8,128)(2,1)S(1)} %get-tuple-element.80), channel_id=1, source_target_pairs={{0,2},{1,3},{2,0},{3,1},{4,6},{5,7},{6,4},{7,5},{8,10},{9,11},{10,... | collective-permute-start | bytes 1769480 | tf_op jit(solution)/shard_map/ppermute | solution.py:639
  439.8 9.5 %collective-permute-start.24 = (bf16[48,3072]{1,0:T(8,128)(2,1)}, bf16[48,3072]{1,0:T(8,128)(2,1)}, u32[]{:S(2)}, u32[]{:S(2)}) collective-permute-start(bf16[48,3072]{1,0:T(8,128)(2,1)} %get-tuple-element.94), channel_id=1, source_target_pairs={{0,2},{1,3},{2,0},{3,1},{4,6},{5,7},{6,4},{7,5},{8,10},{9,11},{10,... | collective-permute-start | bytes 884744 | tf_op jit(solution)/shard_map/ppermute | solution.py:639
  442.1 96.8 %all-reduce.8.cloned.1.call-start = ((), (), s32[]{:S(2)}) async-start(), calls=%async_computation.1 | async-start | bytes 1179648 | tf_op jit(solution)/shard_map/psum | solution.py:743
  442.1 7.2 %copy-start.3 = (f32[1,96,3072]{2,1,0:T(8,128)S(1)}, f32[1,96,3072]{2,1,0:T(8,128)}, u32[]{:S(2)}) copy-start(f32[1,96,3072]{2,1,0:T(8,128)} %slice_convert_fusion.2) | copy-start | bytes 3538948
  444.3 52.9 %collective-permute-start.17 = (bf16[48,3840]{1,0:T(8,128)(2,1)}, bf16[48,3840]{1,0:T(8,128)(2,1)S(1)}, u32[]{:S(2)}, u32[]{:S(2)}) collective-permute-start(bf16[48,3840]{1,0:T(8,128)(2,1)} %get-tuple-element.85), channel_id=1, source_target_pairs={{0,4},{1,5},{2,6},{3,7},{4,0},{5,1},{6,2},{7,3},{8,12},{9,13},{10,... | collective-permute-start | bytes 1105928 | tf_op jit(solution)/shard_map/ppermute | solution.py:639
  444.7 52.5 %collective-permute-start.19 = (bf16[48,3840]{1,0:T(8,128)(2,1)}, bf16[48,3840]{1,0:T(8,128)(2,1)S(1)}, u32[]{:S(2)}, u32[]{:S(2)}) collective-permute-start(bf16[48,3840]{1,0:T(8,128)(2,1)} %get-tuple-element.86), channel_id=1, source_target_pairs={{0,2},{1,3},{2,0},{3,1},{4,6},{5,7},{6,4},{7,5},{8,10},{9,11},{10,... | collective-permute-start | bytes 1105928 | tf_op jit(solution)/shard_map/ppermute | solution.py:639
  450.7 46.6 %copy-start = (f32[1,96,3840]{2,1,0:T(8,128)S(1)}, f32[1,96,3840]{2,1,0:T(8,128)}, u32[]{:S(2)}) copy-start(f32[1,96,3840]{2,1,0:T(8,128)} %slice_convert_fusion.1) | copy-start | bytes 4423684
  497.2 87.0 %all-reduce.10.cloned.1.call-start = ((), (), s32[]{:S(2)}) async-start(), calls=%async_computation.2 | async-start | bytes 1474560 | tf_op jit(solution)/shard_map/psum | solution.py:745
  498.6 40.4 %copy-start.22 = (f32[18,768]{1,0:T(8,128)S(1)}, f32[18,768]{1,0:T(8,128)}, u32[]{:S(2)}) copy-start(f32[18,768]{1,0:T(8,128)} %psum.31) | copy-start | bytes 165892
  498.6 41.8 %slice-start.3 = ((f32[18,768]{1,0:T(8,128)}), f32[4,768]{1,0:T(4,128)S(1)}, s32[]{:S(2)}) async-start(f32[18,768]{1,0:T(8,128)} %psum.31), calls=%async_computation.6 | async-start | bytes 24576 | tf_op jit(solution)/shard_map/slice | solution.py:760
  498.6 41.8 %copy-start.8 = (bf16[2,1,196,768]{3,2,1,0:T(8,128)(2,1)S(1)}, bf16[2,1,196,768]{3,2,1,0:T(8,128)(2,1)}, u32[]{:S(2)}) copy-start(bf16[2,1,196,768]{3,2,1,0:T(8,128)(2,1)} %get-tuple-element.102) | copy-start | bytes 1806340
  499.5 41.3 %copy-start.7 = (bf16[2,1,196,768]{3,2,1,0:T(8,128)(2,1)S(1)}, bf16[2,1,196,768]{3,2,1,0:T(8,128)(2,1)}, u32[]{:S(2)}) copy-start(bf16[2,1,196,768]{3,2,1,0:T(8,128)(2,1)} %get-tuple-element.101) | copy-start | bytes 1806340
  (20 other events, 55.2 us)
Sparse Core Ops, SparseCore 0:
  442.2 54.8 all-reduce.5
  500.1 38.7 all-reduce.7
  541.9 42.2 all-reduce.9

commit v3 on v2

v3 whole, which is shorter than its diff:
```python
import functools
import math

import jax
import jax.numpy as jnp
from jax import lax
from jax.experimental import pallas as pl
from jax.experimental.pallas import tpu as pltpu
from jax.sharding import PartitionSpec as P

FRAMES = 2
PLACES = 196
HD = 64
EPSILON = 1e-06
BLOCK = 208
EDGE = 192
CLASS = PLACES - EDGE
CHUNK = 2 * BLOCK
WIDE = 256
BF = jnp.bfloat16
F32 = jnp.float32
SMALL = 32
MICRO = 4_000_000_000
VMEM_LIMIT = 60 * 1024 * 1024


def nn(a, b):
    return lax.dot_general(a, b, (((1,), (0,)), ((), ())), preferred_element_type=F32)


def nt(a, b):
    return lax.dot_general(a, b, (((1,), (1,)), ((), ())), preferred_element_type=F32)


def tn(a, b):
    return lax.dot_general(a, b, (((0,), (0,)), ((), ())), preferred_element_type=F32)


def loop(count, body):
    def step(i, carry):
        body(i)
        return carry

    lax.fori_loop(0, count, step, 0)


def rows_of(i, size):
    return pl.ds(pl.multiple_of(i * size, size), size)


def cols_of(i, size, base=0):
    return pl.ds(pl.multiple_of(base + i * size, 128), size)


def unit(x):
    center = x - jnp.mean(x, axis=-1, keepdims=True)
    factor = lax.rsqrt(jnp.mean(center * center, axis=-1, keepdims=True) + EPSILON)
    return center * factor, factor


def norm_chunks(src, dst, gain, shift):
    def body(i):
        at = rows_of(i, CHUNK)
        w, _ = unit(src[at, :].astype(F32))
        dst[at, :] = (w * gain + shift).astype(BF)

    loop(src.shape[0] // CHUNK, body)


def fold(x):
    return jnp.sum(x.reshape(x.shape[0] // 8, 8, x.shape[1]), axis=0)


def norm_back_chunks(gn_ref, x_ref, gain, base_of, store):
    columns = x_ref.shape[1]

    def body(i, carry):
        gain_sum, shift_sum = carry
        at = rows_of(i, CHUNK)
        gn = gn_ref[at, :]
        w, factor = unit(x_ref[at, :].astype(F32))
        scaled = gn * gain
        plain = jnp.mean(scaled, axis=-1, keepdims=True)
        cross = jnp.mean(scaled * w, axis=-1, keepdims=True)
        store(at, base_of(at) + factor * (scaled - plain - w * cross))
        return gain_sum + fold(gn * w), shift_sum + fold(gn)

    zero = jnp.zeros((8, columns), F32)
    gain_sum, shift_sum = lax.fori_loop(0, x_ref.shape[0] // CHUNK, body, (zero, zero))
    return jnp.sum(gain_sum, axis=0, keepdims=True), jnp.sum(shift_sum, axis=0, keepdims=True)


def column_sums(ref, start, size):
    def body(i, total):
        return total + fold(ref[rows_of(i, CHUNK), start : start + size].astype(F32))

    total = lax.fori_loop(0, ref.shape[0] // CHUNK, body, jnp.zeros((8, size), F32))
    return jnp.sum(total, axis=0, keepdims=True)


def head_map(columns):
    feature = lax.broadcasted_iota(jnp.int32, (columns, 128), 0) // HD
    head = lax.broadcasted_iota(jnp.int32, (columns, 128), 1)
    return (feature == head).astype(BF)


def head_sums(a_ref, a_rows, a_base, b_ref, b_rows, b_base, heads):
    total = None
    for j in range(heads.shape[0] // WIDE):
        a = a_ref[a_rows, a_base + j * WIDE : a_base + (j + 1) * WIDE].astype(F32)
        b = b_ref[b_rows, b_base + j * WIDE : b_base + (j + 1) * WIDE].astype(F32)
        top = (a * b).astype(BF)
        rest = (a * b - top.astype(F32)).astype(BF)
        part = heads[j * WIDE : (j + 1) * WIDE, :]
        term = nn(top, part) + nn(rest, part)
        total = term if total is None else total + term
    return total


def row_in_block(i, size, columns):
    return (i * size + lax.broadcasted_iota(jnp.int32, (size, columns), 0)) % BLOCK


def start(pairs, sems):
    copies = [pltpu.make_async_copy(s, d, sems.at[n]) for n, (s, d) in enumerate(pairs)]
    for copy in copies:
        copy.start()
    return copies


def wait(copies):
    for copy in copies:
        copy.wait()


def piece_views(bufs):
    rows = bufs[2].shape[0]
    return [b.at[k * rows : (k + 1) * rows] for b in bufs for k in range(b.shape[0] // rows)]


def rows_at(place, rows, share=1, k=0):
    return pl.ds(pl.multiple_of((place * share + k) * rows, 16), rows)


def load(bufs, place_ref, w, sems):
    if len(bufs) == 1:
        return start([(bufs[0], w)], sems)
    views = piece_views(bufs)
    rows = views[0].shape[0]
    return start([(v, w.at[rows_at(place_ref[n], rows), :]) for n, v in enumerate(views)], sems)


ORDER = ((3, 0), (1, 0), (3, 1), (2, 1), (1, 1), (2, 0), (0, 0), (0, 1))


def store_pieces(dw, outs, place_ref, sems, share=1):
    if len(outs) == 1:
        return start([(dw, outs[0])], sems)
    half, columns = outs[0].shape[1], dw.shape[1]
    pairs = []
    for side, out in enumerate(outs):
        for n, (chip, top) in enumerate(ORDER):
            place = place_ref[8 + side * 4 + chip]
            for k in range(share):
                source = dw.at[pl.ds(pl.multiple_of(((place * share + k) * 2 + top) * half, 16), half), :]
                pairs.append((source, out.at[n, :, k * columns : (k + 1) * columns]))
    return start(pairs, sems)


def piece_select(piece, rows, columns):
    lane = lax.broadcasted_iota(jnp.int32, (128, columns), 0)
    column = lax.broadcasted_iota(jnp.int32, (128, columns), 1)
    return ((lane < rows) & (column == piece * rows + lane)).astype(BF)


def spread_small(w, small_ref, hb_ref):
    columns = small_ref.shape[1]
    rows = columns // 8
    start = w.shape[1] - 128
    total = jnp.zeros((SMALL, columns), F32)
    for piece in range(8):
        block = w[piece * rows : piece * rows + SMALL, start:]
        total = total + nn(block, piece_select(piece, rows, columns))
        wide = block.astype(F32)
        for r in range(3):
            at = (piece * 3 + r) * 128
            hb_ref[0:1, at : at + 128] = wide[8 + r : 9 + r, :]
    small_ref[...] = total


def gather_small(dw, sums):
    sums_t, sums_s, sums_f, ghb = sums
    columns = sums_t.shape[1]
    rows = columns // 8
    start = dw.shape[1] - 128
    zero = jnp.zeros((3, columns), F32)
    order = [sums_t[0:4, :], sums_s[0:3, :], sums_f[0:1, :], zero, sums_t[4:5, :], sums_s[3:4, :], sums_f[1:2, :]]
    order += [sums_t[5:6, :], sums_s[4:5, :], sums_f[2:3, :], jnp.zeros((SMALL - 17, columns), F32)]
    values = jnp.concatenate(order, axis=0).astype(BF)
    for piece in range(8):
        block = nt(values, piece_select(piece, rows, columns))
        hidden = [ghb[0:1, (piece * 3 + r) * 128 : (piece * 3 + r + 1) * 128] for r in range(3)]
        block = jnp.concatenate([block[0:8, :]] + hidden + [block[11:, :]], axis=0)
        dw[piece * rows : piece * rows + SMALL, start:] = block.astype(BF)
        dw[piece * rows + SMALL : (piece + 1) * rows, start:] = jnp.zeros((rows - SMALL, 128), BF)


def load_feed(bufs, place_ref, we, wr, sems):
    if len(bufs) == 2:
        return start([(bufs[0], we)], sems), start([(bufs[1], wr)], sems.at[8:])
    views = piece_views(bufs)
    rows, units, columns = views[0].shape[0], we.shape[1], wr.shape[1]
    share = units // columns
    first = start([(v.at[:, 0:units], we.at[rows_at(place_ref[n], rows), :]) for n, v in enumerate(views)], sems)
    pairs = []
    for n, v in enumerate(views):
        for k in range(share):
            to = rows_at(place_ref[n], rows, share, k)
            pairs.append((v.at[:, units + k * columns : units + (k + 1) * columns], wr.at[to, :]))
    return first, start(pairs, sems.at[8:])


class Late:
    def __init__(self, source, target, sem):
        self.target = target
        self.copy = pltpu.make_async_copy(source, target, sem)
        self.copy.start()

    def get(self):
        if self.copy is not None:
            self.copy.wait()
            self.copy = None
        return self.target


class Early:
    def __init__(self, ref, target, sem):
        self.ref = ref
        self.copy = pltpu.make_async_copy(ref, target, sem)

    def send(self):
        self.copy.start()


SPACES = {
    "v": pl.BlockSpec(memory_space=pltpu.VMEM),
    "a": pl.BlockSpec(memory_space=pl.ANY),
    "l": pl.BlockSpec(memory_space=pl.ANY),
    "e": pl.BlockSpec(memory_space=pl.ANY),
    "s": pl.BlockSpec(memory_space=pltpu.SMEM),
}


def call(body, operands, spaces, outs, out_spaces, scratch, micros, name):
    late = [n for n, space in enumerate(spaces) if space == "l"]
    early = [n for n, space in enumerate(out_spaces) if space == "e"]
    n_in, n_out, n_scratch = len(operands), len(outs), len(scratch)

    def kernel(*refs):
        ins, refs = list(refs[:n_in]), refs[n_in:]
        results, refs = list(refs[:n_out]), refs[n_out:]
        own, refs = refs[:n_scratch], refs[n_scratch:]
        held, refs = refs[: len(late)], refs[len(late) :]
        filled, refs = refs[: len(early)], refs[len(early) :]
        late_sems, early_sems = refs
        for k, n in enumerate(late):
            ins[n] = Late(ins[n], held[k], late_sems.at[k])
        for k, n in enumerate(early):
            results[n] = Early(filled[k], results[n], early_sems.at[k])
        body(ins, results, own)
        for n in late:
            ins[n].get()
        for n in early:
            results[n].copy.wait()

    more = [pltpu.VMEM(operands[n].shape, operands[n].dtype) for n in late]
    more += [pltpu.VMEM(*outs[n]) for n in early]
    more += [pltpu.SemaphoreType.DMA((max(1, len(late)),)), pltpu.SemaphoreType.DMA((max(1, len(early)),))]
    return pl.pallas_call(
        kernel,
        out_shape=[jax.ShapeDtypeStruct(s, d) for s, d in outs],
        in_specs=[SPACES[space] for space in spaces],
        out_specs=[SPACES[space] for space in out_spaces],
        scratch_shapes=list(scratch) + more,
        compiler_params=pltpu.CompilerParams(vmem_limit_bytes=VMEM_LIMIT),
        cost_estimate=pl.CostEstimate(flops=micros * MICRO, bytes_accessed=0, transcendentals=0),
        name=name,
    )(*operands)


def blocks_of(count):
    return [slice(j * WIDE, (j + 1) * WIDE) for j in range(count // WIDE)]


def shifted(at, base):
    return slice(at.start + base, at.stop + base)


def entry(normed, w, qkv, query_bias, value_bias):
    columns = normed.shape[1]
    for part, bias in enumerate((query_bias, None, value_bias)):
        for at in blocks_of(columns):
            to = shifted(at, part * columns)
            packed = nn(normed[...], w[:, to])
            qkv[:, to] = (packed if bias is None else packed + bias[:, at]).astype(BF)


def time_forward(n, ins, results, own):
    place_ref, x_ref, *rest = ins
    given, bufs = rest[: len(rest) - n], rest[len(rest) - n :]
    nt_out, qkv_out, o_out, e_out, p_out, y_ref, small_ref, hb_ref = results
    w, sems = own
    columns = x_ref.shape[1]
    wait(load(bufs, place_ref, w, sems))
    if given:
        small_ref[...] = given[0][...]
        hb_ref[...] = given[1][...]
    else:
        spread_small(w, small_ref, hb_ref)
    norm_chunks(x_ref, nt_out.ref, small_ref[11:12, :], small_ref[14:15, :])
    nt_out.send()
    qkv_ref, o_ref, e_ref, p_ref = qkv_out.ref, o_out.ref, e_out.ref, p_out.ref
    entry(nt_out.ref, w, qkv_ref, small_ref[0:1, :], small_ref[1:2, :])
    qkv_out.send()
    heads = head_map(columns)
    for clip in range(x_ref.shape[0] // (FRAMES * BLOCK)):
        at = [slice((clip * FRAMES + f) * BLOCK, (clip * FRAMES + f + 1) * BLOCK) for f in range(FRAMES)]
        weights = []
        for f in range(FRAMES):
            s = [head_sums(qkv_ref, at[f], 0, qkv_ref, at[g], columns, heads) * HD ** (-0.5) for g in range(FRAMES)]
            peak = jnp.maximum(s[0], s[1])
            powered = [jnp.exp(score - peak) for score in s]
            inverse = 1.0 / (powered[0] + powered[1])
            for g in range(FRAMES):
                m = (clip * FRAMES + f) * FRAMES + g
                p = powered[g] * inverse
                p_ref[m * BLOCK : (m + 1) * BLOCK, :] = p
                weights.append(p.astype(BF))
        for to in blocks_of(columns):
            v = [qkv_ref[a, shifted(to, 2 * columns)].astype(F32) for a in at]
            for f in range(FRAMES):
                spread = [nt(weights[FRAMES * f + g], heads[to, :]) for g in range(FRAMES)]
                o_ref[at[f], to] = (spread[0] * v[0] + spread[1] * v[1]).astype(BF)
    p_out.send()
    o_out.send()
    for at in blocks_of(columns):
        e_ref[:, at] = (nn(o_ref[...], w[:, shifted(at, 3 * columns)]) + small_ref[2:3, at]).astype(BF)
    e_out.send()
    patch = row_in_block(0, x_ref.shape[0], WIDE) < PLACES
    for at in blocks_of(columns):
        branch = nn(e_ref[...], w[:, shifted(at, 4 * columns)]) + small_ref[3:4, at]
        y_ref[:, at] = x_ref[:, at].astype(F32) + jnp.where(patch, branch, 0.0)


def half_masks():
    lane = lax.broadcasted_iota(jnp.int32, (1, 128), 1)
    return (lane < HD).astype(BF), (lane >= HD).astype(BF)


def space_forward(n, ins, results, own):
    place_ref, y_ref, small_ref, *bufs = ins
    ns_out, qkv_out, p_out, o_out, z_ref = results
    w, sems = own
    columns = y_ref.shape[1]
    blocks = y_ref.shape[0] // BLOCK
    pairs = columns // 128
    copies = load(bufs, place_ref, w, sems)
    norm_chunks(y_ref, ns_out.ref, small_ref[12:13, :], small_ref[15:16, :])
    ns_out.send()
    wait(copies)
    qkv_ref, p_ref, o_ref = qkv_out.ref, p_out.ref, o_out.ref
    entry(ns_out.ref, w, qkv_ref, small_ref[4:5, :], small_ref[5:6, :])
    qkv_out.send()
    masks = half_masks()
    first = lax.broadcasted_iota(jnp.int32, (BLOCK, 128), 1) < HD
    column = lax.broadcasted_iota(jnp.int32, (1, BLOCK), 1)
    hidden = jnp.where(column <= PLACES, 0.0, -1e30)

    def attend(block):
        at = rows_of(block, BLOCK)
        columns_of = [[slice(part * columns + k * 128, part * columns + (k + 1) * 128) for k in range(pairs)] for part in range(3)]
        scores = []
        for k in range(pairs):
            query, key = qkv_ref[at, columns_of[0][k]], qkv_ref[at, columns_of[1][k]]
            scores += [nt(query * mask, key) * HD ** (-0.5) + hidden for mask in masks]
        powered = [jnp.exp(s - jnp.max(s, axis=-1, keepdims=True)) for s in scores]
        weights = [(e * (1.0 / jnp.sum(e, axis=-1, keepdims=True))).astype(BF) for e in powered]
        for k in range(pairs):
            value = qkv_ref[at, columns_of[2][k]]
            for half in range(2):
                p_ref[(block * pairs + k) * 2 + half] = weights[2 * k + half]
            mixed = jnp.where(first, nn(weights[2 * k], value), nn(weights[2 * k + 1], value))
            o_ref[at, columns_of[0][k]] = mixed.astype(BF)

    loop(blocks, attend)
    p_out.send()
    o_out.send()
    is_class = lax.broadcasted_iota(jnp.int32, (BLOCK - EDGE, WIDE), 0) == CLASS
    for at in blocks_of(columns):
        branch = nn(o_ref[...], w[:, shifted(at, 3 * columns)]) + small_ref[6:7, at]
        z_ref[:, at] = y_ref[:, at] + branch
        for clip in range(blocks // FRAMES):
            edges = [slice((clip * FRAMES + f) * BLOCK + EDGE, (clip * FRAMES + f + 1) * BLOCK) for f in range(FRAMES)]
            mean = (branch[edges[0], :] + branch[edges[1], :]) * (1.0 / FRAMES)
            for edge in edges:
                z_ref[edge, at] = y_ref[edge, at] + jnp.where(is_class, mean, branch[edge, :])


def gelu_both(h):
    cdf = 0.5 * (1.0 + lax.erf(h * 0.5**0.5))
    density = jnp.exp(h * h * -0.5) * 0.3989422804014327
    return h * cdf, cdf + h * density


def feed(ins, results, own):
    place_ref, z_ref, g_ref, small_ref, hb_ref, *bufs = ins
    out_ref, gh_out, sums_ref, ghb_ref, dwr_out, *outs = results
    we, wr, dwe, nm, a, sems, out_sems = own
    gh, dwr = gh_out.ref, dwr_out.ref
    columns = z_ref.shape[1]
    units = we.shape[1]
    copies, more = load_feed(bufs, place_ref, we, wr, sems)
    norm_chunks(z_ref, nm, small_ref[13:14, :], small_ref[16:17, :])
    wait(copies + more)

    def inner(j):
        at = cols_of(j, WIDE)
        h = nn(nm[...], we[:, at]) + hb_ref[0:1, at]
        active, slope = gelu_both(h)
        a[:, at] = active.astype(BF)
        gh[:, at] = (nt(g_ref[...], wr[rows_of(j, WIDE), :]) * slope).astype(BF)

    loop(units // WIDE, inner)
    gh_out.send()

    def left(j):
        dwr[rows_of(j, WIDE), :] = tn(a[:, cols_of(j, WIDE)], g_ref[...]).astype(BF)

    loop(units // WIDE, left)
    dwr_out.send()

    def right(j):
        at = cols_of(j, WIDE)
        block = gh[:, at]
        dwe[:, at] = tn(nm[...], block).astype(BF)
        ghb_ref[0:1, at] = jnp.sum(block.astype(F32), axis=0, keepdims=True)

    loop(units // WIDE, right)
    copies = store_pieces(dwe, outs, place_ref, out_sems)
    for at in blocks_of(columns):
        out_ref[:, at] = (z_ref[:, at] + (nn(a[...], wr[:, at]) + small_ref[7:8, at])).astype(BF)
    sums_ref[0:1, :] = column_sums(g_ref, 0, columns)
    wait(copies)


def norm_backward(row, n, ins, results, own):
    place_ref, gh_ref, x_in, base_in, small_ref, *bufs = ins
    gz_ref, sums_ref = results
    w, gn, sems = own
    columns = gz_ref.shape[1]
    views = [b.at[:, 0 : w.shape[1]] for b in bufs]
    wait(load(views, place_ref, w, sems))
    for at in blocks_of(columns):
        gn[:, at] = nt(gh_ref[...], w[at, :])
    x_ref, base = x_in.get(), base_in.get()

    def store(at, value):
        gz_ref[at, :] = value

    gain_sum, shift_sum = norm_back_chunks(
        gn, x_ref, small_ref[row : row + 1, :], lambda at: base[at, :].astype(F32), store
    )
    sums_ref[0:1, :] = gain_sum
    sums_ref[1:2, :] = shift_sum


def space_backward(n, ins, results, own):
    place_ref, gz_ref, ns_in, qkv_in, p_in, o_in, *rest = ins
    bufs = rest[:n]
    gqkv_out, sums_ref, *outs = results
    w, dw_ref, gbs, go, sems, out_sems = own
    columns = gz_ref.shape[1]
    rows = gz_ref.shape[0]
    clips = rows // (BLOCK * FRAMES)
    pairs = columns // 128
    copies = load([b.at[:, 3 * columns : 4 * columns] for b in bufs], place_ref, w, sems)

    def lower(i):
        at = rows_of(i, CHUNK)
        gbs[at, :] = gz_ref[at, :].astype(BF)

    loop(rows // CHUNK, lower)
    is_class = lax.broadcasted_iota(jnp.int32, (BLOCK - EDGE, columns), 0) == CLASS
    for clip in range(clips):
        edges = [slice((clip * FRAMES + f) * BLOCK + EDGE, (clip * FRAMES + f + 1) * BLOCK) for f in range(FRAMES)]
        share = gz_ref[edges[0], :] * (1.0 / FRAMES)
        for edge in edges:
            gbs[edge, :] = jnp.where(is_class, share, gz_ref[edge, :]).astype(BF)
    wait(copies)
    for at in blocks_of(columns):
        go[:, at] = nt(gbs[...], w[at, :]).astype(BF)
    o_ref, qkv_ref, p_ref, gqkv = o_in.get(), qkv_in.get(), p_in.get(), gqkv_out.ref
    for at in blocks_of(columns):
        dw_ref[:, shifted(at, 3 * columns)] = tn(o_ref[...], gbs[:, at]).astype(BF)
    masks = half_masks()
    first = lax.broadcasted_iota(jnp.int32, (BLOCK, 128), 1) < HD
    class_row = lax.broadcasted_iota(jnp.int32, (BLOCK - EDGE, 128), 0) == CLASS
    together = 2

    def attend(step):
        parts = []
        for u in range(together):
            clip, pair = (step * together + u) // pairs, (step * together + u) % pairs
            for f in range(FRAMES):
                block = clip * FRAMES + f
                at = rows_of(block, BLOCK)
                q, k, v = (qkv_ref[at, cols_of(pair, 128, part * columns)] for part in range(3))
                grad = go[at, cols_of(pair, 128)]
                parts += [(q, k, v, grad, mask, p_ref[2 * (block * pairs + pair) + half]) for half, mask in enumerate(masks)]
        gp = [nt(grad * mask, v) for _, _, v, grad, mask, _ in parts]
        p = [part[5].astype(F32) for part in parts]
        shared = [jnp.sum(a * b, axis=-1, keepdims=True) for a, b in zip(gp, p)]
        gs = [(b * (a - c)).astype(BF) for a, b, c in zip(gp, p, shared)]
        scale = HD ** (-0.5)
        gq = [nn(a, part[1]) * scale for a, part in zip(gs, parts)]
        gv = [tn(part[5], part[3]) for part in parts]
        gk = [tn(a, part[0]) * scale for a, part in zip(gs, parts)]
        for u in range(together):
            clip, pair = (step * together + u) // pairs, (step * together + u) % pairs
            for part, values in enumerate((gq, gk, gv)):
                to = cols_of(pair, 128, part * columns)
                one, two = (jnp.where(first, values[4 * u + 2 * f], values[4 * u + 2 * f + 1]) for f in range(FRAMES))
                top = pl.multiple_of(clip * FRAMES * BLOCK, 16)
                gqkv[pl.ds(top, EDGE), to] = one[:EDGE].astype(BF)
                gqkv[pl.ds(top + BLOCK, EDGE), to] = two[:EDGE].astype(BF)
                both = jnp.where(class_row, one[EDGE:] + two[EDGE:], one[EDGE:])
                gqkv[pl.ds(top + EDGE, BLOCK - EDGE), to] = both.astype(BF)
                rest = jnp.where(class_row, 0.0, two[EDGE:])
                gqkv[pl.ds(top + BLOCK + EDGE, BLOCK - EDGE), to] = rest.astype(BF)

    loop(clips * pairs // together, attend)
    gqkv_out.send()
    ns_ref = ns_in.get()
    for at in blocks_of(3 * columns):
        dw_ref[:, at] = tn(ns_ref[...], gqkv[:, at]).astype(BF)
    copies = store_pieces(dw_ref, outs, place_ref, out_sems)
    sums_ref[0:1, :] = column_sums(gqkv, 0, columns)
    sums_ref[1:2, :] = column_sums(gqkv, 2 * columns, columns)
    sums_ref[2:3, :] = column_sums(gbs, 0, columns)
    wait(copies)


def time_backward(n, ins, results, own):
    place_ref, gy_ref, x_in, nt_in, qkv_in, p_in, o_in, e_in, small_ref, *others = ins
    others, bufs = others[: len(others) - n], others[len(others) - n :]
    gx_ref, sums_ref, *outs = results
    w, dw_ref, grt, get, go, gqkv, gn, sems, out_sems = own
    columns = gy_ref.shape[1]
    rows = gy_ref.shape[0]
    copies = load(bufs, place_ref, w, sems)

    def lower(i):
        at = rows_of(i, CHUNK)
        patch = row_in_block(i, CHUNK, columns) < PLACES
        grt[at, :] = jnp.where(patch, gy_ref[at, :], 0.0).astype(BF)

    loop(rows // CHUNK, lower)
    wait(copies)
    for at in blocks_of(columns):
        get[:, at] = nt(grt[...], w[at, 4 * columns : 5 * columns]).astype(BF)
    for at in blocks_of(columns):
        go[:, at] = nt(get[...], w[at, 3 * columns : 4 * columns]).astype(BF)
    e_ref, o_ref = e_in.get(), o_in.get()
    for at in blocks_of(columns):
        dw_ref[:, shifted(at, 4 * columns)] = tn(e_ref[...], grt[:, at]).astype(BF)
    for at in blocks_of(columns):
        dw_ref[:, shifted(at, 3 * columns)] = tn(o_ref[...], get[:, at]).astype(BF)
    qkv_ref, p_ref = qkv_in.get(), p_in.get()
    heads = head_map(columns)
    for clip in range(rows // (FRAMES * BLOCK)):
        at = [slice((clip * FRAMES + f) * BLOCK, (clip * FRAMES + f + 1) * BLOCK) for f in range(FRAMES)]
        gs, kept = [], []
        for f in range(FRAMES):
            gp = [head_sums(go, at[f], 0, qkv_ref, at[g], 2 * columns, heads) for g in range(FRAMES)]
            first = ((clip * FRAMES + f) * FRAMES) * BLOCK
            p = [p_ref[first + g * BLOCK : first + (g + 1) * BLOCK, :] for g in range(FRAMES)]
            shared = gp[0] * p[0] + gp[1] * p[1]
            gs += [(p[g] * (gp[g] - shared)).astype(BF) for g in range(FRAMES)]
            kept += [p[g].astype(BF) for g in range(FRAMES)]
        for block in blocks_of(columns):
            to = [shifted(block, part * columns) for part in range(3)]
            q, k = ([qkv_ref[a, to[part]].astype(F32) for a in at] for part in range(2))
            grad = [go[a, block].astype(F32) for a in at]
            scaled = heads[block, :] * BF(HD ** (-0.5))
            spread = [nt(value, scaled) for value in gs]
            for f in range(FRAMES):
                gqkv[at[f], to[0]] = (spread[2 * f] * k[0] + spread[2 * f + 1] * k[1]).astype(BF)
                gqkv[at[f], to[1]] = (spread[f] * q[0] + spread[2 + f] * q[1]).astype(BF)
            spread = [nt(value, heads[block, :]) for value in kept]
            for f in range(FRAMES):
                gqkv[at[f], to[2]] = (spread[f] * grad[0] + spread[2 + f] * grad[1]).astype(BF)
    nt_ref = nt_in.get()
    for at in blocks_of(3 * columns):
        dw_ref[:, at] = tn(nt_ref[...], gqkv[:, at]).astype(BF)
    main = slice(0, 5 * columns)
    copies = store_pieces(dw_ref.at[:, main], [out.at[..., main] for out in outs], place_ref, out_sems)
    for at in blocks_of(columns):
        gn[:, at] = nt(gqkv[...], w[at, 0 : 3 * columns])
    x_ref = x_in.get()

    def store(at, value):
        gx_ref[at, :] = value.astype(BF)

    gain_sum, shift_sum = norm_back_chunks(gn, x_ref, small_ref[11:12, :], lambda at: gy_ref[at, :], store)
    sums_ref[0:1, :] = column_sums(gqkv, 0, columns)
    sums_ref[1:2, :] = column_sums(gqkv, 2 * columns, columns)
    sums_ref[2:3, :] = column_sums(get, 0, columns)
    sums_ref[3:4, :] = column_sums(grt, 0, columns)
    sums_ref[4:5, :] = gain_sum
    sums_ref[5:6, :] = shift_sum
    wait(copies)
    if others:
        gather_small(dw_ref, (sums_ref, *others))
        last = slice(5 * columns, 5 * columns + 128)
        wait(store_pieces(dw_ref.at[:, last], [out.at[..., last] for out in outs], place_ref, out_sems))


def pack_rows(tokens, once):
    clips, _, columns = tokens.shape
    frames = []
    for f in range(FRAMES):
        places = tokens[:, 1 + f * PLACES : 1 + (f + 1) * PLACES]
        head = tokens[:, :1] if f == 0 or not once else jnp.zeros_like(tokens[:, :1])
        frames.append(jnp.concatenate([places, head, jnp.zeros((clips, BLOCK - PLACES - 1, columns), tokens.dtype)], axis=1))
    return jnp.stack(frames, axis=1).reshape(clips * FRAMES * BLOCK, columns)


def unpack_rows(rows, clips):
    framed = rows.reshape(clips, FRAMES, BLOCK, rows.shape[-1])
    return jnp.concatenate(
        [framed[:, 0, PLACES : PLACES + 1]] + [framed[:, f, :PLACES] for f in range(FRAMES)], axis=1
    )


class Layer:
    def __init__(self, rows, columns, units, shards, pieced, place):
        self.rows, self.columns, self.units = rows, columns, units
        self.pieced, self.place = pieced, place
        self.piece = columns // shards
        self.act = ((rows, columns), BF)
        self.act3 = ((rows, 3 * columns), BF)
        self.tall = ((rows, units), BF)
        self.wide = ((rows, columns), F32)
        self.sums = ((8, columns), F32)

    def grads(self, width):
        if self.pieced:
            return [((8, self.piece // 2, width), BF)] * 2
        return [((self.columns, width), BF)]

    def vmem(self, *shapes):
        return [pltpu.VMEM(s, d) for s, d in shapes]

    def sems(self, *counts):
        return [pltpu.SemaphoreType.DMA((count,)) for count in counts]

    def time_forward(self, x, given, bufs):
        c, n = self.columns, len(bufs)
        extra = [((SMALL, c), F32), ((8, self.units), F32)]
        return call(
            functools.partial(time_forward, n), (self.place, x, *given, *bufs), "sv" + "v" * len(given) + "a" * n,
            [self.act, self.act3, self.act, self.act, ((self.rows * FRAMES, 128), F32), self.wide] + extra, "eeeeevvv",
            self.vmem(((c, bufs[0].shape[1]), BF)) + self.sems(8), 14, "time_forward",
        )

    def space_forward(self, y, small, bufs):
        c, n = self.columns, len(bufs)
        probs = ((self.rows // BLOCK * (c // 128) * 2, BLOCK, BLOCK), BF)
        return call(
            functools.partial(space_forward, n), (self.place, y, small, *bufs), "svv" + "a" * n,
            [self.act, self.act3, probs, self.act, self.wide], "eeeev",
            self.vmem(((c, 4 * c), BF)) + self.sems(8), 16, "space_forward",
        )

    def feed(self, z, g, small, hb, bufs):
        c, u, n = self.columns, self.units, len(bufs)
        outs = self.grads(u)
        return call(
            feed, (self.place, z, g, small, hb, *bufs), "svvvv" + "a" * n,
            [self.act, self.tall, self.sums, ((8, u), F32), ((u, c), BF)] + outs, "vevve" + "a" * len(outs),
            self.vmem(((c, u), BF), ((u, c), BF), ((c, u), BF), self.act, self.tall) + self.sems(40, 16), 38, "feed",
        )

    def norm_backward(self, row, gh, x, base, small, bufs, name):
        c, n, wide = self.columns, len(bufs), gh.shape[1]
        return call(
            functools.partial(norm_backward, row, n), (self.place, gh, x, base, small, *bufs), "svllv" + "a" * n,
            [self.wide, self.sums], "vv", self.vmem(((c, wide), BF), self.wide) + self.sems(8), 10, name,
        )

    def space_backward(self, gz, normed, qkv, p, o, bufs):
        c, n = self.columns, len(bufs)
        outs = self.grads(4 * c)
        return call(
            functools.partial(space_backward, n), (self.place, gz, normed, qkv, p, o, *bufs), "svllll" + "a" * n,
            [self.act3, self.sums] + outs, "ev" + "a" * len(outs),
            self.vmem(((c, c), BF), ((c, 4 * c), BF), self.act, self.act) + self.sems(8, 16), 20, "space_backward",
        )

    def time_backward(self, gy, x, normed, qkv, p, o, e, small, others, bufs):
        c, n = self.columns, len(bufs)
        width = bufs[0].shape[1]
        outs = self.grads(width)
        return call(
            functools.partial(time_backward, n), (self.place, gy, x, normed, qkv, p, o, e, small, *others, *bufs),
            "svllllllv" + "v" * len(others) + "a" * n, [self.act, self.sums] + outs, "vv" + "a" * len(outs),
            self.vmem(((c, width), BF), ((c, width), BF), self.act, self.act, self.act, self.act3, self.wide) + self.sems(8, 16),
            24, "time_backward",
        )


BOTH = ("grp", "shard")


def permute(value, target):
    shards = lax.axis_size("shard")
    pairs = [(z * shards + s, z * shards + target(s)) for z in range(lax.axis_size("grp")) for s in range(shards)]
    return lax.ppermute(value, BOTH, pairs)


def to_sibling(value):
    return permute(value, lambda s: s ^ 1)


def along_x(value):
    return permute(value, lambda s: s ^ 2)


def along_y(value):
    return permute(value, lambda s: s ^ 4)


def gather_start(own):
    return jnp.concatenate([own, to_sibling(own)], axis=0)


def gather_hop(both):
    return permute(both, lambda s: s ^ (2 if s % 2 == 0 else 4))


def gather_second(hop):
    return permute(hop[: hop.shape[0] // 2], lambda s: s ^ (4 if s % 2 == 0 else 2))


def places(s):
    near = jnp.where(s % 2 == 0, 2, 4)
    far = 6 - near
    gathered = [s, s ^ 1, s ^ near, s ^ near ^ 1, s ^ 6, s ^ 1 ^ far, s ^ far, s ^ 7]
    kept = [s, s ^ 2, s ^ 4, s ^ 6]
    return jnp.stack(gathered + kept + [k ^ 1 for k in kept]).astype(jnp.int32)


def total(*terms):
    return sum(t.astype(F32) for t in terms).astype(BF)


class Reduction:
    def __init__(self, keep, give):
        self.keep = keep
        self.got = to_sibling(give)

    def own(self, start, stop):
        return self.keep[start:stop], self.got[start:stop]

    def first(self):
        return total(*self.own(0, 2)), total(*self.own(2, 4))

    def cross(self, sent):
        self.from_x, self.from_y = along_x(sent[0]), along_y(sent[1])

    def second(self):
        return total(*self.own(4, 5), self.from_y[:1]), total(*self.own(5, 6), self.from_x[:1])

    def cross_again(self, sent):
        self.last_x, self.last_y = along_x(sent[0]), along_y(sent[1])

    def finish(self):
        top = total(*self.own(6, 7), self.from_x[1:], self.last_y)
        bottom = total(*self.own(7, 8), self.from_y[1:], self.last_x)
        return top[0], bottom[0]


def tie(*values):
    leaves, shape = jax.tree.flatten(values)
    return jax.tree.unflatten(shape, lax.optimization_barrier(tuple(leaves)))


def swap_z(value):
    shards = lax.axis_size("shard")
    pairs = [(z * shards + s, (z ^ 1) * shards + s) for z in range(lax.axis_size("grp")) for s in range(shards)]
    return lax.ppermute(value, BOTH, pairs)


def sum_groups(halves, even):
    top, bottom = halves
    held = total(jnp.where(even, top, bottom), swap_z(jnp.where(even, bottom, top)))
    held = total(held, lax.ppermute(held, "grp", [(z, z ^ 2) for z in range(4)]))
    other = swap_z(held)
    return jnp.concatenate([jnp.where(even, held, other), jnp.where(even, other, held)], axis=0)


def local(video, cotangent, live, time_entry, time_exit, time_mixer, space_entry, space_exit, hidden_expand, hidden_reduce, bias_rows, hidden_bias, norm_gain, norm_shift):
    clips, _, tokens, columns = video.shape
    shards, groups = lax.axis_size("shard"), lax.axis_size("grp")
    mine = lax.axis_index("shard")
    part = columns // shards
    units = hidden_bias.shape[0] * shards
    share = units // columns
    pieced = shards == 8 and groups == 4

    def gather(value):
        return lax.all_gather(value, "shard", axis=0, tiled=True)

    flags = live.astype(BF)[:, :, None]
    x = pack_rows(video[:, 0], False)
    g = pack_rows(cotangent[:, 0] * flags, True)
    own_t = jnp.concatenate([time_entry, time_exit, time_mixer], axis=1)
    own_s = jnp.concatenate([space_entry, space_exit], axis=1)
    if pieced:
        narrow = jnp.concatenate([norm_gain, norm_shift], axis=0)
        narrow = jnp.concatenate(
            [jnp.pad(bias_rows, ((0, 0), (0, 128 - part))), hidden_bias.reshape(-1, 128), jnp.pad(narrow, ((0, 0), (0, 128 - part)))], axis=0
        )
        own_t = jnp.concatenate([own_t, jnp.pad(narrow, ((0, part - narrow.shape[0]), (0, 0)))], axis=1)
        own_f = jnp.concatenate([hidden_expand] + [hidden_reduce[k * part : (k + 1) * part] for k in range(share)], axis=1)
        net = Layer(x.shape[0], columns, units, shards, pieced, places(mine))
        both_t = gather_start(own_t)
        both_s, both_f = gather_start(own_s), gather_start(own_f)
        hop_t, both_s, both_f, x, g = tie(gather_hop(both_t), both_s, both_f, x, g)
        second_t, both_s, both_f = tie(gather_second(hop_t), both_s, both_f)
        wt = (both_t, hop_t, second_t, to_sibling(hop_t), to_sibling(second_t))
        hop_s = gather_hop(both_s)
        normed_t, qkv_t, o_t, e_t, p_t, y, small, hb = net.time_forward(x, (), wt)
        hop_s, y, both_f = tie(hop_s, y, both_f)
        second_s = gather_second(hop_s)
        hop_f = gather_hop(both_f)
        ws = (both_s, hop_s, second_s, to_sibling(hop_s), to_sibling(second_s))
        normed_s, qkv_s, p_s, o_s, z = net.space_forward(y, small, ws)
        hop_f, z = tie(hop_f, z)
        second_f = gather_second(hop_f)
        wf = (both_f, hop_f, second_f, to_sibling(hop_f), to_sibling(second_f))
    else:
        net = Layer(x.shape[0], columns, units, shards, pieced, jnp.zeros((16,), jnp.int32))
        packed = jnp.concatenate([bias_rows, norm_gain, norm_shift], axis=0)
        spread = lax.all_gather(packed, "shard", axis=0).transpose(1, 0, 2).reshape(-1, columns).astype(F32)
        small = jnp.concatenate([spread[:8], jnp.zeros((3, columns), F32), spread[8:], jnp.zeros((SMALL - 17, columns), F32)], axis=0)
        given = (small, jnp.pad(gather(hidden_bias).astype(F32)[None], ((0, 7), (0, 0))))
        wt, ws, wf = (gather(own_t),), (gather(own_s),), (gather(hidden_expand), gather(hidden_reduce))
        normed_t, qkv_t, o_t, e_t, p_t, y, small, hb = net.time_forward(x, given, wt)
        normed_s, qkv_s, p_s, o_s, z = net.space_forward(y, small, ws)

    out, gh, sums_f, ghb, grad_r, *grad_e = net.feed(z, g, small, hb, wf)
    gz, norm_f = net.norm_backward(13, gh, z, g, small, wf if pieced else wf[:1], "feed_norm")
    if pieced:
        sum_e = Reduction(*grad_e)
        sent_e, gz = tie(sum_e.first(), gz)
        sum_e.cross(sent_e)
    gqkv, sums_s, *grad_s = net.space_backward(gz, normed_s, qkv_s, p_s, o_s, ws)
    if pieced:
        sum_s = Reduction(*grad_s)
        sent_e, gqkv = tie(sum_e.second(), gqkv)
        sum_e.cross_again(sent_e)
    gy, norm_s = net.norm_backward(12, gqkv, y, gz, small, ws, "space_norm")
    if pieced:
        kept_e, sent_s, gy = tie(sum_e.finish(), sum_s.first(), gy)
        sum_s.cross(sent_s)
        sums_s = jnp.concatenate([sums_s[0:3], norm_s[0:2], sums_s[5:]], axis=0)
        sums_f = jnp.concatenate([sums_f[0:1], norm_f[0:2], sums_f[3:]], axis=0)
    others = (sums_s, sums_f, ghb) if pieced else ()
    gx, sums_t, *grad_t = net.time_backward(gy, x, normed_t, qkv_t, p_t, o_t, e_t, small, others, wt)

    if pieced:
        even = lax.axis_index("grp") % 2 == 0
        kept_r = lax.psum_scatter(grad_r, "shard", scatter_dimension=0, tiled=True)
        re, rr = lax.psum((jnp.concatenate(kept_e, axis=0), kept_r), "grp")
        sum_t = Reduction(*grad_t)
        _, gx = tie(kept_r, gx)
        sent_s, sent_t = tie(sum_s.second(), sum_t.first())
        sum_s.cross_again(sent_s)
        sum_t.cross(sent_t)
        kept_s, sent_t = tie(sum_s.finish(), sum_t.second())
        sum_t.cross_again(sent_t)
        rs = sum_groups(kept_s, even).astype(F32)
        rt = sum_groups(sum_t.finish(), even)
        re, rr, rt = (v.astype(F32) for v in tie(re, rr, rt))
        narrow = rt[:, 5 * columns :]
        biases, rows_hidden = narrow[0:8, :part], narrow[8:11].reshape(-1)
        gains, shifts = narrow[11:14, :part], narrow[14:17, :part]
    else:
        re, rr, rs, rt = (
            lax.psum(lax.psum_scatter(v, "shard", scatter_dimension=0, tiled=True), "grp").astype(F32)
            for v in (*grad_e, grad_r, *grad_s, *grad_t)
        )
        rows = [sums_t[0:4], sums_s[0:3], sums_f[0:1], sums_t[4:5], norm_s[0:1], norm_f[0:1], sums_t[5:6], norm_s[1:2], norm_f[1:2]]
        cut = lax.dynamic_slice_in_dim(lax.psum(jnp.concatenate(rows, axis=0), BOTH), mine * part, part, axis=1)
        biases, gains, shifts = cut[0:8], cut[8:11], cut[11:14]
        rows_hidden = lax.dynamic_slice_in_dim(lax.psum(ghb[0], BOTH), mine * hidden_bias.shape[0], hidden_bias.shape[0])
    return (
        (unpack_rows(out, clips) * flags)[:, None],
        unpack_rows(gx, clips)[:, None],
        rt[:, : 3 * columns],
        rt[:, 3 * columns : 4 * columns],
        rt[:, 4 * columns : 5 * columns],
        rs[:, : 3 * columns],
        rs[:, 3 * columns :],
        re,
        rr,
        biases,
        rows_hidden,
        gains,
        shifts,
    )


def solution(mesh):
    clips = P(None, ("grp", "shard"), None, None)
    rows = P("shard", None)
    cols = P(None, "shard")
    return jax.shard_map(
        local,
        mesh=mesh,
        in_specs=(clips, clips, P(None, ("grp", "shard"))) + (rows,) * 7 + (cols, P("shard"), cols, cols),
        out_specs=(clips, clips) + (rows,) * 7 + (cols, P("shard"), cols, cols),
        check_vma=False,
    )
```

time: 602 us -> 422 us (0.70)
  waiting for transfers between devices: 232 us -> 143 us
  blocking collectives: 54.9 us -> 0 us
  Pallas kernels: 174 us -> 151 us
  local copies, waits for them, and re-layouts: 44.9 us -> 29.4 us
  starting transfers between devices: 26.9 us -> 33.5 us
    psum x3 -> x1, waiting for transfers between devices: 120 us -> 0.02 us  [local(): re, rr = lax.psum((jnp.concatenate(kept_e, axis=0), kept_r), 'grp')]
    ppermute x0 -> x6, waiting for transfers between devices: none -> 64.5 us  [the longest x4 39.1 us: swap_z(): return lax.ppermute(value, BOTH, pairs)]
    psum x1 -> x0, blocking collectives: 40.7 us -> none  [local(): sums = lax.psum(sums, ('grp', 'shard'))]
    ppermute x30, waiting for transfers between devices: 112 us -> 78.6 us  [permute(): return lax.ppermute(value, BOTH, pairs)]
    pallas_call x5 -> x7, Pallas kernels: 174 us -> 151 us  [call(): pl.pallas_call(kernel, out_shape=[jax.ShapeDtypeStruct(s, d) for s, d in...]
    all_gather x1 -> x0, blocking collectives: 14.1 us -> none  [local(): spread = lax.all_gather(packed, 'shard', axis=0)]
    convert_element_type x3 -> x14, other arithmetic: 2.53 us -> 16.3 us  [the longest x10 13.9 us: total(): return sum((t.astype(F32) for t in terms)).astype(BF)]
    add x6 -> x0, other arithmetic: 13.5 us -> none  [the longest x3 9.37 us: reduce_pieces(): summed = keep + to_sibling(give)]
  transfers between devices with their start and end apart: 33 -> 38, of which waited for: 11 -> 18; matrix products, arithmetic and copies ran while one was open for 14% -> 13% of each run, Pallas kernels for 14% -> 27%
where the time goes in v3:
time: 422 us; the launch traced here: 417 us
  Pallas kernels  151 us (36%)
  waiting for transfers between devices  143 us (34%)
  other arithmetic  45 us (11%)
  starting transfers between devices  33.5 us (8%)
  local copies, waits for them, and re-layouts  29.4 us (7%)
  between operations  14.9 us (4%)
    pallas_call x7, Pallas kernels, call(): pl.pallas_call(kernel, out_shape=[jax.ShapeDtypeStruct(s, d) for s, d in...  151 us
    ppermute x30, waiting for transfers between devices, permute(): return lax.ppermute(value, BOTH, pairs)  78.6 us
    ppermute x4, waiting for transfers between devices, swap_z(): return lax.ppermute(value, BOTH, pairs)  39.1 us
    ppermute x30, starting transfers between devices, permute(): return lax.ppermute(value, BOTH, pairs)  28.5 us
    ppermute x2, waiting for transfers between devices, sum_groups(): lax.ppermute(held, 'grp', [(z, z ^ 2) for z in range(4)])  25.4 us
    convert_element_type x10, other arithmetic, total(): return sum((t.astype(F32) for t in terms)).astype(BF)  13.9 us
    unnamed x79, local copies, waits for them, and re-layouts  9.74 us
    another operation x2, other arithmetic, pack_rows(): return jnp.stack(frames, axis=1).reshape(clips * FRAMES * BLOCK, columns)  8.94 us
  transfers between devices with their start and end apart: 38, of which 18 were waited for; matrix products, arithmetic and copies ran while one was open for 13% of the time, Pallas kernels for 27%

profile of v3, /device:TPU:0, one launch (start us, length us, event | category | flops | bytes accessed | tf_op | source)
XLA Modules:
  0.0 417.2 jit_solution(15882432974813477837)
XLA Ops:
  15.3 5.2 %maximum_bitcast_fusion.1 = (bf16[2,1,208,768]{3,0,2,1:T(2,128)(2,1)S(1)}, bf16[2,1,208,768]{3,0,2,1:T(2,128)(2,1)S(1)}, bf16[2,1,208,768]{3,0,2,1:T(2,128)(2,1)S(1)}, bf16[2,1,208,768]{3,0,2,1:T(2,128)(2,1)S(1)}) fusion(bf16[2,1,768]{2,0,1:T(2,128)(2,1)S(1)} %slice.338, bf16[2,196,768]{2,0,1:T(2,128)(2,1)S(1)} %get-tuple-element.172, ...), kind=kLoop, calls=%fused_computation.29 | loop fusion | flops 2555904 | bytes 4971328 | tf_op jit(solution)/shard_map/stack | solution.py:635
  20.7 2.6 collective-permute-start.1
  23.3 3.7 pad_maximum_fusion.2
  29.8 11.5 %collective-permute-done.1.refs_3_.refs_13_ = bf16[192,3968]{1,0:T(8,128)(2,1)} collective-permute-done((bf16[192,3968]{1,0:T(8,128)(2,1)S(1)}, bf16[192,3968]{1,0:T(8,128)(2,1)}, u32[]{:S(2)}, u32[]{:S(2)}) %collective-permute-start.1) | collective-permute-done | bytes 1523744 | tf_op jit(solution)/shard_map/ppermute | solution.py:728
  42.5 2.1 collective-permute-start.4
  44.6 9.8 %collective-permute-done.4.refs_4_.refs_14_ = bf16[96,3968]{1,0:T(8,128)(2,1)} collective-permute-done((bf16[96,3968]{1,0:T(8,128)(2,1)S(1)}, bf16[96,3968]{1,0:T(8,128)(2,1)}, u32[]{:S(2)}, u32[]{:S(2)}) %collective-permute-start.4) | collective-permute-done | bytes 761888 | tf_op jit(solution)/shard_map/ppermute | solution.py:728
  55.1 2.0 collective-permute-start.5
  57.1 14.6 %time_forward.1 = (bf16[832,768]{1,0:T(8,128)(2,1)}, bf16[832,2304]{1,0:T(8,128)(2,1)}, bf16[832,768]{1,0:T(8,128)(2,1)}, bf16[832,768]{1,0:T(8,128)(2,1)}, f32[...) custom-call(s32[16]{0:T(128)} %stack.76.refs_0_, bf16[832,768]{1,0:T(8,128)(2,1)} %bitcast.60, ...), custom_call_target="tpu_custom_call" | custom-call | flops 56000000000 | tf_op jit(solution)/shard_map/time_forward/pallas_call | solution.py:279
  72.8 2.0 collective-permute-start.9
  74.8 7.9 %collective-permute-done.9.refs_5_.refs_8_.refs_7_ = bf16[96,3072]{1,0:T(8,128)(2,1)S(1)} collective-permute-done((bf16[96,3072]{1,0:T(8,128)(2,1)S(1)}, bf16[96,3072]{1,0:T(8,128)(2,1)S(1)}, u32[]{:S(2)}, u32[]{:S(2)}) %collective-permute-start.9) | collective-permute-done | bytes 589856 | tf_op jit(solution)/shard_map/ppermute | solution.py:728
  82.8 2.0 collective-permute-start.8
  86.6 17.0 %space_forward.1 = (bf16[832,768]{1,0:T(8,128)(2,1)}, bf16[832,2304]{1,0:T(8,128)(2,1)}, bf16[48,208,208]{2,1,0:T(8,128)(2,1)}, bf16[832,768]{1,0:T(8,128)(2,1)}, f32[832,768]{1,0:T(8,128)}) custom-call(s32[16]{0:T(128)} %stack.76.refs_0_, f32[832,768]{1,0:T(8,128)} %get-tuple-element.89.refs_1_.refs_2_, ...), custom_call_target="tpu_custom_call" | custom-call | flops 64000000000 | tf_op jit(solution)/shard_map/space_forward/pallas_call | solution.py:279
  103.7 8.1 %collective-permute-done.8.refs_6_ = bf16[192,6144]{1,0:T(8,128)(2,1)} collective-permute-done((bf16[192,6144]{1,0:T(8,128)(2,1)S(1)}, bf16[192,6144]{1,0:T(8,128)(2,1)}, u32[]{:S(2)}, u32[]{:S(2)}) %collective-permute-start.8) | collective-permute-done | bytes 2359328 | tf_op jit(solution)/shard_map/ppermute | solution.py:728
  113.1 2.0 collective-permute-start.12
  115.1 14.3 %collective-permute-done.12.refs_7_ = bf16[96,6144]{1,0:T(8,128)(2,1)S(1)} collective-permute-done((bf16[96,6144]{1,0:T(8,128)(2,1)S(1)}, bf16[96,6144]{1,0:T(8,128)(2,1)S(1)}, u32[]{:S(2)}, u32[]{:S(2)}) %collective-permute-start.12) | collective-permute-done | bytes 1179680 | tf_op jit(solution)/shard_map/ppermute | solution.py:728
  129.4 2.8 collective-permute-done.14.refs_9_
  134.7 39.6 %feed.1 = (bf16[832,768]{1,0:T(8,128)(2,1)}, bf16[832,3072]{1,0:T(8,128)(2,1)}, f32[8,768]{1,0:T(8,128)}, f32[8,3072]{1,0:T(8,128)}, bf16[3072,768]{1,0:T(8,128)...) custom-call(s32[16]{0:T(128)} %stack.76.refs_0_, f32[832,768]{1,0:T(8,128)} %get-tuple-element.93.refs_1_.refs_2_, ...), custom_call_target="tpu_custom_call" | custom-call | flops 152000004096 | tf_op jit(solution)/shard_map/feed/pallas_call | solution.py:279
  176.1 13.8 %feed_norm.1 = (f32[832,768]{1,0:T(8,128)}, f32[8,768]{1,0:T(8,128)}) custom-call(s32[16]{0:T(128)} %stack.76.refs_0_, bf16[832,3072]{1,0:T(8,128)(2,1)} %get-tuple-element.101.refs_1_, f32[832,768]{1,0:T(8,128)} %get-tuple-element.93.refs_1_.refs_2_, bf16[832,768]{1,0:T(8,128)(2,1)} %bitcast.63, ...), custom_call_target="tpu_custom_call" | custom-call | flops 40000000000 | tf_op jit(solution)/shard_map/feed_norm/pallas_call | solution.py:279
  191.2 2.5 add_convert_fusion.4
  193.8 1.9 collective-permute-start.16
  195.7 1.5 collective-permute-start.17
  197.2 25.3 %space_backward.1 = (bf16[832,2304]{1,0:T(8,128)(2,1)}, f32[8,768]{1,0:T(8,128)}, bf16[8,48,3072]{2,1,0:T(8,128)(2,1)}, bf16[8,48,3072]{2,1,0:T(8,128)(2,1)}) custom-call(s32[16]{0:T(128)} %stack.76.refs_0_, f32[832,768]{1,0:T(8,128)} %get-tuple-element.105.refs_1_.refs_3_, bf16[832,768]{1,0:T(8,128)(2,1)} %get-tuple-element.106.refs_2_, ...), custom_call_target="tpu_custom_call" | custom-call | flops 80000000000 | tf_op jit(solution)/shard_map/space_backward/pallas_call | solution.py:279
  224.0 2.2 add_convert_fusion.19
  226.7 12.4 %space_norm.1 = (f32[832,768]{1,0:T(8,128)}, f32[8,768]{1,0:T(8,128)}) custom-call(s32[16]{0:T(128)} %stack.76.refs_0_, bf16[832,2304]{1,0:T(8,128)(2,1)} %get-tuple-element.115.refs_1_, f32[832,768]{1,0:T(8,128)} %get-tuple-element.89.refs_1_.refs_2_, f32[832,768]{1,0:T(8,128)} %get-tuple-element.105.refs_1_.refs_3_, ...), custom_call_target="tpu_custom_call" | custom-call | flops 40000000000 | tf_op jit(solution)/shard_map/space_norm/pallas_call | solution.py:279
  242.0 2.6 fusion.6
  244.6 1.8 add_convert_fusion.2
  246.4 28.7 %time_backward.1 = (bf16[832,768]{1,0:T(8,128)(2,1)}, f32[8,768]{1,0:T(8,128)}, bf16[8,48,3968]{2,1,0:T(8,128)(2,1)}, bf16[8,48,3968]{2,1,0:T(8,128)(2,1)}) custom-call(s32[16]{0:T(128)} %stack.76.refs_0_, f32[832,768]{1,0:T(8,128)} %get-tuple-element.117.refs_1_, bf16[832,768]{1,0:T(8,128)(2,1)} %bitcast.61, bf16[832,768]{1,0:T(8,128)(2,1)} %get-tuple-element.118.refs_3_, ...), custom_call_target="tpu_custom_call" | custom-call | flops 96000000000 | tf_op jit(solution)/shard_map/time_backward/pallas_call | solution.py:279
  275.4 1.8 collective-permute-start.23
  277.2 1.5 collective-permute-start.22
  279.9 2.8 maximum_multiply_fusion
  282.7 8.6 %collective-permute-done.23 = bf16[2,48,3072]{2,1,0:T(8,128)(2,1)S(1)} collective-permute-done((bf16[2,48,3072]{2,1,0:T(8,128)(2,1)}, bf16[2,48,3072]{2,1,0:T(8,128)(2,1)S(1)}, u32[]{:S(2)}, u32[]{:S(2)}) %collective-permute-start.23) | collective-permute-done | bytes 589856 | tf_op jit(solution)/shard_map/ppermute | solution.py:728
  292.8 2.5 add_convert_fusion.15
  295.3 2.9 add_convert_fusion
  298.7 1.6 collective-permute-start.25
  309.0 1.9 fusion.8
  310.9 12.2 %collective-permute-done.24 = bf16[2,48,3968]{2,1,0:T(8,128)(2,1)} collective-permute-done((bf16[2,48,3968]{2,1,0:T(8,128)(2,1)}, bf16[2,48,3968]{2,1,0:T(8,128)(2,1)}, u32[]{:S(2)}, u32[]{:S(2)}) %collective-permute-start.24) | collective-permute-done | bytes 761888 | tf_op jit(solution)/shard_map/ppermute | solution.py:728
  323.6 1.6 add_convert_fusion.9
  325.3 1.6 collective-permute-start.33
  326.9 2.6 maximum_bitcast_fusion
  329.5 1.5 collective-permute-start.28
  332.2 8.9 %collective-permute-done.33 = bf16[48,3072]{1,0:T(8,128)(2,1)S(1)} collective-permute-done((bf16[48,3072]{1,0:T(8,128)(2,1)S(1)}, bf16[48,3072]{1,0:T(8,128)(2,1)S(1)}, u32[]{:S(2)}, u32[]{:S(2)}) %collective-permute-start.33) | collective-permute-done | bytes 294944 | tf_op jit(solution)/shard_map/ppermute | solution.py:801
  341.2 2.3 collective-permute-start.34
  343.6 1.8 select_bitcast_fusion
  346.1 20.3 %collective-permute-done.34 = bf16[48,3072]{1,0:T(8,128)(2,1)S(1)} collective-permute-done((bf16[48,3072]{1,0:T(8,128)(2,1)S(1)}, bf16[48,3072]{1,0:T(8,128)(2,1)S(1)}, u32[]{:S(2)}, u32[]{:S(2)}) %collective-permute-start.34) | collective-permute-done | bytes 294944 | tf_op jit(solution)/shard_map/ppermute | solution.py:807
  366.5 16.7 %collective-permute-done.30 = bf16[48,3968]{1,0:T(8,128)(2,1)S(1)} collective-permute-done((bf16[48,3968]{1,0:T(8,128)(2,1)S(1)}, bf16[48,3968]{1,0:T(8,128)(2,1)S(1)}, u32[]{:S(2)}, u32[]{:S(2)}) %collective-permute-start.30) | collective-permute-done | bytes 380960 | tf_op jit(solution)/shard_map/ppermute | solution.py:801
  383.4 7.7 %collective-permute-done.35 = bf16[48,3072]{1,0:T(8,128)(2,1)S(1)} collective-permute-done((bf16[48,3072]{1,0:T(8,128)(2,1)S(1)}, bf16[48,3072]{1,0:T(8,128)(2,1)S(1)}, u32[]{:S(2)}, u32[]{:S(2)}) %collective-permute-start.35) | collective-permute-done | bytes 294944 | tf_op jit(solution)/shard_map/ppermute | solution.py:801
  391.2 5.1 %collective-permute-done.31 = bf16[48,3968]{1,0:T(8,128)(2,1)S(1)} collective-permute-done((bf16[48,3968]{1,0:T(8,128)(2,1)S(1)}, bf16[48,3968]{1,0:T(8,128)(2,1)S(1)}, u32[]{:S(2)}, u32[]{:S(2)}) %collective-permute-start.31) | collective-permute-done | bytes 380960 | tf_op jit(solution)/shard_map/ppermute | solution.py:807
  398.3 5.8 %collective-permute-done.32 = bf16[48,3968]{1,0:T(8,128)(2,1)S(1)} collective-permute-done((bf16[48,3968]{1,0:T(8,128)(2,1)S(1)}, bf16[48,3968]{1,0:T(8,128)(2,1)S(1)}, u32[]{:S(2)}, u32[]{:S(2)}) %collective-permute-start.32) | collective-permute-done | bytes 380960 | tf_op jit(solution)/shard_map/ppermute | solution.py:801
  (184 shorter events, 50.5 us)
Async XLA Ops:
  7.2 294.0 %reduce-scatter.2.cloned.1.call-start = ((), (), s32[]{:S(2)}) async-start(), calls=%async_computation.1 | async-start | bytes 5308416 | tf_op jit(solution)/shard_map/reduce_scatter | solution.py:884
  10.0 10.6 %collective-permute-start = (bf16[96,3968]{1,0:T(8,128)(2,1)S(1)}, bf16[96,3968]{1,0:T(8,128)(2,1)S(1)}, u32[]{:S(2)}, u32[]{:S(2)}) collective-permute-start(bf16[96,3968]{1,0:T(8,128)(2,1)S(1)} %pad_maximum_fusion.5), channel_id=1, source_target_pairs={{0,1},{1,0},{2,3},{3,2},{4,5},{5,4},{6,7},{7,6},{8,9},{9,8},{10,11... | collective-permute-start | bytes 2285576 | tf_op jit(solution)/shard_map/ppermute | solution.py:728
  10.6 18.8 %collective-permute-start.2 = (bf16[96,3072]{1,0:T(8,128)(2,1)S(1)}, bf16[96,3072]{1,0:T(8,128)(2,1)S(1)}, u32[]{:S(2)}, u32[]{:S(2)}) collective-permute-start(bf16[96,3072]{1,0:T(8,128)(2,1)S(1)} %constant_dynamic-update-slice_fusion), channel_id=1, source_target_pairs={{0,1},{1,0},{2,3},{3,2},{4,5},{5,4},{6,7},{7,6},{8,9},{9,8},{10,11... | collective-permute-start | bytes 1769480 | tf_op jit(solution)/shard_map/ppermute | solution.py:728
  11.2 18.4 %collective-permute-start.3 = (bf16[96,6144]{1,0:T(8,128)(2,1)S(1)}, bf16[96,6144]{1,0:T(8,128)(2,1)S(1)}, u32[]{:S(2)}, u32[]{:S(2)}) collective-permute-start(bf16[96,6144]{1,0:T(8,128)(2,1)S(1)} %slice_dynamic-update-slice_fusion), channel_id=1, source_target_pairs={{0,1},{1,0},{2,3},{3,2},{4,5},{5,4},{6,7},{7,6},{8,9},{9,8},{10,11... | collective-permute-start | bytes 3538952 | tf_op jit(solution)/shard_map/ppermute | solution.py:728
  15.3 5.3 %copy-start.16 = (bf16[96,768]{1,0:T(8,128)(2,1)S(1)}, bf16[96,768]{1,0:T(8,128)(2,1)}, u32[]{:S(2)}) copy-start(bf16[96,768]{1,0:T(8,128)(2,1)} %param.19) | copy-start | bytes 442372
  15.3 5.3 %copy-start.17 = (bf16[96,768]{1,0:T(8,128)(2,1)S(1)}, bf16[96,768]{1,0:T(8,128)(2,1)}, u32[]{:S(2)}) copy-start(bf16[96,768]{1,0:T(8,128)(2,1)} %param.18) | copy-start | bytes 442372
  20.7 6.3 %copy-start.8 = (bf16[192,3968]{1,0:T(8,128)(2,1)}, bf16[192,3968]{1,0:T(8,128)(2,1)S(1)}, u32[]{:S(2)}) copy-start(bf16[192,3968]{1,0:T(8,128)(2,1)S(1)} %pad_maximum_fusion.1.refs_2_.refs_12_) | copy-start | bytes 4571140
  20.7 20.6 %collective-permute-start.1 = (bf16[192,3968]{1,0:T(8,128)(2,1)S(1)}, bf16[192,3968]{1,0:T(8,128)(2,1)}, u32[]{:S(2)}, u32[]{:S(2)}) collective-permute-start(bf16[192,3968]{1,0:T(8,128)(2,1)S(1)} %pad_maximum_fusion.1.refs_2_.refs_12_), channel_id=1, source_target_pairs={{0,2},{1,5},{2,0},{3,7},{4,6},{5,1},{6,4},{7,3},{8,10},{9,13},{10,... | collective-permute-start | bytes 4571144 | tf_op jit(solution)/shard_map/ppermute | solution.py:728
  29.5 25.6 %copy-start.13 = (bf16[192,3072]{1,0:T(8,128)(2,1)}, bf16[192,3072]{1,0:T(8,128)(2,1)S(1)}, u32[]{:S(2)}) copy-start(bf16[192,3072]{1,0:T(8,128)(2,1)S(1)} %pad_maximum_fusion.4.refs_3_.refs_6_.refs_5_) | copy-start | bytes 3538948
  29.8 53.0 %copy-start.5 = (bf16[192,6144]{1,0:T(8,128)(2,1)}, bf16[192,6144]{1,0:T(8,128)(2,1)S(1)}, u32[]{:S(2)}) copy-start(bf16[192,6144]{1,0:T(8,128)(2,1)S(1)} %pad_maximum_fusion.refs_5_) | copy-start | bytes 7077892
  42.5 11.9 %collective-permute-start.4 = (bf16[96,3968]{1,0:T(8,128)(2,1)S(1)}, bf16[96,3968]{1,0:T(8,128)(2,1)}, u32[]{:S(2)}, u32[]{:S(2)}) collective-permute-start(bf16[96,3968]{1,0:T(8,128)(2,1)S(1)} %slice.262), channel_id=1, source_target_pairs={{0,4},{1,3},{2,6},{3,1},{4,0},{5,7},{6,2},{7,5},{8,12},{9,11},{10,... | collective-permute-start | bytes 2285576 | tf_op jit(solution)/shard_map/ppermute | solution.py:728
  44.6 12.5 %collective-permute-start.6 = (bf16[192,3968]{1,0:T(8,128)(2,1)}, bf16[192,3968]{1,0:T(8,128)(2,1)}, u32[]{:S(2)}, u32[]{:S(2)}) collective-permute-start(bf16[192,3968]{1,0:T(8,128)(2,1)} %collective-permute-done.1.refs_3_.refs_13_), channel_id=1, source_target_pairs={{0,1},{1,0},{2,3},{3,2},{4,5},{5,4},{6,7},{7,6},{8,9},{9,8},{10,11... | collective-permute-start | bytes 4571144 | tf_op jit(solution)/shard_map/ppermute | solution.py:728
  54.4 2.7 collective-permute-start.7
  55.1 16.6 %collective-permute-start.5 = (bf16[192,3072]{1,0:T(8,128)(2,1)S(1)}, bf16[192,3072]{1,0:T(8,128)(2,1)}, u32[]{:S(2)}, u32[]{:S(2)}) collective-permute-start(bf16[192,3072]{1,0:T(8,128)(2,1)S(1)} %pad_maximum_fusion.4.refs_3_.refs_6_.refs_5_), channel_id=1, source_target_pairs={{0,2},{1,5},{2,0},{3,7},{4,6},{5,1},{6,4},{7,3},{8,10},{9,13},{10,... | collective-permute-start | bytes 3538952 | tf_op jit(solution)/shard_map/ppermute | solution.py:728
  72.8 9.9 %collective-permute-start.9 = (bf16[96,3072]{1,0:T(8,128)(2,1)S(1)}, bf16[96,3072]{1,0:T(8,128)(2,1)S(1)}, u32[]{:S(2)}, u32[]{:S(2)}) collective-permute-start(bf16[96,3072]{1,0:T(8,128)(2,1)S(1)} %slice.263), channel_id=1, source_target_pairs={{0,4},{1,3},{2,6},{3,1},{4,0},{5,7},{6,2},{7,5},{8,12},{9,11},{10,... | collective-permute-start | bytes 1769480 | tf_op jit(solution)/shard_map/ppermute | solution.py:728
  74.8 10.0 %collective-permute-start.10 = (bf16[192,3072]{1,0:T(8,128)(2,1)}, bf16[192,3072]{1,0:T(8,128)(2,1)S(1)}, u32[]{:S(2)}, u32[]{:S(2)}) collective-permute-start(bf16[192,3072]{1,0:T(8,128)(2,1)} %collective-permute-done.5.refs_4_.refs_7_.refs_6_), channel_id=1, source_target_pairs={{0,1},{1,0},{2,3},{3,2},{4,5},{5,4},{6,7},{7,6},{8,9},{9,8},{10,11... | collective-permute-start | bytes 3538952 | tf_op jit(solution)/shard_map/ppermute | solution.py:728
  82.8 2.0 collective-permute-start.11
  82.8 29.0 %collective-permute-start.8 = (bf16[192,6144]{1,0:T(8,128)(2,1)S(1)}, bf16[192,6144]{1,0:T(8,128)(2,1)}, u32[]{:S(2)}, u32[]{:S(2)}) collective-permute-start(bf16[192,6144]{1,0:T(8,128)(2,1)S(1)} %pad_maximum_fusion.refs_5_), channel_id=1, source_target_pairs={{0,2},{1,5},{2,0},{3,7},{4,6},{5,1},{6,4},{7,3},{8,10},{9,13},{10,... | collective-permute-start | bytes 7077896 | tf_op jit(solution)/shard_map/ppermute | solution.py:728
  113.1 16.3 %collective-permute-start.12 = (bf16[96,6144]{1,0:T(8,128)(2,1)S(1)}, bf16[96,6144]{1,0:T(8,128)(2,1)S(1)}, u32[]{:S(2)}, u32[]{:S(2)}) collective-permute-start(bf16[96,6144]{1,0:T(8,128)(2,1)S(1)} %slice.264), channel_id=1, source_target_pairs={{0,4},{1,3},{2,6},{3,1},{4,0},{5,7},{6,2},{7,5},{8,12},{9,11},{10,... | collective-permute-start | bytes 3538952 | tf_op jit(solution)/shard_map/ppermute | solution.py:728
  115.1 17.1 %collective-permute-start.13 = (bf16[192,6144]{1,0:T(8,128)(2,1)}, bf16[192,6144]{1,0:T(8,128)(2,1)S(1)}, u32[]{:S(2)}, u32[]{:S(2)}) collective-permute-start(bf16[192,6144]{1,0:T(8,128)(2,1)} %collective-permute-done.8.refs_6_), channel_id=1, source_target_pairs={{0,1},{1,0},{2,3},{3,2},{4,5},{5,4},{6,7},{7,6},{8,9},{9,8},{10,11... | collective-permute-start | bytes 7077896 | tf_op jit(solution)/shard_map/ppermute | solution.py:728
  129.4 2.8 collective-permute-start.14
  175.9 228.4 %all-reduce.6.cloned.1.call-start = ((), (), s32[]{:S(2)}) async-start(), calls=%async_computation.2 | async-start | bytes 2359296 | tf_op jit(solution)/shard_map/psum | solution.py:885
  175.9 15.3 %collective-permute-start.15 = (bf16[8,48,3072]{2,1,0:T(8,128)(2,1)}, bf16[8,48,3072]{2,1,0:T(8,128)(2,1)}, u32[]{:S(2)}, u32[]{:S(2)}) collective-permute-start(bf16[8,48,3072]{2,1,0:T(8,128)(2,1)} %get-tuple-element.100), channel_id=1, source_target_pairs={{0,1},{1,0},{2,3},{3,2},{4,5},{5,4},{6,7},{7,6},{8,9},{9,8},{10,11... | collective-permute-start | bytes 7077896 | tf_op jit(solution)/shard_map/ppermute | solution.py:728
  176.1 15.1 %copy-start.6 = (bf16[8,48,3072]{2,1,0:T(8,128)(2,1)S(1)}, bf16[8,48,3072]{2,1,0:T(8,128)(2,1)}, u32[]{:S(2)}) copy-start(bf16[8,48,3072]{2,1,0:T(8,128)(2,1)} %get-tuple-element.99) | copy-start | bytes 7077892
  193.8 30.2 %collective-permute-start.16 = (bf16[2,48,3072]{2,1,0:T(8,128)(2,1)}, bf16[2,48,3072]{2,1,0:T(8,128)(2,1)S(1)}, u32[]{:S(2)}, u32[]{:S(2)}) collective-permute-start(bf16[2,48,3072]{2,1,0:T(8,128)(2,1)} %get-tuple-element.103), channel_id=1, source_target_pairs={{0,2},{1,3},{2,0},{3,1},{4,6},{5,7},{6,4},{7,5},{8,10},{9,11},{10,... | collective-permute-start | bytes 1769480 | tf_op jit(solution)/shard_map/ppermute | solution.py:728
  195.7 28.3 %collective-permute-start.17 = (bf16[2,48,3072]{2,1,0:T(8,128)(2,1)S(1)}, bf16[2,48,3072]{2,1,0:T(8,128)(2,1)S(1)}, u32[]{:S(2)}, u32[]{:S(2)}) collective-permute-start(bf16[2,48,3072]{2,1,0:T(8,128)(2,1)S(1)} %get-tuple-element.104), channel_id=1, source_target_pairs={{0,4},{1,5},{2,6},{3,7},{4,0},{5,1},{6,2},{7,3},{8,12},{9,13},{10,... | collective-permute-start | bytes 1769480 | tf_op jit(solution)/shard_map/ppermute | solution.py:728
  222.5 22.1 %collective-permute-start.20 = (bf16[8,48,3072]{2,1,0:T(8,128)(2,1)}, bf16[8,48,3072]{2,1,0:T(8,128)(2,1)S(1)}, u32[]{:S(2)}, u32[]{:S(2)}) collective-permute-start(bf16[8,48,3072]{2,1,0:T(8,128)(2,1)} %get-tuple-element.114), channel_id=1, source_target_pairs={{0,1},{1,0},{2,3},{3,2},{4,5},{5,4},{6,7},{7,6},{8,9},{9,8},{10,11... | collective-permute-start | bytes 7077896 | tf_op jit(solution)/shard_map/ppermute | solution.py:728
  226.2 15.1 %collective-permute-start.19 = (bf16[1,48,3072]{2,1,0:T(8,128)(2,1)}, bf16[1,48,3072]{2,1,0:T(8,128)(2,1)S(1)}, u32[]{:S(2)}, u32[]{:S(2)}) collective-permute-start(bf16[1,48,3072]{2,1,0:T(8,128)(2,1)} %get-tuple-element.112), channel_id=1, source_target_pairs={{0,2},{1,3},{2,0},{3,1},{4,6},{5,7},{6,4},{7,5},{8,10},{9,11},{10,... | collective-permute-start | bytes 884744 | tf_op jit(solution)/shard_map/ppermute | solution.py:728
  226.7 15.3 %collective-permute-start.18 = (bf16[1,48,3072]{2,1,0:T(8,128)(2,1)S(1)}, bf16[1,48,3072]{2,1,0:T(8,128)(2,1)}, u32[]{:S(2)}, u32[]{:S(2)}) collective-permute-start(bf16[1,48,3072]{2,1,0:T(8,128)(2,1)S(1)} %get-tuple-element.111), channel_id=1, source_target_pairs={{0,4},{1,5},{2,6},{3,7},{4,0},{5,1},{6,2},{7,3},{8,12},{9,13},{10,... | collective-permute-start | bytes 884744 | tf_op jit(solution)/shard_map/ppermute | solution.py:728
  246.4 32.4 %copy-start.11 = (bf16[832,768]{1,0:T(8,128)(2,1)S(1)}, bf16[832,768]{1,0:T(8,128)(2,1)}, u32[]{:S(2)}) copy-start(bf16[832,768]{1,0:T(8,128)(2,1)} %get-tuple-element.97) | copy-start | bytes 3833860
  275.1 20.2 %collective-permute-start.21 = (bf16[8,48,3968]{2,1,0:T(8,128)(2,1)}, bf16[8,48,3968]{2,1,0:T(8,128)(2,1)}, u32[]{:S(2)}, u32[]{:S(2)}) collective-permute-start(bf16[8,48,3968]{2,1,0:T(8,128)(2,1)} %get-tuple-element.133), channel_id=1, source_target_pairs={{0,1},{1,0},{2,3},{3,2},{4,5},{5,4},{6,7},{7,6},{8,9},{9,8},{10,11... | collective-permute-start | bytes 9142280 | tf_op jit(solution)/shard_map/ppermute | solution.py:728
  275.4 15.9 %collective-permute-start.23 = (bf16[2,48,3072]{2,1,0:T(8,128)(2,1)}, bf16[2,48,3072]{2,1,0:T(8,128)(2,1)S(1)}, u32[]{:S(2)}, u32[]{:S(2)}) collective-permute-start(bf16[2,48,3072]{2,1,0:T(8,128)(2,1)} %get-tuple-element.135), channel_id=1, source_target_pairs={{0,2},{1,3},{2,0},{3,1},{4,6},{5,7},{6,4},{7,5},{8,10},{9,11},{10,... | collective-permute-start | bytes 1769480 | tf_op jit(solution)/shard_map/ppermute | solution.py:728
  277.2 15.6 %collective-permute-start.22 = (bf16[2,48,3072]{2,1,0:T(8,128)(2,1)}, bf16[2,48,3072]{2,1,0:T(8,128)(2,1)S(1)}, u32[]{:S(2)}, u32[]{:S(2)}) collective-permute-start(bf16[2,48,3072]{2,1,0:T(8,128)(2,1)} %get-tuple-element.134), channel_id=1, source_target_pairs={{0,4},{1,5},{2,6},{3,7},{4,0},{5,1},{6,2},{7,3},{8,12},{9,13},{10,... | collective-permute-start | bytes 1769480 | tf_op jit(solution)/shard_map/ppermute | solution.py:728
  279.9 15.5 %copy-start = (bf16[8,48,3968]{2,1,0:T(8,128)(2,1)S(1)}, bf16[8,48,3968]{2,1,0:T(8,128)(2,1)}, u32[]{:S(2)}) copy-start(bf16[8,48,3968]{2,1,0:T(8,128)(2,1)} %get-tuple-element.132) | copy-start | bytes 9142276
  298.2 10.3 %collective-permute-start.26 = (bf16[1,48,3072]{2,1,0:T(8,128)(2,1)}, bf16[1,48,3072]{2,1,0:T(8,128)(2,1)}, u32[]{:S(2)}, u32[]{:S(2)}) collective-permute-start(bf16[1,48,3072]{2,1,0:T(8,128)(2,1)} %get-tuple-element.138), channel_id=1, source_target_pairs={{0,2},{1,3},{2,0},{3,1},{4,6},{5,7},{6,4},{7,5},{8,10},{9,11},{10,... | collective-permute-start | bytes 884744 | tf_op jit(solution)/shard_map/ppermute | solution.py:728
  298.7 10.3 %collective-permute-start.25 = (bf16[1,48,3072]{2,1,0:T(8,128)(2,1)}, bf16[1,48,3072]{2,1,0:T(8,128)(2,1)}, u32[]{:S(2)}, u32[]{:S(2)}) collective-permute-start(bf16[1,48,3072]{2,1,0:T(8,128)(2,1)} %get-tuple-element.137), channel_id=1, source_target_pairs={{0,4},{1,5},{2,6},{3,7},{4,0},{5,1},{6,2},{7,3},{8,12},{9,13},{10,... | collective-permute-start | bytes 884744 | tf_op jit(solution)/shard_map/ppermute | solution.py:728
  301.2 21.9 %collective-permute-start.24 = (bf16[2,48,3968]{2,1,0:T(8,128)(2,1)}, bf16[2,48,3968]{2,1,0:T(8,128)(2,1)}, u32[]{:S(2)}, u32[]{:S(2)}) collective-permute-start(bf16[2,48,3968]{2,1,0:T(8,128)(2,1)} %get-tuple-element.136), channel_id=1, source_target_pairs={{0,2},{1,3},{2,0},{3,1},{4,6},{5,7},{6,4},{7,5},{8,10},{9,11},{10,... | collective-permute-start | bytes 2285576 | tf_op jit(solution)/shard_map/ppermute | solution.py:728
  302.6 21.0 %collective-permute-start.27 = (bf16[2,48,3968]{2,1,0:T(8,128)(2,1)}, bf16[2,48,3968]{2,1,0:T(8,128)(2,1)}, u32[]{:S(2)}, u32[]{:S(2)}) collective-permute-start(bf16[2,48,3968]{2,1,0:T(8,128)(2,1)} %get-tuple-element.139), channel_id=1, source_target_pairs={{0,4},{1,5},{2,6},{3,7},{4,0},{5,1},{6,2},{7,3},{8,12},{9,13},{10,... | collective-permute-start | bytes 2285576 | tf_op jit(solution)/shard_map/ppermute | solution.py:728
  310.9 16.0 %copy-start.1 = (bf16[2,1,196,768]{3,0,2,1:T(2,128)(2,1)S(1)}, bf16[2,1,196,768]{3,0,2,1:T(2,128)(2,1)}, u32[]{:S(2)}) copy-start(bf16[2,1,196,768]{3,0,2,1:T(2,128)(2,1)} %copy.44) | copy-start | bytes 1806340
  310.9 16.0 %copy-start.2 = (bf16[2,1,196,768]{3,0,2,1:T(2,128)(2,1)S(1)}, bf16[2,1,196,768]{3,0,2,1:T(2,128)(2,1)}, u32[]{:S(2)}) copy-start(bf16[2,1,196,768]{3,0,2,1:T(2,128)(2,1)} %copy.45) | copy-start | bytes 1806340
  325.3 15.8 %collective-permute-start.33 = (bf16[48,3072]{1,0:T(8,128)(2,1)S(1)}, bf16[48,3072]{1,0:T(8,128)(2,1)S(1)}, u32[]{:S(2)}, u32[]{:S(2)}) collective-permute-start(bf16[48,3072]{1,0:T(8,128)(2,1)S(1)} %broadcast_select_fusion.4), channel_id=1, source_target_pairs={{0,8},{1,9},{2,10},{3,11},{4,12},{5,13},{6,14},{7,15},{8,0},{9,1},... | collective-permute-start | bytes 884744 | tf_op jit(solution)/shard_map/ppermute | solution.py:801
  329.5 14.0 %collective-permute-start.28 = (bf16[1,48,3968]{2,1,0:T(8,128)(2,1)S(1)}, bf16[1,48,3968]{2,1,0:T(8,128)(2,1)S(1)}, u32[]{:S(2)}, u32[]{:S(2)}) collective-permute-start(bf16[1,48,3968]{2,1,0:T(8,128)(2,1)S(1)} %get-tuple-element.140), channel_id=1, source_target_pairs={{0,4},{1,5},{2,6},{3,7},{4,0},{5,1},{6,2},{7,3},{8,12},{9,13},{10,... | collective-permute-start | bytes 1142792 | tf_op jit(solution)/shard_map/ppermute | solution.py:728
  331.0 12.5 %collective-permute-start.29 = (bf16[1,48,3968]{2,1,0:T(8,128)(2,1)S(1)}, bf16[1,48,3968]{2,1,0:T(8,128)(2,1)S(1)}, u32[]{:S(2)}, u32[]{:S(2)}) collective-permute-start(bf16[1,48,3968]{2,1,0:T(8,128)(2,1)S(1)} %get-tuple-element.141), channel_id=1, source_target_pairs={{0,2},{1,3},{2,0},{3,1},{4,6},{5,7},{6,4},{7,5},{8,10},{9,11},{10,... | collective-permute-start | bytes 1142792 | tf_op jit(solution)/shard_map/ppermute | solution.py:728
  341.2 25.1 %collective-permute-start.34 = (bf16[48,3072]{1,0:T(8,128)(2,1)S(1)}, bf16[48,3072]{1,0:T(8,128)(2,1)S(1)}, u32[]{:S(2)}, u32[]{:S(2)}) collective-permute-start(bf16[48,3072]{1,0:T(8,128)(2,1)S(1)} %add_convert_fusion.12), channel_id=1, source_target_pairs={{0,16},{8,24},{16,0},{24,8},{1,17},{9,25},{17,1},{25,9},{2,18},{10... | collective-permute-start | bytes 884744 | tf_op jit(solution)/shard_map/ppermute | solution.py:807
  345.3 37.8 %collective-permute-start.30 = (bf16[48,3968]{1,0:T(8,128)(2,1)S(1)}, bf16[48,3968]{1,0:T(8,128)(2,1)S(1)}, u32[]{:S(2)}, u32[]{:S(2)}) collective-permute-start(bf16[48,3968]{1,0:T(8,128)(2,1)S(1)} %get-tuple-element.149), channel_id=1, source_target_pairs={{0,8},{1,9},{2,10},{3,11},{4,12},{5,13},{6,14},{7,15},{8,0},{9,1},... | collective-permute-start | bytes 1142792 | tf_op jit(solution)/shard_map/ppermute | solution.py:801
  366.4 24.7 %collective-permute-start.35 = (bf16[48,3072]{1,0:T(8,128)(2,1)S(1)}, bf16[48,3072]{1,0:T(8,128)(2,1)S(1)}, u32[]{:S(2)}, u32[]{:S(2)}) collective-permute-start(bf16[48,3072]{1,0:T(8,128)(2,1)S(1)} %add_convert_fusion.11), channel_id=1, source_target_pairs={{0,8},{1,9},{2,10},{3,11},{4,12},{5,13},{6,14},{7,15},{8,0},{9,1},... | collective-permute-start | bytes 884744 | tf_op jit(solution)/shard_map/ppermute | solution.py:801
  383.3 13.0 %collective-permute-start.31 = (bf16[48,3968]{1,0:T(8,128)(2,1)S(1)}, bf16[48,3968]{1,0:T(8,128)(2,1)S(1)}, u32[]{:S(2)}, u32[]{:S(2)}) collective-permute-start(bf16[48,3968]{1,0:T(8,128)(2,1)S(1)} %fusion), channel_id=1, source_target_pairs={{0,16},{8,24},{16,0},{24,8},{1,17},{9,25},{17,1},{25,9},{2,18},{10... | collective-permute-start | bytes 1142792 | tf_op jit(solution)/shard_map/ppermute | solution.py:807
  396.4 7.7 %collective-permute-start.32 = (bf16[48,3968]{1,0:T(8,128)(2,1)S(1)}, bf16[48,3968]{1,0:T(8,128)(2,1)S(1)}, u32[]{:S(2)}, u32[]{:S(2)}) collective-permute-start(bf16[48,3968]{1,0:T(8,128)(2,1)S(1)} %add_convert_fusion.6), channel_id=1, source_target_pairs={{0,8},{1,9},{2,10},{3,11},{4,12},{5,13},{6,14},{7,15},{8,0},{9,1},... | collective-permute-start | bytes 1142792 | tf_op jit(solution)/shard_map/ppermute | solution.py:801
  (24 other events, 52.2 us)
Sparse Core Ops, SparseCore 0:
  176.0 67.4 reduce-scatter.1
  307.9 81.7 all-reduce.5

commit v4 on v3

--- a/solution.py
+++ b/solution.py
@@ -21,6 +21,7 @@
 F32 = jnp.float32
 SMALL = 32
 MICRO = 4_000_000_000
+SPARE = 12 * 1024 * 1024
 VMEM_LIMIT = 60 * 1024 * 1024
 
 
@@ -37,19 +38,16 @@
 
 
 def loop(count, body):
-    def step(i, carry):
+    for i in range(count):
         body(i)
-        return carry
-
-    lax.fori_loop(0, count, step, 0)
 
 
 def rows_of(i, size):
-    return pl.ds(pl.multiple_of(i * size, size), size)
+    return slice(i * size, (i + 1) * size)
 
 
 def cols_of(i, size, base=0):
-    return pl.ds(pl.multiple_of(base + i * size, 128), size)
+    return slice(base + i * size, base + (i + 1) * size)
 
 
 def unit(x):
@@ -86,7 +84,9 @@
         return gain_sum + fold(gn * w), shift_sum + fold(gn)
 
     zero = jnp.zeros((8, columns), F32)
-    gain_sum, shift_sum = lax.fori_loop(0, x_ref.shape[0] // CHUNK, body, (zero, zero))
+    gain_sum, shift_sum = zero, zero
+    for i in range(x_ref.shape[0] // CHUNK):
+        gain_sum, shift_sum = body(i, (gain_sum, shift_sum))
     return jnp.sum(gain_sum, axis=0, keepdims=True), jnp.sum(shift_sum, axis=0, keepdims=True)
 
 
@@ -94,7 +94,9 @@
     def body(i, total):
         return total + fold(ref[rows_of(i, CHUNK), start : start + size].astype(F32))
 
-    total = lax.fori_loop(0, ref.shape[0] // CHUNK, body, jnp.zeros((8, size), F32))
+    total = jnp.zeros((8, size), F32)
+    for i in range(ref.shape[0] // CHUNK):
+        total = body(i, total)
     return jnp.sum(total, axis=0, keepdims=True)
 
 
@@ -153,7 +155,7 @@
 ORDER = ((3, 0), (1, 0), (3, 1), (2, 1), (1, 1), (2, 0), (0, 0), (0, 1))
 
 
-def store_pieces(dw, outs, place_ref, sems, share=1):
+def store_pieces(dw, outs, place_ref, sems, share=1, base=0):
     if len(outs) == 1:
         return start([(dw, outs[0])], sems)
     half, columns = outs[0].shape[1], dw.shape[1]
@@ -163,7 +165,7 @@
             place = place_ref[8 + side * 4 + chip]
             for k in range(share):
                 source = dw.at[pl.ds(pl.multiple_of(((place * share + k) * 2 + top) * half, 16), half), :]
-                pairs.append((source, out.at[n, :, k * columns : (k + 1) * columns]))
+                pairs.append((source, out.at[n, :, base + k * columns : base + (k + 1) * columns]))
     return start(pairs, sems)
 
 
@@ -251,7 +253,7 @@
 }
 
 
-def call(body, operands, spaces, outs, out_spaces, scratch, micros, name):
+def call(body, operands, spaces, outs, out_spaces, scratch, micros, name, tight=True):
     late = [n for n, space in enumerate(spaces) if space == "l"]
     early = [n for n, space in enumerate(out_spaces) if space == "e"]
     n_in, n_out, n_scratch = len(operands), len(outs), len(scratch)
@@ -273,6 +275,10 @@
         for n in early:
             results[n].copy.wait()
 
+    held = [operands[n].size * operands[n].dtype.itemsize for n, space in enumerate(spaces) if space in "vl"]
+    held += [math.prod(outs[n][0]) * jnp.dtype(outs[n][1]).itemsize for n, space in enumerate(out_spaces) if space in "ve"]
+    held += [math.prod(ref.shape) * jnp.dtype(ref.dtype).itemsize for ref in scratch if "semaphore" not in str(ref.memory_space)]
+    limit = min(VMEM_LIMIT, sum(held) + SPARE) if tight else VMEM_LIMIT
     more = [pltpu.VMEM(operands[n].shape, operands[n].dtype) for n in late]
     more += [pltpu.VMEM(*outs[n]) for n in early]
     more += [pltpu.SemaphoreType.DMA((max(1, len(late)),)), pltpu.SemaphoreType.DMA((max(1, len(early)),))]
@@ -282,7 +288,7 @@
         in_specs=[SPACES[space] for space in spaces],
         out_specs=[SPACES[space] for space in out_spaces],
         scratch_shapes=list(scratch) + more,
-        compiler_params=pltpu.CompilerParams(vmem_limit_bytes=VMEM_LIMIT),
+        compiler_params=pltpu.CompilerParams(vmem_limit_bytes=limit),
         cost_estimate=pl.CostEstimate(flops=micros * MICRO, bytes_accessed=0, transcendentals=0),
         name=name,
     )(*operands)
@@ -412,15 +418,16 @@
     return h * cdf, cdf + h * density
 
 
-def feed(ins, results, own):
+def feed_out(ins, results, own):
     place_ref, z_ref, g_ref, small_ref, hb_ref, *bufs = ins
-    out_ref, gh_out, sums_ref, ghb_ref, dwr_out, *outs = results
-    we, wr, dwe, nm, a, sems, out_sems = own
-    gh, dwr = gh_out.ref, dwr_out.ref
+    out_ref, nm_out, gh_out, *outs = results
+    we, wr, dwr, a, sems, out_sems = own
+    nm, gh = nm_out.ref, gh_out.ref
     columns = z_ref.shape[1]
     units = we.shape[1]
     copies, more = load_feed(bufs, place_ref, we, wr, sems)
     norm_chunks(z_ref, nm, small_ref[13:14, :], small_ref[16:17, :])
+    nm_out.send()
     wait(copies + more)
 
     def inner(j):
@@ -437,7 +444,17 @@
         dwr[rows_of(j, WIDE), :] = tn(a[:, cols_of(j, WIDE)], g_ref[...]).astype(BF)
 
     loop(units // WIDE, left)
-    dwr_out.send()
+    copies = store_pieces(dwr, outs, place_ref, out_sems, units // columns)
+    for at in blocks_of(columns):
+        out_ref[:, at] = (z_ref[:, at] + (nn(a[...], wr[:, at]) + small_ref[7:8, at])).astype(BF)
+    wait(copies)
+
+
+def feed_in(ins, results, own):
+    place_ref, gh, nm, g_in = ins
+    sums_ref, ghb_ref, *outs = results
+    dwe, out_sems = own
+    units = gh.shape[1]
 
     def right(j):
         at = cols_of(j, WIDE)
@@ -447,9 +464,7 @@
 
     loop(units // WIDE, right)
     copies = store_pieces(dwe, outs, place_ref, out_sems)
-    for at in blocks_of(columns):
-        out_ref[:, at] = (z_ref[:, at] + (nn(a[...], wr[:, at]) + small_ref[7:8, at])).astype(BF)
-    sums_ref[0:1, :] = column_sums(g_ref, 0, columns)
+    sums_ref[0:1, :] = column_sums(g_in.get(), 0, nm.shape[1])
     wait(copies)
 
 
@@ -530,7 +545,7 @@
             for part, values in enumerate((gq, gk, gv)):
                 to = cols_of(pair, 128, part * columns)
                 one, two = (jnp.where(first, values[4 * u + 2 * f], values[4 * u + 2 * f + 1]) for f in range(FRAMES))
-                top = pl.multiple_of(clip * FRAMES * BLOCK, 16)
+                top = clip * FRAMES * BLOCK
                 gqkv[pl.ds(top, EDGE), to] = one[:EDGE].astype(BF)
                 gqkv[pl.ds(top + BLOCK, EDGE), to] = two[:EDGE].astype(BF)
                 both = jnp.where(class_row, one[EDGE:] + two[EDGE:], one[EDGE:])
@@ -550,14 +565,13 @@
     wait(copies)
 
 
-def time_backward(n, ins, results, own):
-    place_ref, gy_ref, x_in, nt_in, qkv_in, p_in, o_in, e_in, small_ref, *others = ins
-    others, bufs = others[: len(others) - n], others[len(others) - n :]
-    gx_ref, sums_ref, *outs = results
-    w, dw_ref, grt, get, go, gqkv, gn, sems, out_sems = own
+def mixer_backward(n, ins, results, own):
+    place_ref, gy_ref, o_in, e_in, *bufs = ins
+    go_out, sums_ref, *outs = results
+    w, dw_ref, grt, get, sems, out_sems = own
     columns = gy_ref.shape[1]
     rows = gy_ref.shape[0]
-    copies = load(bufs, place_ref, w, sems)
+    copies = load([b.at[:, 3 * columns : 5 * columns] for b in bufs], place_ref, w, sems)
 
     def lower(i):
         at = rows_of(i, CHUNK)
@@ -566,16 +580,31 @@
 
     loop(rows // CHUNK, lower)
     wait(copies)
-    for at in blocks_of(columns):
-        get[:, at] = nt(grt[...], w[at, 4 * columns : 5 * columns]).astype(BF)
-    for at in blocks_of(columns):
-        go[:, at] = nt(get[...], w[at, 3 * columns : 4 * columns]).astype(BF)
+    go = go_out.ref
+    for at in blocks_of(columns):
+        get[:, at] = nt(grt[...], w[at, columns : 2 * columns]).astype(BF)
     e_ref, o_ref = e_in.get(), o_in.get()
     for at in blocks_of(columns):
-        dw_ref[:, shifted(at, 4 * columns)] = tn(e_ref[...], grt[:, at]).astype(BF)
-    for at in blocks_of(columns):
-        dw_ref[:, shifted(at, 3 * columns)] = tn(o_ref[...], get[:, at]).astype(BF)
-    qkv_ref, p_ref = qkv_in.get(), p_in.get()
+        dw_ref[:, shifted(at, columns)] = tn(e_ref[...], grt[:, at]).astype(BF)
+    for at in blocks_of(columns):
+        dw_ref[:, at] = tn(o_ref[...], get[:, at]).astype(BF)
+    copies = store_pieces(dw_ref, outs, place_ref, out_sems)
+    for at in blocks_of(columns):
+        go[:, at] = nt(get[...], w[at, 0:columns]).astype(BF)
+    go_out.send()
+    sums_ref[2:3, :] = column_sums(get, 0, columns)
+    sums_ref[3:4, :] = column_sums(grt, 0, columns)
+    wait(copies)
+
+
+def time_backward(n, ins, results, own):
+    place_ref, go, qkv_ref, p_ref, nt_in, x_in, gy_in, small_ref, before, *others = ins
+    others, bufs = others[: len(others) - n], others[len(others) - n :]
+    gx_ref, sums_ref, *outs = results
+    w, dw_ref, gqkv, gn, sems, out_sems = own
+    columns = gx_ref.shape[1]
+    rows = gx_ref.shape[0]
+    copies = load([b.at[:, 0 : 3 * columns] for b in bufs], place_ref, w, sems)
     heads = head_map(columns)
     for clip in range(rows // (FRAMES * BLOCK)):
         at = [slice((clip * FRAMES + f) * BLOCK, (clip * FRAMES + f + 1) * BLOCK) for f in range(FRAMES)]
@@ -602,11 +631,12 @@
     nt_ref = nt_in.get()
     for at in blocks_of(3 * columns):
         dw_ref[:, at] = tn(nt_ref[...], gqkv[:, at]).astype(BF)
-    main = slice(0, 5 * columns)
-    copies = store_pieces(dw_ref.at[:, main], [out.at[..., main] for out in outs], place_ref, out_sems)
-    for at in blocks_of(columns):
-        gn[:, at] = nt(gqkv[...], w[at, 0 : 3 * columns])
-    x_ref = x_in.get()
+    main = slice(0, 3 * columns)
+    stores = store_pieces(dw_ref.at[:, main], [out.at[..., main] for out in outs], place_ref, out_sems)
+    wait(copies)
+    for at in blocks_of(columns):
+        gn[:, at] = nt(gqkv[...], w[at, :])
+    x_ref, gy_ref = x_in.get(), gy_in.get()
 
     def store(at, value):
         gx_ref[at, :] = value.astype(BF)
@@ -614,14 +644,13 @@
     gain_sum, shift_sum = norm_back_chunks(gn, x_ref, small_ref[11:12, :], lambda at: gy_ref[at, :], store)
     sums_ref[0:1, :] = column_sums(gqkv, 0, columns)
     sums_ref[1:2, :] = column_sums(gqkv, 2 * columns, columns)
-    sums_ref[2:3, :] = column_sums(get, 0, columns)
-    sums_ref[3:4, :] = column_sums(grt, 0, columns)
+    sums_ref[2:4, :] = before[2:4, :]
     sums_ref[4:5, :] = gain_sum
     sums_ref[5:6, :] = shift_sum
-    wait(copies)
+    wait(stores)
     if others:
         gather_small(dw_ref, (sums_ref, *others))
-        last = slice(5 * columns, 5 * columns + 128)
+        last = slice(3 * columns, 3 * columns + 128)
         wait(store_pieces(dw_ref.at[:, last], [out.at[..., last] for out in outs], place_ref, out_sems))
 
 
@@ -670,7 +699,7 @@
         return call(
             functools.partial(time_forward, n), (self.place, x, *given, *bufs), "sv" + "v" * len(given) + "a" * n,
             [self.act, self.act3, self.act, self.act, ((self.rows * FRAMES, 128), F32), self.wide] + extra, "eeeeevvv",
-            self.vmem(((c, bufs[0].shape[1]), BF)) + self.sems(8), 14, "time_forward",
+            self.vmem(((c, bufs[0].shape[1]), BF)) + self.sems(8), 14, "time_forward", False,
         )
 
     def space_forward(self, y, small, bufs):
@@ -679,16 +708,24 @@
         return call(
             functools.partial(space_forward, n), (self.place, y, small, *bufs), "svv" + "a" * n,
             [self.act, self.act3, probs, self.act, self.wide], "eeeev",
-            self.vmem(((c, 4 * c), BF)) + self.sems(8), 16, "space_forward",
+            self.vmem(((c, 4 * c), BF)) + self.sems(8), 16, "space_forward", False,
         )
 
-    def feed(self, z, g, small, hb, bufs):
+    def feed_out(self, z, g, small, hb, bufs):
         c, u, n = self.columns, self.units, len(bufs)
+        outs = self.grads(u) if self.pieced else [((u, c), BF)]
+        return call(
+            feed_out, (self.place, z, g, small, hb, *bufs), "svvvv" + "a" * n,
+            [self.act, self.act, self.tall] + outs, "vee" + "a" * len(outs),
+            self.vmem(((c, u), BF), ((u, c), BF), ((u, c), BF), self.tall) + self.sems(40, 64), 30, "feed_out", False,
+        )
+
+    def feed_in(self, gh, normed, g):
+        c, u = self.columns, self.units
         outs = self.grads(u)
         return call(
-            feed, (self.place, z, g, small, hb, *bufs), "svvvv" + "a" * n,
-            [self.act, self.tall, self.sums, ((8, u), F32), ((u, c), BF)] + outs, "vevve" + "a" * len(outs),
-            self.vmem(((c, u), BF), ((u, c), BF), ((c, u), BF), self.act, self.tall) + self.sems(40, 16), 38, "feed",
+            feed_in, (self.place, gh, normed, g), "svvl", [self.sums, ((8, u), F32)] + outs, "vv" + "a" * len(outs),
+            self.vmem(((c, u), BF)) + self.sems(16), 8, "feed_in",
         )
 
     def norm_backward(self, row, gh, x, base, small, bufs, name):
@@ -707,15 +744,23 @@
             self.vmem(((c, c), BF), ((c, 4 * c), BF), self.act, self.act) + self.sems(8, 16), 20, "space_backward",
         )
 
-    def time_backward(self, gy, x, normed, qkv, p, o, e, small, others, bufs):
+    def mixer_backward(self, gy, o, e, bufs):
         c, n = self.columns, len(bufs)
-        width = bufs[0].shape[1]
+        outs = self.grads(2 * c)
+        return call(
+            functools.partial(mixer_backward, n), (self.place, gy, o, e, *bufs), "svll" + "a" * n,
+            [self.act, self.sums] + outs, "ev" + "a" * len(outs),
+            self.vmem(((c, 2 * c), BF), ((c, 2 * c), BF), self.act, self.act) + self.sems(8, 16), 8, "mixer_backward",
+        )
+
+    def time_backward(self, go, qkv, p, normed, x, gy, small, before, others, bufs):
+        c, n = self.columns, len(bufs)
+        width = 3 * c + (128 if others else 0)
         outs = self.grads(width)
         return call(
-            functools.partial(time_backward, n), (self.place, gy, x, normed, qkv, p, o, e, small, *others, *bufs),
-            "svllllllv" + "v" * len(others) + "a" * n, [self.act, self.sums] + outs, "vv" + "a" * len(outs),
-            self.vmem(((c, width), BF), ((c, width), BF), self.act, self.act, self.act, self.act3, self.wide) + self.sems(8, 16),
-            24, "time_backward",
+            functools.partial(time_backward, n), (self.place, go, qkv, p, normed, x, gy, small, before, *others, *bufs),
+            "svvvlllvv" + "v" * len(others) + "a" * n, [self.act, self.sums] + outs, "vv" + "a" * len(outs),
+            self.vmem(((c, 3 * c), BF), ((c, width), BF), self.act3, self.wide) + self.sems(8, 16), 20, "time_backward",
         )
 
 
@@ -790,6 +835,15 @@
         return top[0], bottom[0]
 
 
+def beside(*values):
+    return jnp.concatenate([v[n : n + 1] for v in values for n in range(v.shape[0])], axis=2)
+
+
+def apart(value, widths):
+    stops = [sum(widths[: n + 1]) for n in range(len(widths))]
+    return [value[..., stop - width : stop] for stop, width in zip(stops, widths)]
+
+
 def tie(*values):
     leaves, shape = jax.tree.flatten(values)
     return jax.tree.unflatten(shape, lax.optimization_barrier(tuple(leaves)))
@@ -801,12 +855,20 @@
     return lax.ppermute(value, BOTH, pairs)
 
 
-def sum_groups(halves, even):
-    top, bottom = halves
-    held = total(jnp.where(even, top, bottom), swap_z(jnp.where(even, bottom, top)))
-    held = total(held, lax.ppermute(held, "grp", [(z, z ^ 2) for z in range(4)]))
-    other = swap_z(held)
-    return jnp.concatenate([jnp.where(even, held, other), jnp.where(even, other, held)], axis=0)
+def across_pairs(value):
+    return lax.ppermute(value, "grp", [(z, z ^ 2) for z in range(4)])
+
+
+def inward(value):
+    return lax.ppermute(value, "grp", [(0, 1), (3, 2)])
+
+
+def across(value):
+    return lax.ppermute(value, "grp", [(1, 2), (2, 1)])
+
+
+def outward(value):
+    return lax.ppermute(value, "grp", [(1, 0), (2, 3)])
 
 
 def local(video, cotangent, live, time_entry, time_exit, time_mixer, space_entry, space_exit, hidden_expand, hidden_reduce, bias_rows, hidden_bias, norm_gain, norm_shift):
@@ -822,8 +884,7 @@
         return lax.all_gather(value, "shard", axis=0, tiled=True)
 
     flags = live.astype(BF)[:, :, None]
-    x = pack_rows(video[:, 0], False)
-    g = pack_rows(cotangent[:, 0] * flags, True)
+
     own_t = jnp.concatenate([time_entry, time_exit, time_mixer], axis=1)
     own_s = jnp.concatenate([space_entry, space_exit], axis=1)
     if pieced:
@@ -833,24 +894,28 @@
         )
         own_t = jnp.concatenate([own_t, jnp.pad(narrow, ((0, part - narrow.shape[0]), (0, 0)))], axis=1)
         own_f = jnp.concatenate([hidden_expand] + [hidden_reduce[k * part : (k + 1) * part] for k in range(share)], axis=1)
-        net = Layer(x.shape[0], columns, units, shards, pieced, places(mine))
+        net = Layer(clips * FRAMES * BLOCK, columns, units, shards, pieced, places(mine))
         both_t = gather_start(own_t)
+        both_t, video, own_s, own_f = tie(both_t, video, own_s, own_f)
+        hop_t = gather_hop(both_t)
+        x = pack_rows(video[:, 0], False)
         both_s, both_f = gather_start(own_s), gather_start(own_f)
-        hop_t, both_s, both_f, x, g = tie(gather_hop(both_t), both_s, both_f, x, g)
+        hop_t, both_s, both_f, x = tie(hop_t, both_s, both_f, x)
         second_t, both_s, both_f = tie(gather_second(hop_t), both_s, both_f)
         wt = (both_t, hop_t, second_t, to_sibling(hop_t), to_sibling(second_t))
-        hop_s = gather_hop(both_s)
+        hop_s, hop_f = gather_hop(both_s), gather_hop(both_f)
         normed_t, qkv_t, o_t, e_t, p_t, y, small, hb = net.time_forward(x, (), wt)
-        hop_s, y, both_f = tie(hop_s, y, both_f)
+        hop_s, y, cotangent = tie(hop_s, y, cotangent)
+        g = pack_rows(cotangent[:, 0] * flags, True)
         second_s = gather_second(hop_s)
-        hop_f = gather_hop(both_f)
         ws = (both_s, hop_s, second_s, to_sibling(hop_s), to_sibling(second_s))
+        hop_f, y, ws, g = tie(hop_f, y, ws, g)
         normed_s, qkv_s, p_s, o_s, z = net.space_forward(y, small, ws)
-        hop_f, z = tie(hop_f, z)
-        second_f = gather_second(hop_f)
+        second_f, z = tie(gather_second(hop_f), z)
         wf = (both_f, hop_f, second_f, to_sibling(hop_f), to_sibling(second_f))
     else:
-        net = Layer(x.shape[0], columns, units, shards, pieced, jnp.zeros((16,), jnp.int32))
+        x, g = pack_rows(video[:, 0], False), pack_rows(cotangent[:, 0] * flags, True)
+        net = Layer(clips * FRAMES * BLOCK, columns, units, shards, pieced, jnp.zeros((16,), jnp.int32))
         packed = jnp.concatenate([bias_rows, norm_gain, norm_shift], axis=0)
         spread = lax.all_gather(packed, "shard", axis=0).transpose(1, 0, 2).reshape(-1, columns).astype(F32)
         small = jnp.concatenate([spread[:8], jnp.zeros((3, columns), F32), spread[8:], jnp.zeros((SMALL - 17, columns), F32)], axis=0)
@@ -859,47 +924,88 @@
         normed_t, qkv_t, o_t, e_t, p_t, y, small, hb = net.time_forward(x, given, wt)
         normed_s, qkv_s, p_s, o_s, z = net.space_forward(y, small, ws)
 
-    out, gh, sums_f, ghb, grad_r, *grad_e = net.feed(z, g, small, hb, wf)
+    out, normed_f, gh, *grad_r = net.feed_out(z, g, small, hb, wf)
+    if pieced:
+        sum_r = Reduction(*grad_r)
+    sums_f, ghb, *grad_e = net.feed_in(gh, normed_f, g)
+    if pieced:
+        sum_e = Reduction(*grad_e)
+        sent_r, gh, ghb, sums_f, sum_e.keep = tie(sum_r.first(), gh, ghb, sums_f, sum_e.keep)
+        sum_r.cross(sent_r)
     gz, norm_f = net.norm_backward(13, gh, z, g, small, wf if pieced else wf[:1], "feed_norm")
     if pieced:
-        sum_e = Reduction(*grad_e)
-        sent_e, gz = tie(sum_e.first(), gz)
+        sent_r, sent_e, gz, norm_f = tie(sum_r.second(), sum_e.first(), gz, norm_f)
+        sum_r.cross_again(sent_r)
         sum_e.cross(sent_e)
     gqkv, sums_s, *grad_s = net.space_backward(gz, normed_s, qkv_s, p_s, o_s, ws)
     if pieced:
         sum_s = Reduction(*grad_s)
-        sent_e, gqkv = tie(sum_e.second(), gqkv)
+        kept_r, sent_e, gqkv, sums_s, sum_s.keep = tie(jnp.concatenate(sum_r.finish(), axis=0), sum_e.second(), gqkv, sums_s, sum_s.keep)
         sum_e.cross_again(sent_e)
+        got_r = inward(kept_r)
     gy, norm_s = net.norm_backward(12, gqkv, y, gz, small, ws, "space_norm")
     if pieced:
-        kept_e, sent_s, gy = tie(sum_e.finish(), sum_s.first(), gy)
+        got_r, sum_e.last_x, sum_e.last_y, gy, norm_s = tie(got_r, sum_e.last_x, sum_e.last_y, gy, norm_s)
+        kept_e = jnp.concatenate(sum_e.finish(), axis=0)
+        kept_r, kept_e, sent_s, gy, norm_s = tie(total(kept_r, got_r), kept_e, sum_s.first(), gy, norm_s)
         sum_s.cross(sent_s)
+        got_r, got_e = across(kept_r), inward(kept_e)
         sums_s = jnp.concatenate([sums_s[0:3], norm_s[0:2], sums_s[5:]], axis=0)
         sums_f = jnp.concatenate([sums_f[0:1], norm_f[0:2], sums_f[3:]], axis=0)
     others = (sums_s, sums_f, ghb) if pieced else ()
-    gx, sums_t, *grad_t = net.time_backward(gy, x, normed_t, qkv_t, p_t, o_t, e_t, small, others, wt)
-
+    go, sums_m, *grad_m = net.mixer_backward(gy, o_t, e_t, wt)
     if pieced:
-        even = lax.axis_index("grp") % 2 == 0
-        kept_r = lax.psum_scatter(grad_r, "shard", scatter_dimension=0, tiled=True)
-        re, rr = lax.psum((jnp.concatenate(kept_e, axis=0), kept_r), "grp")
+        sum_m = Reduction(*grad_m)
+        sent = [beside(last, both) for last, both in zip(sum_s.second(), sum_m.first())]
+        kept_r, kept_e, sent, go, sums_m, sum_m.keep = tie(total(kept_r, got_r), total(kept_e, got_e), sent, go, sums_m, sum_m.keep)
+        arrived = (along_x(sent[0]), along_y(sent[1]), outward(kept_r), across(kept_e))
+    gx, sums_t, *grad_t = net.time_backward(go, qkv_t, p_t, normed_t, x, gy, small, sums_m, others, wt)
+
+    if pieced:
+        group = lax.axis_index("grp")
+        even = group % 2 == 0
+        inner = (group == 1) | (group == 2)
+        (came_x, came_y, got_r, got_e), grad_t, gx, sums_t = tie(arrived, grad_t, gx, sums_t)
+        widths = (sum_s.keep.shape[2], sum_m.keep.shape[2], sum_m.keep.shape[2])
+        sum_s.last_x, *from_x = apart(came_x, widths)
+        sum_s.last_y, *from_y = apart(came_y, widths)
+        sum_m.from_x, sum_m.from_y = jnp.concatenate(from_x, axis=0), jnp.concatenate(from_y, axis=0)
         sum_t = Reduction(*grad_t)
-        _, gx = tie(kept_r, gx)
-        sent_s, sent_t = tie(sum_s.second(), sum_t.first())
-        sum_s.cross_again(sent_s)
-        sum_t.cross(sent_t)
-        kept_s, sent_t = tie(sum_s.finish(), sum_t.second())
-        sum_t.cross_again(sent_t)
-        rs = sum_groups(kept_s, even).astype(F32)
-        rt = sum_groups(sum_t.finish(), even)
-        re, rr, rt = (v.astype(F32) for v in tie(re, rr, rt))
-        narrow = rt[:, 5 * columns :]
+        low_s, high_s = sum_s.finish()
+        kept_e = total(kept_e, got_e)
+        sent_s, kept_e = tie(jnp.where(even, high_s, low_s), kept_e)
+        got_s, got_e = swap_z(sent_s), outward(kept_e)
+        sent_x, sent_y = (beside(last, both) for last, both in zip(sum_m.second(), sum_t.first()))
+        came_x, came_y = along_x(sent_x), along_y(sent_y)
+        held_s = total(jnp.where(even, low_s, high_s), got_s)
+        held_s, came_x, came_y = tie(held_s, came_x, came_y)
+        got_s = across_pairs(held_s)
+        widths = (sum_m.keep.shape[2], sum_t.keep.shape[2], sum_t.keep.shape[2])
+        sum_m.last_x, *from_x = apart(came_x, widths)
+        sum_m.last_y, *from_y = apart(came_y, widths)
+        sum_t.from_x, sum_t.from_y = jnp.concatenate(from_x, axis=0), jnp.concatenate(from_y, axis=0)
+        sum_t.cross_again(tie(*sum_t.second()))
+        low_t, high_t = (jnp.concatenate(pair, axis=1) for pair in zip(sum_m.finish(), sum_t.finish()))
+        sent_t, held_t, got_s, got_e = tie(jnp.where(even, high_t, low_t), jnp.where(even, low_t, high_t), got_s, got_e)
+        got_t = swap_z(sent_t)
+        held_s = total(held_s, got_s)
+        got_s = swap_z(held_s)
+        held_t, got_s = tie(total(held_t, got_t), got_s)
+        held_t = total(held_t, across_pairs(held_t))
+        got_t = swap_z(held_t)
+        rt = jnp.concatenate([jnp.where(even, held_t, got_t), jnp.where(even, got_t, held_t)], axis=0).astype(F32)
+        rs = jnp.concatenate([jnp.where(even, held_s, got_s), jnp.where(even, got_s, held_s)], axis=0).astype(F32)
+        re = jnp.where(inner, kept_e, got_e).astype(F32)
+        rr = jnp.where(inner, kept_r, got_r).astype(F32)
+        rr = jnp.concatenate([rr[:, k * columns : (k + 1) * columns] for k in range(share)], axis=0)
+        rm, rt = rt[:, : 2 * columns], rt[:, 2 * columns :]
+        narrow = rt[:, 3 * columns :]
         biases, rows_hidden = narrow[0:8, :part], narrow[8:11].reshape(-1)
         gains, shifts = narrow[11:14, :part], narrow[14:17, :part]
     else:
-        re, rr, rs, rt = (
+        re, rr, rs, rm, rt = (
             lax.psum(lax.psum_scatter(v, "shard", scatter_dimension=0, tiled=True), "grp").astype(F32)
-            for v in (*grad_e, grad_r, *grad_s, *grad_t)
+            for v in (*grad_e, *grad_r, *grad_s, *grad_m, *grad_t)
         )
         rows = [sums_t[0:4], sums_s[0:3], sums_f[0:1], sums_t[4:5], norm_s[0:1], norm_f[0:1], sums_t[5:6], norm_s[1:2], norm_f[1:2]]
         cut = lax.dynamic_slice_in_dim(lax.psum(jnp.concatenate(rows, axis=0), BOTH), mine * part, part, axis=1)
@@ -909,8 +1015,8 @@
         (unpack_rows(out, clips) * flags)[:, None],
         unpack_rows(gx, clips)[:, None],
         rt[:, : 3 * columns],
-        rt[:, 3 * columns : 4 * columns],
-        rt[:, 4 * columns : 5 * columns],
+        rm[:, :columns],
+        rm[:, columns:],
         rs[:, : 3 * columns],
         rs[:, 3 * columns :],
         re,

time: 422 us -> 376 us (0.89)
  waiting for transfers between devices: 143 us -> 118 us
  starting transfers between devices: 33.5 us -> 55 us
  Pallas kernels: 151 us -> 136 us
  between operations: 14.9 us -> 2.63 us
  other arithmetic: 45 us -> 35.1 us
    ppermute x4, waiting for transfers between devices: 39.1 us -> 21.8 us  [swap_z(): return lax.ppermute(value, BOTH, pairs)]
    ppermute x2 -> x8, starting transfers between devices: 2.42 us -> 18.4 us  [the longest x2 10.7 us: inward(): return lax.ppermute(value, 'grp', [(0, 1), (3, 2)])]
    pallas_call x7 -> x9, Pallas kernels: 151 us -> 136 us  [call(): pl.pallas_call(kernel, out_shape=[jax.ShapeDtypeStruct(s, d) for s, d in...]
    ppermute x30 -> x36, waiting for transfers between devices: 78.6 us -> 69.2 us  [permute(): return lax.ppermute(value, BOTH, pairs)]
    convert_element_type x10 -> x18, other arithmetic: 13.9 us -> 4.74 us  [total(): return sum((t.astype(F32) for t in terms)).astype(BF)]
    ppermute x2 -> x8, waiting for transfers between devices: 25.4 us -> 27 us  [the longest x2 22.1 us: across_pairs(): return lax.ppermute(value, 'grp', [(z, z ^ 2) for z in range(4)])]
    ppermute x30 -> x36, starting transfers between devices: 28.5 us -> 30 us  [permute(): return lax.ppermute(value, BOTH, pairs)]
    unnamed x79 -> x116, local copies, waits for them, and re-layouts: 9.74 us -> 8.58 us
  transfers between devices with their start and end apart: 38 -> 48, of which waited for: 18 -> 19; matrix products, arithmetic and copies ran while one was open for 13% -> 10% of each run, Pallas kernels for 27% -> 29%
where the time goes in v4:
time: 376 us; the launch traced here: 372 us
  Pallas kernels  136 us (36%)
  waiting for transfers between devices  118 us (31%)
  starting transfers between devices  55 us (15%)
  other arithmetic  35.1 us (9%)
  local copies, waits for them, and re-layouts  25.6 us (7%)
    pallas_call x9, Pallas kernels, call(): pl.pallas_call(kernel, out_shape=[jax.ShapeDtypeStruct(s, d) for s, d in...  136 us
    ppermute x36, waiting for transfers between devices, permute(): return lax.ppermute(value, BOTH, pairs)  69.2 us
    ppermute x36, starting transfers between devices, permute(): return lax.ppermute(value, BOTH, pairs)  30 us
    ppermute x2, waiting for transfers between devices, across_pairs(): return lax.ppermute(value, 'grp', [(z, z ^ 2) for z in range(4)])  22.1 us
    ppermute x4, waiting for transfers between devices, swap_z(): return lax.ppermute(value, BOTH, pairs)  21.8 us
    ppermute x2, starting transfers between devices, inward(): return lax.ppermute(value, 'grp', [(0, 1), (3, 2)])  10.7 us
    another operation x4, other arithmetic, pack_rows(): return jnp.stack(frames, axis=1).reshape(clips * FRAMES * BLOCK, columns)  9.79 us
    unnamed x116, local copies, waits for them, and re-layouts  8.58 us
  transfers between devices with their start and end apart: 48, of which 19 were waited for; matrix products, arithmetic and copies ran while one was open for 10% of the time, Pallas kernels for 29%

profile of v4, /device:TPU:0, one launch (start us, length us, event | category | flops | bytes accessed | tf_op | source)
XLA Modules:
  0.0 372.2 jit_solution(17500875652055687056)
XLA Ops:
  6.6 2.9 collective-permute-start.1
  10.3 3.2 fusion.2
  13.5 1.8 pad_maximum_fusion.2
  16.9 10.5 %collective-permute-done.1.refs_3_.refs_5_.refs_13_ = bf16[192,3968]{1,0:T(8,128)(2,1)} collective-permute-done((bf16[192,3968]{1,0:T(8,128)(2,1)S(1)}, bf16[192,3968]{1,0:T(8,128)(2,1)}, u32[]{:S(2)}, u32[]{:S(2)}) %collective-permute-start.1) | collective-permute-done | bytes 1523744 | tf_op jit(solution)/shard_map/ppermute | solution.py:773
  28.6 2.1 collective-permute-start.4
  30.7 9.8 %collective-permute-done.4.refs_4_.refs_6_.refs_14_ = bf16[96,3968]{1,0:T(8,128)(2,1)} collective-permute-done((bf16[96,3968]{1,0:T(8,128)(2,1)S(1)}, bf16[96,3968]{1,0:T(8,128)(2,1)}, u32[]{:S(2)}, u32[]{:S(2)}) %collective-permute-start.4) | collective-permute-done | bytes 761888 | tf_op jit(solution)/shard_map/ppermute | solution.py:773
  41.2 2.0 collective-permute-start.6
  43.2 14.1 %time_forward.1 = (bf16[832,768]{1,0:T(8,128)(2,1)}, bf16[832,2304]{1,0:T(8,128)(2,1)}, bf16[832,768]{1,0:T(8,128)(2,1)}, bf16[832,768]{1,0:T(8,128)(2,1)}, f32[...) custom-call(s32[16]{0:T(128)} %stack.76.refs_0_, bf16[832,768]{1,0:T(8,128)(2,1)} %bitcast.66, ...), custom_call_target="tpu_custom_call" | custom-call | flops 56000000000 | tf_op jit(solution)/shard_map/time_forward/pallas_call | solution.py:285
  58.7 2.0 collective-permute-start.9
  60.8 2.4 bitcast_multiply_fusion
  64.1 10.9 %collective-permute-done.9.refs_5_.refs_8_.refs_7_ = bf16[96,3072]{1,0:T(8,128)(2,1)S(1)} collective-permute-done((bf16[96,3072]{1,0:T(8,128)(2,1)S(1)}, bf16[96,3072]{1,0:T(8,128)(2,1)S(1)}, u32[]{:S(2)}, u32[]{:S(2)}) %collective-permute-start.9) | collective-permute-done | bytes 589856 | tf_op jit(solution)/shard_map/ppermute | solution.py:773
  75.5 2.9 maximum_bitcast_fusion.1
  78.4 1.8 pad_maximum_fusion.3
  81.5 7.6 %collective-permute-done.5.refs_6_ = bf16[192,6144]{1,0:T(8,128)(2,1)} collective-permute-done((bf16[192,6144]{1,0:T(8,128)(2,1)S(1)}, bf16[192,6144]{1,0:T(8,128)(2,1)}, u32[]{:S(2)}, u32[]{:S(2)}) %collective-permute-start.5) | collective-permute-done | bytes 2359328 | tf_op jit(solution)/shard_map/ppermute | solution.py:773
  89.1 2.8 slice.414
  91.9 2.0 collective-permute-start.12
  93.9 16.8 %space_forward.1 = (bf16[832,768]{1,0:T(8,128)(2,1)}, bf16[832,2304]{1,0:T(8,128)(2,1)}, bf16[48,208,208]{2,1,0:T(8,128)(2,1)}, bf16[832,768]{1,0:T(8,128)(2,1)}, f32[832,768]{1,0:T(8,128)}) custom-call(s32[16]{0:T(128)} %stack.76.refs_0_, f32[832,768]{1,0:T(8,128)} %get-tuple-element.146.refs_1_.refs_2_, ...), custom_call_target="tpu_custom_call" | custom-call | flops 64000000000 | tf_op jit(solution)/shard_map/space_forward/pallas_call | solution.py:285
  111.0 2.9 collective-permute-done.14.refs_9_
  114.9 27.8 %feed_out.1 = (bf16[832,768]{1,0:T(8,128)(2,1)}, bf16[832,768]{1,0:T(8,128)(2,1)}, bf16[832,3072]{1,0:T(8,128)(2,1)}, bf16[8,48,3072]{2,1,0:T(8,128)(2,1)}, bf16[8,48,3072]{2,1,0:T(8,128)(2,1)}) custom-call(s32[16]{0:T(128)} %stack.76.refs_0_, f32[832,768]{1,0:T(8,128)} %get-tuple-element.154.refs_1_.refs_2_, bf16[832,768]{1,0:T(8,128)(2,1)} %bitcast.68, ...), custom_call_target="tpu_custom_call" | custom-call | flops 120000004096 | tf_op jit(solution)/shard_map/feed_out/pallas_call | solution.py:285
  146.3 2.4 copy-done.19
  148.7 7.4 %feed_in.1 = (f32[8,768]{1,0:T(8,128)S(1)}, f32[8,3072]{1,0:T(8,128)S(1)}, bf16[8,48,3072]{2,1,0:T(8,128)(2,1)S(1)}, bf16[8,48,3072]{2,1,0:T(8,128)(2,1)S(1)}) custom-call(s32[16]{0:T(128)S(1)} %copy-done.8, bf16[832,3072]{1,0:T(8,128)(2,1)S(1)} %copy-done.19, bf16[832,768]{1,0:T(8,128)(2,1)S(1)} %copy-done.28, bf16[832,768]{1,0:T(8,128)(2,1)S(1)} %bitcast.69), custom_call_target="tpu_custom_call" | custom-call | flops 32000000000 | tf_op jit(solution)/shard_map/feed_in/pallas_call | solution.py:285
  156.4 3.0 maximum_multiply_fusion
  162.0 1.5 collective-permute-start.16
  164.1 8.9 %feed_norm.1 = (f32[832,768]{1,0:T(8,128)S(1)}, f32[8,768]{1,0:T(8,128)S(1)}) custom-call(s32[16]{0:T(128)S(1)} %copy-done.8, bf16[832,3072]{1,0:T(8,128)(2,1)S(1)} %copy-done.20, f32[832,768]{1,0:T(8,128)S(1)} %copy-done.22, bf16[832,768]{1,0:T(8,128)(2,1)S(1)} %bitcast.70, f32[32,768]{1,0:T(8,128)S(1)} %copy-done.33, bf16[192,6144]{1,0:T(8,128)(2,1)S(1)} %copy-done.1, ...), custom_call_target="tpu_custom_call" | custom-call | flops 40000000000 | tf_op jit(solution)/shard_map/feed_norm/pallas_call | solution.py:285
  175.0 2.6 collective-permute-done.16
  183.4 1.5 collective-permute-start.22
  184.9 20.9 %space_backward.1 = (bf16[832,2304]{1,0:T(8,128)(2,1)S(1)}, f32[8,768]{1,0:T(8,128)S(1)}, bf16[8,48,3072]{2,1,0:T(8,128)(2,1)S(1)}, bf16[8,48,3072]{2,1,0:T(8,128)(2,1)S(1)}) custom-call(s32[16]{0:T(128)S(1)} %copy-done.8, f32[832,768]{1,0:T(8,128)S(1)} %get-tuple-element.177.refs_1_.refs_3_, bf16[832,768]{1,0:T(8,128)(2,1)S(1)} %copy-done.30, ...), custom_call_target="tpu_custom_call" | custom-call | flops 80000000000 | tf_op jit(solution)/shard_map/space_backward/pallas_call | solution.py:285
  205.9 1.7 fusion.5
  210.2 3.5 collective-permute-start.23
  213.7 7.6 %space_norm.1 = (f32[832,768]{1,0:T(8,128)S(1)}, f32[8,768]{1,0:T(8,128)S(1)}) custom-call(s32[16]{0:T(128)S(1)} %copy-done.8, bf16[832,2304]{1,0:T(8,128)(2,1)S(1)} %get-tuple-element.188.refs_1_, f32[832,768]{1,0:T(8,128)S(1)} %copy-done.25, f32[832,768]{1,0:T(8,128)S(1)} %copy-done.24, f32[32,768]{1,0:T(8,128)S(1)} %copy-done.33, ...), custom_call_target="tpu_custom_call" | custom-call | flops 40000000000 | tf_op jit(solution)/shard_map/space_norm/pallas_call | solution.py:285
  221.4 4.9 %collective-permute-done.23 = bf16[96,3072]{1,0:T(8,128)(2,1)S(1)} collective-permute-done((bf16[96,3072]{1,0:T(8,128)(2,1)S(1)}, bf16[96,3072]{1,0:T(8,128)(2,1)S(1)}, u32[]{:S(2)}, u32[]{:S(2)}) %collective-permute-start.23) | collective-permute-done | bytes 589856 | tf_op jit(solution)/shard_map/ppermute | solution.py:863
  228.0 1.5 collective-permute-start.31
  230.2 7.2 %collective-permute-start.28 = (bf16[96,3072]{1,0:T(8,128)(2,1)S(1)}, bf16[96,3072]{1,0:T(8,128)(2,1)S(1)}, u32[]{:S(2)}, u32[]{:S(2)}) collective-permute-start(bf16[96,3072]{1,0:T(8,128)(2,1)S(1)} %pad_maximum_fusion.13), channel_id=1, source_target_pairs={{0,8},{24,16},{1,9},{25,17},{2,10},{26,18},{3,11},{27,19},{4,12},{... | collective-permute-start | bytes 1769480 | tf_op jit(solution)/shard_map/ppermute | solution.py:863
  237.5 12.8 %mixer_backward.1 = (bf16[832,768]{1,0:T(8,128)(2,1)S(1)}, f32[8,768]{1,0:T(8,128)S(1)}, bf16[8,48,1536]{2,1,0:T(8,128)(2,1)S(1)}, bf16[8,48,1536]{2,1,0:T(8,128)(2,1)S(1)}) custom-call(s32[16]{0:T(128)S(1)} %copy-done.8, f32[832,768]{1,0:T(8,128)S(1)} %get-tuple-element.201.refs_1_.refs_6_, bf16[832,768]{1,0:T(8,128)(2,1)S(1)} %copy-done.26, ...), custom_call_target="tpu_custom_call" | custom-call | flops 32000000000 | tf_op jit(solution)/shard_map/mixer_backward/pallas_call | solution.py:285
  251.1 2.2 collective-permute-done.30
  257.6 19.3 %time_backward.1 = (bf16[832,768]{1,0:T(8,128)(2,1)S(1)}, f32[8,768]{1,0:T(8,128)}, bf16[8,48,2432]{2,1,0:T(8,128)(2,1)S(1)}, bf16[8,48,2432]{2,1,0:T(8,128)(2,1)S(1)}) custom-call(s32[16]{0:T(128)S(1)} %copy-done.8, bf16[832,768]{1,0:T(8,128)(2,1)S(1)} %get-tuple-element.213.refs_1_, bf16[832,2304]{1,0:T(8,128)(2,1)} %get-tuple-element.214.refs_2_, ...), custom_call_target="tpu_custom_call" | custom-call | flops 80000000000 | tf_op jit(solution)/shard_map/time_backward/pallas_call | solution.py:285
  279.2 4.4 %collective-permute-start.36 = (bf16[48,3072]{1,0:T(8,128)(2,1)S(1)}, bf16[48,3072]{1,0:T(8,128)(2,1)S(1)}, u32[]{:S(2)}, u32[]{:S(2)}) collective-permute-start(bf16[48,3072]{1,0:T(8,128)(2,1)S(1)} %get-tuple-element.231), channel_id=1, source_target_pairs={{0,8},{1,9},{2,10},{3,11},{4,12},{5,13},{6,14},{7,15},{8,0},{9,1},... | collective-permute-start | bytes 884744 | tf_op jit(solution)/shard_map/ppermute | solution.py:855
  286.7 2.6 maximum_bitcast_fusion
  290.5 1.6 collective-permute-start.39
  292.2 13.9 %collective-permute-done.38 = bf16[1,48,6400]{2,1,0:T(8,128)(2,1)S(1)} collective-permute-done((bf16[1,48,6400]{2,1,0:T(8,128)(2,1)S(1)}, bf16[1,48,6400]{2,1,0:T(8,128)(2,1)S(1)}, u32[]{:S(2)}, u32[]{:S(2)}) %collective-permute-start.38) | collective-permute-done | bytes 614432 | tf_op jit(solution)/shard_map/ppermute | solution.py:773
  306.5 3.7 collective-permute-start.42
  310.4 1.5 collective-permute-start.40
  312.7 4.5 %collective-permute-done.40 = bf16[1,48,2432]{2,1,0:T(8,128)(2,1)S(1)} collective-permute-done((bf16[1,48,2432]{2,1,0:T(8,128)(2,1)S(1)}, bf16[1,48,2432]{2,1,0:T(8,128)(2,1)S(1)}, u32[]{:S(2)}, u32[]{:S(2)}) %collective-permute-start.40) | collective-permute-done | bytes 233504 | tf_op jit(solution)/shard_map/ppermute | solution.py:773
  318.7 4.4 %collective-permute-done.42 = bf16[48,3072]{1,0:T(8,128)(2,1)S(1)} collective-permute-done((bf16[48,3072]{1,0:T(8,128)(2,1)S(1)}, bf16[48,3072]{1,0:T(8,128)(2,1)S(1)}, u32[]{:S(2)}, u32[]{:S(2)}) %collective-permute-start.42) | collective-permute-done | bytes 294944 | tf_op jit(solution)/shard_map/ppermute | solution.py:859
  323.3 2.0 collective-permute-start.44
  326.4 12.9 %collective-permute-done.44 = bf16[48,3968]{1,0:T(8,128)(2,1)S(1)} collective-permute-done((bf16[48,3968]{1,0:T(8,128)(2,1)S(1)}, bf16[48,3968]{1,0:T(8,128)(2,1)S(1)}, u32[]{:S(2)}, u32[]{:S(2)}) %collective-permute-start.44) | collective-permute-done | bytes 380960 | tf_op jit(solution)/shard_map/ppermute | solution.py:855
  339.5 17.7 %collective-permute-done.46 = bf16[48,3968]{1,0:T(8,128)(2,1)S(1)} collective-permute-done((bf16[48,3968]{1,0:T(8,128)(2,1)S(1)}, bf16[48,3968]{1,0:T(8,128)(2,1)S(1)}, u32[]{:S(2)}, u32[]{:S(2)}) %collective-permute-start.46) | collective-permute-done | bytes 380960 | tf_op jit(solution)/shard_map/ppermute | solution.py:859
  359.2 8.9 %collective-permute-done.47 = bf16[48,3968]{1,0:T(8,128)(2,1)S(1)} collective-permute-done((bf16[48,3968]{1,0:T(8,128)(2,1)S(1)}, bf16[48,3968]{1,0:T(8,128)(2,1)S(1)}, u32[]{:S(2)}, u32[]{:S(2)}) %collective-permute-start.47) | collective-permute-done | bytes 380960 | tf_op jit(solution)/shard_map/ppermute | solution.py:855
  (261 shorter events, 56.0 us)
Async XLA Ops:
  3.4 2.4 collective-permute-start
  6.0 10.5 %collective-permute-start.2 = (bf16[96,3072]{1,0:T(8,128)(2,1)S(1)}, bf16[96,3072]{1,0:T(8,128)(2,1)S(1)}, u32[]{:S(2)}, u32[]{:S(2)}) collective-permute-start(bf16[96,3072]{1,0:T(8,128)(2,1)S(1)} %pad_maximum_fusion.11), channel_id=1, source_target_pairs={{0,1},{1,0},{2,3},{3,2},{4,5},{5,4},{6,7},{7,6},{8,9},{9,8},{10,11... | collective-permute-start | bytes 1769480 | tf_op jit(solution)/shard_map/ppermute | solution.py:773
  6.4 10.2 %collective-permute-start.3 = (bf16[96,6144]{1,0:T(8,128)(2,1)S(1)}, bf16[96,6144]{1,0:T(8,128)(2,1)S(1)}, u32[]{:S(2)}, u32[]{:S(2)}) collective-permute-start(bf16[96,6144]{1,0:T(8,128)(2,1)S(1)} %slice_dynamic-update-slice_fusion), channel_id=1, source_target_pairs={{0,1},{1,0},{2,3},{3,2},{4,5},{5,4},{6,7},{7,6},{8,9},{9,8},{10,11... | collective-permute-start | bytes 3538952 | tf_op jit(solution)/shard_map/ppermute | solution.py:773
  6.6 20.8 %collective-permute-start.1 = (bf16[192,3968]{1,0:T(8,128)(2,1)S(1)}, bf16[192,3968]{1,0:T(8,128)(2,1)}, u32[]{:S(2)}, u32[]{:S(2)}) collective-permute-start(bf16[192,3968]{1,0:T(8,128)(2,1)S(1)} %pad_maximum_fusion.1.refs_2_.refs_4_.refs_12_), channel_id=1, source_target_pairs={{0,2},{1,5},{2,0},{3,7},{4,6},{5,1},{6,4},{7,3},{8,10},{9,13},{10,... | collective-permute-start | bytes 4571144 | tf_op jit(solution)/shard_map/ppermute | solution.py:773
  28.6 11.9 %collective-permute-start.4 = (bf16[96,3968]{1,0:T(8,128)(2,1)S(1)}, bf16[96,3968]{1,0:T(8,128)(2,1)}, u32[]{:S(2)}, u32[]{:S(2)}) collective-permute-start(bf16[96,3968]{1,0:T(8,128)(2,1)S(1)} %slice.409), channel_id=1, source_target_pairs={{0,4},{1,3},{2,6},{3,1},{4,0},{5,7},{6,2},{7,5},{8,12},{9,11},{10,... | collective-permute-start | bytes 2285576 | tf_op jit(solution)/shard_map/ppermute | solution.py:773
  30.7 12.5 %collective-permute-start.7 = (bf16[192,3968]{1,0:T(8,128)(2,1)}, bf16[192,3968]{1,0:T(8,128)(2,1)}, u32[]{:S(2)}, u32[]{:S(2)}) collective-permute-start(bf16[192,3968]{1,0:T(8,128)(2,1)} %collective-permute-done.1.refs_3_.refs_5_.refs_13_), channel_id=1, source_target_pairs={{0,1},{1,0},{2,3},{3,2},{4,5},{5,4},{6,7},{7,6},{8,9},{9,8},{10,11... | collective-permute-start | bytes 4571144 | tf_op jit(solution)/shard_map/ppermute | solution.py:773
  40.5 2.7 collective-permute-start.8
  41.2 16.3 %collective-permute-start.6 = (bf16[192,3072]{1,0:T(8,128)(2,1)S(1)}, bf16[192,3072]{1,0:T(8,128)(2,1)}, u32[]{:S(2)}, u32[]{:S(2)}) collective-permute-start(bf16[192,3072]{1,0:T(8,128)(2,1)S(1)} %pad_maximum_fusion.4.refs_3_.refs_6_.refs_5_), channel_id=1, source_target_pairs={{0,2},{1,5},{2,0},{3,7},{4,6},{5,1},{6,4},{7,3},{8,10},{9,13},{10,... | collective-permute-start | bytes 3538952 | tf_op jit(solution)/shard_map/ppermute | solution.py:773
  43.2 45.9 %collective-permute-start.5 = (bf16[192,6144]{1,0:T(8,128)(2,1)S(1)}, bf16[192,6144]{1,0:T(8,128)(2,1)}, u32[]{:S(2)}, u32[]{:S(2)}) collective-permute-start(bf16[192,6144]{1,0:T(8,128)(2,1)S(1)} %pad_maximum_fusion.refs_5_), channel_id=1, source_target_pairs={{0,2},{1,5},{2,0},{3,7},{4,6},{5,1},{6,4},{7,3},{8,10},{9,13},{10,... | collective-permute-start | bytes 7077896 | tf_op jit(solution)/shard_map/ppermute | solution.py:773
  58.6 30.5 %collective-permute-start.10 = (bf16[192,3072]{1,0:T(8,128)(2,1)}, bf16[192,3072]{1,0:T(8,128)(2,1)S(1)}, u32[]{:S(2)}, u32[]{:S(2)}) collective-permute-start(bf16[192,3072]{1,0:T(8,128)(2,1)} %collective-permute-done.6.refs_4_.refs_7_.refs_6_), channel_id=1, source_target_pairs={{0,1},{1,0},{2,3},{3,2},{4,5},{5,4},{6,7},{7,6},{8,9},{9,8},{10,11... | collective-permute-start | bytes 3538952 | tf_op jit(solution)/shard_map/ppermute | solution.py:773
  58.7 16.3 %collective-permute-start.9 = (bf16[96,3072]{1,0:T(8,128)(2,1)S(1)}, bf16[96,3072]{1,0:T(8,128)(2,1)S(1)}, u32[]{:S(2)}, u32[]{:S(2)}) collective-permute-start(bf16[96,3072]{1,0:T(8,128)(2,1)S(1)} %slice.410), channel_id=1, source_target_pairs={{0,4},{1,3},{2,6},{3,1},{4,0},{5,7},{6,2},{7,5},{8,12},{9,11},{10,... | collective-permute-start | bytes 1769480 | tf_op jit(solution)/shard_map/ppermute | solution.py:773
  75.4 6.1 %collective-permute-start.11 = (bf16[96,3072]{1,0:T(8,128)(2,1)S(1)}, bf16[96,3072]{1,0:T(8,128)(2,1)S(1)}, u32[]{:S(2)}, u32[]{:S(2)}) collective-permute-start(bf16[96,3072]{1,0:T(8,128)(2,1)S(1)} %collective-permute-done.9.refs_5_.refs_8_.refs_7_), channel_id=1, source_target_pairs={{0,1},{1,0},{2,3},{3,2},{4,5},{5,4},{6,7},{7,6},{8,9},{9,8},{10,11... | collective-permute-start | bytes 1769480 | tf_op jit(solution)/shard_map/ppermute | solution.py:773
  91.9 19.1 %collective-permute-start.13 = (bf16[192,6144]{1,0:T(8,128)(2,1)}, bf16[192,6144]{1,0:T(8,128)(2,1)S(1)}, u32[]{:S(2)}, u32[]{:S(2)}) collective-permute-start(bf16[192,6144]{1,0:T(8,128)(2,1)} %collective-permute-done.5.refs_6_), channel_id=1, source_target_pairs={{0,1},{1,0},{2,3},{3,2},{4,5},{5,4},{6,7},{7,6},{8,9},{9,8},{10,11... | collective-permute-start | bytes 7077896 | tf_op jit(solution)/shard_map/ppermute | solution.py:773
  91.9 18.9 %collective-permute-start.12 = (bf16[96,6144]{1,0:T(8,128)(2,1)}, bf16[96,6144]{1,0:T(8,128)(2,1)}, u32[]{:S(2)}, u32[]{:S(2)}) collective-permute-start(bf16[96,6144]{1,0:T(8,128)(2,1)} %slice.414), channel_id=1, source_target_pairs={{0,4},{1,3},{2,6},{3,1},{4,0},{5,7},{6,2},{7,5},{8,12},{9,11},{10,... | collective-permute-start | bytes 3538952 | tf_op jit(solution)/shard_map/ppermute | solution.py:773
  110.7 3.1 collective-permute-start.14
  145.9 13.6 %collective-permute-start.15 = (bf16[8,48,3072]{2,1,0:T(8,128)(2,1)}, bf16[8,48,3072]{2,1,0:T(8,128)(2,1)S(1)}, u32[]{:S(2)}, u32[]{:S(2)}) collective-permute-start(bf16[8,48,3072]{2,1,0:T(8,128)(2,1)} %get-tuple-element.160), channel_id=1, source_target_pairs={{0,1},{1,0},{2,3},{3,2},{4,5},{5,4},{6,7},{7,6},{8,9},{9,8},{10,11... | collective-permute-start | bytes 7077896 | tf_op jit(solution)/shard_map/ppermute | solution.py:773
  156.2 16.9 %collective-permute-start.18 = (bf16[8,48,3072]{2,1,0:T(8,128)(2,1)S(1)}, bf16[8,48,3072]{2,1,0:T(8,128)(2,1)S(1)}, u32[]{:S(2)}, u32[]{:S(2)}) collective-permute-start(bf16[8,48,3072]{2,1,0:T(8,128)(2,1)S(1)} %get-tuple-element.169), channel_id=1, source_target_pairs={{0,1},{1,0},{2,3},{3,2},{4,5},{5,4},{6,7},{7,6},{8,9},{9,8},{10,11... | collective-permute-start | bytes 7077896 | tf_op jit(solution)/shard_map/ppermute | solution.py:773
  162.0 15.5 %collective-permute-start.16 = (bf16[2,48,3072]{2,1,0:T(8,128)(2,1)S(1)}, bf16[2,48,3072]{2,1,0:T(8,128)(2,1)S(1)}, u32[]{:S(2)}, u32[]{:S(2)}) collective-permute-start(bf16[2,48,3072]{2,1,0:T(8,128)(2,1)S(1)} %get-tuple-element.166), channel_id=1, source_target_pairs={{0,2},{1,3},{2,0},{3,1},{4,6},{5,7},{6,4},{7,5},{8,10},{9,11},{10,... | collective-permute-start | bytes 1769480 | tf_op jit(solution)/shard_map/ppermute | solution.py:773
  163.5 15.3 %collective-permute-start.17 = (bf16[2,48,3072]{2,1,0:T(8,128)(2,1)S(1)}, bf16[2,48,3072]{2,1,0:T(8,128)(2,1)S(1)}, u32[]{:S(2)}, u32[]{:S(2)}) collective-permute-start(bf16[2,48,3072]{2,1,0:T(8,128)(2,1)S(1)} %get-tuple-element.167), channel_id=1, source_target_pairs={{0,4},{1,5},{2,6},{3,7},{4,0},{5,1},{6,2},{7,3},{8,12},{9,13},{10,... | collective-permute-start | bytes 1769480 | tf_op jit(solution)/shard_map/ppermute | solution.py:773
  180.8 25.1 %collective-permute-start.19 = (bf16[1,48,3072]{2,1,0:T(8,128)(2,1)S(1)}, bf16[1,48,3072]{2,1,0:T(8,128)(2,1)S(1)}, u32[]{:S(2)}, u32[]{:S(2)}) collective-permute-start(bf16[1,48,3072]{2,1,0:T(8,128)(2,1)S(1)} %get-tuple-element.173), channel_id=1, source_target_pairs={{0,4},{1,5},{2,6},{3,7},{4,0},{5,1},{6,2},{7,3},{8,12},{9,13},{10,... | collective-permute-start | bytes 884744 | tf_op jit(solution)/shard_map/ppermute | solution.py:773
  181.3 24.6 %collective-permute-start.20 = (bf16[1,48,3072]{2,1,0:T(8,128)(2,1)S(1)}, bf16[1,48,3072]{2,1,0:T(8,128)(2,1)S(1)}, u32[]{:S(2)}, u32[]{:S(2)}) collective-permute-start(bf16[1,48,3072]{2,1,0:T(8,128)(2,1)S(1)} %get-tuple-element.174), channel_id=1, source_target_pairs={{0,2},{1,3},{2,0},{3,1},{4,6},{5,7},{6,4},{7,5},{8,10},{9,11},{10,... | collective-permute-start | bytes 884744 | tf_op jit(solution)/shard_map/ppermute | solution.py:773
  182.8 24.9 %collective-permute-start.21 = (bf16[2,48,3072]{2,1,0:T(8,128)(2,1)S(1)}, bf16[2,48,3072]{2,1,0:T(8,128)(2,1)S(1)}, u32[]{:S(2)}, u32[]{:S(2)}) collective-permute-start(bf16[2,48,3072]{2,1,0:T(8,128)(2,1)S(1)} %get-tuple-element.175), channel_id=1, source_target_pairs={{0,4},{1,5},{2,6},{3,7},{4,0},{5,1},{6,2},{7,3},{8,12},{9,13},{10,... | collective-permute-start | bytes 1769480 | tf_op jit(solution)/shard_map/ppermute | solution.py:773
  183.4 24.3 %collective-permute-start.22 = (bf16[2,48,3072]{2,1,0:T(8,128)(2,1)S(1)}, bf16[2,48,3072]{2,1,0:T(8,128)(2,1)S(1)}, u32[]{:S(2)}, u32[]{:S(2)}) collective-permute-start(bf16[2,48,3072]{2,1,0:T(8,128)(2,1)S(1)} %get-tuple-element.176), channel_id=1, source_target_pairs={{0,2},{1,3},{2,0},{3,1},{4,6},{5,7},{6,4},{7,5},{8,10},{9,11},{10,... | collective-permute-start | bytes 1769480 | tf_op jit(solution)/shard_map/ppermute | solution.py:773
  205.8 21.1 %collective-permute-start.26 = (bf16[8,48,3072]{2,1,0:T(8,128)(2,1)S(1)}, bf16[8,48,3072]{2,1,0:T(8,128)(2,1)S(1)}, u32[]{:S(2)}, u32[]{:S(2)}) collective-permute-start(bf16[8,48,3072]{2,1,0:T(8,128)(2,1)S(1)} %get-tuple-element.195), channel_id=1, source_target_pairs={{0,1},{1,0},{2,3},{3,2},{4,5},{5,4},{6,7},{7,6},{8,9},{9,8},{10,11... | collective-permute-start | bytes 7077896 | tf_op jit(solution)/shard_map/ppermute | solution.py:773
  208.2 13.2 %collective-permute-start.24 = (bf16[1,48,3072]{2,1,0:T(8,128)(2,1)S(1)}, bf16[1,48,3072]{2,1,0:T(8,128)(2,1)S(1)}, u32[]{:S(2)}, u32[]{:S(2)}) collective-permute-start(bf16[1,48,3072]{2,1,0:T(8,128)(2,1)S(1)} %get-tuple-element.186), channel_id=1, source_target_pairs={{0,2},{1,3},{2,0},{3,1},{4,6},{5,7},{6,4},{7,5},{8,10},{9,11},{10,... | collective-permute-start | bytes 884744 | tf_op jit(solution)/shard_map/ppermute | solution.py:773
  208.8 12.6 %collective-permute-start.25 = (bf16[1,48,3072]{2,1,0:T(8,128)(2,1)S(1)}, bf16[1,48,3072]{2,1,0:T(8,128)(2,1)S(1)}, u32[]{:S(2)}, u32[]{:S(2)}) collective-permute-start(bf16[1,48,3072]{2,1,0:T(8,128)(2,1)S(1)} %get-tuple-element.187), channel_id=1, source_target_pairs={{0,4},{1,5},{2,6},{3,7},{4,0},{5,1},{6,2},{7,3},{8,12},{9,13},{10,... | collective-permute-start | bytes 884744 | tf_op jit(solution)/shard_map/ppermute | solution.py:773
  210.2 16.1 %collective-permute-start.23 = (bf16[96,3072]{1,0:T(8,128)(2,1)S(1)}, bf16[96,3072]{1,0:T(8,128)(2,1)S(1)}, u32[]{:S(2)}, u32[]{:S(2)}) collective-permute-start(bf16[96,3072]{1,0:T(8,128)(2,1)S(1)} %pad_maximum_fusion.12), channel_id=1, source_target_pairs={{0,8},{24,16},{1,9},{25,17},{2,10},{26,18},{3,11},{27,19},{4,12},{... | collective-permute-start | bytes 1769480 | tf_op jit(solution)/shard_map/ppermute | solution.py:863
  227.3 23.5 %collective-permute-start.29 = (bf16[2,48,3072]{2,1,0:T(8,128)(2,1)S(1)}, bf16[2,48,3072]{2,1,0:T(8,128)(2,1)S(1)}, u32[]{:S(2)}, u32[]{:S(2)}) collective-permute-start(bf16[2,48,3072]{2,1,0:T(8,128)(2,1)S(1)} %get-tuple-element.200), channel_id=1, source_target_pairs={{0,4},{1,5},{2,6},{3,7},{4,0},{5,1},{6,2},{7,3},{8,12},{9,13},{10,... | collective-permute-start | bytes 1769480 | tf_op jit(solution)/shard_map/ppermute | solution.py:773
  228.0 22.8 %collective-permute-start.31 = (bf16[2,48,3072]{2,1,0:T(8,128)(2,1)S(1)}, bf16[2,48,3072]{2,1,0:T(8,128)(2,1)S(1)}, u32[]{:S(2)}, u32[]{:S(2)}) collective-permute-start(bf16[2,48,3072]{2,1,0:T(8,128)(2,1)S(1)} %get-tuple-element.206), channel_id=1, source_target_pairs={{0,2},{1,3},{2,0},{3,1},{4,6},{5,7},{6,4},{7,5},{8,10},{9,11},{10,... | collective-permute-start | bytes 1769480 | tf_op jit(solution)/shard_map/ppermute | solution.py:773
  229.5 21.0 %collective-permute-start.27 = (bf16[96,3072]{1,0:T(8,128)(2,1)S(1)}, bf16[96,3072]{1,0:T(8,128)(2,1)S(1)}, u32[]{:S(2)}, u32[]{:S(2)}) collective-permute-start(bf16[96,3072]{1,0:T(8,128)(2,1)S(1)} %add_convert_fusion.5), channel_id=1, source_target_pairs={{8,16},{16,8},{9,17},{17,9},{10,18},{18,10},{11,19},{19,11},{12,20... | collective-permute-start | bytes 1769480 | tf_op jit(solution)/shard_map/ppermute | solution.py:867
  230.2 20.4 %collective-permute-start.28 = (bf16[96,3072]{1,0:T(8,128)(2,1)S(1)}, bf16[96,3072]{1,0:T(8,128)(2,1)S(1)}, u32[]{:S(2)}, u32[]{:S(2)}) collective-permute-start(bf16[96,3072]{1,0:T(8,128)(2,1)S(1)} %pad_maximum_fusion.13), channel_id=1, source_target_pairs={{0,8},{24,16},{1,9},{25,17},{2,10},{26,18},{3,11},{27,19},{4,12},{... | collective-permute-start | bytes 1769480 | tf_op jit(solution)/shard_map/ppermute | solution.py:863
  250.3 2.9 collective-permute-start.30
  253.6 23.4 %collective-permute-start.32 = (bf16[1,48,6144]{2,1,0:T(8,128)(2,1)S(1)}, bf16[1,48,6144]{2,1,0:T(8,128)(2,1)S(1)}, u32[]{:S(2)}, u32[]{:S(2)}) collective-permute-start(bf16[1,48,6144]{2,1,0:T(8,128)(2,1)S(1)} %pad_maximum_fusion.14), channel_id=1, source_target_pairs={{0,2},{1,3},{2,0},{3,1},{4,6},{5,7},{6,4},{7,5},{8,10},{9,11},{10,... | collective-permute-start | bytes 1769480 | tf_op jit(solution)/shard_map/ppermute | solution.py:773
  254.2 22.8 %collective-permute-start.33 = (bf16[1,48,6144]{2,1,0:T(8,128)(2,1)S(1)}, bf16[1,48,6144]{2,1,0:T(8,128)(2,1)S(1)}, u32[]{:S(2)}, u32[]{:S(2)}) collective-permute-start(bf16[1,48,6144]{2,1,0:T(8,128)(2,1)S(1)} %pad_maximum_fusion.15), channel_id=1, source_target_pairs={{0,4},{1,5},{2,6},{3,7},{4,0},{5,1},{6,2},{7,3},{8,12},{9,13},{10,... | collective-permute-start | bytes 1769480 | tf_op jit(solution)/shard_map/ppermute | solution.py:773
  255.6 21.4 %collective-permute-start.34 = (bf16[96,3072]{1,0:T(8,128)(2,1)S(1)}, bf16[96,3072]{1,0:T(8,128)(2,1)S(1)}, u32[]{:S(2)}, u32[]{:S(2)}) collective-permute-start(bf16[96,3072]{1,0:T(8,128)(2,1)S(1)} %add_convert_fusion.2), channel_id=1, source_target_pairs={{8,0},{16,24},{9,1},{17,25},{10,2},{18,26},{11,3},{19,27},{12,4},{... | collective-permute-start | bytes 1769480 | tf_op jit(solution)/shard_map/ppermute | solution.py:871
  256.8 20.1 %collective-permute-start.35 = (bf16[96,3072]{1,0:T(8,128)(2,1)S(1)}, bf16[96,3072]{1,0:T(8,128)(2,1)S(1)}, u32[]{:S(2)}, u32[]{:S(2)}) collective-permute-start(bf16[96,3072]{1,0:T(8,128)(2,1)S(1)} %add_convert_fusion.1), channel_id=1, source_target_pairs={{8,16},{16,8},{9,17},{17,9},{10,18},{18,10},{11,19},{19,11},{12,20... | collective-permute-start | bytes 1769480 | tf_op jit(solution)/shard_map/ppermute | solution.py:867
  279.2 12.9 %collective-permute-start.36 = (bf16[48,3072]{1,0:T(8,128)(2,1)S(1)}, bf16[48,3072]{1,0:T(8,128)(2,1)S(1)}, u32[]{:S(2)}, u32[]{:S(2)}) collective-permute-start(bf16[48,3072]{1,0:T(8,128)(2,1)S(1)} %get-tuple-element.231), channel_id=1, source_target_pairs={{0,8},{1,9},{2,10},{3,11},{4,12},{5,13},{6,14},{7,15},{8,0},{9,1},... | collective-permute-start | bytes 884744 | tf_op jit(solution)/shard_map/ppermute | solution.py:855
  283.6 35.2 %collective-permute-start.43 = (bf16[96,3072]{1,0:T(8,128)(2,1)S(1)}, bf16[96,3072]{1,0:T(8,128)(2,1)S(1)}, u32[]{:S(2)}, u32[]{:S(2)}) collective-permute-start(bf16[96,3072]{1,0:T(8,128)(2,1)S(1)} %add_convert_fusion), channel_id=1, source_target_pairs={{8,0},{16,24},{9,1},{17,25},{10,2},{18,26},{11,3},{19,27},{12,4},{... | collective-permute-start | bytes 1769480 | tf_op jit(solution)/shard_map/ppermute | solution.py:871
  285.3 4.1 %collective-permute-start.37 = (bf16[8,48,2432]{2,1,0:T(8,128)(2,1)S(1)}, bf16[8,48,2432]{2,1,0:T(8,128)(2,1)S(1)}, u32[]{:S(2)}, u32[]{:S(2)}) collective-permute-start(bf16[8,48,2432]{2,1,0:T(8,128)(2,1)S(1)} %get-tuple-element.233), channel_id=1, source_target_pairs={{0,1},{1,0},{2,3},{3,2},{4,5},{5,4},{6,7},{7,6},{8,9},{9,8},{10,11... | collective-permute-start | bytes 5603336 | tf_op jit(solution)/shard_map/ppermute | solution.py:773
  289.8 16.3 %collective-permute-start.38 = (bf16[1,48,6400]{2,1,0:T(8,128)(2,1)S(1)}, bf16[1,48,6400]{2,1,0:T(8,128)(2,1)S(1)}, u32[]{:S(2)}, u32[]{:S(2)}) collective-permute-start(bf16[1,48,6400]{2,1,0:T(8,128)(2,1)S(1)} %pad_maximum_fusion.9), channel_id=1, source_target_pairs={{0,2},{1,3},{2,0},{3,1},{4,6},{5,7},{6,4},{7,5},{8,10},{9,11},{10,... | collective-permute-start | bytes 1843208 | tf_op jit(solution)/shard_map/ppermute | solution.py:773
  290.5 16.0 %collective-permute-start.39 = (bf16[1,48,6400]{2,1,0:T(8,128)(2,1)S(1)}, bf16[1,48,6400]{2,1,0:T(8,128)(2,1)S(1)}, u32[]{:S(2)}, u32[]{:S(2)}) collective-permute-start(bf16[1,48,6400]{2,1,0:T(8,128)(2,1)S(1)} %pad_maximum_fusion.10), channel_id=1, source_target_pairs={{0,4},{1,5},{2,6},{3,7},{4,0},{5,1},{6,2},{7,3},{8,12},{9,13},{10,... | collective-permute-start | bytes 1843208 | tf_op jit(solution)/shard_map/ppermute | solution.py:773
  306.5 16.6 %collective-permute-start.42 = (bf16[48,3072]{1,0:T(8,128)(2,1)S(1)}, bf16[48,3072]{1,0:T(8,128)(2,1)S(1)}, u32[]{:S(2)}, u32[]{:S(2)}) collective-permute-start(bf16[48,3072]{1,0:T(8,128)(2,1)S(1)} %fusion.4), channel_id=1, source_target_pairs={{0,16},{8,24},{16,0},{24,8},{1,17},{9,25},{17,1},{25,9},{2,18},{10... | collective-permute-start | bytes 884744 | tf_op jit(solution)/shard_map/ppermute | solution.py:859
  310.4 6.8 %collective-permute-start.40 = (bf16[1,48,2432]{2,1,0:T(8,128)(2,1)S(1)}, bf16[1,48,2432]{2,1,0:T(8,128)(2,1)S(1)}, u32[]{:S(2)}, u32[]{:S(2)}) collective-permute-start(bf16[1,48,2432]{2,1,0:T(8,128)(2,1)S(1)} %get-tuple-element.236), channel_id=1, source_target_pairs={{0,2},{1,3},{2,0},{3,1},{4,6},{5,7},{6,4},{7,5},{8,10},{9,11},{10,... | collective-permute-start | bytes 700424 | tf_op jit(solution)/shard_map/ppermute | solution.py:773
  311.9 6.4 %collective-permute-start.41 = (bf16[1,48,2432]{2,1,0:T(8,128)(2,1)S(1)}, bf16[1,48,2432]{2,1,0:T(8,128)(2,1)S(1)}, u32[]{:S(2)}, u32[]{:S(2)}) collective-permute-start(bf16[1,48,2432]{2,1,0:T(8,128)(2,1)S(1)} %get-tuple-element.237), channel_id=1, source_target_pairs={{0,4},{1,5},{2,6},{3,7},{4,0},{5,1},{6,2},{7,3},{8,12},{9,13},{10,... | collective-permute-start | bytes 700424 | tf_op jit(solution)/shard_map/ppermute | solution.py:773
  323.2 16.2 %collective-permute-start.45 = (bf16[48,3072]{1,0:T(8,128)(2,1)S(1)}, bf16[48,3072]{1,0:T(8,128)(2,1)S(1)}, u32[]{:S(2)}, u32[]{:S(2)}) collective-permute-start(bf16[48,3072]{1,0:T(8,128)(2,1)S(1)} %add_convert_fusion.14), channel_id=1, source_target_pairs={{0,8},{1,9},{2,10},{3,11},{4,12},{5,13},{6,14},{7,15},{8,0},{9,1},... | collective-permute-start | bytes 884744 | tf_op jit(solution)/shard_map/ppermute | solution.py:855
  323.3 16.0 %collective-permute-start.44 = (bf16[48,3968]{1,0:T(8,128)(2,1)S(1)}, bf16[48,3968]{1,0:T(8,128)(2,1)S(1)}, u32[]{:S(2)}, u32[]{:S(2)}) collective-permute-start(bf16[48,3968]{1,0:T(8,128)(2,1)S(1)} %get-tuple-element.241), channel_id=1, source_target_pairs={{0,8},{1,9},{2,10},{3,11},{4,12},{5,13},{6,14},{7,15},{8,0},{9,1},... | collective-permute-start | bytes 1142792 | tf_op jit(solution)/shard_map/ppermute | solution.py:855
  339.3 17.9 %collective-permute-start.46 = (bf16[48,3968]{1,0:T(8,128)(2,1)S(1)}, bf16[48,3968]{1,0:T(8,128)(2,1)S(1)}, u32[]{:S(2)}, u32[]{:S(2)}) collective-permute-start(bf16[48,3968]{1,0:T(8,128)(2,1)S(1)} %add_convert_fusion.13), channel_id=1, source_target_pairs={{0,16},{8,24},{16,0},{24,8},{1,17},{9,25},{17,1},{25,9},{2,18},{10... | collective-permute-start | bytes 1142792 | tf_op jit(solution)/shard_map/ppermute | solution.py:859
  357.3 10.8 %collective-permute-start.47 = (bf16[48,3968]{1,0:T(8,128)(2,1)S(1)}, bf16[48,3968]{1,0:T(8,128)(2,1)S(1)}, u32[]{:S(2)}, u32[]{:S(2)}) collective-permute-start(bf16[48,3968]{1,0:T(8,128)(2,1)S(1)} %add_convert_fusion.12), channel_id=1, source_target_pairs={{0,8},{1,9},{2,10},{3,11},{4,12},{5,13},{6,14},{7,15},{8,0},{9,1},... | collective-permute-start | bytes 1142792 | tf_op jit(solution)/shard_map/ppermute | solution.py:855
  (53 other events, 453.0 us)

commit v5 on v4

--- a/solution.py
+++ b/solution.py
@@ -844,6 +844,13 @@
     return [value[..., stop - width : stop] for stop, width in zip(stops, widths)]
 
 
+def hand_over(arrived, ahead, behind):
+    widths = (ahead.keep.shape[2], behind.keep.shape[2], behind.keep.shape[2])
+    ahead.last_x, *from_x = apart(arrived[0], widths)
+    ahead.last_y, *from_y = apart(arrived[1], widths)
+    behind.from_x, behind.from_y = jnp.concatenate(from_x, axis=0), jnp.concatenate(from_y, axis=0)
+
+
 def tie(*values):
     leaves, shape = jax.tree.flatten(values)
     return jax.tree.unflatten(shape, lax.optimization_barrier(tuple(leaves)))
@@ -859,16 +866,13 @@
     return lax.ppermute(value, "grp", [(z, z ^ 2) for z in range(4)])
 
 
-def inward(value):
-    return lax.ppermute(value, "grp", [(0, 1), (3, 2)])
-
-
-def across(value):
-    return lax.ppermute(value, "grp", [(1, 2), (2, 1)])
-
-
-def outward(value):
-    return lax.ppermute(value, "grp", [(1, 0), (2, 3)])
+def split_groups(halves, even):
+    low, high = halves
+    return jnp.where(even, low, high), jnp.where(even, high, low)
+
+
+def join_groups(held, other, even):
+    return jnp.concatenate([jnp.where(even, held, other), jnp.where(even, other, held)], axis=0)
 
 
 def local(video, cotangent, live, time_entry, time_exit, time_mixer, space_entry, space_exit, hidden_expand, hidden_reduce, bias_rows, hidden_bias, norm_gain, norm_shift):
@@ -934,69 +938,68 @@
         sum_r.cross(sent_r)
     gz, norm_f = net.norm_backward(13, gh, z, g, small, wf if pieced else wf[:1], "feed_norm")
     if pieced:
-        sent_r, sent_e, gz, norm_f = tie(sum_r.second(), sum_e.first(), gz, norm_f)
-        sum_r.cross_again(sent_r)
-        sum_e.cross(sent_e)
+        sent = [beside(last, both) for last, both in zip(sum_r.second(), sum_e.first())]
+        sent, gz, norm_f = tie(sent, gz, norm_f)
+        arrived = (along_x(sent[0]), along_y(sent[1]))
     gqkv, sums_s, *grad_s = net.space_backward(gz, normed_s, qkv_s, p_s, o_s, ws)
     if pieced:
         sum_s = Reduction(*grad_s)
-        kept_r, sent_e, gqkv, sums_s, sum_s.keep = tie(jnp.concatenate(sum_r.finish(), axis=0), sum_e.second(), gqkv, sums_s, sum_s.keep)
+        hand_over(arrived, sum_r, sum_e)
+        even = lax.axis_index("grp") % 2 == 0
+        held_r, sent_r = split_groups(sum_r.finish(), even)
+        held_r, sent_r, sent_e, gqkv, sums_s, sum_s.keep = tie(held_r, sent_r, sum_e.second(), gqkv, sums_s, sum_s.keep)
         sum_e.cross_again(sent_e)
-        got_r = inward(kept_r)
+        got_r = swap_z(sent_r)
     gy, norm_s = net.norm_backward(12, gqkv, y, gz, small, ws, "space_norm")
     if pieced:
         got_r, sum_e.last_x, sum_e.last_y, gy, norm_s = tie(got_r, sum_e.last_x, sum_e.last_y, gy, norm_s)
-        kept_e = jnp.concatenate(sum_e.finish(), axis=0)
-        kept_r, kept_e, sent_s, gy, norm_s = tie(total(kept_r, got_r), kept_e, sum_s.first(), gy, norm_s)
+        held_e, sent_e = split_groups(sum_e.finish(), even)
+        held_r, held_e, sent_e, sent_s, gy, norm_s = tie(total(held_r, got_r), held_e, sent_e, sum_s.first(), gy, norm_s)
         sum_s.cross(sent_s)
-        got_r, got_e = across(kept_r), inward(kept_e)
+        got_r, got_e = across_pairs(held_r), swap_z(sent_e)
         sums_s = jnp.concatenate([sums_s[0:3], norm_s[0:2], sums_s[5:]], axis=0)
         sums_f = jnp.concatenate([sums_f[0:1], norm_f[0:2], sums_f[3:]], axis=0)
     others = (sums_s, sums_f, ghb) if pieced else ()
     go, sums_m, *grad_m = net.mixer_backward(gy, o_t, e_t, wt)
     if pieced:
         sum_m = Reduction(*grad_m)
+        arrived = (got_r, got_e, sum_s.from_x, sum_s.from_y)
+        arrived, go, sums_m, sum_m.keep = tie(arrived, go, sums_m, sum_m.keep)
+        got_r, got_e, sum_s.from_x, sum_s.from_y = arrived
         sent = [beside(last, both) for last, both in zip(sum_s.second(), sum_m.first())]
-        kept_r, kept_e, sent, go, sums_m, sum_m.keep = tie(total(kept_r, got_r), total(kept_e, got_e), sent, go, sums_m, sum_m.keep)
-        arrived = (along_x(sent[0]), along_y(sent[1]), outward(kept_r), across(kept_e))
+        held_r, held_e, sent, go = tie(total(held_r, got_r), total(held_e, got_e), sent, go)
+        arrived = (along_x(sent[0]), along_y(sent[1]), swap_z(held_r), across_pairs(held_e))
     gx, sums_t, *grad_t = net.time_backward(go, qkv_t, p_t, normed_t, x, gy, small, sums_m, others, wt)
 
     if pieced:
-        group = lax.axis_index("grp")
-        even = group % 2 == 0
-        inner = (group == 1) | (group == 2)
-        (came_x, came_y, got_r, got_e), grad_t, gx, sums_t = tie(arrived, grad_t, gx, sums_t)
-        widths = (sum_s.keep.shape[2], sum_m.keep.shape[2], sum_m.keep.shape[2])
-        sum_s.last_x, *from_x = apart(came_x, widths)
-        sum_s.last_y, *from_y = apart(came_y, widths)
-        sum_m.from_x, sum_m.from_y = jnp.concatenate(from_x, axis=0), jnp.concatenate(from_y, axis=0)
+        (came_x, came_y, got_r, got_e), grad_t, gx, sums_t, out = tie(arrived, grad_t, gx, sums_t, out)
+        hand_over((came_x, came_y), sum_s, sum_m)
         sum_t = Reduction(*grad_t)
-        low_s, high_s = sum_s.finish()
-        kept_e = total(kept_e, got_e)
-        sent_s, kept_e = tie(jnp.where(even, high_s, low_s), kept_e)
-        got_s, got_e = swap_z(sent_s), outward(kept_e)
-        sent_x, sent_y = (beside(last, both) for last, both in zip(sum_m.second(), sum_t.first()))
-        came_x, came_y = along_x(sent_x), along_y(sent_y)
-        held_s = total(jnp.where(even, low_s, high_s), got_s)
-        held_s, came_x, came_y = tie(held_s, came_x, came_y)
-        got_s = across_pairs(held_s)
-        widths = (sum_m.keep.shape[2], sum_t.keep.shape[2], sum_t.keep.shape[2])
-        sum_m.last_x, *from_x = apart(came_x, widths)
-        sum_m.last_y, *from_y = apart(came_y, widths)
-        sum_t.from_x, sum_t.from_y = jnp.concatenate(from_x, axis=0), jnp.concatenate(from_y, axis=0)
+        held_e = total(held_e, got_e)
+        sent = [beside(last, both) for last, both in zip(sum_m.second(), sum_t.first())]
+        held_s, sent_s = split_groups(sum_s.finish(), even)
+        sent, held_s, sent_s, held_e = tie(sent, held_s, sent_s, held_e)
+        came_x, came_y = along_x(sent[0]), along_y(sent[1])
+        got_s, got_e = swap_z(sent_s), swap_z(held_e)
+        came_x, came_y, got_s = tie(came_x, came_y, got_s)
+        hand_over((came_x, came_y), sum_m, sum_t)
         sum_t.cross_again(tie(*sum_t.second()))
-        low_t, high_t = (jnp.concatenate(pair, axis=1) for pair in zip(sum_m.finish(), sum_t.finish()))
-        sent_t, held_t, got_s, got_e = tie(jnp.where(even, high_t, low_t), jnp.where(even, low_t, high_t), got_s, got_e)
-        got_t = swap_z(sent_t)
         held_s = total(held_s, got_s)
-        got_s = swap_z(held_s)
-        held_t, got_s = tie(total(held_t, got_t), got_s)
-        held_t = total(held_t, across_pairs(held_t))
+        sum_t.last_x, sum_t.last_y, held_s = tie(sum_t.last_x, sum_t.last_y, held_s)
+        halves = [jnp.concatenate(pair, axis=1) for pair in zip(sum_m.finish(), sum_t.finish())]
+        held_t, sent_t = split_groups(halves, even)
+        sent_t, held_t, held_s, got_e = tie(sent_t, held_t, held_s, got_e)
+        got_t, got_s = swap_z(sent_t), across_pairs(held_s)
+        got_t, got_s = tie(got_t, got_s)
+        held_t, held_s = tie(total(held_t, got_t), total(held_s, got_s))
+        got_t, got_s = across_pairs(held_t), swap_z(held_s)
+        got_t, got_s = tie(got_t, got_s)
+        held_t = total(held_t, got_t)
         got_t = swap_z(held_t)
-        rt = jnp.concatenate([jnp.where(even, held_t, got_t), jnp.where(even, got_t, held_t)], axis=0).astype(F32)
-        rs = jnp.concatenate([jnp.where(even, held_s, got_s), jnp.where(even, got_s, held_s)], axis=0).astype(F32)
-        re = jnp.where(inner, kept_e, got_e).astype(F32)
-        rr = jnp.where(inner, kept_r, got_r).astype(F32)
+        rt = join_groups(held_t, got_t, even).astype(F32)
+        rs = join_groups(held_s, got_s, even).astype(F32)
+        re = join_groups(held_e, got_e, even).astype(F32)
+        rr = join_groups(held_r, got_r, even).astype(F32)
         rr = jnp.concatenate([rr[:, k * columns : (k + 1) * columns] for k in range(share)], axis=0)
         rm, rt = rt[:, : 2 * columns], rt[:, 2 * columns :]
         narrow = rt[:, 3 * columns :]

time: 376 us -> 347 us (0.923)
  waiting for transfers between devices: 118 us -> 84.4 us
  other arithmetic: 35.1 us -> 40.3 us
  local copies, waits for them, and re-layouts: 25.6 us -> 21.3 us
    ppermute x2 -> x4, waiting for transfers between devices: 22.1 us -> 5.49 us  [across_pairs(): return lax.ppermute(value, 'grp', [(z, z ^ 2) for z in range(4)])]
    ppermute x4 -> x8, starting transfers between devices: 6.56 us -> 22.1 us  [swap_z(): return lax.ppermute(value, BOTH, pairs)]
    ppermute x6 -> x0, starting transfers between devices: 14.7 us -> none  [the longest x2 10.7 us: inward(): return lax.ppermute(value, 'grp', [(0, 1), (3, 2)])]
    ppermute x36 -> x34, waiting for transfers between devices: 69.2 us -> 59.1 us  [permute(): return lax.ppermute(value, BOTH, pairs)]
    ppermute x6 -> x0, waiting for transfers between devices: 4.93 us -> none  [the longest x2 4.92 us: inward(): return lax.ppermute(value, 'grp', [(0, 1), (3, 2)])]
    select_n x4 -> x11, other arithmetic: 1.71 us -> 6.38 us  [the longest x7 6.16 us: split_groups(): return (jnp.where(even, low, high), jnp.where(even, high, low))]
    ppermute x36 -> x34, starting transfers between devices: 30 us -> 27.9 us  [permute(): return lax.ppermute(value, BOTH, pairs)]
    ppermute x4 -> x8, waiting for transfers between devices: 21.8 us -> 19.8 us  [swap_z(): return lax.ppermute(value, BOTH, pairs)]
  transfers between devices with their start and end apart: 48 -> 46, of which waited for: 19 -> 19; matrix products, arithmetic and copies ran while one was open for 10% -> 12% of each run, Pallas kernels for 29% -> 32%
where the time goes in v5:
time: 347 us; the launch traced here: 342 us
  Pallas kernels  136 us (39%)
  waiting for transfers between devices  84.4 us (24%)
  starting transfers between devices  57.1 us (16%)
  other arithmetic  40.3 us (12%)
  local copies, waits for them, and re-layouts  21.3 us (6%)
    pallas_call x9, Pallas kernels, call(): pl.pallas_call(kernel, out_shape=[jax.ShapeDtypeStruct(s, d) for s, d in...  136 us
    ppermute x34, waiting for transfers between devices, permute(): return lax.ppermute(value, BOTH, pairs)  59.1 us
    ppermute x34, starting transfers between devices, permute(): return lax.ppermute(value, BOTH, pairs)  27.9 us
    ppermute x8, starting transfers between devices, swap_z(): return lax.ppermute(value, BOTH, pairs)  22.1 us
    ppermute x8, waiting for transfers between devices, swap_z(): return lax.ppermute(value, BOTH, pairs)  19.8 us
    another operation x4, other arithmetic, pack_rows(): return jnp.stack(frames, axis=1).reshape(clips * FRAMES * BLOCK, columns)  9.75 us
    unnamed x112, local copies, waits for them, and re-layouts  9.58 us
    convert_element_type x18, other arithmetic, total(): return sum((t.astype(F32) for t in terms)).astype(BF)  7.51 us
  transfers between devices with their start and end apart: 46, of which 19 were waited for; matrix products, arithmetic and copies ran while one was open for 12% of the time, Pallas kernels for 32%

profile of v5, /device:TPU:0, one launch (start us, length us, event | category | flops | bytes accessed | tf_op | source)
XLA Modules:
  0.0 341.7 jit_solution(8515955980046143987)
XLA Ops:
  6.6 2.9 collective-permute-start.1
  10.3 3.2 fusion.2
  13.5 1.8 pad_maximum_fusion.2
  16.8 10.6 %collective-permute-done.1.refs_3_.refs_5_.refs_13_ = bf16[192,3968]{1,0:T(8,128)(2,1)} collective-permute-done((bf16[192,3968]{1,0:T(8,128)(2,1)S(1)}, bf16[192,3968]{1,0:T(8,128)(2,1)}, u32[]{:S(2)}, u32[]{:S(2)}) %collective-permute-start.1) | collective-permute-done | bytes 1523744 | tf_op jit(solution)/shard_map/ppermute | solution.py:773
  28.6 2.1 collective-permute-start.4
  30.7 9.8 %collective-permute-done.4.refs_4_.refs_6_.refs_14_ = bf16[96,3968]{1,0:T(8,128)(2,1)} collective-permute-done((bf16[96,3968]{1,0:T(8,128)(2,1)S(1)}, bf16[96,3968]{1,0:T(8,128)(2,1)}, u32[]{:S(2)}, u32[]{:S(2)}) %collective-permute-start.4) | collective-permute-done | bytes 761888 | tf_op jit(solution)/shard_map/ppermute | solution.py:773
  41.2 2.0 collective-permute-start.6
  43.3 14.0 %time_forward.1 = (bf16[832,768]{1,0:T(8,128)(2,1)}, bf16[832,2304]{1,0:T(8,128)(2,1)}, bf16[832,768]{1,0:T(8,128)(2,1)}, bf16[832,768]{1,0:T(8,128)(2,1)}, f32[...) custom-call(s32[16]{0:T(128)} %stack.76.refs_0_, bf16[832,768]{1,0:T(8,128)(2,1)} %bitcast.65, ...), custom_call_target="tpu_custom_call" | custom-call | flops 56000000000 | tf_op jit(solution)/shard_map/time_forward/pallas_call | solution.py:285
  58.7 2.0 collective-permute-start.9
  60.9 2.4 bitcast_multiply_fusion
  64.5 10.5 %collective-permute-done.9.refs_5_.refs_8_.refs_7_ = bf16[96,3072]{1,0:T(8,128)(2,1)S(1)} collective-permute-done((bf16[96,3072]{1,0:T(8,128)(2,1)S(1)}, bf16[96,3072]{1,0:T(8,128)(2,1)S(1)}, u32[]{:S(2)}, u32[]{:S(2)}) %collective-permute-start.9) | collective-permute-done | bytes 589856 | tf_op jit(solution)/shard_map/ppermute | solution.py:773
  75.0 2.9 maximum_bitcast_fusion.1
  77.9 1.8 pad_maximum_fusion.3
  80.9 8.2 %collective-permute-done.5.refs_6_ = bf16[192,6144]{1,0:T(8,128)(2,1)} collective-permute-done((bf16[192,6144]{1,0:T(8,128)(2,1)S(1)}, bf16[192,6144]{1,0:T(8,128)(2,1)}, u32[]{:S(2)}, u32[]{:S(2)}) %collective-permute-start.5) | collective-permute-done | bytes 2359328 | tf_op jit(solution)/shard_map/ppermute | solution.py:773
  91.6 2.1 collective-permute-start.12
  93.7 16.8 %space_forward.1 = (bf16[832,768]{1,0:T(8,128)(2,1)}, bf16[832,2304]{1,0:T(8,128)(2,1)}, bf16[48,208,208]{2,1,0:T(8,128)(2,1)}, bf16[832,768]{1,0:T(8,128)(2,1)}, f32[832,768]{1,0:T(8,128)}) custom-call(s32[16]{0:T(128)} %stack.76.refs_0_, f32[832,768]{1,0:T(8,128)} %get-tuple-element.162.refs_1_.refs_2_, ...), custom_call_target="tpu_custom_call" | custom-call | flops 64000000000 | tf_op jit(solution)/shard_map/space_forward/pallas_call | solution.py:285
  110.7 3.1 collective-permute-done.14.refs_9_
  113.7 27.9 %feed_out.1 = (bf16[832,768]{1,0:T(8,128)(2,1)}, bf16[832,768]{1,0:T(8,128)(2,1)}, bf16[832,3072]{1,0:T(8,128)(2,1)}, bf16[8,48,3072]{2,1,0:T(8,128)(2,1)}, bf16[8,48,3072]{2,1,0:T(8,128)(2,1)}) custom-call(s32[16]{0:T(128)} %stack.76.refs_0_, f32[832,768]{1,0:T(8,128)} %get-tuple-element.170.refs_1_.refs_2_, bf16[832,768]{1,0:T(8,128)(2,1)} %bitcast.67, ...), custom_call_target="tpu_custom_call" | custom-call | flops 120000004096 | tf_op jit(solution)/shard_map/feed_out/pallas_call | solution.py:285
  141.9 2.4 copy-done.17
  145.6 7.4 %feed_in.1 = (f32[8,768]{1,0:T(8,128)S(1)}, f32[8,3072]{1,0:T(8,128)S(1)}, bf16[8,48,3072]{2,1,0:T(8,128)(2,1)S(1)}, bf16[8,48,3072]{2,1,0:T(8,128)(2,1)S(1)}) custom-call(s32[16]{0:T(128)S(1)} %copy-done.8, bf16[832,3072]{1,0:T(8,128)(2,1)S(1)} %copy-done.17, bf16[832,768]{1,0:T(8,128)(2,1)S(1)} %copy-done.28, bf16[832,768]{1,0:T(8,128)(2,1)S(1)} %bitcast.68), custom_call_target="tpu_custom_call" | custom-call | flops 32000000000 | tf_op jit(solution)/shard_map/feed_in/pallas_call | solution.py:285
  156.8 9.1 %feed_norm.1 = (f32[832,768]{1,0:T(8,128)S(1)}, f32[8,768]{1,0:T(8,128)S(1)}) custom-call(s32[16]{0:T(128)S(1)} %copy-done.8, bf16[832,3072]{1,0:T(8,128)(2,1)S(1)} %copy-done.18, f32[832,768]{1,0:T(8,128)S(1)} %copy-done.24, bf16[832,768]{1,0:T(8,128)(2,1)S(1)} %bitcast.69, f32[32,768]{1,0:T(8,128)S(1)} %copy-done.33, bf16[192,6144]{1,0:T(8,128)(2,1)S(1)} %copy-done.1, ...), custom_call_target="tpu_custom_call" | custom-call | flops 40000000000 | tf_op jit(solution)/shard_map/feed_norm/pallas_call | solution.py:285
  166.0 2.5 add_convert_fusion.2
  168.7 1.7 collective-permute-done.16
  174.4 20.9 %space_backward.1 = (bf16[832,2304]{1,0:T(8,128)(2,1)S(1)}, f32[8,768]{1,0:T(8,128)S(1)}, bf16[8,48,3072]{2,1,0:T(8,128)(2,1)S(1)}, bf16[8,48,3072]{2,1,0:T(8,128)(2,1)S(1)}) custom-call(s32[16]{0:T(128)S(1)} %copy-done.8, f32[832,768]{1,0:T(8,128)S(1)} %get-tuple-element.190.refs_1_.refs_3_, bf16[832,768]{1,0:T(8,128)(2,1)S(1)} %copy-done.30, ...), custom_call_target="tpu_custom_call" | custom-call | flops 80000000000 | tf_op jit(solution)/shard_map/space_backward/pallas_call | solution.py:285
  195.3 1.9 copy-done.20
  197.3 2.1 select_bitcast_fusion.4
  199.4 1.6 add_convert_fusion.24
  201.0 1.6 collective-permute-start.21
  204.7 7.6 %space_norm.1 = (f32[832,768]{1,0:T(8,128)S(1)}, f32[8,768]{1,0:T(8,128)S(1)}) custom-call(s32[16]{0:T(128)S(1)} %copy-done.8, bf16[832,2304]{1,0:T(8,128)(2,1)S(1)} %copy-done.21, f32[832,768]{1,0:T(8,128)S(1)} %copy-done.25, f32[832,768]{1,0:T(8,128)S(1)} %copy-done.23, f32[32,768]{1,0:T(8,128)S(1)} %copy-done.33, bf16[192,3072]{1,0:T(8,128)(2,1)S(1)} %copy-done.7, ...), custom_call_target="tpu_custom_call" | custom-call | flops 40000000000 | tf_op jit(solution)/shard_map/space_norm/pallas_call | solution.py:285
  212.5 2.4 select_bitcast_fusion.2
  215.9 2.6 collective-permute-start.25
  220.5 12.8 %mixer_backward.1 = (bf16[832,768]{1,0:T(8,128)(2,1)S(1)}, f32[8,768]{1,0:T(8,128)S(1)}, bf16[8,48,1536]{2,1,0:T(8,128)(2,1)S(1)}, bf16[8,48,1536]{2,1,0:T(8,128)(2,1)S(1)}) custom-call(s32[16]{0:T(128)S(1)} %copy-done.8, f32[832,768]{1,0:T(8,128)S(1)} %get-tuple-element.216.refs_1_.refs_6_, bf16[832,768]{1,0:T(8,128)(2,1)S(1)} %copy-done.26, ...), custom_call_target="tpu_custom_call" | custom-call | flops 32000000000 | tf_op jit(solution)/shard_map/mixer_backward/pallas_call | solution.py:285
  233.9 2.4 collective-permute-done.29
  236.6 1.6 collective-permute-start.32
  240.6 19.4 %time_backward.1 = (bf16[832,768]{1,0:T(8,128)(2,1)S(1)}, f32[8,768]{1,0:T(8,128)}, bf16[8,48,2432]{2,1,0:T(8,128)(2,1)S(1)}, bf16[8,48,2432]{2,1,0:T(8,128)(2,1)S(1)}) custom-call(s32[16]{0:T(128)S(1)} %copy-done.8, bf16[832,768]{1,0:T(8,128)(2,1)S(1)} %get-tuple-element.234.refs_1_, bf16[832,2304]{1,0:T(8,128)(2,1)} %get-tuple-element.235.refs_2_, ...), custom_call_target="tpu_custom_call" | custom-call | flops 80000000000 | tf_op jit(solution)/shard_map/time_backward/pallas_call | solution.py:285
  261.4 2.8 maximum_multiply_fusion
  269.3 1.6 collective-permute-start.40
  270.9 7.6 %collective-permute-done.37 = bf16[48,3072]{1,0:T(8,128)(2,1)S(1)} collective-permute-done((bf16[48,3072]{1,0:T(8,128)(2,1)S(1)}, bf16[48,3072]{1,0:T(8,128)(2,1)S(1)}, u32[]{:S(2)}, u32[]{:S(2)}) %collective-permute-start.37) | collective-permute-done | bytes 294944 | tf_op jit(solution)/shard_map/ppermute | solution.py:862
  278.5 4.1 %collective-permute-done.35 = bf16[1,48,6400]{2,1,0:T(8,128)(2,1)S(1)} collective-permute-done((bf16[1,48,6400]{2,1,0:T(8,128)(2,1)S(1)}, bf16[1,48,6400]{2,1,0:T(8,128)(2,1)S(1)}, u32[]{:S(2)}, u32[]{:S(2)}) %collective-permute-start.35) | collective-permute-done | bytes 614432 | tf_op jit(solution)/shard_map/ppermute | solution.py:773
  285.5 4.7 %collective-permute-done.38 = bf16[1,48,2432]{2,1,0:T(8,128)(2,1)S(1)} collective-permute-done((bf16[1,48,2432]{2,1,0:T(8,128)(2,1)S(1)}, bf16[1,48,2432]{2,1,0:T(8,128)(2,1)S(1)}, u32[]{:S(2)}, u32[]{:S(2)}) %collective-permute-start.38) | collective-permute-done | bytes 233504 | tf_op jit(solution)/shard_map/ppermute | solution.py:773
  294.3 2.7 collective-permute-start.42
  297.0 2.6 maximum_bitcast_fusion
  299.6 5.5 %collective-permute-done.42 = bf16[48,3072]{1,0:T(8,128)(2,1)S(1)} collective-permute-done((bf16[48,3072]{1,0:T(8,128)(2,1)S(1)}, bf16[48,3072]{1,0:T(8,128)(2,1)S(1)}, u32[]{:S(2)}, u32[]{:S(2)}) %collective-permute-start.42) | collective-permute-done | bytes 294944 | tf_op jit(solution)/shard_map/ppermute | solution.py:866
  305.1 2.0 collective-permute-done.41
  308.8 13.9 %collective-permute-start.44 = (bf16[48,3072]{1,0:T(8,128)(2,1)S(1)}, bf16[48,3072]{1,0:T(8,128)(2,1)S(1)}, u32[]{:S(2)}, u32[]{:S(2)}) collective-permute-start(bf16[48,3072]{1,0:T(8,128)(2,1)S(1)} %add_convert_fusion.10), channel_id=1, source_target_pairs={{0,8},{1,9},{2,10},{3,11},{4,12},{5,13},{6,14},{7,15},{8,0},{9,1},... | collective-permute-start | bytes 884744 | tf_op jit(solution)/shard_map/ppermute | solution.py:862
  323.8 6.1 %collective-permute-done.44 = bf16[48,3072]{1,0:T(8,128)(2,1)S(1)} collective-permute-done((bf16[48,3072]{1,0:T(8,128)(2,1)S(1)}, bf16[48,3072]{1,0:T(8,128)(2,1)S(1)}, u32[]{:S(2)}, u32[]{:S(2)}) %collective-permute-start.44) | collective-permute-done | bytes 294944 | tf_op jit(solution)/shard_map/ppermute | solution.py:862
  330.0 1.8 collective-permute-start.45
  333.6 4.1 %collective-permute-done.45 = bf16[48,3968]{1,0:T(8,128)(2,1)S(1)} collective-permute-done((bf16[48,3968]{1,0:T(8,128)(2,1)S(1)}, bf16[48,3968]{1,0:T(8,128)(2,1)S(1)}, u32[]{:S(2)}, u32[]{:S(2)}) %collective-permute-start.45) | collective-permute-done | bytes 380960 | tf_op jit(solution)/shard_map/ppermute | solution.py:862
  (261 shorter events, 55.3 us)
Async XLA Ops:
  3.4 2.4 collective-permute-start
  6.0 10.5 %collective-permute-start.2 = (bf16[96,3072]{1,0:T(8,128)(2,1)S(1)}, bf16[96,3072]{1,0:T(8,128)(2,1)S(1)}, u32[]{:S(2)}, u32[]{:S(2)}) collective-permute-start(bf16[96,3072]{1,0:T(8,128)(2,1)S(1)} %pad_maximum_fusion.13), channel_id=1, source_target_pairs={{0,1},{1,0},{2,3},{3,2},{4,5},{5,4},{6,7},{7,6},{8,9},{9,8},{10,11... | collective-permute-start | bytes 1769480 | tf_op jit(solution)/shard_map/ppermute | solution.py:773
  6.4 10.2 %collective-permute-start.3 = (bf16[96,6144]{1,0:T(8,128)(2,1)S(1)}, bf16[96,6144]{1,0:T(8,128)(2,1)S(1)}, u32[]{:S(2)}, u32[]{:S(2)}) collective-permute-start(bf16[96,6144]{1,0:T(8,128)(2,1)S(1)} %slice_dynamic-update-slice_fusion), channel_id=1, source_target_pairs={{0,1},{1,0},{2,3},{3,2},{4,5},{5,4},{6,7},{7,6},{8,9},{9,8},{10,11... | collective-permute-start | bytes 3538952 | tf_op jit(solution)/shard_map/ppermute | solution.py:773
  6.6 20.8 %collective-permute-start.1 = (bf16[192,3968]{1,0:T(8,128)(2,1)S(1)}, bf16[192,3968]{1,0:T(8,128)(2,1)}, u32[]{:S(2)}, u32[]{:S(2)}) collective-permute-start(bf16[192,3968]{1,0:T(8,128)(2,1)S(1)} %pad_maximum_fusion.1.refs_2_.refs_4_.refs_12_), channel_id=1, source_target_pairs={{0,2},{1,5},{2,0},{3,7},{4,6},{5,1},{6,4},{7,3},{8,10},{9,13},{10,... | collective-permute-start | bytes 4571144 | tf_op jit(solution)/shard_map/ppermute | solution.py:773
  16.8 40.5 %copy-start = (bf16[192,6144]{1,0:T(8,128)(2,1)}, bf16[192,6144]{1,0:T(8,128)(2,1)S(1)}, u32[]{:S(2)}) copy-start(bf16[192,6144]{1,0:T(8,128)(2,1)S(1)} %pad_maximum_fusion.refs_5_) | copy-start | bytes 7077892
  28.6 11.9 %collective-permute-start.4 = (bf16[96,3968]{1,0:T(8,128)(2,1)S(1)}, bf16[96,3968]{1,0:T(8,128)(2,1)}, u32[]{:S(2)}, u32[]{:S(2)}) collective-permute-start(bf16[96,3968]{1,0:T(8,128)(2,1)S(1)} %slice.427), channel_id=1, source_target_pairs={{0,4},{1,3},{2,6},{3,1},{4,0},{5,7},{6,2},{7,5},{8,12},{9,11},{10,... | collective-permute-start | bytes 2285576 | tf_op jit(solution)/shard_map/ppermute | solution.py:773
  30.7 12.6 %collective-permute-start.7 = (bf16[192,3968]{1,0:T(8,128)(2,1)}, bf16[192,3968]{1,0:T(8,128)(2,1)}, u32[]{:S(2)}, u32[]{:S(2)}) collective-permute-start(bf16[192,3968]{1,0:T(8,128)(2,1)} %collective-permute-done.1.refs_3_.refs_5_.refs_13_), channel_id=1, source_target_pairs={{0,1},{1,0},{2,3},{3,2},{4,5},{5,4},{6,7},{7,6},{8,9},{9,8},{10,11... | collective-permute-start | bytes 4571144 | tf_op jit(solution)/shard_map/ppermute | solution.py:773
  40.5 2.7 collective-permute-start.8
  41.2 16.3 %collective-permute-start.6 = (bf16[192,3072]{1,0:T(8,128)(2,1)S(1)}, bf16[192,3072]{1,0:T(8,128)(2,1)}, u32[]{:S(2)}, u32[]{:S(2)}) collective-permute-start(bf16[192,3072]{1,0:T(8,128)(2,1)S(1)} %pad_maximum_fusion.4.refs_3_.refs_6_.refs_5_), channel_id=1, source_target_pairs={{0,2},{1,5},{2,0},{3,7},{4,6},{5,1},{6,4},{7,3},{8,10},{9,13},{10,... | collective-permute-start | bytes 3538952 | tf_op jit(solution)/shard_map/ppermute | solution.py:773
  43.2 45.9 %collective-permute-start.5 = (bf16[192,6144]{1,0:T(8,128)(2,1)S(1)}, bf16[192,6144]{1,0:T(8,128)(2,1)}, u32[]{:S(2)}, u32[]{:S(2)}) collective-permute-start(bf16[192,6144]{1,0:T(8,128)(2,1)S(1)} %pad_maximum_fusion.refs_5_), channel_id=1, source_target_pairs={{0,2},{1,5},{2,0},{3,7},{4,6},{5,1},{6,4},{7,3},{8,10},{9,13},{10,... | collective-permute-start | bytes 7077896 | tf_op jit(solution)/shard_map/ppermute | solution.py:773
  58.6 30.5 %collective-permute-start.10 = (bf16[192,3072]{1,0:T(8,128)(2,1)}, bf16[192,3072]{1,0:T(8,128)(2,1)S(1)}, u32[]{:S(2)}, u32[]{:S(2)}) collective-permute-start(bf16[192,3072]{1,0:T(8,128)(2,1)} %collective-permute-done.6.refs_4_.refs_7_.refs_6_), channel_id=1, source_target_pairs={{0,1},{1,0},{2,3},{3,2},{4,5},{5,4},{6,7},{7,6},{8,9},{9,8},{10,11... | collective-permute-start | bytes 3538952 | tf_op jit(solution)/shard_map/ppermute | solution.py:773
  58.7 16.3 %collective-permute-start.9 = (bf16[96,3072]{1,0:T(8,128)(2,1)S(1)}, bf16[96,3072]{1,0:T(8,128)(2,1)S(1)}, u32[]{:S(2)}, u32[]{:S(2)}) collective-permute-start(bf16[96,3072]{1,0:T(8,128)(2,1)S(1)} %slice.428), channel_id=1, source_target_pairs={{0,4},{1,3},{2,6},{3,1},{4,0},{5,7},{6,2},{7,5},{8,12},{9,11},{10,... | collective-permute-start | bytes 1769480 | tf_op jit(solution)/shard_map/ppermute | solution.py:773
  75.0 5.9 %collective-permute-start.11 = (bf16[96,3072]{1,0:T(8,128)(2,1)S(1)}, bf16[96,3072]{1,0:T(8,128)(2,1)S(1)}, u32[]{:S(2)}, u32[]{:S(2)}) collective-permute-start(bf16[96,3072]{1,0:T(8,128)(2,1)S(1)} %collective-permute-done.9.refs_5_.refs_8_.refs_7_), channel_id=1, source_target_pairs={{0,1},{1,0},{2,3},{3,2},{4,5},{5,4},{6,7},{7,6},{8,9},{9,8},{10,11... | collective-permute-start | bytes 1769480 | tf_op jit(solution)/shard_map/ppermute | solution.py:773
  91.5 19.2 %collective-permute-start.13 = (bf16[192,6144]{1,0:T(8,128)(2,1)}, bf16[192,6144]{1,0:T(8,128)(2,1)S(1)}, u32[]{:S(2)}, u32[]{:S(2)}) collective-permute-start(bf16[192,6144]{1,0:T(8,128)(2,1)} %collective-permute-done.5.refs_6_), channel_id=1, source_target_pairs={{0,1},{1,0},{2,3},{3,2},{4,5},{5,4},{6,7},{7,6},{8,9},{9,8},{10,11... | collective-permute-start | bytes 7077896 | tf_op jit(solution)/shard_map/ppermute | solution.py:773
  91.6 18.9 %collective-permute-start.12 = (bf16[96,6144]{1,0:T(8,128)(2,1)S(1)}, bf16[96,6144]{1,0:T(8,128)(2,1)}, u32[]{:S(2)}, u32[]{:S(2)}) collective-permute-start(bf16[96,6144]{1,0:T(8,128)(2,1)S(1)} %slice.432), channel_id=1, source_target_pairs={{0,4},{1,3},{2,6},{3,1},{4,0},{5,7},{6,2},{7,5},{8,12},{9,11},{10,... | collective-permute-start | bytes 3538952 | tf_op jit(solution)/shard_map/ppermute | solution.py:773
  110.5 3.3 collective-permute-start.14
  141.7 11.9 %collective-permute-start.15 = (bf16[8,48,3072]{2,1,0:T(8,128)(2,1)}, bf16[8,48,3072]{2,1,0:T(8,128)(2,1)S(1)}, u32[]{:S(2)}, u32[]{:S(2)}) collective-permute-start(bf16[8,48,3072]{2,1,0:T(8,128)(2,1)} %get-tuple-element.175), channel_id=1, source_target_pairs={{0,1},{1,0},{2,3},{3,2},{4,5},{5,4},{6,7},{7,6},{8,9},{9,8},{10,11... | collective-permute-start | bytes 7077896 | tf_op jit(solution)/shard_map/ppermute | solution.py:773
  153.1 12.9 %collective-permute-start.18 = (bf16[8,48,3072]{2,1,0:T(8,128)(2,1)S(1)}, bf16[8,48,3072]{2,1,0:T(8,128)(2,1)}, u32[]{:S(2)}, u32[]{:S(2)}) collective-permute-start(bf16[8,48,3072]{2,1,0:T(8,128)(2,1)S(1)} %get-tuple-element.184), channel_id=1, source_target_pairs={{0,1},{1,0},{2,3},{3,2},{4,5},{5,4},{6,7},{7,6},{8,9},{9,8},{10,11... | collective-permute-start | bytes 7077896 | tf_op jit(solution)/shard_map/ppermute | solution.py:773
  154.7 15.6 %collective-permute-start.16 = (bf16[2,48,3072]{2,1,0:T(8,128)(2,1)}, bf16[2,48,3072]{2,1,0:T(8,128)(2,1)S(1)}, u32[]{:S(2)}, u32[]{:S(2)}) collective-permute-start(bf16[2,48,3072]{2,1,0:T(8,128)(2,1)} %get-tuple-element.181), channel_id=1, source_target_pairs={{0,2},{1,3},{2,0},{3,1},{4,6},{5,7},{6,4},{7,5},{8,10},{9,11},{10,... | collective-permute-start | bytes 1769480 | tf_op jit(solution)/shard_map/ppermute | solution.py:773
  156.3 15.1 %collective-permute-start.17 = (bf16[2,48,3072]{2,1,0:T(8,128)(2,1)S(1)}, bf16[2,48,3072]{2,1,0:T(8,128)(2,1)S(1)}, u32[]{:S(2)}, u32[]{:S(2)}) collective-permute-start(bf16[2,48,3072]{2,1,0:T(8,128)(2,1)S(1)} %get-tuple-element.182), channel_id=1, source_target_pairs={{0,4},{1,5},{2,6},{3,7},{4,0},{5,1},{6,2},{7,3},{8,12},{9,13},{10,... | collective-permute-start | bytes 1769480 | tf_op jit(solution)/shard_map/ppermute | solution.py:773
  172.3 25.0 %collective-permute-start.19 = (bf16[1,48,9216]{2,1,0:T(8,128)(2,1)S(1)}, bf16[1,48,9216]{2,1,0:T(8,128)(2,1)}, u32[]{:S(2)}, u32[]{:S(2)}) collective-permute-start(bf16[1,48,9216]{2,1,0:T(8,128)(2,1)S(1)} %pad_maximum_fusion.7), channel_id=1, source_target_pairs={{0,4},{1,5},{2,6},{3,7},{4,0},{5,1},{6,2},{7,3},{8,12},{9,13},{10,... | collective-permute-start | bytes 2654216 | tf_op jit(solution)/shard_map/ppermute | solution.py:773
  173.0 24.2 %collective-permute-start.20 = (bf16[1,48,9216]{2,1,0:T(8,128)(2,1)S(1)}, bf16[1,48,9216]{2,1,0:T(8,128)(2,1)}, u32[]{:S(2)}, u32[]{:S(2)}) collective-permute-start(bf16[1,48,9216]{2,1,0:T(8,128)(2,1)S(1)} %pad_maximum_fusion.6), channel_id=1, source_target_pairs={{0,2},{1,3},{2,0},{3,1},{4,6},{5,7},{6,4},{7,5},{8,10},{9,11},{10,... | collective-permute-start | bytes 2654216 | tf_op jit(solution)/shard_map/ppermute | solution.py:773
  174.4 30.3 %copy-start.25 = (f32[832,768]{1,0:T(8,128)S(1)}, f32[832,768]{1,0:T(8,128)}, u32[]{:S(2)}) copy-start(f32[832,768]{1,0:T(8,128)} %get-tuple-element.162.refs_1_.refs_2_) | copy-start | bytes 7667716
  197.2 17.7 %collective-permute-start.24 = (bf16[8,48,3072]{2,1,0:T(8,128)(2,1)S(1)}, bf16[8,48,3072]{2,1,0:T(8,128)(2,1)S(1)}, u32[]{:S(2)}, u32[]{:S(2)}) collective-permute-start(bf16[8,48,3072]{2,1,0:T(8,128)(2,1)S(1)} %get-tuple-element.209), channel_id=1, source_target_pairs={{0,1},{1,0},{2,3},{3,2},{4,5},{5,4},{6,7},{7,6},{8,9},{9,8},{10,11... | collective-permute-start | bytes 7077896 | tf_op jit(solution)/shard_map/ppermute | solution.py:773
  201.0 11.3 %collective-permute-start.21 = (bf16[48,3072]{1,0:T(8,128)(2,1)S(1)}, bf16[48,3072]{1,0:T(8,128)(2,1)S(1)}, u32[]{:S(2)}, u32[]{:S(2)}) collective-permute-start(bf16[48,3072]{1,0:T(8,128)(2,1)S(1)} %get-tuple-element.199), channel_id=1, source_target_pairs={{0,8},{1,9},{2,10},{3,11},{4,12},{5,13},{6,14},{7,15},{8,0},{9,1},... | collective-permute-start | bytes 884744 | tf_op jit(solution)/shard_map/ppermute | solution.py:862
  202.7 9.7 %collective-permute-start.22 = (bf16[1,48,3072]{2,1,0:T(8,128)(2,1)S(1)}, bf16[1,48,3072]{2,1,0:T(8,128)(2,1)S(1)}, u32[]{:S(2)}, u32[]{:S(2)}) collective-permute-start(bf16[1,48,3072]{2,1,0:T(8,128)(2,1)S(1)} %get-tuple-element.200), channel_id=1, source_target_pairs={{0,2},{1,3},{2,0},{3,1},{4,6},{5,7},{6,4},{7,5},{8,10},{9,11},{10,... | collective-permute-start | bytes 884744 | tf_op jit(solution)/shard_map/ppermute | solution.py:773
  203.4 9.0 %collective-permute-start.23 = (bf16[1,48,3072]{2,1,0:T(8,128)(2,1)S(1)}, bf16[1,48,3072]{2,1,0:T(8,128)(2,1)S(1)}, u32[]{:S(2)}, u32[]{:S(2)}) collective-permute-start(bf16[1,48,3072]{2,1,0:T(8,128)(2,1)S(1)} %get-tuple-element.201), channel_id=1, source_target_pairs={{0,4},{1,5},{2,6},{3,7},{4,0},{5,1},{6,2},{7,3},{8,12},{9,13},{10,... | collective-permute-start | bytes 884744 | tf_op jit(solution)/shard_map/ppermute | solution.py:773
  215.4 18.1 %collective-permute-start.26 = (bf16[48,3072]{1,0:T(8,128)(2,1)S(1)}, bf16[48,3072]{1,0:T(8,128)(2,1)S(1)}, u32[]{:S(2)}, u32[]{:S(2)}) collective-permute-start(bf16[48,3072]{1,0:T(8,128)(2,1)S(1)} %get-tuple-element.213), channel_id=1, source_target_pairs={{0,8},{1,9},{2,10},{3,11},{4,12},{5,13},{6,14},{7,15},{8,0},{9,1},... | collective-permute-start | bytes 884744 | tf_op jit(solution)/shard_map/ppermute | solution.py:862
  215.9 17.6 %collective-permute-start.25 = (bf16[48,3072]{1,0:T(8,128)(2,1)S(1)}, bf16[48,3072]{1,0:T(8,128)(2,1)S(1)}, u32[]{:S(2)}, u32[]{:S(2)}) collective-permute-start(bf16[48,3072]{1,0:T(8,128)(2,1)S(1)} %add_convert_fusion.23), channel_id=1, source_target_pairs={{0,16},{8,24},{16,0},{24,8},{1,17},{9,25},{17,1},{25,9},{2,18},{10... | collective-permute-start | bytes 884744 | tf_op jit(solution)/shard_map/ppermute | solution.py:866
  218.5 15.0 %collective-permute-start.27 = (bf16[2,48,3072]{2,1,0:T(8,128)(2,1)S(1)}, bf16[2,48,3072]{2,1,0:T(8,128)(2,1)S(1)}, u32[]{:S(2)}, u32[]{:S(2)}) collective-permute-start(bf16[2,48,3072]{2,1,0:T(8,128)(2,1)S(1)} %get-tuple-element.214), channel_id=1, source_target_pairs={{0,2},{1,3},{2,0},{3,1},{4,6},{5,7},{6,4},{7,5},{8,10},{9,11},{10,... | collective-permute-start | bytes 1769480 | tf_op jit(solution)/shard_map/ppermute | solution.py:773
  219.1 14.4 %collective-permute-start.28 = (bf16[2,48,3072]{2,1,0:T(8,128)(2,1)S(1)}, bf16[2,48,3072]{2,1,0:T(8,128)(2,1)S(1)}, u32[]{:S(2)}, u32[]{:S(2)}) collective-permute-start(bf16[2,48,3072]{2,1,0:T(8,128)(2,1)S(1)} %get-tuple-element.215), channel_id=1, source_target_pairs={{0,4},{1,5},{2,6},{3,7},{4,0},{5,1},{6,2},{7,3},{8,12},{9,13},{10,... | collective-permute-start | bytes 1769480 | tf_op jit(solution)/shard_map/ppermute | solution.py:773
  233.4 2.9 collective-permute-start.29
  236.6 23.4 %collective-permute-start.32 = (bf16[48,3072]{1,0:T(8,128)(2,1)S(1)}, bf16[48,3072]{1,0:T(8,128)(2,1)S(1)}, u32[]{:S(2)}, u32[]{:S(2)}) collective-permute-start(bf16[48,3072]{1,0:T(8,128)(2,1)S(1)} %add_convert_fusion.20), channel_id=1, source_target_pairs={{0,8},{1,9},{2,10},{3,11},{4,12},{5,13},{6,14},{7,15},{8,0},{9,1},... | collective-permute-start | bytes 884744 | tf_op jit(solution)/shard_map/ppermute | solution.py:862
  238.3 21.8 %collective-permute-start.33 = (bf16[48,3072]{1,0:T(8,128)(2,1)S(1)}, bf16[48,3072]{1,0:T(8,128)(2,1)S(1)}, u32[]{:S(2)}, u32[]{:S(2)}) collective-permute-start(bf16[48,3072]{1,0:T(8,128)(2,1)S(1)} %add_convert_fusion.19), channel_id=1, source_target_pairs={{0,16},{8,24},{16,0},{24,8},{1,17},{9,25},{17,1},{25,9},{2,18},{10... | collective-permute-start | bytes 884744 | tf_op jit(solution)/shard_map/ppermute | solution.py:866
  238.6 21.5 %collective-permute-start.30 = (bf16[1,48,6144]{2,1,0:T(8,128)(2,1)S(1)}, bf16[1,48,6144]{2,1,0:T(8,128)(2,1)S(1)}, u32[]{:S(2)}, u32[]{:S(2)}) collective-permute-start(bf16[1,48,6144]{2,1,0:T(8,128)(2,1)S(1)} %pad_maximum_fusion.14), channel_id=1, source_target_pairs={{0,2},{1,3},{2,0},{3,1},{4,6},{5,7},{6,4},{7,5},{8,10},{9,11},{10,... | collective-permute-start | bytes 1769480 | tf_op jit(solution)/shard_map/ppermute | solution.py:773
  239.2 20.9 %collective-permute-start.31 = (bf16[1,48,6144]{2,1,0:T(8,128)(2,1)S(1)}, bf16[1,48,6144]{2,1,0:T(8,128)(2,1)S(1)}, u32[]{:S(2)}, u32[]{:S(2)}) collective-permute-start(bf16[1,48,6144]{2,1,0:T(8,128)(2,1)S(1)} %pad_maximum_fusion.15), channel_id=1, source_target_pairs={{0,4},{1,5},{2,6},{3,7},{4,0},{5,1},{6,2},{7,3},{8,12},{9,13},{10,... | collective-permute-start | bytes 1769480 | tf_op jit(solution)/shard_map/ppermute | solution.py:773
  261.3 4.6 %collective-permute-start.34 = (bf16[8,48,2432]{2,1,0:T(8,128)(2,1)S(1)}, bf16[8,48,2432]{2,1,0:T(8,128)(2,1)S(1)}, u32[]{:S(2)}, u32[]{:S(2)}) collective-permute-start(bf16[8,48,2432]{2,1,0:T(8,128)(2,1)S(1)} %get-tuple-element.252), channel_id=1, source_target_pairs={{0,1},{1,0},{2,3},{3,2},{4,5},{5,4},{6,7},{7,6},{8,9},{9,8},{10,11... | collective-permute-start | bytes 5603336 | tf_op jit(solution)/shard_map/ppermute | solution.py:773
  266.3 16.3 %collective-permute-start.35 = (bf16[1,48,6400]{2,1,0:T(8,128)(2,1)S(1)}, bf16[1,48,6400]{2,1,0:T(8,128)(2,1)S(1)}, u32[]{:S(2)}, u32[]{:S(2)}) collective-permute-start(bf16[1,48,6400]{2,1,0:T(8,128)(2,1)S(1)} %pad_maximum_fusion.11), channel_id=1, source_target_pairs={{0,2},{1,3},{2,0},{3,1},{4,6},{5,7},{6,4},{7,5},{8,10},{9,11},{10,... | collective-permute-start | bytes 1843208 | tf_op jit(solution)/shard_map/ppermute | solution.py:773
  267.0 15.9 %collective-permute-start.36 = (bf16[1,48,6400]{2,1,0:T(8,128)(2,1)S(1)}, bf16[1,48,6400]{2,1,0:T(8,128)(2,1)S(1)}, u32[]{:S(2)}, u32[]{:S(2)}) collective-permute-start(bf16[1,48,6400]{2,1,0:T(8,128)(2,1)S(1)} %pad_maximum_fusion.12), channel_id=1, source_target_pairs={{0,4},{1,5},{2,6},{3,7},{4,0},{5,1},{6,2},{7,3},{8,12},{9,13},{10,... | collective-permute-start | bytes 1843208 | tf_op jit(solution)/shard_map/ppermute | solution.py:773
  268.6 9.9 %collective-permute-start.37 = (bf16[48,3072]{1,0:T(8,128)(2,1)S(1)}, bf16[48,3072]{1,0:T(8,128)(2,1)S(1)}, u32[]{:S(2)}, u32[]{:S(2)}) collective-permute-start(bf16[48,3072]{1,0:T(8,128)(2,1)S(1)} %get-tuple-element.257), channel_id=1, source_target_pairs={{0,8},{1,9},{2,10},{3,11},{4,12},{5,13},{6,14},{7,15},{8,0},{9,1},... | collective-permute-start | bytes 884744 | tf_op jit(solution)/shard_map/ppermute | solution.py:862
  269.3 22.5 %collective-permute-start.40 = (bf16[48,3072]{1,0:T(8,128)(2,1)S(1)}, bf16[48,3072]{1,0:T(8,128)(2,1)S(1)}, u32[]{:S(2)}, u32[]{:S(2)}) collective-permute-start(bf16[48,3072]{1,0:T(8,128)(2,1)S(1)} %add_convert_fusion.12), channel_id=1, source_target_pairs={{0,8},{1,9},{2,10},{3,11},{4,12},{5,13},{6,14},{7,15},{8,0},{9,1},... | collective-permute-start | bytes 884744 | tf_op jit(solution)/shard_map/ppermute | solution.py:862
  283.2 7.0 %collective-permute-start.38 = (bf16[1,48,2432]{2,1,0:T(8,128)(2,1)S(1)}, bf16[1,48,2432]{2,1,0:T(8,128)(2,1)S(1)}, u32[]{:S(2)}, u32[]{:S(2)}) collective-permute-start(bf16[1,48,2432]{2,1,0:T(8,128)(2,1)S(1)} %get-tuple-element.260), channel_id=1, source_target_pairs={{0,2},{1,3},{2,0},{3,1},{4,6},{5,7},{6,4},{7,5},{8,10},{9,11},{10,... | collective-permute-start | bytes 700424 | tf_op jit(solution)/shard_map/ppermute | solution.py:773
  284.6 6.7 %collective-permute-start.39 = (bf16[1,48,2432]{2,1,0:T(8,128)(2,1)S(1)}, bf16[1,48,2432]{2,1,0:T(8,128)(2,1)S(1)}, u32[]{:S(2)}, u32[]{:S(2)}) collective-permute-start(bf16[1,48,2432]{2,1,0:T(8,128)(2,1)S(1)} %get-tuple-element.261), channel_id=1, source_target_pairs={{0,4},{1,5},{2,6},{3,7},{4,0},{5,1},{6,2},{7,3},{8,12},{9,13},{10,... | collective-permute-start | bytes 700424 | tf_op jit(solution)/shard_map/ppermute | solution.py:773
  291.7 15.3 %collective-permute-start.41 = (bf16[48,3968]{1,0:T(8,128)(2,1)S(1)}, bf16[48,3968]{1,0:T(8,128)(2,1)S(1)}, u32[]{:S(2)}, u32[]{:S(2)}) collective-permute-start(bf16[48,3968]{1,0:T(8,128)(2,1)S(1)} %get-tuple-element.269), channel_id=1, source_target_pairs={{0,8},{1,9},{2,10},{3,11},{4,12},{5,13},{6,14},{7,15},{8,0},{9,1},... | collective-permute-start | bytes 1142792 | tf_op jit(solution)/shard_map/ppermute | solution.py:862
  294.3 10.7 %collective-permute-start.42 = (bf16[48,3072]{1,0:T(8,128)(2,1)S(1)}, bf16[48,3072]{1,0:T(8,128)(2,1)S(1)}, u32[]{:S(2)}, u32[]{:S(2)}) collective-permute-start(bf16[48,3072]{1,0:T(8,128)(2,1)S(1)} %add_convert_fusion.11), channel_id=1, source_target_pairs={{0,16},{8,24},{16,0},{24,8},{1,17},{9,25},{17,1},{25,9},{2,18},{10... | collective-permute-start | bytes 884744 | tf_op jit(solution)/shard_map/ppermute | solution.py:866
  307.2 22.6 %collective-permute-start.43 = (bf16[48,3968]{1,0:T(8,128)(2,1)S(1)}, bf16[48,3968]{1,0:T(8,128)(2,1)S(1)}, u32[]{:S(2)}, u32[]{:S(2)}) collective-permute-start(bf16[48,3968]{1,0:T(8,128)(2,1)S(1)} %add_convert_fusion.9), channel_id=1, source_target_pairs={{0,16},{8,24},{16,0},{24,8},{1,17},{9,25},{17,1},{25,9},{2,18},{10... | collective-permute-start | bytes 1142792 | tf_op jit(solution)/shard_map/ppermute | solution.py:866
  308.8 21.1 %collective-permute-start.44 = (bf16[48,3072]{1,0:T(8,128)(2,1)S(1)}, bf16[48,3072]{1,0:T(8,128)(2,1)S(1)}, u32[]{:S(2)}, u32[]{:S(2)}) collective-permute-start(bf16[48,3072]{1,0:T(8,128)(2,1)S(1)} %add_convert_fusion.10), channel_id=1, source_target_pairs={{0,8},{1,9},{2,10},{3,11},{4,12},{5,13},{6,14},{7,15},{8,0},{9,1},... | collective-permute-start | bytes 884744 | tf_op jit(solution)/shard_map/ppermute | solution.py:862
  330.0 7.7 %collective-permute-start.45 = (bf16[48,3968]{1,0:T(8,128)(2,1)S(1)}, bf16[48,3968]{1,0:T(8,128)(2,1)S(1)}, u32[]{:S(2)}, u32[]{:S(2)}) collective-permute-start(bf16[48,3968]{1,0:T(8,128)(2,1)S(1)} %add_convert_fusion.8), channel_id=1, source_target_pairs={{0,8},{1,9},{2,10},{3,11},{4,12},{5,13},{6,14},{7,15},{8,0},{9,1},... | collective-permute-start | bytes 1142792 | tf_op jit(solution)/shard_map/ppermute | solution.py:862
  (49 other events, 335.4 us)

commit v6 on v5

--- a/solution.py
+++ b/solution.py
@@ -136,8 +136,7 @@
 
 
 def piece_views(bufs):
-    rows = bufs[2].shape[0]
-    return [b.at[k * rows : (k + 1) * rows] for b in bufs for k in range(b.shape[0] // rows)]
+    return list(bufs)
 
 
 def rows_at(place, rows, share=1, k=0):
@@ -785,16 +784,12 @@
     return permute(value, lambda s: s ^ 4)
 
 
-def gather_start(own):
-    return jnp.concatenate([own, to_sibling(own)], axis=0)
-
-
-def gather_hop(both):
-    return permute(both, lambda s: s ^ (2 if s % 2 == 0 else 4))
-
-
-def gather_second(hop):
-    return permute(hop[: hop.shape[0] // 2], lambda s: s ^ (4 if s % 2 == 0 else 2))
+def near_hop(value):
+    return permute(value, lambda s: s ^ (2 if s % 2 == 0 else 4))
+
+
+def far_hop(value):
+    return permute(value, lambda s: s ^ (4 if s % 2 == 0 else 2))
 
 
 def places(s):
@@ -899,24 +894,25 @@
         own_t = jnp.concatenate([own_t, jnp.pad(narrow, ((0, part - narrow.shape[0]), (0, 0)))], axis=1)
         own_f = jnp.concatenate([hidden_expand] + [hidden_reduce[k * part : (k + 1) * part] for k in range(share)], axis=1)
         net = Layer(clips * FRAMES * BLOCK, columns, units, shards, pieced, places(mine))
-        both_t = gather_start(own_t)
-        both_t, video, own_s, own_f = tie(both_t, video, own_s, own_f)
-        hop_t = gather_hop(both_t)
+        pair_t = to_sibling(own_t)
+        pair_t, own_t, video, own_s, own_f = tie(pair_t, own_t, video, own_s, own_f)
+        hop_t = (near_hop(own_t), near_hop(pair_t))
         x = pack_rows(video[:, 0], False)
-        both_s, both_f = gather_start(own_s), gather_start(own_f)
-        hop_t, both_s, both_f, x = tie(hop_t, both_s, both_f, x)
-        second_t, both_s, both_f = tie(gather_second(hop_t), both_s, both_f)
-        wt = (both_t, hop_t, second_t, to_sibling(hop_t), to_sibling(second_t))
-        hop_s, hop_f = gather_hop(both_s), gather_hop(both_f)
+        pair_s, pair_f = to_sibling(own_s), to_sibling(own_f)
+        first_t, x, pair_s, pair_f = tie(hop_t[0], x, pair_s, pair_f)
+        second_t, own_s, own_f, pair_s, pair_f = tie(far_hop(first_t), own_s, own_f, pair_s, pair_f)
+        gone_t = tuple(to_sibling(v) for v in (first_t, hop_t[1], second_t))
+        wt = (own_t, pair_t, first_t, hop_t[1], second_t, *gone_t)
+        hop_s, hop_f = ((near_hop(own), near_hop(pair)) for own, pair in ((own_s, pair_s), (own_f, pair_f)))
         normed_t, qkv_t, o_t, e_t, p_t, y, small, hb = net.time_forward(x, (), wt)
-        hop_s, y, cotangent = tie(hop_s, y, cotangent)
+        first_s, y, cotangent = tie(hop_s[0], y, cotangent)
         g = pack_rows(cotangent[:, 0] * flags, True)
-        second_s = gather_second(hop_s)
-        ws = (both_s, hop_s, second_s, to_sibling(hop_s), to_sibling(second_s))
-        hop_f, y, ws, g = tie(hop_f, y, ws, g)
+        second_s = far_hop(first_s)
+        ws = (own_s, pair_s, first_s, hop_s[1], second_s, *(to_sibling(v) for v in (first_s, hop_s[1], second_s)))
+        first_f, y, ws, g = tie(hop_f[0], y, ws, g)
         normed_s, qkv_s, p_s, o_s, z = net.space_forward(y, small, ws)
-        second_f, z = tie(gather_second(hop_f), z)
-        wf = (both_f, hop_f, second_f, to_sibling(hop_f), to_sibling(second_f))
+        second_f, last_f, z = tie(far_hop(first_f), hop_f[1], z)
+        wf = (own_f, pair_f, first_f, last_f, second_f, *(to_sibling(v) for v in (first_f, last_f, second_f)))
     else:
         x, g = pack_rows(video[:, 0], False), pack_rows(cotangent[:, 0] * flags, True)
         net = Layer(clips * FRAMES * BLOCK, columns, units, shards, pieced, jnp.zeros((16,), jnp.int32))
@@ -978,18 +974,17 @@
         held_e = total(held_e, got_e)
         sent = [beside(last, both) for last, both in zip(sum_m.second(), sum_t.first())]
         held_s, sent_s = split_groups(sum_s.finish(), even)
-        sent, held_s, sent_s, held_e = tie(sent, held_s, sent_s, held_e)
+        sent, held_s, sent_s, held_e, gx, out = tie(sent, held_s, sent_s, held_e, gx, out)
         came_x, came_y = along_x(sent[0]), along_y(sent[1])
         got_s, got_e = swap_z(sent_s), swap_z(held_e)
-        came_x, came_y, got_s = tie(came_x, came_y, got_s)
         hand_over((came_x, came_y), sum_m, sum_t)
         sum_t.cross_again(tie(*sum_t.second()))
         held_s = total(held_s, got_s)
-        sum_t.last_x, sum_t.last_y, held_s = tie(sum_t.last_x, sum_t.last_y, held_s)
+        got_s = across_pairs(held_s)
         halves = [jnp.concatenate(pair, axis=1) for pair in zip(sum_m.finish(), sum_t.finish())]
         held_t, sent_t = split_groups(halves, even)
-        sent_t, held_t, held_s, got_e = tie(sent_t, held_t, held_s, got_e)
-        got_t, got_s = swap_z(sent_t), across_pairs(held_s)
+        sent_t, held_t, got_e = tie(sent_t, held_t, got_e)
+        got_t = swap_z(sent_t)
         got_t, got_s = tie(got_t, got_s)
         held_t, held_s = tie(total(held_t, got_t), total(held_s, got_s))
         got_t, got_s = across_pairs(held_t), swap_z(held_s)

time: 347 us -> 332 us (0.957)
  starting transfers between devices: 57.1 us -> 49.4 us
  waiting for transfers between devices: 84.4 us -> 78.9 us
    ppermute x8, starting transfers between devices: 22.1 us -> 8.68 us  [swap_z(): return lax.ppermute(value, BOTH, pairs)]
    ppermute x34 -> x40, waiting for transfers between devices: 59.1 us -> 47.2 us  [permute(): return lax.ppermute(value, BOTH, pairs)]
    ppermute x4, waiting for transfers between devices: 5.49 us -> 11.9 us  [across_pairs(): return lax.ppermute(value, 'grp', [(z, z ^ 2) for z in range(4)])]
    ppermute x34 -> x40, starting transfers between devices: 27.9 us -> 33.6 us  [permute(): return lax.ppermute(value, BOTH, pairs)]
    slice x3 -> x0, local copies, waits for them, and re-layouts: 3.63 us -> none  [gather_second(): hop[:hop.shape[0] // 2]]
    unnamed x112 -> x136, local copies, waits for them, and re-layouts: 9.58 us -> 11.7 us
  transfers between devices with their start and end apart: 46 -> 52, of which waited for: 19 -> 21; matrix products, arithmetic and copies ran while one was open for 12% -> 13% of each run, Pallas kernels for 32% -> 33%
where the time goes in v6:
time: 332 us; the launch traced here: 328 us
  Pallas kernels  137 us (41%)
  waiting for transfers between devices  78.9 us (24%)
  starting transfers between devices  49.4 us (15%)
  other arithmetic  40.8 us (12%)
  local copies, waits for them, and re-layouts  20 us (6%)
    pallas_call x9, Pallas kernels, call(): pl.pallas_call(kernel, out_shape=[jax.ShapeDtypeStruct(s, d) for s, d in...  137 us
    ppermute x40, waiting for transfers between devices, permute(): return lax.ppermute(value, BOTH, pairs)  47.2 us
    ppermute x40, starting transfers between devices, permute(): return lax.ppermute(value, BOTH, pairs)  33.6 us
    ppermute x8, waiting for transfers between devices, swap_z(): return lax.ppermute(value, BOTH, pairs)  19.8 us
    ppermute x4, waiting for transfers between devices, across_pairs(): return lax.ppermute(value, 'grp', [(z, z ^ 2) for z in range(4)])  11.9 us
    unnamed x136, local copies, waits for them, and re-layouts  11.7 us
    another operation x4, other arithmetic, pack_rows(): return jnp.stack(frames, axis=1).reshape(clips * FRAMES * BLOCK, columns)  9.78 us
    convert_element_type x18, other arithmetic, total(): return sum((t.astype(F32) for t in terms)).astype(BF)  9.12 us
  transfers between devices with their start and end apart: 52, of which 21 were waited for; matrix products, arithmetic and copies ran while one was open for 13% of the time, Pallas kernels for 33%

profile of v6, /device:TPU:0, one launch (start us, length us, event | category | flops | bytes accessed | tf_op | source)
XLA Modules:
  0.0 328.3 jit_solution(6449503774553435446)
XLA Ops:
  6.5 2.9 collective-permute-start.1
  10.2 3.2 fusion.4
  13.5 1.8 pad_maximum_fusion
  16.5 2.7 collective-permute-done.1.refs_4_.refs_6_.refs_14_
  20.2 2.1 collective-permute-start.4
  22.2 9.7 %collective-permute-done.7.refs_5_.refs_7_.refs_15_ = bf16[96,3968]{1,0:T(8,128)(2,1)} collective-permute-done((bf16[96,3968]{1,0:T(8,128)(2,1)S(1)}, bf16[96,3968]{1,0:T(8,128)(2,1)}, u32[]{:S(2)}, u32[]{:S(2)}) %collective-permute-start.7) | collective-permute-done | bytes 761888 | tf_op jit(solution)/shard_map/ppermute | solution.py:772
  32.4 2.6 collective-permute-done.4.refs_6_.refs_8_.refs_16_
  36.0 2.0 collective-permute-start.6
  38.1 2.0 collective-permute-start.5
  40.2 14.1 %time_forward.1 = (bf16[832,768]{1,0:T(8,128)(2,1)}, bf16[832,2304]{1,0:T(8,128)(2,1)}, bf16[832,768]{1,0:T(8,128)(2,1)}, bf16[832,768]{1,0:T(8,128)(2,1)}, f32[...) custom-call(s32[16]{0:T(128)} %stack.76.refs_0_, bf16[832,768]{1,0:T(8,128)(2,1)} %bitcast.65, ...), custom_call_target="tpu_custom_call" | custom-call | flops 56000000000 | tf_op jit(solution)/shard_map/time_forward/pallas_call | solution.py:284
  54.3 1.6 collective-permute-start.12
  57.2 2.4 bitcast_multiply_fusion
  60.5 10.3 %collective-permute-done.12.refs_7_.refs_10_.refs_9_ = bf16[96,3072]{1,0:T(8,128)(2,1)S(1)} collective-permute-done((bf16[96,3072]{1,0:T(8,128)(2,1)}, bf16[96,3072]{1,0:T(8,128)(2,1)S(1)}, u32[]{:S(2)}, u32[]{:S(2)}) %collective-permute-start.12) | collective-permute-done | bytes 589856 | tf_op jit(solution)/shard_map/ppermute | solution.py:772
  71.2 2.9 maximum_bitcast_fusion.1
  74.2 1.8 pad_maximum_fusion.1
  80.0 16.8 %space_forward.1 = (bf16[832,768]{1,0:T(8,128)(2,1)}, bf16[832,2304]{1,0:T(8,128)(2,1)}, bf16[48,208,208]{2,1,0:T(8,128)(2,1)}, bf16[832,768]{1,0:T(8,128)(2,1)}, f32[832,768]{1,0:T(8,128)}) custom-call(s32[16]{0:T(128)} %stack.76.refs_0_, f32[832,768]{1,0:T(8,128)} %get-tuple-element.167.refs_1_.refs_2_, ...), custom_call_target="tpu_custom_call" | custom-call | flops 64000000000 | tf_op jit(solution)/shard_map/space_forward/pallas_call | solution.py:284
  97.5 3.6 %collective-permute-done.19.refs_11_ = bf16[96,6144]{1,0:T(8,128)(2,1)} collective-permute-done((bf16[96,6144]{1,0:T(8,128)(2,1)}, bf16[96,6144]{1,0:T(8,128)(2,1)}, u32[]{:S(2)}, u32[]{:S(2)}) %collective-permute-start.19) | collective-permute-done | bytes 1179680 | tf_op jit(solution)/shard_map/ppermute | solution.py:772
  101.6 28.0 %feed_out.1 = (bf16[832,768]{1,0:T(8,128)(2,1)}, bf16[832,768]{1,0:T(8,128)(2,1)}, bf16[832,3072]{1,0:T(8,128)(2,1)}, bf16[8,48,3072]{2,1,0:T(8,128)(2,1)}, bf16[8,48,3072]{2,1,0:T(8,128)(2,1)}) custom-call(s32[16]{0:T(128)} %stack.76.refs_0_, f32[832,768]{1,0:T(8,128)} %get-tuple-element.178.refs_1_.refs_2_, bf16[832,768]{1,0:T(8,128)(2,1)} %bitcast.67, ...), custom_call_target="tpu_custom_call" | custom-call | flops 120000004096 | tf_op jit(solution)/shard_map/feed_out/pallas_call | solution.py:284
  129.8 2.4 copy-done.28
  133.6 7.4 %feed_in.1 = (f32[8,768]{1,0:T(8,128)S(1)}, f32[8,3072]{1,0:T(8,128)S(1)}, bf16[8,48,3072]{2,1,0:T(8,128)(2,1)S(1)}, bf16[8,48,3072]{2,1,0:T(8,128)(2,1)S(1)}) custom-call(s32[16]{0:T(128)S(1)} %copy-done.8, bf16[832,3072]{1,0:T(8,128)(2,1)S(1)} %copy-done.28, bf16[832,768]{1,0:T(8,128)(2,1)S(1)} %copy-done.39, bf16[832,768]{1,0:T(8,128)(2,1)S(1)} %bitcast.68), custom_call_target="tpu_custom_call" | custom-call | flops 32000000000 | tf_op jit(solution)/shard_map/feed_in/pallas_call | solution.py:284
  144.7 9.2 %feed_norm.1 = (f32[832,768]{1,0:T(8,128)S(1)}, f32[8,768]{1,0:T(8,128)S(1)}) custom-call(s32[16]{0:T(128)S(1)} %copy-done.8, bf16[832,3072]{1,0:T(8,128)(2,1)S(1)} %copy-done.29, f32[832,768]{1,0:T(8,128)S(1)} %copy-done.35, bf16[832,768]{1,0:T(8,128)(2,1)S(1)} %bitcast.69, f32[32,768]{1,0:T(8,128)S(1)} %copy-done.44, bf16[96,6144]{1,0:T(8,128)(2,1)S(1)} %copy-done.7, ...), custom_call_target="tpu_custom_call" | custom-call | flops 40000000000 | tf_op jit(solution)/shard_map/feed_norm/pallas_call | solution.py:284
  153.9 2.5 add_convert_fusion.2
  159.3 1.6 collective-permute-start.25
  161.6 21.2 %space_backward.1 = (bf16[832,2304]{1,0:T(8,128)(2,1)S(1)}, f32[8,768]{1,0:T(8,128)S(1)}, bf16[8,48,3072]{2,1,0:T(8,128)(2,1)S(1)}, bf16[8,48,3072]{2,1,0:T(8,128)(2,1)S(1)}) custom-call(s32[16]{0:T(128)S(1)} %copy-done.8, f32[832,768]{1,0:T(8,128)S(1)} %get-tuple-element.199.refs_1_.refs_3_, bf16[832,768]{1,0:T(8,128)(2,1)S(1)} %copy-done.41, ...), custom_call_target="tpu_custom_call" | custom-call | flops 80000000000 | tf_op jit(solution)/shard_map/space_backward/pallas_call | solution.py:284
  182.7 1.9 copy-done.31
  185.6 1.9 select_bitcast_fusion.4
  187.6 1.6 add_convert_fusion.24
  189.2 1.6 collective-permute-start.27
  192.9 7.7 %space_norm.1 = (f32[832,768]{1,0:T(8,128)S(1)}, f32[8,768]{1,0:T(8,128)S(1)}) custom-call(s32[16]{0:T(128)S(1)} %copy-done.8, bf16[832,2304]{1,0:T(8,128)(2,1)S(1)} %copy-done.32, f32[832,768]{1,0:T(8,128)S(1)} %copy-done.36, f32[832,768]{1,0:T(8,128)S(1)} %copy-done.34, f32[32,768]{1,0:T(8,128)S(1)} %copy-done.44, bf16[96,3072]{1,0:T(8,128)(2,1)S(1)} %copy-done.5, ...), custom_call_target="tpu_custom_call" | custom-call | flops 40000000000 | tf_op jit(solution)/shard_map/space_norm/pallas_call | solution.py:284
  201.3 1.8 select_bitcast_fusion.2
  203.2 1.8 add_convert_fusion
  205.5 2.6 collective-permute-start.31
  210.2 13.2 %mixer_backward.1 = (bf16[832,768]{1,0:T(8,128)(2,1)S(1)}, f32[8,768]{1,0:T(8,128)S(1)}, bf16[8,48,1536]{2,1,0:T(8,128)(2,1)S(1)}, bf16[8,48,1536]{2,1,0:T(8,128)(2,1)S(1)}) custom-call(s32[16]{0:T(128)S(1)} %copy-done.8, f32[832,768]{1,0:T(8,128)S(1)} %get-tuple-element.225.refs_1_.refs_6_, bf16[832,768]{1,0:T(8,128)(2,1)S(1)} %copy-done.37, ...), custom_call_target="tpu_custom_call" | custom-call | flops 32000000000 | tf_op jit(solution)/shard_map/mixer_backward/pallas_call | solution.py:284
  226.7 1.6 collective-permute-start.38
  230.6 19.6 %time_backward.1 = (bf16[832,768]{1,0:T(8,128)(2,1)S(1)}, f32[8,768]{1,0:T(8,128)}, bf16[8,48,2432]{2,1,0:T(8,128)(2,1)S(1)}, bf16[8,48,2432]{2,1,0:T(8,128)(2,1)S(1)}) custom-call(s32[16]{0:T(128)S(1)} %copy-done.8, bf16[832,768]{1,0:T(8,128)(2,1)S(1)} %get-tuple-element.243.refs_1_, bf16[832,2304]{1,0:T(8,128)(2,1)} %get-tuple-element.244.refs_2_, ...), custom_call_target="tpu_custom_call" | custom-call | flops 80000000000 | tf_op jit(solution)/shard_map/time_backward/pallas_call | solution.py:284
  258.8 1.6 collective-permute-start.45
  261.3 2.8 maximum_multiply_fusion
  264.2 6.8 %collective-permute-done.41 = bf16[1,48,6400]{2,1,0:T(8,128)(2,1)S(1)} collective-permute-done((bf16[1,48,6400]{2,1,0:T(8,128)(2,1)S(1)}, bf16[1,48,6400]{2,1,0:T(8,128)(2,1)S(1)}, u32[]{:S(2)}, u32[]{:S(2)}) %collective-permute-start.41) | collective-permute-done | bytes 614432 | tf_op jit(solution)/shard_map/ppermute | solution.py:772
  273.0 1.6 collective-permute-start.44
  274.7 3.7 %collective-permute-done.43 = bf16[1,48,2432]{2,1,0:T(8,128)(2,1)S(1)} collective-permute-done((bf16[1,48,2432]{2,1,0:T(8,128)(2,1)S(1)}, bf16[1,48,2432]{2,1,0:T(8,128)(2,1)S(1)}, u32[]{:S(2)}, u32[]{:S(2)}) %collective-permute-start.43) | collective-permute-done | bytes 233504 | tf_op jit(solution)/shard_map/ppermute | solution.py:772
  280.3 2.6 collective-permute-start.48
  283.0 2.6 maximum_bitcast_fusion
  285.6 7.1 %collective-permute-done.48 = bf16[48,3072]{1,0:T(8,128)(2,1)S(1)} collective-permute-done((bf16[48,3072]{1,0:T(8,128)(2,1)S(1)}, bf16[48,3072]{1,0:T(8,128)(2,1)S(1)}, u32[]{:S(2)}, u32[]{:S(2)}) %collective-permute-start.48) | collective-permute-done | bytes 294944 | tf_op jit(solution)/shard_map/ppermute | solution.py:861
  292.7 2.0 collective-permute-done.46
  296.4 2.2 collective-permute-start.50
  299.7 8.8 %collective-permute-done.50 = bf16[48,3072]{1,0:T(8,128)(2,1)S(1)} collective-permute-done((bf16[48,3072]{1,0:T(8,128)(2,1)S(1)}, bf16[48,3072]{1,0:T(8,128)(2,1)S(1)}, u32[]{:S(2)}, u32[]{:S(2)}) %collective-permute-start.50) | collective-permute-done | bytes 294944 | tf_op jit(solution)/shard_map/ppermute | solution.py:857
  308.5 4.8 %collective-permute-done.49 = bf16[48,3968]{1,0:T(8,128)(2,1)S(1)} collective-permute-done((bf16[48,3968]{1,0:T(8,128)(2,1)S(1)}, bf16[48,3968]{1,0:T(8,128)(2,1)S(1)}, u32[]{:S(2)}, u32[]{:S(2)}) %collective-permute-start.49) | collective-permute-done | bytes 380960 | tf_op jit(solution)/shard_map/ppermute | solution.py:861
  315.3 9.0 %collective-permute-done.51 = bf16[48,3968]{1,0:T(8,128)(2,1)S(1)} collective-permute-done((bf16[48,3968]{1,0:T(8,128)(2,1)S(1)}, bf16[48,3968]{1,0:T(8,128)(2,1)S(1)}, u32[]{:S(2)}, u32[]{:S(2)}) %collective-permute-start.51) | collective-permute-done | bytes 380960 | tf_op jit(solution)/shard_map/ppermute | solution.py:857
  (290 shorter events, 60.6 us)
Async XLA Ops:
  5.8 13.3 %collective-permute-start.3 = (bf16[96,6144]{1,0:T(8,128)(2,1)S(1)}, bf16[96,6144]{1,0:T(8,128)(2,1)S(1)}, u32[]{:S(2)}, u32[]{:S(2)}) collective-permute-start(bf16[96,6144]{1,0:T(8,128)(2,1)S(1)} %slice_dynamic-update-slice_fusion.refs_5_), channel_id=1, source_target_pairs={{0,1},{1,0},{2,3},{3,2},{4,5},{5,4},{6,7},{7,6},{8,9},{9,8},{10,11... | collective-permute-start | bytes 3538952 | tf_op jit(solution)/shard_map/ppermute | solution.py:772
  6.3 10.2 %collective-permute-start.2 = (bf16[96,3072]{1,0:T(8,128)(2,1)S(1)}, bf16[96,3072]{1,0:T(8,128)(2,1)}, u32[]{:S(2)}, u32[]{:S(2)}) collective-permute-start(bf16[96,3072]{1,0:T(8,128)(2,1)S(1)} %pad_maximum_fusion.9.refs_3_.refs_6_.refs_5_), channel_id=1, source_target_pairs={{0,1},{1,0},{2,3},{3,2},{4,5},{5,4},{6,7},{7,6},{8,9},{9,8},{10,11... | collective-permute-start | bytes 1769480 | tf_op jit(solution)/shard_map/ppermute | solution.py:772
  6.5 12.7 %collective-permute-start.1 = (bf16[96,3968]{1,0:T(8,128)(2,1)S(1)}, bf16[96,3968]{1,0:T(8,128)(2,1)}, u32[]{:S(2)}, u32[]{:S(2)}) collective-permute-start(bf16[96,3968]{1,0:T(8,128)(2,1)S(1)} %fusion.1.refs_2_.refs_4_.refs_12_), channel_id=1, source_target_pairs={{0,2},{1,5},{2,0},{3,7},{4,6},{5,1},{6,4},{7,3},{8,10},{9,13},{10,... | collective-permute-start | bytes 2285576 | tf_op jit(solution)/shard_map/ppermute | solution.py:772
  9.4 22.5 %collective-permute-start.7 = (bf16[96,3968]{1,0:T(8,128)(2,1)S(1)}, bf16[96,3968]{1,0:T(8,128)(2,1)}, u32[]{:S(2)}, u32[]{:S(2)}) collective-permute-start(bf16[96,3968]{1,0:T(8,128)(2,1)S(1)} %collective-permute-done.refs_3_.refs_5_.refs_13_), channel_id=1, source_target_pairs={{0,2},{1,5},{2,0},{3,7},{4,6},{5,1},{6,4},{7,3},{8,10},{9,13},{10,... | collective-permute-start | bytes 2285576 | tf_op jit(solution)/shard_map/ppermute | solution.py:772
  20.2 14.8 %collective-permute-start.4 = (bf16[96,3968]{1,0:T(8,128)(2,1)}, bf16[96,3968]{1,0:T(8,128)(2,1)}, u32[]{:S(2)}, u32[]{:S(2)}) collective-permute-start(bf16[96,3968]{1,0:T(8,128)(2,1)} %collective-permute-done.1.refs_4_.refs_6_.refs_14_), channel_id=1, source_target_pairs={{0,4},{1,3},{2,6},{3,1},{4,0},{5,7},{6,2},{7,5},{8,12},{9,11},{10,... | collective-permute-start | bytes 2285576 | tf_op jit(solution)/shard_map/ppermute | solution.py:772
  31.9 6.2 %collective-permute-start.9 = (bf16[96,3968]{1,0:T(8,128)(2,1)}, bf16[96,3968]{1,0:T(8,128)(2,1)S(1)}, u32[]{:S(2)}, u32[]{:S(2)}) collective-permute-start(bf16[96,3968]{1,0:T(8,128)(2,1)} %collective-permute-done.7.refs_5_.refs_7_.refs_15_), channel_id=1, source_target_pairs={{0,1},{1,0},{2,3},{3,2},{4,5},{5,4},{6,7},{7,6},{8,9},{9,8},{10,11... | collective-permute-start | bytes 2285576 | tf_op jit(solution)/shard_map/ppermute | solution.py:772
  31.9 8.2 %collective-permute-start.8 = (bf16[96,3968]{1,0:T(8,128)(2,1)}, bf16[96,3968]{1,0:T(8,128)(2,1)}, u32[]{:S(2)}, u32[]{:S(2)}) collective-permute-start(bf16[96,3968]{1,0:T(8,128)(2,1)} %collective-permute-done.1.refs_4_.refs_6_.refs_14_), channel_id=1, source_target_pairs={{0,1},{1,0},{2,3},{3,2},{4,5},{5,4},{6,7},{7,6},{8,9},{9,8},{10,11... | collective-permute-start | bytes 2285576 | tf_op jit(solution)/shard_map/ppermute | solution.py:772
  35.0 5.2 %collective-permute-start.10 = (bf16[96,3968]{1,0:T(8,128)(2,1)}, bf16[96,3968]{1,0:T(8,128)(2,1)}, u32[]{:S(2)}, u32[]{:S(2)}) collective-permute-start(bf16[96,3968]{1,0:T(8,128)(2,1)} %collective-permute-done.4.refs_6_.refs_8_.refs_16_), channel_id=1, source_target_pairs={{0,1},{1,0},{2,3},{3,2},{4,5},{5,4},{6,7},{7,6},{8,9},{9,8},{10,11... | collective-permute-start | bytes 2285576 | tf_op jit(solution)/shard_map/ppermute | solution.py:772
  36.0 18.2 %collective-permute-start.6 = (bf16[96,3072]{1,0:T(8,128)(2,1)S(1)}, bf16[96,3072]{1,0:T(8,128)(2,1)}, u32[]{:S(2)}, u32[]{:S(2)}) collective-permute-start(bf16[96,3072]{1,0:T(8,128)(2,1)S(1)} %pad_maximum_fusion.9.refs_3_.refs_6_.refs_5_), channel_id=1, source_target_pairs={{0,2},{1,5},{2,0},{3,7},{4,6},{5,1},{6,4},{7,3},{8,10},{9,13},{10,... | collective-permute-start | bytes 1769480 | tf_op jit(solution)/shard_map/ppermute | solution.py:772
  38.0 18.7 %collective-permute-start.11 = (bf16[96,3072]{1,0:T(8,128)(2,1)}, bf16[96,3072]{1,0:T(8,128)(2,1)}, u32[]{:S(2)}, u32[]{:S(2)}) collective-permute-start(bf16[96,3072]{1,0:T(8,128)(2,1)} %collective-permute-done.2.refs_4_.refs_7_.refs_6_), channel_id=1, source_target_pairs={{0,2},{1,5},{2,0},{3,7},{4,6},{5,1},{6,4},{7,3},{8,10},{9,13},{10,... | collective-permute-start | bytes 1769480 | tf_op jit(solution)/shard_map/ppermute | solution.py:772
  38.1 39.1 %collective-permute-start.5 = (bf16[96,6144]{1,0:T(8,128)(2,1)S(1)}, bf16[96,6144]{1,0:T(8,128)(2,1)}, u32[]{:S(2)}, u32[]{:S(2)}) collective-permute-start(bf16[96,6144]{1,0:T(8,128)(2,1)S(1)} %slice_dynamic-update-slice_fusion.refs_5_), channel_id=1, source_target_pairs={{0,2},{1,5},{2,0},{3,7},{4,6},{5,1},{6,4},{7,3},{8,10},{9,13},{10,... | collective-permute-start | bytes 3538952 | tf_op jit(solution)/shard_map/ppermute | solution.py:772
  54.3 16.5 %collective-permute-start.12 = (bf16[96,3072]{1,0:T(8,128)(2,1)}, bf16[96,3072]{1,0:T(8,128)(2,1)S(1)}, u32[]{:S(2)}, u32[]{:S(2)}) collective-permute-start(bf16[96,3072]{1,0:T(8,128)(2,1)} %collective-permute-done.6.refs_5_.refs_8_.refs_7_), channel_id=1, source_target_pairs={{0,4},{1,3},{2,6},{3,1},{4,0},{5,7},{6,2},{7,5},{8,12},{9,11},{10,... | collective-permute-start | bytes 1769480 | tf_op jit(solution)/shard_map/ppermute | solution.py:772
  55.9 40.9 %collective-permute-start.17 = (bf16[96,6144]{1,0:T(8,128)(2,1)S(1)}, bf16[96,6144]{1,0:T(8,128)(2,1)}, u32[]{:S(2)}, u32[]{:S(2)}) collective-permute-start(bf16[96,6144]{1,0:T(8,128)(2,1)S(1)} %copy-done.10), channel_id=1, source_target_pairs={{0,2},{1,5},{2,0},{3,7},{4,6},{5,1},{6,4},{7,3},{8,10},{9,13},{10,... | collective-permute-start | bytes 3538952 | tf_op jit(solution)/shard_map/ppermute | solution.py:772
  56.7 20.5 %collective-permute-start.14 = (bf16[96,3072]{1,0:T(8,128)(2,1)}, bf16[96,3072]{1,0:T(8,128)(2,1)S(1)}, u32[]{:S(2)}, u32[]{:S(2)}) collective-permute-start(bf16[96,3072]{1,0:T(8,128)(2,1)} %collective-permute-done.11.refs_6_.refs_9_.refs_8_), channel_id=1, source_target_pairs={{0,1},{1,0},{2,3},{3,2},{4,5},{5,4},{6,7},{7,6},{8,9},{9,8},{10,11... | collective-permute-start | bytes 1769480 | tf_op jit(solution)/shard_map/ppermute | solution.py:772
  56.7 20.5 %collective-permute-start.13 = (bf16[96,3072]{1,0:T(8,128)(2,1)}, bf16[96,3072]{1,0:T(8,128)(2,1)S(1)}, u32[]{:S(2)}, u32[]{:S(2)}) collective-permute-start(bf16[96,3072]{1,0:T(8,128)(2,1)} %collective-permute-done.6.refs_5_.refs_8_.refs_7_), channel_id=1, source_target_pairs={{0,1},{1,0},{2,3},{3,2},{4,5},{5,4},{6,7},{7,6},{8,9},{9,8},{10,11... | collective-permute-start | bytes 1769480 | tf_op jit(solution)/shard_map/ppermute | solution.py:772
  70.8 6.5 %collective-permute-start.15 = (bf16[96,3072]{1,0:T(8,128)(2,1)S(1)}, bf16[96,3072]{1,0:T(8,128)(2,1)S(1)}, u32[]{:S(2)}, u32[]{:S(2)}) collective-permute-start(bf16[96,3072]{1,0:T(8,128)(2,1)S(1)} %collective-permute-done.12.refs_7_.refs_10_.refs_9_), channel_id=1, source_target_pairs={{0,1},{1,0},{2,3},{3,2},{4,5},{5,4},{6,7},{7,6},{8,9},{9,8},{10,11... | collective-permute-start | bytes 1769480 | tf_op jit(solution)/shard_map/ppermute | solution.py:772
  78.1 19.4 %collective-permute-start.18 = (bf16[96,6144]{1,0:T(8,128)(2,1)}, bf16[96,6144]{1,0:T(8,128)(2,1)S(1)}, u32[]{:S(2)}, u32[]{:S(2)}) collective-permute-start(bf16[96,6144]{1,0:T(8,128)(2,1)} %collective-permute-done.5.refs_7_), channel_id=1, source_target_pairs={{0,1},{1,0},{2,3},{3,2},{4,5},{5,4},{6,7},{7,6},{8,9},{9,8},{10,11... | collective-permute-start | bytes 3538952 | tf_op jit(solution)/shard_map/ppermute | solution.py:772
  78.5 18.4 %collective-permute-start.16 = (bf16[96,6144]{1,0:T(8,128)(2,1)}, bf16[96,6144]{1,0:T(8,128)(2,1)S(1)}, u32[]{:S(2)}, u32[]{:S(2)}) collective-permute-start(bf16[96,6144]{1,0:T(8,128)(2,1)} %collective-permute-done.5.refs_7_), channel_id=1, source_target_pairs={{0,4},{1,3},{2,6},{3,1},{4,0},{5,7},{6,2},{7,5},{8,12},{9,11},{10,... | collective-permute-start | bytes 3538952 | tf_op jit(solution)/shard_map/ppermute | solution.py:772
  97.0 4.7 %collective-permute-start.20 = (bf16[96,6144]{1,0:T(8,128)(2,1)S(1)}, bf16[96,6144]{1,0:T(8,128)(2,1)}, u32[]{:S(2)}, u32[]{:S(2)}) collective-permute-start(bf16[96,6144]{1,0:T(8,128)(2,1)S(1)} %collective-permute-done.16.refs_9_), channel_id=1, source_target_pairs={{0,1},{1,0},{2,3},{3,2},{4,5},{5,4},{6,7},{7,6},{8,9},{9,8},{10,11... | collective-permute-start | bytes 3538952 | tf_op jit(solution)/shard_map/ppermute | solution.py:772
  129.6 11.9 %collective-permute-start.21 = (bf16[8,48,3072]{2,1,0:T(8,128)(2,1)}, bf16[8,48,3072]{2,1,0:T(8,128)(2,1)S(1)}, u32[]{:S(2)}, u32[]{:S(2)}) collective-permute-start(bf16[8,48,3072]{2,1,0:T(8,128)(2,1)} %get-tuple-element.184), channel_id=1, source_target_pairs={{0,1},{1,0},{2,3},{3,2},{4,5},{5,4},{6,7},{7,6},{8,9},{9,8},{10,11... | collective-permute-start | bytes 7077896 | tf_op jit(solution)/shard_map/ppermute | solution.py:772
  141.0 12.9 %collective-permute-start.24 = (bf16[8,48,3072]{2,1,0:T(8,128)(2,1)S(1)}, bf16[8,48,3072]{2,1,0:T(8,128)(2,1)}, u32[]{:S(2)}, u32[]{:S(2)}) collective-permute-start(bf16[8,48,3072]{2,1,0:T(8,128)(2,1)S(1)} %get-tuple-element.193), channel_id=1, source_target_pairs={{0,1},{1,0},{2,3},{3,2},{4,5},{5,4},{6,7},{7,6},{8,9},{9,8},{10,11... | collective-permute-start | bytes 7077896 | tf_op jit(solution)/shard_map/ppermute | solution.py:772
  141.9 15.4 %collective-permute-start.22 = (bf16[2,48,3072]{2,1,0:T(8,128)(2,1)S(1)}, bf16[2,48,3072]{2,1,0:T(8,128)(2,1)S(1)}, u32[]{:S(2)}, u32[]{:S(2)}) collective-permute-start(bf16[2,48,3072]{2,1,0:T(8,128)(2,1)S(1)} %get-tuple-element.190), channel_id=1, source_target_pairs={{0,2},{1,3},{2,0},{3,1},{4,6},{5,7},{6,4},{7,5},{8,10},{9,11},{10,... | collective-permute-start | bytes 1769480 | tf_op jit(solution)/shard_map/ppermute | solution.py:772
  143.1 15.3 %collective-permute-start.23 = (bf16[2,48,3072]{2,1,0:T(8,128)(2,1)S(1)}, bf16[2,48,3072]{2,1,0:T(8,128)(2,1)S(1)}, u32[]{:S(2)}, u32[]{:S(2)}) collective-permute-start(bf16[2,48,3072]{2,1,0:T(8,128)(2,1)S(1)} %get-tuple-element.191), channel_id=1, source_target_pairs={{0,4},{1,5},{2,6},{3,7},{4,0},{5,1},{6,2},{7,3},{8,12},{9,13},{10,... | collective-permute-start | bytes 1769480 | tf_op jit(solution)/shard_map/ppermute | solution.py:772
  159.3 25.3 %collective-permute-start.25 = (bf16[1,48,9216]{2,1,0:T(8,128)(2,1)S(1)}, bf16[1,48,9216]{2,1,0:T(8,128)(2,1)S(1)}, u32[]{:S(2)}, u32[]{:S(2)}) collective-permute-start(bf16[1,48,9216]{2,1,0:T(8,128)(2,1)S(1)} %pad_maximum_fusion.4), channel_id=1, source_target_pairs={{0,4},{1,5},{2,6},{3,7},{4,0},{5,1},{6,2},{7,3},{8,12},{9,13},{10,... | collective-permute-start | bytes 2654216 | tf_op jit(solution)/shard_map/ppermute | solution.py:772
  160.9 24.7 %collective-permute-start.26 = (bf16[1,48,9216]{2,1,0:T(8,128)(2,1)S(1)}, bf16[1,48,9216]{2,1,0:T(8,128)(2,1)}, u32[]{:S(2)}, u32[]{:S(2)}) collective-permute-start(bf16[1,48,9216]{2,1,0:T(8,128)(2,1)S(1)} %pad_maximum_fusion.3), channel_id=1, source_target_pairs={{0,2},{1,3},{2,0},{3,1},{4,6},{5,7},{6,4},{7,5},{8,10},{9,11},{10,... | collective-permute-start | bytes 2654216 | tf_op jit(solution)/shard_map/ppermute | solution.py:772
  184.7 18.5 %collective-permute-start.30 = (bf16[8,48,3072]{2,1,0:T(8,128)(2,1)S(1)}, bf16[8,48,3072]{2,1,0:T(8,128)(2,1)}, u32[]{:S(2)}, u32[]{:S(2)}) collective-permute-start(bf16[8,48,3072]{2,1,0:T(8,128)(2,1)S(1)} %get-tuple-element.218), channel_id=1, source_target_pairs={{0,1},{1,0},{2,3},{3,2},{4,5},{5,4},{6,7},{7,6},{8,9},{9,8},{10,11... | collective-permute-start | bytes 7077896 | tf_op jit(solution)/shard_map/ppermute | solution.py:772
  189.2 11.4 %collective-permute-start.27 = (bf16[48,3072]{1,0:T(8,128)(2,1)S(1)}, bf16[48,3072]{1,0:T(8,128)(2,1)S(1)}, u32[]{:S(2)}, u32[]{:S(2)}) collective-permute-start(bf16[48,3072]{1,0:T(8,128)(2,1)S(1)} %get-tuple-element.208), channel_id=1, source_target_pairs={{0,8},{1,9},{2,10},{3,11},{4,12},{5,13},{6,14},{7,15},{8,0},{9,1},... | collective-permute-start | bytes 884744 | tf_op jit(solution)/shard_map/ppermute | solution.py:857
  190.9 9.8 %collective-permute-start.28 = (bf16[1,48,3072]{2,1,0:T(8,128)(2,1)S(1)}, bf16[1,48,3072]{2,1,0:T(8,128)(2,1)S(1)}, u32[]{:S(2)}, u32[]{:S(2)}) collective-permute-start(bf16[1,48,3072]{2,1,0:T(8,128)(2,1)S(1)} %get-tuple-element.209), channel_id=1, source_target_pairs={{0,2},{1,3},{2,0},{3,1},{4,6},{5,7},{6,4},{7,5},{8,10},{9,11},{10,... | collective-permute-start | bytes 884744 | tf_op jit(solution)/shard_map/ppermute | solution.py:772
  192.4 8.9 %collective-permute-start.29 = (bf16[1,48,3072]{2,1,0:T(8,128)(2,1)S(1)}, bf16[1,48,3072]{2,1,0:T(8,128)(2,1)S(1)}, u32[]{:S(2)}, u32[]{:S(2)}) collective-permute-start(bf16[1,48,3072]{2,1,0:T(8,128)(2,1)S(1)} %get-tuple-element.210), channel_id=1, source_target_pairs={{0,4},{1,5},{2,6},{3,7},{4,0},{5,1},{6,2},{7,3},{8,12},{9,13},{10,... | collective-permute-start | bytes 884744 | tf_op jit(solution)/shard_map/ppermute | solution.py:772
  204.9 18.6 %collective-permute-start.32 = (bf16[48,3072]{1,0:T(8,128)(2,1)S(1)}, bf16[48,3072]{1,0:T(8,128)(2,1)S(1)}, u32[]{:S(2)}, u32[]{:S(2)}) collective-permute-start(bf16[48,3072]{1,0:T(8,128)(2,1)S(1)} %get-tuple-element.222), channel_id=1, source_target_pairs={{0,8},{1,9},{2,10},{3,11},{4,12},{5,13},{6,14},{7,15},{8,0},{9,1},... | collective-permute-start | bytes 884744 | tf_op jit(solution)/shard_map/ppermute | solution.py:857
  205.5 18.1 %collective-permute-start.31 = (bf16[48,3072]{1,0:T(8,128)(2,1)S(1)}, bf16[48,3072]{1,0:T(8,128)(2,1)S(1)}, u32[]{:S(2)}, u32[]{:S(2)}) collective-permute-start(bf16[48,3072]{1,0:T(8,128)(2,1)S(1)} %add_convert_fusion.23), channel_id=1, source_target_pairs={{0,16},{8,24},{16,0},{24,8},{1,17},{9,25},{17,1},{25,9},{2,18},{10... | collective-permute-start | bytes 884744 | tf_op jit(solution)/shard_map/ppermute | solution.py:861
  208.0 15.5 %collective-permute-start.33 = (bf16[2,48,3072]{2,1,0:T(8,128)(2,1)S(1)}, bf16[2,48,3072]{2,1,0:T(8,128)(2,1)S(1)}, u32[]{:S(2)}, u32[]{:S(2)}) collective-permute-start(bf16[2,48,3072]{2,1,0:T(8,128)(2,1)S(1)} %get-tuple-element.223), channel_id=1, source_target_pairs={{0,2},{1,3},{2,0},{3,1},{4,6},{5,7},{6,4},{7,5},{8,10},{9,11},{10,... | collective-permute-start | bytes 1769480 | tf_op jit(solution)/shard_map/ppermute | solution.py:772
  208.9 14.7 %collective-permute-start.34 = (bf16[2,48,3072]{2,1,0:T(8,128)(2,1)S(1)}, bf16[2,48,3072]{2,1,0:T(8,128)(2,1)S(1)}, u32[]{:S(2)}, u32[]{:S(2)}) collective-permute-start(bf16[2,48,3072]{2,1,0:T(8,128)(2,1)S(1)} %get-tuple-element.224), channel_id=1, source_target_pairs={{0,4},{1,5},{2,6},{3,7},{4,0},{5,1},{6,2},{7,3},{8,12},{9,13},{10,... | collective-permute-start | bytes 1769480 | tf_op jit(solution)/shard_map/ppermute | solution.py:772
  226.7 23.5 %collective-permute-start.38 = (bf16[48,3072]{1,0:T(8,128)(2,1)S(1)}, bf16[48,3072]{1,0:T(8,128)(2,1)S(1)}, u32[]{:S(2)}, u32[]{:S(2)}) collective-permute-start(bf16[48,3072]{1,0:T(8,128)(2,1)S(1)} %add_convert_fusion.20), channel_id=1, source_target_pairs={{0,8},{1,9},{2,10},{3,11},{4,12},{5,13},{6,14},{7,15},{8,0},{9,1},... | collective-permute-start | bytes 884744 | tf_op jit(solution)/shard_map/ppermute | solution.py:857
  228.3 21.9 %collective-permute-start.39 = (bf16[48,3072]{1,0:T(8,128)(2,1)S(1)}, bf16[48,3072]{1,0:T(8,128)(2,1)S(1)}, u32[]{:S(2)}, u32[]{:S(2)}) collective-permute-start(bf16[48,3072]{1,0:T(8,128)(2,1)S(1)} %add_convert_fusion.19), channel_id=1, source_target_pairs={{0,16},{8,24},{16,0},{24,8},{1,17},{9,25},{17,1},{25,9},{2,18},{10... | collective-permute-start | bytes 884744 | tf_op jit(solution)/shard_map/ppermute | solution.py:861
  228.6 21.6 %collective-permute-start.36 = (bf16[1,48,6144]{2,1,0:T(8,128)(2,1)S(1)}, bf16[1,48,6144]{2,1,0:T(8,128)(2,1)S(1)}, u32[]{:S(2)}, u32[]{:S(2)}) collective-permute-start(bf16[1,48,6144]{2,1,0:T(8,128)(2,1)S(1)} %pad_maximum_fusion.10), channel_id=1, source_target_pairs={{0,2},{1,3},{2,0},{3,1},{4,6},{5,7},{6,4},{7,5},{8,10},{9,11},{10,... | collective-permute-start | bytes 1769480 | tf_op jit(solution)/shard_map/ppermute | solution.py:772
  230.1 20.1 %collective-permute-start.37 = (bf16[1,48,6144]{2,1,0:T(8,128)(2,1)S(1)}, bf16[1,48,6144]{2,1,0:T(8,128)(2,1)S(1)}, u32[]{:S(2)}, u32[]{:S(2)}) collective-permute-start(bf16[1,48,6144]{2,1,0:T(8,128)(2,1)S(1)} %pad_maximum_fusion.11), channel_id=1, source_target_pairs={{0,4},{1,5},{2,6},{3,7},{4,0},{5,1},{6,2},{7,3},{8,12},{9,13},{10,... | collective-permute-start | bytes 1769480 | tf_op jit(solution)/shard_map/ppermute | solution.py:772
  255.0 16.0 %collective-permute-start.41 = (bf16[1,48,6400]{2,1,0:T(8,128)(2,1)S(1)}, bf16[1,48,6400]{2,1,0:T(8,128)(2,1)S(1)}, u32[]{:S(2)}, u32[]{:S(2)}) collective-permute-start(bf16[1,48,6400]{2,1,0:T(8,128)(2,1)S(1)} %pad_maximum_fusion.7), channel_id=1, source_target_pairs={{0,2},{1,3},{2,0},{3,1},{4,6},{5,7},{6,4},{7,5},{8,10},{9,11},{10,... | collective-permute-start | bytes 1843208 | tf_op jit(solution)/shard_map/ppermute | solution.py:772
  255.9 15.6 %collective-permute-start.42 = (bf16[1,48,6400]{2,1,0:T(8,128)(2,1)S(1)}, bf16[1,48,6400]{2,1,0:T(8,128)(2,1)S(1)}, u32[]{:S(2)}, u32[]{:S(2)}) collective-permute-start(bf16[1,48,6400]{2,1,0:T(8,128)(2,1)S(1)} %pad_maximum_fusion.8), channel_id=1, source_target_pairs={{0,4},{1,5},{2,6},{3,7},{4,0},{5,1},{6,2},{7,3},{8,12},{9,13},{10,... | collective-permute-start | bytes 1843208 | tf_op jit(solution)/shard_map/ppermute | solution.py:772
  258.3 21.9 %collective-permute-start.47 = (bf16[48,3072]{1,0:T(8,128)(2,1)S(1)}, bf16[48,3072]{1,0:T(8,128)(2,1)S(1)}, u32[]{:S(2)}, u32[]{:S(2)}) collective-permute-start(bf16[48,3072]{1,0:T(8,128)(2,1)S(1)} %get-tuple-element.274), channel_id=1, source_target_pairs={{0,8},{1,9},{2,10},{3,11},{4,12},{5,13},{6,14},{7,15},{8,0},{9,1},... | collective-permute-start | bytes 884744 | tf_op jit(solution)/shard_map/ppermute | solution.py:857
  258.8 20.9 %collective-permute-start.45 = (bf16[48,3072]{1,0:T(8,128)(2,1)S(1)}, bf16[48,3072]{1,0:T(8,128)(2,1)S(1)}, u32[]{:S(2)}, u32[]{:S(2)}) collective-permute-start(bf16[48,3072]{1,0:T(8,128)(2,1)S(1)} %add_convert_fusion.12), channel_id=1, source_target_pairs={{0,8},{1,9},{2,10},{3,11},{4,12},{5,13},{6,14},{7,15},{8,0},{9,1},... | collective-permute-start | bytes 884744 | tf_op jit(solution)/shard_map/ppermute | solution.py:857
  271.7 6.6 %collective-permute-start.43 = (bf16[1,48,2432]{2,1,0:T(8,128)(2,1)S(1)}, bf16[1,48,2432]{2,1,0:T(8,128)(2,1)S(1)}, u32[]{:S(2)}, u32[]{:S(2)}) collective-permute-start(bf16[1,48,2432]{2,1,0:T(8,128)(2,1)S(1)} %get-tuple-element.268), channel_id=1, source_target_pairs={{0,2},{1,3},{2,0},{3,1},{4,6},{5,7},{6,4},{7,5},{8,10},{9,11},{10,... | collective-permute-start | bytes 700424 | tf_op jit(solution)/shard_map/ppermute | solution.py:772
  273.0 6.3 %collective-permute-start.44 = (bf16[1,48,2432]{2,1,0:T(8,128)(2,1)S(1)}, bf16[1,48,2432]{2,1,0:T(8,128)(2,1)S(1)}, u32[]{:S(2)}, u32[]{:S(2)}) collective-permute-start(bf16[1,48,2432]{2,1,0:T(8,128)(2,1)S(1)} %get-tuple-element.269), channel_id=1, source_target_pairs={{0,4},{1,5},{2,6},{3,7},{4,0},{5,1},{6,2},{7,3},{8,12},{9,13},{10,... | collective-permute-start | bytes 700424 | tf_op jit(solution)/shard_map/ppermute | solution.py:772
  279.7 14.9 %collective-permute-start.46 = (bf16[48,3968]{1,0:T(8,128)(2,1)S(1)}, bf16[48,3968]{1,0:T(8,128)(2,1)S(1)}, u32[]{:S(2)}, u32[]{:S(2)}) collective-permute-start(bf16[48,3968]{1,0:T(8,128)(2,1)S(1)} %get-tuple-element.272), channel_id=1, source_target_pairs={{0,8},{1,9},{2,10},{3,11},{4,12},{5,13},{6,14},{7,15},{8,0},{9,1},... | collective-permute-start | bytes 1142792 | tf_op jit(solution)/shard_map/ppermute | solution.py:857
  280.3 12.3 %collective-permute-start.48 = (bf16[48,3072]{1,0:T(8,128)(2,1)S(1)}, bf16[48,3072]{1,0:T(8,128)(2,1)S(1)}, u32[]{:S(2)}, u32[]{:S(2)}) collective-permute-start(bf16[48,3072]{1,0:T(8,128)(2,1)S(1)} %add_convert_fusion.11), channel_id=1, source_target_pairs={{0,16},{8,24},{16,0},{24,8},{1,17},{9,25},{17,1},{25,9},{2,18},{10... | collective-permute-start | bytes 884744 | tf_op jit(solution)/shard_map/ppermute | solution.py:861
  294.8 18.5 %collective-permute-start.49 = (bf16[48,3968]{1,0:T(8,128)(2,1)S(1)}, bf16[48,3968]{1,0:T(8,128)(2,1)S(1)}, u32[]{:S(2)}, u32[]{:S(2)}) collective-permute-start(bf16[48,3968]{1,0:T(8,128)(2,1)S(1)} %add_convert_fusion.9), channel_id=1, source_target_pairs={{0,16},{8,24},{16,0},{24,8},{1,17},{9,25},{17,1},{25,9},{2,18},{10... | collective-permute-start | bytes 1142792 | tf_op jit(solution)/shard_map/ppermute | solution.py:861
  296.4 12.1 %collective-permute-start.50 = (bf16[48,3072]{1,0:T(8,128)(2,1)S(1)}, bf16[48,3072]{1,0:T(8,128)(2,1)S(1)}, u32[]{:S(2)}, u32[]{:S(2)}) collective-permute-start(bf16[48,3072]{1,0:T(8,128)(2,1)S(1)} %add_convert_fusion.10), channel_id=1, source_target_pairs={{0,8},{1,9},{2,10},{3,11},{4,12},{5,13},{6,14},{7,15},{8,0},{9,1},... | collective-permute-start | bytes 884744 | tf_op jit(solution)/shard_map/ppermute | solution.py:857
  313.4 10.8 %collective-permute-start.51 = (bf16[48,3968]{1,0:T(8,128)(2,1)S(1)}, bf16[48,3968]{1,0:T(8,128)(2,1)S(1)}, u32[]{:S(2)}, u32[]{:S(2)}) collective-permute-start(bf16[48,3968]{1,0:T(8,128)(2,1)S(1)} %add_convert_fusion.8), channel_id=1, source_target_pairs={{0,8},{1,9},{2,10},{3,11},{4,12},{5,13},{6,14},{7,15},{8,0},{9,1},... | collective-permute-start | bytes 1142792 | tf_op jit(solution)/shard_map/ppermute | solution.py:857
  (67 other events, 498.3 us)

commit v7 on v6

--- a/solution.py
+++ b/solution.py
@@ -119,8 +119,8 @@
     return total
 
 
-def row_in_block(i, size, columns):
-    return (i * size + lax.broadcasted_iota(jnp.int32, (size, columns), 0)) % BLOCK
+def places_only(value):
+    return jnp.where(lax.broadcasted_iota(jnp.int32, value.shape, 0) < PLACES, value, 0.0)
 
 
 def start(pairs, sems):
@@ -351,10 +351,11 @@
     for at in blocks_of(columns):
         e_ref[:, at] = (nn(o_ref[...], w[:, shifted(at, 3 * columns)]) + small_ref[2:3, at]).astype(BF)
     e_out.send()
-    patch = row_in_block(0, x_ref.shape[0], WIDE) < PLACES
     for at in blocks_of(columns):
         branch = nn(e_ref[...], w[:, shifted(at, 4 * columns)]) + small_ref[3:4, at]
-        y_ref[:, at] = x_ref[:, at].astype(F32) + jnp.where(patch, branch, 0.0)
+        for block in range(x_ref.shape[0] // BLOCK):
+            rows = rows_of(block, BLOCK)
+            y_ref[rows, at] = x_ref[rows, at].astype(F32) + places_only(branch[rows, :])
 
 
 def half_masks():
@@ -419,7 +420,7 @@
 
 def feed_out(ins, results, own):
     place_ref, z_ref, g_ref, small_ref, hb_ref, *bufs = ins
-    out_ref, nm_out, gh_out, *outs = results
+    out_ref, nm_out, gh_out, sums_ref, *outs = results
     we, wr, dwr, a, sems, out_sems = own
     nm, gh = nm_out.ref, gh_out.ref
     columns = z_ref.shape[1]
@@ -446,12 +447,13 @@
     copies = store_pieces(dwr, outs, place_ref, out_sems, units // columns)
     for at in blocks_of(columns):
         out_ref[:, at] = (z_ref[:, at] + (nn(a[...], wr[:, at]) + small_ref[7:8, at])).astype(BF)
+    sums_ref[0:1, :] = column_sums(g_ref, 0, columns)
     wait(copies)
 
 
 def feed_in(ins, results, own):
-    place_ref, gh, nm, g_in = ins
-    sums_ref, ghb_ref, *outs = results
+    place_ref, gh, nm = ins
+    ghb_ref, *outs = results
     dwe, out_sems = own
     units = gh.shape[1]
 
@@ -462,9 +464,7 @@
         ghb_ref[0:1, at] = jnp.sum(block.astype(F32), axis=0, keepdims=True)
 
     loop(units // WIDE, right)
-    copies = store_pieces(dwe, outs, place_ref, out_sems)
-    sums_ref[0:1, :] = column_sums(g_in.get(), 0, nm.shape[1])
-    wait(copies)
+    wait(store_pieces(dwe, outs, place_ref, out_sems))
 
 
 def norm_backward(row, n, ins, results, own):
@@ -572,12 +572,11 @@
     rows = gy_ref.shape[0]
     copies = load([b.at[:, 3 * columns : 5 * columns] for b in bufs], place_ref, w, sems)
 
-    def lower(i):
-        at = rows_of(i, CHUNK)
-        patch = row_in_block(i, CHUNK, columns) < PLACES
-        grt[at, :] = jnp.where(patch, gy_ref[at, :], 0.0).astype(BF)
-
-    loop(rows // CHUNK, lower)
+    def lower(block):
+        at = rows_of(block, BLOCK)
+        grt[at, :] = places_only(gy_ref[at, :]).astype(BF)
+
+    loop(rows // BLOCK, lower)
     wait(copies)
     go = go_out.ref
     for at in blocks_of(columns):
@@ -597,12 +596,12 @@
 
 
 def time_backward(n, ins, results, own):
-    place_ref, go, qkv_ref, p_ref, nt_in, x_in, gy_in, small_ref, before, *others = ins
-    others, bufs = others[: len(others) - n], others[len(others) - n :]
-    gx_ref, sums_ref, *outs = results
-    w, dw_ref, gqkv, gn, sems, out_sems = own
+    place_ref, go, qkv_ref, p_ref, x_in, gy_in, small_ref, before, *bufs = ins
+    gqkv_out, gx_ref, sums_ref = results
+    w, gn, sems = own
     columns = gx_ref.shape[1]
     rows = gx_ref.shape[0]
+    gqkv = gqkv_out.ref
     copies = load([b.at[:, 0 : 3 * columns] for b in bufs], place_ref, w, sems)
     heads = head_map(columns)
     for clip in range(rows // (FRAMES * BLOCK)):
@@ -627,11 +626,7 @@
             spread = [nt(value, heads[block, :]) for value in kept]
             for f in range(FRAMES):
                 gqkv[at[f], to[2]] = (spread[f] * grad[0] + spread[2 + f] * grad[1]).astype(BF)
-    nt_ref = nt_in.get()
-    for at in blocks_of(3 * columns):
-        dw_ref[:, at] = tn(nt_ref[...], gqkv[:, at]).astype(BF)
-    main = slice(0, 3 * columns)
-    stores = store_pieces(dw_ref.at[:, main], [out.at[..., main] for out in outs], place_ref, out_sems)
+    gqkv_out.send()
     wait(copies)
     for at in blocks_of(columns):
         gn[:, at] = nt(gqkv[...], w[at, :])
@@ -646,11 +641,17 @@
     sums_ref[2:4, :] = before[2:4, :]
     sums_ref[4:5, :] = gain_sum
     sums_ref[5:6, :] = shift_sum
-    wait(stores)
-    if others:
-        gather_small(dw_ref, (sums_ref, *others))
-        last = slice(3 * columns, 3 * columns + 128)
-        wait(store_pieces(dw_ref.at[:, last], [out.at[..., last] for out in outs], place_ref, out_sems))
+
+
+def time_weights(ins, results, own):
+    place_ref, gqkv, nt_ref, *sums = ins
+    dw_ref, out_sems = own
+    columns = nt_ref.shape[1]
+    for at in blocks_of(3 * columns):
+        dw_ref[:, at] = tn(nt_ref[...], gqkv[:, at]).astype(BF)
+    if sums:
+        gather_small(dw_ref, sums)
+    wait(store_pieces(dw_ref, results, place_ref, out_sems))
 
 
 def pack_rows(tokens, once):
@@ -715,15 +716,15 @@
         outs = self.grads(u) if self.pieced else [((u, c), BF)]
         return call(
             feed_out, (self.place, z, g, small, hb, *bufs), "svvvv" + "a" * n,
-            [self.act, self.act, self.tall] + outs, "vee" + "a" * len(outs),
+            [self.act, self.act, self.tall, self.sums] + outs, "veev" + "a" * len(outs),
             self.vmem(((c, u), BF), ((u, c), BF), ((u, c), BF), self.tall) + self.sems(40, 64), 30, "feed_out", False,
         )
 
-    def feed_in(self, gh, normed, g):
+    def feed_in(self, gh, normed):
         c, u = self.columns, self.units
         outs = self.grads(u)
         return call(
-            feed_in, (self.place, gh, normed, g), "svvl", [self.sums, ((8, u), F32)] + outs, "vv" + "a" * len(outs),
+            feed_in, (self.place, gh, normed), "svv", [((8, u), F32)] + outs, "v" + "a" * len(outs),
             self.vmem(((c, u), BF)) + self.sems(16), 8, "feed_in",
         )
 
@@ -752,14 +753,21 @@
             self.vmem(((c, 2 * c), BF), ((c, 2 * c), BF), self.act, self.act) + self.sems(8, 16), 8, "mixer_backward",
         )
 
-    def time_backward(self, go, qkv, p, normed, x, gy, small, before, others, bufs):
+    def time_backward(self, go, qkv, p, x, gy, small, before, bufs):
         c, n = self.columns, len(bufs)
-        width = 3 * c + (128 if others else 0)
+        return call(
+            functools.partial(time_backward, n), (self.place, go, qkv, p, x, gy, small, before, *bufs),
+            "svvvllvv" + "a" * n, [self.act3, self.act, self.sums], "evv",
+            self.vmem(((c, 3 * c), BF), self.wide) + self.sems(8), 12, "time_backward",
+        )
+
+    def time_weights(self, gqkv, normed, sums):
+        c = self.columns
+        width = 3 * c + (128 if sums else 0)
         outs = self.grads(width)
         return call(
-            functools.partial(time_backward, n), (self.place, go, qkv, p, normed, x, gy, small, before, *others, *bufs),
-            "svvvlllvv" + "v" * len(others) + "a" * n, [self.act, self.sums] + outs, "vv" + "a" * len(outs),
-            self.vmem(((c, 3 * c), BF), ((c, width), BF), self.act3, self.wide) + self.sems(8, 16), 20, "time_backward",
+            time_weights, (self.place, gqkv, normed, *sums), "svv" + "v" * len(sums), outs, "a" * len(outs),
+            self.vmem(((c, width), BF)) + self.sems(16), 8, "time_weights",
         )
 
 
@@ -905,10 +913,10 @@
         wt = (own_t, pair_t, first_t, hop_t[1], second_t, *gone_t)
         hop_s, hop_f = ((near_hop(own), near_hop(pair)) for own, pair in ((own_s, pair_s), (own_f, pair_f)))
         normed_t, qkv_t, o_t, e_t, p_t, y, small, hb = net.time_forward(x, (), wt)
-        first_s, y, cotangent = tie(hop_s[0], y, cotangent)
+        first_s, last_s, y, cotangent = tie(*hop_s, y, cotangent)
         g = pack_rows(cotangent[:, 0] * flags, True)
         second_s = far_hop(first_s)
-        ws = (own_s, pair_s, first_s, hop_s[1], second_s, *(to_sibling(v) for v in (first_s, hop_s[1], second_s)))
+        ws = (own_s, pair_s, first_s, last_s, second_s, *(to_sibling(v) for v in (first_s, last_s, second_s)))
         first_f, y, ws, g = tie(hop_f[0], y, ws, g)
         normed_s, qkv_s, p_s, o_s, z = net.space_forward(y, small, ws)
         second_f, last_f, z = tie(far_hop(first_f), hop_f[1], z)
@@ -924,10 +932,10 @@
         normed_t, qkv_t, o_t, e_t, p_t, y, small, hb = net.time_forward(x, given, wt)
         normed_s, qkv_s, p_s, o_s, z = net.space_forward(y, small, ws)
 
-    out, normed_f, gh, *grad_r = net.feed_out(z, g, small, hb, wf)
+    out, normed_f, gh, sums_f, *grad_r = net.feed_out(z, g, small, hb, wf)
     if pieced:
         sum_r = Reduction(*grad_r)
-    sums_f, ghb, *grad_e = net.feed_in(gh, normed_f, g)
+    ghb, *grad_e = net.feed_in(gh, normed_f)
     if pieced:
         sum_e = Reduction(*grad_e)
         sent_r, gh, ghb, sums_f, sum_e.keep = tie(sum_r.first(), gh, ghb, sums_f, sum_e.keep)
@@ -955,7 +963,6 @@
         got_r, got_e = across_pairs(held_r), swap_z(sent_e)
         sums_s = jnp.concatenate([sums_s[0:3], norm_s[0:2], sums_s[5:]], axis=0)
         sums_f = jnp.concatenate([sums_f[0:1], norm_f[0:2], sums_f[3:]], axis=0)
-    others = (sums_s, sums_f, ghb) if pieced else ()
     go, sums_m, *grad_m = net.mixer_backward(gy, o_t, e_t, wt)
     if pieced:
         sum_m = Reduction(*grad_m)
@@ -965,30 +972,37 @@
         sent = [beside(last, both) for last, both in zip(sum_s.second(), sum_m.first())]
         held_r, held_e, sent, go = tie(total(held_r, got_r), total(held_e, got_e), sent, go)
         arrived = (along_x(sent[0]), along_y(sent[1]), swap_z(held_r), across_pairs(held_e))
-    gx, sums_t, *grad_t = net.time_backward(go, qkv_t, p_t, normed_t, x, gy, small, sums_m, others, wt)
-
+    gqkv, gx, sums_t = net.time_backward(go, qkv_t, p_t, x, gy, small, sums_m, wt)
     if pieced:
-        (came_x, came_y, got_r, got_e), grad_t, gx, sums_t, out = tie(arrived, grad_t, gx, sums_t, out)
+        arrived, gqkv, gx, sums_t, out = tie(arrived, gqkv, gx, sums_t, out)
+        came_x, came_y, got_r, got_e = arrived
         hand_over((came_x, came_y), sum_s, sum_m)
+        held_s, sent_s = split_groups(sum_s.finish(), even)
+        held_s, sent_s, sent_m, gqkv = tie(held_s, sent_s, sum_m.second(), gqkv)
+        sum_m.cross_again(sent_m)
+        got_s = swap_z(sent_s)
+    grad_t = net.time_weights(gqkv, normed_t, (sums_t, sums_s, sums_f, ghb) if pieced else ())
+
+    if pieced:
+        got_s, sum_m.last_x, sum_m.last_y, grad_t = tie(got_s, sum_m.last_x, sum_m.last_y, grad_t)
         sum_t = Reduction(*grad_t)
-        held_e = total(held_e, got_e)
-        sent = [beside(last, both) for last, both in zip(sum_m.second(), sum_t.first())]
-        held_s, sent_s = split_groups(sum_s.finish(), even)
-        sent, held_s, sent_s, held_e, gx, out = tie(sent, held_s, sent_s, held_e, gx, out)
-        came_x, came_y = along_x(sent[0]), along_y(sent[1])
-        got_s, got_e = swap_z(sent_s), swap_z(held_e)
-        hand_over((came_x, came_y), sum_m, sum_t)
-        sum_t.cross_again(tie(*sum_t.second()))
-        held_s = total(held_s, got_s)
-        got_s = across_pairs(held_s)
-        halves = [jnp.concatenate(pair, axis=1) for pair in zip(sum_m.finish(), sum_t.finish())]
-        held_t, sent_t = split_groups(halves, even)
-        sent_t, held_t, got_e = tie(sent_t, held_t, got_e)
-        got_t = swap_z(sent_t)
-        got_t, got_s = tie(got_t, got_s)
-        held_t, held_s = tie(total(held_t, got_t), total(held_s, got_s))
-        got_t, got_s = across_pairs(held_t), swap_z(held_s)
-        got_t, got_s = tie(got_t, got_s)
+        held_s, held_e = total(held_s, got_s), total(held_e, got_e)
+        held_m, sent_m = split_groups(sum_m.finish(), even)
+        sent_t, held_s, held_e, held_m, sent_m, gx, out = tie(sum_t.first(), held_s, held_e, held_m, sent_m, gx, out)
+        sum_t.cross(sent_t)
+        got_s, got_m, got_e = across_pairs(held_s), swap_z(sent_m), swap_z(held_e)
+        sum_t.from_x, sum_t.from_y, got_m = tie(sum_t.from_x, sum_t.from_y, got_m)
+        held_m, sent_t = tie(total(held_m, got_m), sum_t.second())
+        sum_t.cross_again(sent_t)
+        got_m = across_pairs(held_m)
+        sum_t.last_x, sum_t.last_y, got_s = tie(sum_t.last_x, sum_t.last_y, got_s)
+        held_t, sent_t = split_groups(sum_t.finish(), even)
+        held_t, sent_t, held_s = tie(held_t, sent_t, total(held_s, got_s))
+        got_t, got_s = swap_z(sent_t), swap_z(held_s)
+        got_t, got_m = tie(got_t, got_m)
+        held_t, held_m = tie(total(held_t, got_t), total(held_m, got_m))
+        got_t, got_m = across_pairs(held_t), swap_z(held_m)
+        got_t, got_m, got_s, got_e = tie(got_t, got_m, got_s, got_e)
         held_t = total(held_t, got_t)
         got_t = swap_z(held_t)
         rt = join_groups(held_t, got_t, even).astype(F32)
@@ -996,7 +1010,7 @@
         re = join_groups(held_e, got_e, even).astype(F32)
         rr = join_groups(held_r, got_r, even).astype(F32)
         rr = jnp.concatenate([rr[:, k * columns : (k + 1) * columns] for k in range(share)], axis=0)
-        rm, rt = rt[:, : 2 * columns], rt[:, 2 * columns :]
+        rm = join_groups(held_m, got_m, even).astype(F32)
         narrow = rt[:, 3 * columns :]
         biases, rows_hidden = narrow[0:8, :part], narrow[8:11].reshape(-1)
         gains, shifts = narrow[11:14, :part], narrow[14:17, :part]

time: 332 us -> 328 us (0.988)
  waiting for transfers between devices: 78.9 us -> 65.9 us
  local copies, waits for them, and re-layouts: 20 us -> 26 us
    ppermute x4 -> x5, waiting for transfers between devices: 11.9 us -> 5.18 us  [across_pairs(): return lax.ppermute(value, 'grp', [(z, z ^ 2) for z in range(4)])]
    ppermute x8 -> x10, waiting for transfers between devices: 19.8 us -> 13.7 us  [swap_z(): return lax.ppermute(value, BOTH, pairs)]
    unnamed x136 -> x134, local copies, waits for them, and re-layouts: 11.7 us -> 15.5 us
    pallas_call x9 -> x10, Pallas kernels: 137 us -> 138 us  [call(): pl.pallas_call(kernel, out_shape=[jax.ShapeDtypeStruct(s, d) for s, d in...]
    ppermute x4 -> x5, starting transfers between devices: 7.09 us -> 7.88 us  [across_pairs(): return lax.ppermute(value, 'grp', [(z, z ^ 2) for z in range(4)])]
    ppermute x40 -> x42, starting transfers between devices: 33.6 us -> 34.2 us  [permute(): return lax.ppermute(value, BOTH, pairs)]
    convert_element_type x18 -> x20, other arithmetic: 9.12 us -> 8.82 us  [total(): return sum((t.astype(F32) for t in terms)).astype(BF)]
    ppermute x40 -> x42, waiting for transfers between devices: 47.2 us -> 47 us  [permute(): return lax.ppermute(value, BOTH, pairs)]
  transfers between devices with their start and end apart: 52 -> 57, of which waited for: 21 -> 18; matrix products, arithmetic and copies ran while one was open for 13% -> 13% of each run, Pallas kernels for 33% -> 34%
where the time goes in v7:
time: 328 us; the launch traced here: 324 us
  Pallas kernels  138 us (42%)
  waiting for transfers between devices  65.9 us (20%)
  starting transfers between devices  50.7 us (15%)
  other arithmetic  40.9 us (12%)
  local copies, waits for them, and re-layouts  26 us (8%)
    pallas_call x10, Pallas kernels, call(): pl.pallas_call(kernel, out_shape=[jax.ShapeDtypeStruct(s, d) for s, d in...  138 us
    ppermute x42, waiting for transfers between devices, permute(): return lax.ppermute(value, BOTH, pairs)  47 us
    ppermute x42, starting transfers between devices, permute(): return lax.ppermute(value, BOTH, pairs)  34.2 us
    unnamed x134, local copies, waits for them, and re-layouts  15.5 us
    ppermute x10, waiting for transfers between devices, swap_z(): return lax.ppermute(value, BOTH, pairs)  13.7 us
    another operation x4, other arithmetic, pack_rows(): return jnp.stack(frames, axis=1).reshape(clips * FRAMES * BLOCK, columns)  10.3 us
    convert_element_type x20, other arithmetic, total(): return sum((t.astype(F32) for t in terms)).astype(BF)  8.82 us
    ppermute x10, starting transfers between devices, swap_z(): return lax.ppermute(value, BOTH, pairs)  8.63 us
  transfers between devices with their start and end apart: 57, of which 18 were waited for; matrix products, arithmetic and copies ran while one was open for 13% of the time, Pallas kernels for 34%

profile of v7, /device:TPU:0, one launch (start us, length us, event | category | flops | bytes accessed | tf_op | source)
XLA Modules:
  0.0 324.2 jit_solution(9674674331881242903)
XLA Ops:
  6.5 2.9 collective-permute-start.1
  10.2 3.6 %fusion.4 = (bf16[2,1,208,768]{3,0,2,1:T(2,128)(2,1)S(1)}, bf16[2,1,208,768]{3,0,2,1:T(2,128)(2,1)S(1)}) fusion(bf16[2,1,768]{2,0,1:T(2,128)(2,1)S(1)} %slice.515, bf16[2,196,768]{2,0,1:T(2,128)(2,1)S(1)} %get-tuple-element.370, bf16[208]{0:T(256)(128)(2,1)S(1)} %pad.68.clone, bf16[2,196,768]{2,0,1:T(2,128)(2,1)S(1)} %get-tuple-element.371), kind=kLoop, calls=%fused_computation.23 | loop fusion | flops 1277952 | bytes 2485664 | tf_op jit(solution)/shard_map/stack | solution.py:664
  13.8 1.8 pad_maximum_fusion
  16.8 2.4 collective-permute-done.1.refs_4_.refs_6_.refs_10_
  20.2 2.1 collective-permute-start.4
  22.2 9.7 %collective-permute-done.8.refs_5_.refs_7_.refs_11_ = bf16[96,3968]{1,0:T(8,128)(2,1)} collective-permute-done((bf16[96,3968]{1,0:T(8,128)(2,1)S(1)}, bf16[96,3968]{1,0:T(8,128)(2,1)}, u32[]{:S(2)}, u32[]{:S(2)}) %collective-permute-start.8) | collective-permute-done | bytes 761888 | tf_op jit(solution)/shard_map/ppermute | solution.py:780
  32.4 2.6 collective-permute-done.4.refs_6_.refs_8_.refs_12_
  36.0 2.0 collective-permute-start.6
  38.1 2.0 collective-permute-start.5
  40.2 14.1 %time_forward.1 = (bf16[832,768]{1,0:T(8,128)(2,1)}, bf16[832,2304]{1,0:T(8,128)(2,1)}, bf16[832,768]{1,0:T(8,128)(2,1)}, bf16[832,768]{1,0:T(8,128)(2,1)}, f32[...) custom-call(s32[16]{0:T(128)} %stack.76.refs_0_, bf16[832,768]{1,0:T(8,128)(2,1)} %bitcast.63, ...), custom_call_target="tpu_custom_call" | custom-call | flops 56000000000 | tf_op jit(solution)/shard_map/time_forward/pallas_call | solution.py:284
  57.3 2.4 bitcast_multiply_fusion
  60.5 10.3 %collective-permute-done.12.refs_7_.refs_10_.refs_9_ = bf16[96,3072]{1,0:T(8,128)(2,1)S(1)} collective-permute-done((bf16[96,3072]{1,0:T(8,128)(2,1)}, bf16[96,3072]{1,0:T(8,128)(2,1)S(1)}, u32[]{:S(2)}, u32[]{:S(2)}) %collective-permute-start.12) | collective-permute-done | bytes 589856 | tf_op jit(solution)/shard_map/ppermute | solution.py:780
  70.8 3.1 maximum_bitcast_fusion.1
  73.9 1.8 pad_maximum_fusion.1
  80.1 16.8 %space_forward.1 = (bf16[832,768]{1,0:T(8,128)(2,1)}, bf16[832,2304]{1,0:T(8,128)(2,1)}, bf16[48,208,208]{2,1,0:T(8,128)(2,1)}, bf16[832,768]{1,0:T(8,128)(2,1)}, f32[832,768]{1,0:T(8,128)}) custom-call(s32[16]{0:T(128)} %stack.76.refs_0_, f32[832,768]{1,0:T(8,128)} %get-tuple-element.191.refs_1_.refs_2_, ...), custom_call_target="tpu_custom_call" | custom-call | flops 64000000000 | tf_op jit(solution)/shard_map/space_forward/pallas_call | solution.py:284
  97.6 3.2 collective-permute-done.19.refs_11_
  102.8 28.1 %feed_out.1 = (bf16[832,768]{1,0:T(8,128)(2,1)}, bf16[832,768]{1,0:T(8,128)(2,1)}, bf16[832,3072]{1,0:T(8,128)(2,1)}, f32[8,768]{1,0:T(8,128)}, bf16[8,48,3072]{...) custom-call(s32[16]{0:T(128)} %stack.76.refs_0_, f32[832,768]{1,0:T(8,128)} %get-tuple-element.202.refs_1_.refs_2_, ...), custom_call_target="tpu_custom_call" | custom-call | flops 120000004096 | tf_op jit(solution)/shard_map/feed_out/pallas_call | solution.py:284
  131.2 2.4 copy-done.32
  134.9 7.8 %feed_in.1 = (f32[8,3072]{1,0:T(8,128)S(1)}, bf16[8,48,3072]{2,1,0:T(8,128)(2,1)S(1)}, bf16[8,48,3072]{2,1,0:T(8,128)(2,1)}) custom-call(s32[16]{0:T(128)S(1)} %copy-done.8, bf16[832,3072]{1,0:T(8,128)(2,1)S(1)} %copy-done.32, bf16[832,768]{1,0:T(8,128)(2,1)S(1)} %copy-done.41), custom_call_target="tpu_custom_call" | custom-call | flops 32000000000 | tf_op jit(solution)/shard_map/feed_in/pallas_call | solution.py:284
  143.7 2.2 add_convert_fusion.4
  151.8 2.4 copy-done.33
  154.3 1.7 copy-done.36
  156.0 8.7 %feed_norm.1 = (f32[832,768]{1,0:T(8,128)S(1)}, f32[8,768]{1,0:T(8,128)S(1)}) custom-call(s32[16]{0:T(128)S(1)} %copy-done.8, bf16[832,3072]{1,0:T(8,128)(2,1)S(1)} %copy-done.33, f32[832,768]{1,0:T(8,128)S(1)} %copy-done.36, bf16[832,768]{1,0:T(8,128)(2,1)S(1)} %bitcast.66, f32[32,768]{1,0:T(8,128)S(1)} %copy-done.48, bf16[96,6144]{1,0:T(8,128)(2,1)S(1)} %copy-done.7, ...), custom_call_target="tpu_custom_call" | custom-call | flops 40000000000 | tf_op jit(solution)/shard_map/feed_norm/pallas_call | solution.py:284
  164.9 1.9 add_convert_fusion.26
  168.6 20.8 %space_backward.1 = (bf16[832,2304]{1,0:T(8,128)(2,1)S(1)}, f32[8,768]{1,0:T(8,128)S(1)}, bf16[8,48,3072]{2,1,0:T(8,128)(2,1)S(1)}, bf16[8,48,3072]{2,1,0:T(8,128)(2,1)S(1)}) custom-call(s32[16]{0:T(128)S(1)} %copy-done.8, f32[832,768]{1,0:T(8,128)S(1)} %get-tuple-element.223.refs_1_.refs_3_, bf16[832,768]{1,0:T(8,128)(2,1)S(1)} %copy-done.44, ...), custom_call_target="tpu_custom_call" | custom-call | flops 80000000000 | tf_op jit(solution)/shard_map/space_backward/pallas_call | solution.py:284
  192.5 1.6 collective-permute-start.28
  196.7 1.7 copy-done.38
  198.4 7.7 %space_norm.1 = (f32[832,768]{1,0:T(8,128)S(1)}, f32[8,768]{1,0:T(8,128)S(1)}) custom-call(s32[16]{0:T(128)S(1)} %copy-done.8, bf16[832,2304]{1,0:T(8,128)(2,1)S(1)} %get-tuple-element.237.refs_1_, f32[832,768]{1,0:T(8,128)S(1)} %copy-done.38, f32[832,768]{1,0:T(8,128)S(1)} %get-tuple-element.223.refs_1_.refs_3_, f32[32,768]{1,0:T(8,128)S(1)} %copy-done.48, ...), custom_call_target="tpu_custom_call" | custom-call | flops 40000000000 | tf_op jit(solution)/shard_map/space_norm/pallas_call | solution.py:284
  206.3 1.9 select_bitcast_fusion.2
  209.1 2.6 collective-permute-start.31
  213.3 13.3 %mixer_backward.1 = (bf16[832,768]{1,0:T(8,128)(2,1)S(1)}, f32[8,768]{1,0:T(8,128)S(1)}, bf16[8,48,1536]{2,1,0:T(8,128)(2,1)S(1)}, bf16[8,48,1536]{2,1,0:T(8,128)(2,1)S(1)}) custom-call(s32[16]{0:T(128)S(1)} %copy-done.8, f32[832,768]{1,0:T(8,128)S(1)} %get-tuple-element.249.refs_1_.refs_5_, bf16[832,768]{1,0:T(8,128)(2,1)S(1)} %copy-done.39, ...), custom_call_target="tpu_custom_call" | custom-call | flops 32000000000 | tf_op jit(solution)/shard_map/mixer_backward/pallas_call | solution.py:284
  227.2 2.4 collective-permute-done.35
  229.9 1.6 collective-permute-start.38
  234.4 11.4 %time_backward.1 = (bf16[832,2304]{1,0:T(8,128)(2,1)S(1)}, bf16[832,768]{1,0:T(8,128)(2,1)S(1)}, f32[8,768]{1,0:T(8,128)S(1)}) custom-call(s32[16]{0:T(128)S(1)} %copy-done.8, bf16[832,768]{1,0:T(8,128)(2,1)S(1)} %get-tuple-element.267.refs_1_, bf16[832,2304]{1,0:T(8,128)(2,1)S(1)} %copy-done.37, f32[1664,128]{1,0:T(8,128)S(1)} %copy-done.43, ...), custom_call_target="tpu_custom_call" | custom-call | flops 48000000000 | tf_op jit(solution)/shard_map/time_backward/pallas_call | solution.py:284
  245.8 1.7 collective-permute-done.39
  251.9 9.7 %time_weights.1 = (bf16[8,48,2432]{2,1,0:T(8,128)(2,1)S(1)}, bf16[8,48,2432]{2,1,0:T(8,128)(2,1)S(1)}) custom-call(s32[16]{0:T(128)S(1)} %copy-done.8, bf16[832,2304]{1,0:T(8,128)(2,1)S(1)} %get-tuple-element.281.refs_1_, bf16[832,768]{1,0:T(8,128)(2,1)S(1)} %copy-done.42, f32[8,768]{1,0:T(8,128)S(1)} %get-tuple-element.283.refs_3_, ...), custom_call_target="tpu_custom_call" | custom-call | flops 32000000000 | tf_op jit(solution)/shard_map/time_weights/pallas_call | solution.py:284
  263.3 2.3 collective-permute-done.43
  266.5 2.1 collective-permute-start.46
  268.6 1.9 collective-permute-start.49
  273.5 3.1 maximum_multiply_fusion
  276.6 6.3 %collective-permute-done.44 = bf16[2,48,2432]{2,1,0:T(8,128)(2,1)S(1)} collective-permute-done((bf16[2,48,2432]{2,1,0:T(8,128)(2,1)S(1)}, bf16[2,48,2432]{2,1,0:T(8,128)(2,1)S(1)}, u32[]{:S(2)}, u32[]{:S(2)}) %collective-permute-start.44) | collective-permute-done | bytes 466976 | tf_op jit(solution)/shard_map/ppermute | solution.py:780
  286.5 4.0 %collective-permute-done.47 = bf16[1,48,2432]{2,1,0:T(8,128)(2,1)S(1)} collective-permute-done((bf16[1,48,2432]{2,1,0:T(8,128)(2,1)S(1)}, bf16[1,48,2432]{2,1,0:T(8,128)(2,1)S(1)}, u32[]{:S(2)}, u32[]{:S(2)}) %collective-permute-start.47) | collective-permute-done | bytes 233504 | tf_op jit(solution)/shard_map/ppermute | solution.py:780
  294.5 8.1 %collective-permute-done.50 = bf16[48,2432]{1,0:T(8,128)(2,1)S(1)} collective-permute-done((bf16[48,2432]{1,0:T(8,128)(2,1)S(1)}, bf16[48,2432]{1,0:T(8,128)(2,1)S(1)}, u32[]{:S(2)}, u32[]{:S(2)}) %collective-permute-start.50) | collective-permute-done | bytes 233504 | tf_op jit(solution)/shard_map/ppermute | solution.py:865
  302.8 2.5 collective-permute-start.52
  305.4 2.6 maximum_bitcast_fusion
  308.0 2.6 collective-permute-done.53
  310.5 3.4 %collective-permute-done.52 = bf16[48,2432]{1,0:T(8,128)(2,1)S(1)} collective-permute-done((bf16[48,2432]{1,0:T(8,128)(2,1)S(1)}, bf16[48,2432]{1,0:T(8,128)(2,1)S(1)}, u32[]{:S(2)}, u32[]{:S(2)}) %collective-permute-start.52) | collective-permute-done | bytes 233504 | tf_op jit(solution)/shard_map/ppermute | solution.py:869
  318.1 3.1 collective-permute-done.56
  (301 shorter events, 67.5 us)
Async XLA Ops:
  5.8 13.3 %collective-permute-start.3 = (bf16[96,6144]{1,0:T(8,128)(2,1)S(1)}, bf16[96,6144]{1,0:T(8,128)(2,1)S(1)}, u32[]{:S(2)}, u32[]{:S(2)}) collective-permute-start(bf16[96,6144]{1,0:T(8,128)(2,1)S(1)} %slice_dynamic-update-slice_fusion.refs_5_), channel_id=1, source_target_pairs={{0,1},{1,0},{2,3},{3,2},{4,5},{5,4},{6,7},{7,6},{8,9},{9,8},{10,11... | collective-permute-start | bytes 3538952 | tf_op jit(solution)/shard_map/ppermute | solution.py:780
  6.3 10.5 %collective-permute-start.2 = (bf16[96,3072]{1,0:T(8,128)(2,1)S(1)}, bf16[96,3072]{1,0:T(8,128)(2,1)}, u32[]{:S(2)}, u32[]{:S(2)}) collective-permute-start(bf16[96,3072]{1,0:T(8,128)(2,1)S(1)} %pad_maximum_fusion.7.refs_3_.refs_6_.refs_5_), channel_id=1, source_target_pairs={{0,1},{1,0},{2,3},{3,2},{4,5},{5,4},{6,7},{7,6},{8,9},{9,8},{10,11... | collective-permute-start | bytes 1769480 | tf_op jit(solution)/shard_map/ppermute | solution.py:780
  6.5 12.7 %collective-permute-start.1 = (bf16[96,3968]{1,0:T(8,128)(2,1)S(1)}, bf16[96,3968]{1,0:T(8,128)(2,1)}, u32[]{:S(2)}, u32[]{:S(2)}) collective-permute-start(bf16[96,3968]{1,0:T(8,128)(2,1)S(1)} %fusion.1.refs_2_.refs_4_.refs_8_), channel_id=1, source_target_pairs={{0,2},{1,5},{2,0},{3,7},{4,6},{5,1},{6,4},{7,3},{8,10},{9,13},{10,... | collective-permute-start | bytes 2285576 | tf_op jit(solution)/shard_map/ppermute | solution.py:780
  9.4 22.5 %collective-permute-start.8 = (bf16[96,3968]{1,0:T(8,128)(2,1)S(1)}, bf16[96,3968]{1,0:T(8,128)(2,1)}, u32[]{:S(2)}, u32[]{:S(2)}) collective-permute-start(bf16[96,3968]{1,0:T(8,128)(2,1)S(1)} %collective-permute-done.refs_3_.refs_5_.refs_9_), channel_id=1, source_target_pairs={{0,2},{1,5},{2,0},{3,7},{4,6},{5,1},{6,4},{7,3},{8,10},{9,13},{10,... | collective-permute-start | bytes 2285576 | tf_op jit(solution)/shard_map/ppermute | solution.py:780
  20.2 14.8 %collective-permute-start.4 = (bf16[96,3968]{1,0:T(8,128)(2,1)}, bf16[96,3968]{1,0:T(8,128)(2,1)}, u32[]{:S(2)}, u32[]{:S(2)}) collective-permute-start(bf16[96,3968]{1,0:T(8,128)(2,1)} %collective-permute-done.1.refs_4_.refs_6_.refs_10_), channel_id=1, source_target_pairs={{0,4},{1,3},{2,6},{3,1},{4,0},{5,7},{6,2},{7,5},{8,12},{9,11},{10,... | collective-permute-start | bytes 2285576 | tf_op jit(solution)/shard_map/ppermute | solution.py:780
  31.9 6.2 %collective-permute-start.10 = (bf16[96,3968]{1,0:T(8,128)(2,1)}, bf16[96,3968]{1,0:T(8,128)(2,1)S(1)}, u32[]{:S(2)}, u32[]{:S(2)}) collective-permute-start(bf16[96,3968]{1,0:T(8,128)(2,1)} %collective-permute-done.8.refs_5_.refs_7_.refs_11_), channel_id=1, source_target_pairs={{0,1},{1,0},{2,3},{3,2},{4,5},{5,4},{6,7},{7,6},{8,9},{9,8},{10,11... | collective-permute-start | bytes 2285576 | tf_op jit(solution)/shard_map/ppermute | solution.py:780
  31.9 8.2 %collective-permute-start.9 = (bf16[96,3968]{1,0:T(8,128)(2,1)}, bf16[96,3968]{1,0:T(8,128)(2,1)}, u32[]{:S(2)}, u32[]{:S(2)}) collective-permute-start(bf16[96,3968]{1,0:T(8,128)(2,1)} %collective-permute-done.1.refs_4_.refs_6_.refs_10_), channel_id=1, source_target_pairs={{0,1},{1,0},{2,3},{3,2},{4,5},{5,4},{6,7},{7,6},{8,9},{9,8},{10,11... | collective-permute-start | bytes 2285576 | tf_op jit(solution)/shard_map/ppermute | solution.py:780
  36.0 18.2 %collective-permute-start.6 = (bf16[96,3072]{1,0:T(8,128)(2,1)S(1)}, bf16[96,3072]{1,0:T(8,128)(2,1)}, u32[]{:S(2)}, u32[]{:S(2)}) collective-permute-start(bf16[96,3072]{1,0:T(8,128)(2,1)S(1)} %pad_maximum_fusion.7.refs_3_.refs_6_.refs_5_), channel_id=1, source_target_pairs={{0,2},{1,5},{2,0},{3,7},{4,6},{5,1},{6,4},{7,3},{8,10},{9,13},{10,... | collective-permute-start | bytes 1769480 | tf_op jit(solution)/shard_map/ppermute | solution.py:780
  38.0 16.2 %collective-permute-start.7 = (bf16[96,3072]{1,0:T(8,128)(2,1)}, bf16[96,3072]{1,0:T(8,128)(2,1)}, u32[]{:S(2)}, u32[]{:S(2)}) collective-permute-start(bf16[96,3072]{1,0:T(8,128)(2,1)} %collective-permute-done.2.refs_4_.refs_7_.refs_6_), channel_id=1, source_target_pairs={{0,2},{1,5},{2,0},{3,7},{4,6},{5,1},{6,4},{7,3},{8,10},{9,13},{10,... | collective-permute-start | bytes 1769480 | tf_op jit(solution)/shard_map/ppermute | solution.py:780
  38.1 38.8 %collective-permute-start.5 = (bf16[96,6144]{1,0:T(8,128)(2,1)S(1)}, bf16[96,6144]{1,0:T(8,128)(2,1)}, u32[]{:S(2)}, u32[]{:S(2)}) collective-permute-start(bf16[96,6144]{1,0:T(8,128)(2,1)S(1)} %slice_dynamic-update-slice_fusion.refs_5_), channel_id=1, source_target_pairs={{0,2},{1,5},{2,0},{3,7},{4,6},{5,1},{6,4},{7,3},{8,10},{9,13},{10,... | collective-permute-start | bytes 3538952 | tf_op jit(solution)/shard_map/ppermute | solution.py:780
  54.3 16.5 %collective-permute-start.12 = (bf16[96,3072]{1,0:T(8,128)(2,1)}, bf16[96,3072]{1,0:T(8,128)(2,1)S(1)}, u32[]{:S(2)}, u32[]{:S(2)}) collective-permute-start(bf16[96,3072]{1,0:T(8,128)(2,1)} %collective-permute-done.6.refs_5_.refs_8_.refs_7_), channel_id=1, source_target_pairs={{0,4},{1,3},{2,6},{3,1},{4,0},{5,7},{6,2},{7,5},{8,12},{9,11},{10,... | collective-permute-start | bytes 1769480 | tf_op jit(solution)/shard_map/ppermute | solution.py:780
  56.0 41.0 %collective-permute-start.17 = (bf16[96,6144]{1,0:T(8,128)(2,1)S(1)}, bf16[96,6144]{1,0:T(8,128)(2,1)S(1)}, u32[]{:S(2)}, u32[]{:S(2)}) collective-permute-start(bf16[96,6144]{1,0:T(8,128)(2,1)S(1)} %copy-done.10), channel_id=1, source_target_pairs={{0,2},{1,5},{2,0},{3,7},{4,6},{5,1},{6,4},{7,3},{8,10},{9,13},{10,... | collective-permute-start | bytes 3538952 | tf_op jit(solution)/shard_map/ppermute | solution.py:780
  56.8 20.2 %collective-permute-start.13 = (bf16[96,3072]{1,0:T(8,128)(2,1)}, bf16[96,3072]{1,0:T(8,128)(2,1)S(1)}, u32[]{:S(2)}, u32[]{:S(2)}) collective-permute-start(bf16[96,3072]{1,0:T(8,128)(2,1)} %collective-permute-done.6.refs_5_.refs_8_.refs_7_), channel_id=1, source_target_pairs={{0,1},{1,0},{2,3},{3,2},{4,5},{5,4},{6,7},{7,6},{8,9},{9,8},{10,11... | collective-permute-start | bytes 1769480 | tf_op jit(solution)/shard_map/ppermute | solution.py:780
  56.8 20.2 %collective-permute-start.14 = (bf16[96,3072]{1,0:T(8,128)(2,1)}, bf16[96,3072]{1,0:T(8,128)(2,1)S(1)}, u32[]{:S(2)}, u32[]{:S(2)}) collective-permute-start(bf16[96,3072]{1,0:T(8,128)(2,1)} %collective-permute-done.7.refs_6_.refs_9_.refs_8_), channel_id=1, source_target_pairs={{0,1},{1,0},{2,3},{3,2},{4,5},{5,4},{6,7},{7,6},{8,9},{9,8},{10,11... | collective-permute-start | bytes 1769480 | tf_op jit(solution)/shard_map/ppermute | solution.py:780
  70.8 6.1 %collective-permute-start.15 = (bf16[96,3072]{1,0:T(8,128)(2,1)S(1)}, bf16[96,3072]{1,0:T(8,128)(2,1)S(1)}, u32[]{:S(2)}, u32[]{:S(2)}) collective-permute-start(bf16[96,3072]{1,0:T(8,128)(2,1)S(1)} %collective-permute-done.12.refs_7_.refs_10_.refs_9_), channel_id=1, source_target_pairs={{0,1},{1,0},{2,3},{3,2},{4,5},{5,4},{6,7},{7,6},{8,9},{9,8},{10,11... | collective-permute-start | bytes 1769480 | tf_op jit(solution)/shard_map/ppermute | solution.py:780
  77.9 19.6 %collective-permute-start.18 = (bf16[96,6144]{1,0:T(8,128)(2,1)}, bf16[96,6144]{1,0:T(8,128)(2,1)S(1)}, u32[]{:S(2)}, u32[]{:S(2)}) collective-permute-start(bf16[96,6144]{1,0:T(8,128)(2,1)} %collective-permute-done.5.refs_7_), channel_id=1, source_target_pairs={{0,1},{1,0},{2,3},{3,2},{4,5},{5,4},{6,7},{7,6},{8,9},{9,8},{10,11... | collective-permute-start | bytes 3538952 | tf_op jit(solution)/shard_map/ppermute | solution.py:780
  78.6 18.4 %collective-permute-start.16 = (bf16[96,6144]{1,0:T(8,128)(2,1)}, bf16[96,6144]{1,0:T(8,128)(2,1)}, u32[]{:S(2)}, u32[]{:S(2)}) collective-permute-start(bf16[96,6144]{1,0:T(8,128)(2,1)} %collective-permute-done.5.refs_7_), channel_id=1, source_target_pairs={{0,4},{1,3},{2,6},{3,1},{4,0},{5,7},{6,2},{7,5},{8,12},{9,11},{10,... | collective-permute-start | bytes 3538952 | tf_op jit(solution)/shard_map/ppermute | solution.py:780
  131.0 12.7 %collective-permute-start.21 = (bf16[8,48,3072]{2,1,0:T(8,128)(2,1)}, bf16[8,48,3072]{2,1,0:T(8,128)(2,1)}, u32[]{:S(2)}, u32[]{:S(2)}) collective-permute-start(bf16[8,48,3072]{2,1,0:T(8,128)(2,1)} %get-tuple-element.208), channel_id=1, source_target_pairs={{0,1},{1,0},{2,3},{3,2},{4,5},{5,4},{6,7},{7,6},{8,9},{9,8},{10,11... | collective-permute-start | bytes 7077896 | tf_op jit(solution)/shard_map/ppermute | solution.py:780
  143.3 6.8 %collective-permute-start.24 = (bf16[8,48,3072]{2,1,0:T(8,128)(2,1)}, bf16[8,48,3072]{2,1,0:T(8,128)(2,1)}, u32[]{:S(2)}, u32[]{:S(2)}) collective-permute-start(bf16[8,48,3072]{2,1,0:T(8,128)(2,1)} %get-tuple-element.217), channel_id=1, source_target_pairs={{0,1},{1,0},{2,3},{3,2},{4,5},{5,4},{6,7},{7,6},{8,9},{9,8},{10,11... | collective-permute-start | bytes 7077896 | tf_op jit(solution)/shard_map/ppermute | solution.py:780
  147.4 17.4 %collective-permute-start.22 = (bf16[2,48,3072]{2,1,0:T(8,128)(2,1)S(1)}, bf16[2,48,3072]{2,1,0:T(8,128)(2,1)S(1)}, u32[]{:S(2)}, u32[]{:S(2)}) collective-permute-start(bf16[2,48,3072]{2,1,0:T(8,128)(2,1)S(1)} %get-tuple-element.214), channel_id=1, source_target_pairs={{0,2},{1,3},{2,0},{3,1},{4,6},{5,7},{6,4},{7,5},{8,10},{9,11},{10,... | collective-permute-start | bytes 1769480 | tf_op jit(solution)/shard_map/ppermute | solution.py:780
  148.6 16.2 %collective-permute-start.23 = (bf16[2,48,3072]{2,1,0:T(8,128)(2,1)S(1)}, bf16[2,48,3072]{2,1,0:T(8,128)(2,1)S(1)}, u32[]{:S(2)}, u32[]{:S(2)}) collective-permute-start(bf16[2,48,3072]{2,1,0:T(8,128)(2,1)S(1)} %get-tuple-element.215), channel_id=1, source_target_pairs={{0,4},{1,5},{2,6},{3,7},{4,0},{5,1},{6,2},{7,3},{8,12},{9,13},{10,... | collective-permute-start | bytes 1769480 | tf_op jit(solution)/shard_map/ppermute | solution.py:780
  167.0 22.6 %collective-permute-start.25 = (bf16[1,48,9216]{2,1,0:T(8,128)(2,1)S(1)}, bf16[1,48,9216]{2,1,0:T(8,128)(2,1)S(1)}, u32[]{:S(2)}, u32[]{:S(2)}) collective-permute-start(bf16[1,48,9216]{2,1,0:T(8,128)(2,1)S(1)} %pad_maximum_fusion.4), channel_id=1, source_target_pairs={{0,4},{1,5},{2,6},{3,7},{4,0},{5,1},{6,2},{7,3},{8,12},{9,13},{10,... | collective-permute-start | bytes 2654216 | tf_op jit(solution)/shard_map/ppermute | solution.py:780
  167.5 22.1 %collective-permute-start.26 = (bf16[1,48,9216]{2,1,0:T(8,128)(2,1)S(1)}, bf16[1,48,9216]{2,1,0:T(8,128)(2,1)S(1)}, u32[]{:S(2)}, u32[]{:S(2)}) collective-permute-start(bf16[1,48,9216]{2,1,0:T(8,128)(2,1)S(1)} %pad_maximum_fusion.3), channel_id=1, source_target_pairs={{0,2},{1,3},{2,0},{3,1},{4,6},{5,7},{6,4},{7,5},{8,10},{9,11},{10,... | collective-permute-start | bytes 2654216 | tf_op jit(solution)/shard_map/ppermute | solution.py:780
  189.5 18.8 %collective-permute-start.27 = (bf16[8,48,3072]{2,1,0:T(8,128)(2,1)S(1)}, bf16[8,48,3072]{2,1,0:T(8,128)(2,1)S(1)}, u32[]{:S(2)}, u32[]{:S(2)}) collective-permute-start(bf16[8,48,3072]{2,1,0:T(8,128)(2,1)S(1)} %get-tuple-element.232), channel_id=1, source_target_pairs={{0,1},{1,0},{2,3},{3,2},{4,5},{5,4},{6,7},{7,6},{8,9},{9,8},{10,11... | collective-permute-start | bytes 7077896 | tf_op jit(solution)/shard_map/ppermute | solution.py:780
  192.5 13.6 %collective-permute-start.28 = (bf16[48,3072]{1,0:T(8,128)(2,1)S(1)}, bf16[48,3072]{1,0:T(8,128)(2,1)S(1)}, u32[]{:S(2)}, u32[]{:S(2)}) collective-permute-start(bf16[48,3072]{1,0:T(8,128)(2,1)S(1)} %get-tuple-element.234), channel_id=1, source_target_pairs={{0,8},{1,9},{2,10},{3,11},{4,12},{5,13},{6,14},{7,15},{8,0},{9,1},... | collective-permute-start | bytes 884744 | tf_op jit(solution)/shard_map/ppermute | solution.py:865
  194.2 12.0 %collective-permute-start.29 = (bf16[1,48,3072]{2,1,0:T(8,128)(2,1)S(1)}, bf16[1,48,3072]{2,1,0:T(8,128)(2,1)S(1)}, u32[]{:S(2)}, u32[]{:S(2)}) collective-permute-start(bf16[1,48,3072]{2,1,0:T(8,128)(2,1)S(1)} %get-tuple-element.235), channel_id=1, source_target_pairs={{0,2},{1,3},{2,0},{3,1},{4,6},{5,7},{6,4},{7,5},{8,10},{9,11},{10,... | collective-permute-start | bytes 884744 | tf_op jit(solution)/shard_map/ppermute | solution.py:780
  195.2 11.0 %collective-permute-start.30 = (bf16[1,48,3072]{2,1,0:T(8,128)(2,1)S(1)}, bf16[1,48,3072]{2,1,0:T(8,128)(2,1)S(1)}, u32[]{:S(2)}, u32[]{:S(2)}) collective-permute-start(bf16[1,48,3072]{2,1,0:T(8,128)(2,1)S(1)} %get-tuple-element.236), channel_id=1, source_target_pairs={{0,4},{1,5},{2,6},{3,7},{4,0},{5,1},{6,2},{7,3},{8,12},{9,13},{10,... | collective-permute-start | bytes 884744 | tf_op jit(solution)/shard_map/ppermute | solution.py:780
  208.6 18.1 %collective-permute-start.32 = (bf16[48,3072]{1,0:T(8,128)(2,1)S(1)}, bf16[48,3072]{1,0:T(8,128)(2,1)S(1)}, u32[]{:S(2)}, u32[]{:S(2)}) collective-permute-start(bf16[48,3072]{1,0:T(8,128)(2,1)S(1)} %get-tuple-element.246), channel_id=1, source_target_pairs={{0,8},{1,9},{2,10},{3,11},{4,12},{5,13},{6,14},{7,15},{8,0},{9,1},... | collective-permute-start | bytes 884744 | tf_op jit(solution)/shard_map/ppermute | solution.py:865
  209.1 17.6 %collective-permute-start.31 = (bf16[48,3072]{1,0:T(8,128)(2,1)S(1)}, bf16[48,3072]{1,0:T(8,128)(2,1)S(1)}, u32[]{:S(2)}, u32[]{:S(2)}) collective-permute-start(bf16[48,3072]{1,0:T(8,128)(2,1)S(1)} %add_convert_fusion.21), channel_id=1, source_target_pairs={{0,16},{8,24},{16,0},{24,8},{1,17},{9,25},{17,1},{25,9},{2,18},{10... | collective-permute-start | bytes 884744 | tf_op jit(solution)/shard_map/ppermute | solution.py:869
  211.7 15.1 %collective-permute-start.33 = (bf16[2,48,3072]{2,1,0:T(8,128)(2,1)S(1)}, bf16[2,48,3072]{2,1,0:T(8,128)(2,1)S(1)}, u32[]{:S(2)}, u32[]{:S(2)}) collective-permute-start(bf16[2,48,3072]{2,1,0:T(8,128)(2,1)S(1)} %get-tuple-element.247), channel_id=1, source_target_pairs={{0,2},{1,3},{2,0},{3,1},{4,6},{5,7},{6,4},{7,5},{8,10},{9,11},{10,... | collective-permute-start | bytes 1769480 | tf_op jit(solution)/shard_map/ppermute | solution.py:780
  212.3 14.5 %collective-permute-start.34 = (bf16[2,48,3072]{2,1,0:T(8,128)(2,1)S(1)}, bf16[2,48,3072]{2,1,0:T(8,128)(2,1)S(1)}, u32[]{:S(2)}, u32[]{:S(2)}) collective-permute-start(bf16[2,48,3072]{2,1,0:T(8,128)(2,1)S(1)} %get-tuple-element.248), channel_id=1, source_target_pairs={{0,4},{1,5},{2,6},{3,7},{4,0},{5,1},{6,2},{7,3},{8,12},{9,13},{10,... | collective-permute-start | bytes 1769480 | tf_op jit(solution)/shard_map/ppermute | solution.py:780
  229.9 15.9 %collective-permute-start.38 = (bf16[48,3072]{1,0:T(8,128)(2,1)S(1)}, bf16[48,3072]{1,0:T(8,128)(2,1)S(1)}, u32[]{:S(2)}, u32[]{:S(2)}) collective-permute-start(bf16[48,3072]{1,0:T(8,128)(2,1)S(1)} %add_convert_fusion.18), channel_id=1, source_target_pairs={{0,8},{1,9},{2,10},{3,11},{4,12},{5,13},{6,14},{7,15},{8,0},{9,1},... | collective-permute-start | bytes 884744 | tf_op jit(solution)/shard_map/ppermute | solution.py:865
  231.5 16.0 %collective-permute-start.39 = (bf16[48,3072]{1,0:T(8,128)(2,1)S(1)}, bf16[48,3072]{1,0:T(8,128)(2,1)S(1)}, u32[]{:S(2)}, u32[]{:S(2)}) collective-permute-start(bf16[48,3072]{1,0:T(8,128)(2,1)S(1)} %add_convert_fusion.17), channel_id=1, source_target_pairs={{0,16},{8,24},{16,0},{24,8},{1,17},{9,25},{17,1},{25,9},{2,18},{10... | collective-permute-start | bytes 884744 | tf_op jit(solution)/shard_map/ppermute | solution.py:869
  231.9 15.7 %collective-permute-start.36 = (bf16[1,48,6144]{2,1,0:T(8,128)(2,1)S(1)}, bf16[1,48,6144]{2,1,0:T(8,128)(2,1)S(1)}, u32[]{:S(2)}, u32[]{:S(2)}) collective-permute-start(bf16[1,48,6144]{2,1,0:T(8,128)(2,1)S(1)} %pad_maximum_fusion.8), channel_id=1, source_target_pairs={{0,2},{1,3},{2,0},{3,1},{4,6},{5,7},{6,4},{7,5},{8,10},{9,11},{10,... | collective-permute-start | bytes 1769480 | tf_op jit(solution)/shard_map/ppermute | solution.py:780
  232.9 14.7 %collective-permute-start.37 = (bf16[1,48,6144]{2,1,0:T(8,128)(2,1)S(1)}, bf16[1,48,6144]{2,1,0:T(8,128)(2,1)S(1)}, u32[]{:S(2)}, u32[]{:S(2)}) collective-permute-start(bf16[1,48,6144]{2,1,0:T(8,128)(2,1)S(1)} %pad_maximum_fusion.9), channel_id=1, source_target_pairs={{0,4},{1,5},{2,6},{3,7},{4,0},{5,1},{6,2},{7,3},{8,12},{9,13},{10,... | collective-permute-start | bytes 1769480 | tf_op jit(solution)/shard_map/ppermute | solution.py:780
  249.3 12.4 %collective-permute-start.41 = (bf16[1,48,1536]{2,1,0:T(8,128)(2,1)S(1)}, bf16[1,48,1536]{2,1,0:T(8,128)(2,1)S(1)}, u32[]{:S(2)}, u32[]{:S(2)}) collective-permute-start(bf16[1,48,1536]{2,1,0:T(8,128)(2,1)S(1)} %get-tuple-element.279), channel_id=1, source_target_pairs={{0,2},{1,3},{2,0},{3,1},{4,6},{5,7},{6,4},{7,5},{8,10},{9,11},{10,... | collective-permute-start | bytes 442376 | tf_op jit(solution)/shard_map/ppermute | solution.py:780
  250.4 11.4 %collective-permute-start.42 = (bf16[1,48,1536]{2,1,0:T(8,128)(2,1)S(1)}, bf16[1,48,1536]{2,1,0:T(8,128)(2,1)S(1)}, u32[]{:S(2)}, u32[]{:S(2)}) collective-permute-start(bf16[1,48,1536]{2,1,0:T(8,128)(2,1)S(1)} %get-tuple-element.280), channel_id=1, source_target_pairs={{0,4},{1,5},{2,6},{3,7},{4,0},{5,1},{6,2},{7,3},{8,12},{9,13},{10,... | collective-permute-start | bytes 442376 | tf_op jit(solution)/shard_map/ppermute | solution.py:780
  251.9 9.8 %collective-permute-start.40 = (bf16[48,3072]{1,0:T(8,128)(2,1)S(1)}, bf16[48,3072]{1,0:T(8,128)(2,1)S(1)}, u32[]{:S(2)}, u32[]{:S(2)}) collective-permute-start(bf16[48,3072]{1,0:T(8,128)(2,1)S(1)} %get-tuple-element.278), channel_id=1, source_target_pairs={{0,8},{1,9},{2,10},{3,11},{4,12},{5,13},{6,14},{7,15},{8,0},{9,1},... | collective-permute-start | bytes 884744 | tf_op jit(solution)/shard_map/ppermute | solution.py:865
  266.5 10.0 %collective-permute-start.46 = (bf16[48,1536]{1,0:T(8,128)(2,1)S(1)}, bf16[48,1536]{1,0:T(8,128)(2,1)S(1)}, u32[]{:S(2)}, u32[]{:S(2)}) collective-permute-start(bf16[48,1536]{1,0:T(8,128)(2,1)S(1)} %get-tuple-element.304), channel_id=1, source_target_pairs={{0,8},{1,9},{2,10},{3,11},{4,12},{5,13},{6,14},{7,15},{8,0},{9,1},... | collective-permute-start | bytes 442376 | tf_op jit(solution)/shard_map/ppermute | solution.py:865
  268.6 17.9 %collective-permute-start.49 = (bf16[48,3072]{1,0:T(8,128)(2,1)S(1)}, bf16[48,3072]{1,0:T(8,128)(2,1)S(1)}, u32[]{:S(2)}, u32[]{:S(2)}) collective-permute-start(bf16[48,3072]{1,0:T(8,128)(2,1)S(1)} %add_convert_fusion.10), channel_id=1, source_target_pairs={{0,16},{8,24},{16,0},{24,8},{1,17},{9,25},{17,1},{25,9},{2,18},{10... | collective-permute-start | bytes 884744 | tf_op jit(solution)/shard_map/ppermute | solution.py:869
  270.5 37.4 %collective-permute-start.55 = (bf16[48,3072]{1,0:T(8,128)(2,1)S(1)}, bf16[48,3072]{1,0:T(8,128)(2,1)S(1)}, u32[]{:S(2)}, u32[]{:S(2)}) collective-permute-start(bf16[48,3072]{1,0:T(8,128)(2,1)S(1)} %add_convert_fusion.9), channel_id=1, source_target_pairs={{0,8},{1,9},{2,10},{3,11},{4,12},{5,13},{6,14},{7,15},{8,0},{9,1},... | collective-permute-start | bytes 884744 | tf_op jit(solution)/shard_map/ppermute | solution.py:865
  271.0 11.9 %collective-permute-start.44 = (bf16[2,48,2432]{2,1,0:T(8,128)(2,1)S(1)}, bf16[2,48,2432]{2,1,0:T(8,128)(2,1)S(1)}, u32[]{:S(2)}, u32[]{:S(2)}) collective-permute-start(bf16[2,48,2432]{2,1,0:T(8,128)(2,1)S(1)} %get-tuple-element.302), channel_id=1, source_target_pairs={{0,2},{1,3},{2,0},{3,1},{4,6},{5,7},{6,4},{7,5},{8,10},{9,11},{10,... | collective-permute-start | bytes 1400840 | tf_op jit(solution)/shard_map/ppermute | solution.py:780
  272.5 11.6 %collective-permute-start.45 = (bf16[2,48,2432]{2,1,0:T(8,128)(2,1)S(1)}, bf16[2,48,2432]{2,1,0:T(8,128)(2,1)S(1)}, u32[]{:S(2)}, u32[]{:S(2)}) collective-permute-start(bf16[2,48,2432]{2,1,0:T(8,128)(2,1)S(1)} %get-tuple-element.303), channel_id=1, source_target_pairs={{0,4},{1,5},{2,6},{3,7},{4,0},{5,1},{6,2},{7,3},{8,12},{9,13},{10,... | collective-permute-start | bytes 1400840 | tf_op jit(solution)/shard_map/ppermute | solution.py:780
  286.0 8.5 %collective-permute-start.51 = (bf16[48,1536]{1,0:T(8,128)(2,1)S(1)}, bf16[48,1536]{1,0:T(8,128)(2,1)S(1)}, u32[]{:S(2)}, u32[]{:S(2)}) collective-permute-start(bf16[48,1536]{1,0:T(8,128)(2,1)S(1)} %add_convert_fusion.35), channel_id=1, source_target_pairs={{0,16},{8,24},{16,0},{24,8},{1,17},{9,25},{17,1},{25,9},{2,18},{10... | collective-permute-start | bytes 442376 | tf_op jit(solution)/shard_map/ppermute | solution.py:869
  291.4 11.2 %collective-permute-start.50 = (bf16[48,2432]{1,0:T(8,128)(2,1)S(1)}, bf16[48,2432]{1,0:T(8,128)(2,1)S(1)}, u32[]{:S(2)}, u32[]{:S(2)}) collective-permute-start(bf16[48,2432]{1,0:T(8,128)(2,1)S(1)} %get-tuple-element.316), channel_id=1, source_target_pairs={{0,8},{1,9},{2,10},{3,11},{4,12},{5,13},{6,14},{7,15},{8,0},{9,1},... | collective-permute-start | bytes 700424 | tf_op jit(solution)/shard_map/ppermute | solution.py:865
  294.0 14.0 %collective-permute-start.54 = (bf16[48,3072]{1,0:T(8,128)(2,1)S(1)}, bf16[48,3072]{1,0:T(8,128)(2,1)S(1)}, u32[]{:S(2)}, u32[]{:S(2)}) collective-permute-start(bf16[48,3072]{1,0:T(8,128)(2,1)S(1)} %add_convert_fusion.8), channel_id=1, source_target_pairs={{0,8},{1,9},{2,10},{3,11},{4,12},{5,13},{6,14},{7,15},{8,0},{9,1},... | collective-permute-start | bytes 884744 | tf_op jit(solution)/shard_map/ppermute | solution.py:865
  302.7 7.8 %collective-permute-start.53 = (bf16[48,1536]{1,0:T(8,128)(2,1)S(1)}, bf16[48,1536]{1,0:T(8,128)(2,1)S(1)}, u32[]{:S(2)}, u32[]{:S(2)}) collective-permute-start(bf16[48,1536]{1,0:T(8,128)(2,1)S(1)} %add_convert_fusion.34), channel_id=1, source_target_pairs={{0,8},{1,9},{2,10},{3,11},{4,12},{5,13},{6,14},{7,15},{8,0},{9,1},... | collective-permute-start | bytes 442376 | tf_op jit(solution)/shard_map/ppermute | solution.py:865
  302.8 11.1 %collective-permute-start.52 = (bf16[48,2432]{1,0:T(8,128)(2,1)S(1)}, bf16[48,2432]{1,0:T(8,128)(2,1)S(1)}, u32[]{:S(2)}, u32[]{:S(2)}) collective-permute-start(bf16[48,2432]{1,0:T(8,128)(2,1)S(1)} %add_convert_fusion.29), channel_id=1, source_target_pairs={{0,16},{8,24},{16,0},{24,8},{1,17},{9,25},{17,1},{25,9},{2,18},{10... | collective-permute-start | bytes 700424 | tf_op jit(solution)/shard_map/ppermute | solution.py:869
  (72 other events, 463.4 us)

commit v8 on v7

--- a/solution.py
+++ b/solution.py
@@ -190,13 +190,13 @@
 
 
 def gather_small(dw, sums):
-    sums_t, sums_s, sums_f, ghb = sums
+    sums_t, sums_s, norm_s, sums_f, norm_f, ghb = sums
     columns = sums_t.shape[1]
     rows = columns // 8
     start = dw.shape[1] - 128
     zero = jnp.zeros((3, columns), F32)
-    order = [sums_t[0:4, :], sums_s[0:3, :], sums_f[0:1, :], zero, sums_t[4:5, :], sums_s[3:4, :], sums_f[1:2, :]]
-    order += [sums_t[5:6, :], sums_s[4:5, :], sums_f[2:3, :], jnp.zeros((SMALL - 17, columns), F32)]
+    order = [sums_t[0:4, :], sums_s[0:3, :], sums_f[0:1, :], zero, sums_t[4:5, :], norm_s[0:1, :], norm_f[0:1, :]]
+    order += [sums_t[5:6, :], norm_s[1:2, :], norm_f[1:2, :], jnp.zeros((SMALL - 17, columns), F32)]
     values = jnp.concatenate(order, axis=0).astype(BF)
     for piece in range(8):
         block = nt(values, piece_select(piece, rows, columns))
@@ -961,8 +961,6 @@
         held_r, held_e, sent_e, sent_s, gy, norm_s = tie(total(held_r, got_r), held_e, sent_e, sum_s.first(), gy, norm_s)
         sum_s.cross(sent_s)
         got_r, got_e = across_pairs(held_r), swap_z(sent_e)
-        sums_s = jnp.concatenate([sums_s[0:3], norm_s[0:2], sums_s[5:]], axis=0)
-        sums_f = jnp.concatenate([sums_f[0:1], norm_f[0:2], sums_f[3:]], axis=0)
     go, sums_m, *grad_m = net.mixer_backward(gy, o_t, e_t, wt)
     if pieced:
         sum_m = Reduction(*grad_m)
@@ -981,15 +979,17 @@
         held_s, sent_s, sent_m, gqkv = tie(held_s, sent_s, sum_m.second(), gqkv)
         sum_m.cross_again(sent_m)
         got_s = swap_z(sent_s)
-    grad_t = net.time_weights(gqkv, normed_t, (sums_t, sums_s, sums_f, ghb) if pieced else ())
+    grad_t = net.time_weights(gqkv, normed_t, (sums_t, sums_s, norm_s, sums_f, norm_f, ghb) if pieced else ())
 
     if pieced:
         got_s, sum_m.last_x, sum_m.last_y, grad_t = tie(got_s, sum_m.last_x, sum_m.last_y, grad_t)
         sum_t = Reduction(*grad_t)
+        sent_t, got_s, got_e, sum_m.last_x, sum_m.last_y, gx, out = tie(
+            sum_t.first(), got_s, got_e, sum_m.last_x, sum_m.last_y, gx, out
+        )
+        sum_t.cross(sent_t)
         held_s, held_e = total(held_s, got_s), total(held_e, got_e)
         held_m, sent_m = split_groups(sum_m.finish(), even)
-        sent_t, held_s, held_e, held_m, sent_m, gx, out = tie(sum_t.first(), held_s, held_e, held_m, sent_m, gx, out)
-        sum_t.cross(sent_t)
         got_s, got_m, got_e = across_pairs(held_s), swap_z(sent_m), swap_z(held_e)
         sum_t.from_x, sum_t.from_y, got_m = tie(sum_t.from_x, sum_t.from_y, got_m)
         held_m, sent_t = tie(total(held_m, got_m), sum_t.second())

time: 328 us -> 327 us (level)
    unnamed x134 -> x136, local copies, waits for them, and re-layouts: 15.5 us -> 15.4 us
  transfers between devices with their start and end apart: 57 -> 57, of which waited for: 18 -> 19; matrix products, arithmetic and copies ran while one was open for 13% -> 12% of each run, Pallas kernels for 34% -> 34%
where the time goes in v8:
time: 327 us; the launch traced here: 323 us
  Pallas kernels  139 us (43%)
  waiting for transfers between devices  66 us (20%)
  starting transfers between devices  51 us (16%)
  other arithmetic  40.9 us (13%)
  local copies, waits for them, and re-layouts  24.4 us (7%)
    pallas_call x10, Pallas kernels, call(): pl.pallas_call(kernel, out_shape=[jax.ShapeDtypeStruct(s, d) for s, d in...  139 us
    ppermute x42, waiting for transfers between devices, permute(): return lax.ppermute(value, BOTH, pairs)  46.2 us
    ppermute x42, starting transfers between devices, permute(): return lax.ppermute(value, BOTH, pairs)  34.4 us
    unnamed x136, local copies, waits for them, and re-layouts  15.4 us
    ppermute x10, waiting for transfers between devices, swap_z(): return lax.ppermute(value, BOTH, pairs)  14.5 us
    another operation x4, other arithmetic, pack_rows(): return jnp.stack(frames, axis=1).reshape(clips * FRAMES * BLOCK, columns)  10.3 us
    convert_element_type x20, other arithmetic, total(): return sum((t.astype(F32) for t in terms)).astype(BF)  8.9 us
    ppermute x10, starting transfers between devices, swap_z(): return lax.ppermute(value, BOTH, pairs)  8.63 us
  transfers between devices with their start and end apart: 57, of which 19 were waited for; matrix products, arithmetic and copies ran while one was open for 12% of the time, Pallas kernels for 34%

profile of v8, /device:TPU:0, one launch (start us, length us, event | category | flops | bytes accessed | tf_op | source)
XLA Modules:
  0.0 322.9 jit_solution(3687633020023710273)
XLA Ops:
  6.5 2.9 collective-permute-start.1
  10.2 3.6 %fusion.4 = (bf16[2,1,208,768]{3,0,2,1:T(2,128)(2,1)S(1)}, bf16[2,1,208,768]{3,0,2,1:T(2,128)(2,1)S(1)}) fusion(bf16[2,1,768]{2,0,1:T(2,128)(2,1)S(1)} %slice.491, bf16[2,196,768]{2,0,1:T(2,128)(2,1)S(1)} %get-tuple-element.370, bf16[208]{0:T(256)(128)(2,1)S(1)} %pad.62.clone, bf16[2,196,768]{2,0,1:T(2,128)(2,1)S(1)} %get-tuple-element.371), kind=kLoop, calls=%fused_computation.23 | loop fusion | flops 1277952 | bytes 2485664 | tf_op jit(solution)/shard_map/stack | solution.py:664
  13.8 1.8 pad_maximum_fusion
  16.8 2.4 collective-permute-done.1.refs_4_.refs_6_.refs_10_
  20.2 2.1 collective-permute-start.4
  22.2 9.7 %collective-permute-done.8.refs_5_.refs_7_.refs_11_ = bf16[96,3968]{1,0:T(8,128)(2,1)} collective-permute-done((bf16[96,3968]{1,0:T(8,128)(2,1)S(1)}, bf16[96,3968]{1,0:T(8,128)(2,1)}, u32[]{:S(2)}, u32[]{:S(2)}) %collective-permute-start.8) | collective-permute-done | bytes 761888 | tf_op jit(solution)/shard_map/ppermute | solution.py:780
  32.4 2.6 collective-permute-done.4.refs_6_.refs_8_.refs_12_
  36.0 2.0 collective-permute-start.6
  38.1 2.0 collective-permute-start.5
  40.2 14.1 %time_forward.1 = (bf16[832,768]{1,0:T(8,128)(2,1)}, bf16[832,2304]{1,0:T(8,128)(2,1)}, bf16[832,768]{1,0:T(8,128)(2,1)}, bf16[832,768]{1,0:T(8,128)(2,1)}, f32[...) custom-call(s32[16]{0:T(128)} %stack.76.refs_0_, bf16[832,768]{1,0:T(8,128)(2,1)} %bitcast.64, ...), custom_call_target="tpu_custom_call" | custom-call | flops 56000000000 | tf_op jit(solution)/shard_map/time_forward/pallas_call | solution.py:284
  57.3 2.4 bitcast_multiply_fusion
  60.5 10.3 %collective-permute-done.12.refs_7_.refs_10_.refs_9_ = bf16[96,3072]{1,0:T(8,128)(2,1)S(1)} collective-permute-done((bf16[96,3072]{1,0:T(8,128)(2,1)}, bf16[96,3072]{1,0:T(8,128)(2,1)S(1)}, u32[]{:S(2)}, u32[]{:S(2)}) %collective-permute-start.12) | collective-permute-done | bytes 589856 | tf_op jit(solution)/shard_map/ppermute | solution.py:780
  70.8 3.1 maximum_bitcast_fusion.1
  73.9 1.8 pad_maximum_fusion.1
  80.1 16.8 %space_forward.1 = (bf16[832,768]{1,0:T(8,128)(2,1)}, bf16[832,2304]{1,0:T(8,128)(2,1)}, bf16[48,208,208]{2,1,0:T(8,128)(2,1)}, bf16[832,768]{1,0:T(8,128)(2,1)}, f32[832,768]{1,0:T(8,128)}) custom-call(s32[16]{0:T(128)} %stack.76.refs_0_, f32[832,768]{1,0:T(8,128)} %get-tuple-element.191.refs_1_.refs_2_, ...), custom_call_target="tpu_custom_call" | custom-call | flops 64000000000 | tf_op jit(solution)/shard_map/space_forward/pallas_call | solution.py:284
  97.6 3.2 collective-permute-done.19.refs_11_
  102.8 28.1 %feed_out.1 = (bf16[832,768]{1,0:T(8,128)(2,1)}, bf16[832,768]{1,0:T(8,128)(2,1)}, bf16[832,3072]{1,0:T(8,128)(2,1)}, f32[8,768]{1,0:T(8,128)}, bf16[8,48,3072]{...) custom-call(s32[16]{0:T(128)} %stack.76.refs_0_, f32[832,768]{1,0:T(8,128)} %get-tuple-element.202.refs_1_.refs_2_, ...), custom_call_target="tpu_custom_call" | custom-call | flops 120000004096 | tf_op jit(solution)/shard_map/feed_out/pallas_call | solution.py:284
  131.2 2.4 copy-done.32
  134.9 7.8 %feed_in.1 = (f32[8,3072]{1,0:T(8,128)S(1)}, bf16[8,48,3072]{2,1,0:T(8,128)(2,1)S(1)}, bf16[8,48,3072]{2,1,0:T(8,128)(2,1)}) custom-call(s32[16]{0:T(128)S(1)} %copy-done.8, bf16[832,3072]{1,0:T(8,128)(2,1)S(1)} %copy-done.32, bf16[832,768]{1,0:T(8,128)(2,1)S(1)} %copy-done.41), custom_call_target="tpu_custom_call" | custom-call | flops 32000000000 | tf_op jit(solution)/shard_map/feed_in/pallas_call | solution.py:284
  143.7 2.1 add_convert_fusion.4
  150.4 2.4 copy-done.33
  152.9 1.7 copy-done.36
  154.6 8.7 %feed_norm.1 = (f32[832,768]{1,0:T(8,128)S(1)}, f32[8,768]{1,0:T(8,128)S(1)}) custom-call(s32[16]{0:T(128)S(1)} %copy-done.8, bf16[832,3072]{1,0:T(8,128)(2,1)S(1)} %copy-done.33, f32[832,768]{1,0:T(8,128)S(1)} %copy-done.36, bf16[832,768]{1,0:T(8,128)(2,1)S(1)} %bitcast.67, f32[32,768]{1,0:T(8,128)S(1)} %copy-done.48, bf16[96,6144]{1,0:T(8,128)(2,1)S(1)} %copy-done.7, ...), custom_call_target="tpu_custom_call" | custom-call | flops 40000000000 | tf_op jit(solution)/shard_map/feed_norm/pallas_call | solution.py:284
  163.4 1.9 add_convert_fusion.26
  168.1 20.8 %space_backward.1 = (bf16[832,2304]{1,0:T(8,128)(2,1)S(1)}, f32[8,768]{1,0:T(8,128)S(1)}, bf16[8,48,3072]{2,1,0:T(8,128)(2,1)S(1)}, bf16[8,48,3072]{2,1,0:T(8,128)(2,1)S(1)}) custom-call(s32[16]{0:T(128)S(1)} %copy-done.8, f32[832,768]{1,0:T(8,128)S(1)} %get-tuple-element.223.refs_1_.refs_3_, bf16[832,768]{1,0:T(8,128)(2,1)S(1)} %copy-done.44, ...), custom_call_target="tpu_custom_call" | custom-call | flops 80000000000 | tf_op jit(solution)/shard_map/space_backward/pallas_call | solution.py:284
  192.0 1.6 collective-permute-start.28
  195.3 1.7 copy-done.38
  197.0 7.7 %space_norm.1 = (f32[832,768]{1,0:T(8,128)S(1)}, f32[8,768]{1,0:T(8,128)S(1)}) custom-call(s32[16]{0:T(128)S(1)} %copy-done.8, bf16[832,2304]{1,0:T(8,128)(2,1)S(1)} %get-tuple-element.237.refs_1_, f32[832,768]{1,0:T(8,128)S(1)} %copy-done.38, f32[832,768]{1,0:T(8,128)S(1)} %get-tuple-element.223.refs_1_.refs_3_, f32[32,768]{1,0:T(8,128)S(1)} %copy-done.48, ...), custom_call_target="tpu_custom_call" | custom-call | flops 40000000000 | tf_op jit(solution)/shard_map/space_norm/pallas_call | solution.py:284
  204.8 1.9 select_bitcast_fusion.2
  207.7 2.6 collective-permute-start.31
  212.8 13.3 %mixer_backward.1 = (bf16[832,768]{1,0:T(8,128)(2,1)S(1)}, f32[8,768]{1,0:T(8,128)S(1)}, bf16[8,48,1536]{2,1,0:T(8,128)(2,1)S(1)}, bf16[8,48,1536]{2,1,0:T(8,128)(2,1)S(1)}) custom-call(s32[16]{0:T(128)S(1)} %copy-done.8, f32[832,768]{1,0:T(8,128)S(1)} %get-tuple-element.249.refs_1_.refs_5_, bf16[832,768]{1,0:T(8,128)(2,1)S(1)} %copy-done.39, ...), custom_call_target="tpu_custom_call" | custom-call | flops 32000000000 | tf_op jit(solution)/shard_map/mixer_backward/pallas_call | solution.py:284
  226.7 2.4 collective-permute-done.35
  233.0 11.4 %time_backward.1 = (bf16[832,2304]{1,0:T(8,128)(2,1)S(1)}, bf16[832,768]{1,0:T(8,128)(2,1)S(1)}, f32[8,768]{1,0:T(8,128)S(1)}) custom-call(s32[16]{0:T(128)S(1)} %copy-done.8, bf16[832,768]{1,0:T(8,128)(2,1)S(1)} %get-tuple-element.267.refs_1_, bf16[832,2304]{1,0:T(8,128)(2,1)S(1)} %copy-done.37, f32[1664,128]{1,0:T(8,128)S(1)} %copy-done.43, ...), custom_call_target="tpu_custom_call" | custom-call | flops 48000000000 | tf_op jit(solution)/shard_map/time_backward/pallas_call | solution.py:284
  244.4 2.6 collective-permute-done.39
  250.5 9.7 %time_weights.1 = (bf16[8,48,2432]{2,1,0:T(8,128)(2,1)S(1)}, bf16[8,48,2432]{2,1,0:T(8,128)(2,1)S(1)}) custom-call(s32[16]{0:T(128)S(1)} %copy-done.8, bf16[832,2304]{1,0:T(8,128)(2,1)S(1)} %get-tuple-element.281.refs_1_, bf16[832,768]{1,0:T(8,128)(2,1)S(1)} %copy-done.42, f32[8,768]{1,0:T(8,128)S(1)} %get-tuple-element.283.refs_3_, ...), custom_call_target="tpu_custom_call" | custom-call | flops 32000000000 | tf_op jit(solution)/shard_map/time_weights/pallas_call | solution.py:284
  261.7 2.5 collective-permute-done.43
  265.3 1.9 collective-permute-start.46
  267.3 2.4 collective-permute-start.49
  272.6 3.1 maximum_multiply_fusion
  275.7 6.3 %collective-permute-done.44 = bf16[2,48,2432]{2,1,0:T(8,128)(2,1)S(1)} collective-permute-done((bf16[2,48,2432]{2,1,0:T(8,128)(2,1)S(1)}, bf16[2,48,2432]{2,1,0:T(8,128)(2,1)S(1)}, u32[]{:S(2)}, u32[]{:S(2)}) %collective-permute-start.44) | collective-permute-done | bytes 466976 | tf_op jit(solution)/shard_map/ppermute | solution.py:780
  286.1 3.1 collective-permute-done.47
  290.5 1.6 collective-permute-start.50
  293.6 8.1 %collective-permute-done.50 = bf16[48,2432]{1,0:T(8,128)(2,1)S(1)} collective-permute-done((bf16[48,2432]{1,0:T(8,128)(2,1)S(1)}, bf16[48,2432]{1,0:T(8,128)(2,1)S(1)}, u32[]{:S(2)}, u32[]{:S(2)}) %collective-permute-start.50) | collective-permute-done | bytes 233504 | tf_op jit(solution)/shard_map/ppermute | solution.py:865
  301.9 2.2 collective-permute-start.52
  304.1 2.6 maximum_bitcast_fusion
  307.8 2.2 collective-permute-done.53
  310.0 2.6 collective-permute-done.52
  316.8 3.1 collective-permute-done.56
  (295 shorter events, 67.4 us)
Async XLA Ops:
  5.8 13.3 %collective-permute-start.3 = (bf16[96,6144]{1,0:T(8,128)(2,1)S(1)}, bf16[96,6144]{1,0:T(8,128)(2,1)S(1)}, u32[]{:S(2)}, u32[]{:S(2)}) collective-permute-start(bf16[96,6144]{1,0:T(8,128)(2,1)S(1)} %slice_dynamic-update-slice_fusion.refs_5_), channel_id=1, source_target_pairs={{0,1},{1,0},{2,3},{3,2},{4,5},{5,4},{6,7},{7,6},{8,9},{9,8},{10,11... | collective-permute-start | bytes 3538952 | tf_op jit(solution)/shard_map/ppermute | solution.py:780
  6.3 10.5 %collective-permute-start.2 = (bf16[96,3072]{1,0:T(8,128)(2,1)S(1)}, bf16[96,3072]{1,0:T(8,128)(2,1)}, u32[]{:S(2)}, u32[]{:S(2)}) collective-permute-start(bf16[96,3072]{1,0:T(8,128)(2,1)S(1)} %pad_maximum_fusion.7.refs_3_.refs_6_.refs_5_), channel_id=1, source_target_pairs={{0,1},{1,0},{2,3},{3,2},{4,5},{5,4},{6,7},{7,6},{8,9},{9,8},{10,11... | collective-permute-start | bytes 1769480 | tf_op jit(solution)/shard_map/ppermute | solution.py:780
  6.5 12.7 %collective-permute-start.1 = (bf16[96,3968]{1,0:T(8,128)(2,1)S(1)}, bf16[96,3968]{1,0:T(8,128)(2,1)}, u32[]{:S(2)}, u32[]{:S(2)}) collective-permute-start(bf16[96,3968]{1,0:T(8,128)(2,1)S(1)} %fusion.1.refs_2_.refs_4_.refs_8_), channel_id=1, source_target_pairs={{0,2},{1,5},{2,0},{3,7},{4,6},{5,1},{6,4},{7,3},{8,10},{9,13},{10,... | collective-permute-start | bytes 2285576 | tf_op jit(solution)/shard_map/ppermute | solution.py:780
  9.4 22.5 %collective-permute-start.8 = (bf16[96,3968]{1,0:T(8,128)(2,1)S(1)}, bf16[96,3968]{1,0:T(8,128)(2,1)}, u32[]{:S(2)}, u32[]{:S(2)}) collective-permute-start(bf16[96,3968]{1,0:T(8,128)(2,1)S(1)} %collective-permute-done.refs_3_.refs_5_.refs_9_), channel_id=1, source_target_pairs={{0,2},{1,5},{2,0},{3,7},{4,6},{5,1},{6,4},{7,3},{8,10},{9,13},{10,... | collective-permute-start | bytes 2285576 | tf_op jit(solution)/shard_map/ppermute | solution.py:780
  20.2 14.8 %collective-permute-start.4 = (bf16[96,3968]{1,0:T(8,128)(2,1)}, bf16[96,3968]{1,0:T(8,128)(2,1)}, u32[]{:S(2)}, u32[]{:S(2)}) collective-permute-start(bf16[96,3968]{1,0:T(8,128)(2,1)} %collective-permute-done.1.refs_4_.refs_6_.refs_10_), channel_id=1, source_target_pairs={{0,4},{1,3},{2,6},{3,1},{4,0},{5,7},{6,2},{7,5},{8,12},{9,11},{10,... | collective-permute-start | bytes 2285576 | tf_op jit(solution)/shard_map/ppermute | solution.py:780
  31.9 6.2 %collective-permute-start.10 = (bf16[96,3968]{1,0:T(8,128)(2,1)}, bf16[96,3968]{1,0:T(8,128)(2,1)S(1)}, u32[]{:S(2)}, u32[]{:S(2)}) collective-permute-start(bf16[96,3968]{1,0:T(8,128)(2,1)} %collective-permute-done.8.refs_5_.refs_7_.refs_11_), channel_id=1, source_target_pairs={{0,1},{1,0},{2,3},{3,2},{4,5},{5,4},{6,7},{7,6},{8,9},{9,8},{10,11... | collective-permute-start | bytes 2285576 | tf_op jit(solution)/shard_map/ppermute | solution.py:780
  31.9 8.2 %collective-permute-start.9 = (bf16[96,3968]{1,0:T(8,128)(2,1)}, bf16[96,3968]{1,0:T(8,128)(2,1)}, u32[]{:S(2)}, u32[]{:S(2)}) collective-permute-start(bf16[96,3968]{1,0:T(8,128)(2,1)} %collective-permute-done.1.refs_4_.refs_6_.refs_10_), channel_id=1, source_target_pairs={{0,1},{1,0},{2,3},{3,2},{4,5},{5,4},{6,7},{7,6},{8,9},{9,8},{10,11... | collective-permute-start | bytes 2285576 | tf_op jit(solution)/shard_map/ppermute | solution.py:780
  36.0 18.2 %collective-permute-start.6 = (bf16[96,3072]{1,0:T(8,128)(2,1)S(1)}, bf16[96,3072]{1,0:T(8,128)(2,1)}, u32[]{:S(2)}, u32[]{:S(2)}) collective-permute-start(bf16[96,3072]{1,0:T(8,128)(2,1)S(1)} %pad_maximum_fusion.7.refs_3_.refs_6_.refs_5_), channel_id=1, source_target_pairs={{0,2},{1,5},{2,0},{3,7},{4,6},{5,1},{6,4},{7,3},{8,10},{9,13},{10,... | collective-permute-start | bytes 1769480 | tf_op jit(solution)/shard_map/ppermute | solution.py:780
  38.0 16.2 %collective-permute-start.7 = (bf16[96,3072]{1,0:T(8,128)(2,1)}, bf16[96,3072]{1,0:T(8,128)(2,1)}, u32[]{:S(2)}, u32[]{:S(2)}) collective-permute-start(bf16[96,3072]{1,0:T(8,128)(2,1)} %collective-permute-done.2.refs_4_.refs_7_.refs_6_), channel_id=1, source_target_pairs={{0,2},{1,5},{2,0},{3,7},{4,6},{5,1},{6,4},{7,3},{8,10},{9,13},{10,... | collective-permute-start | bytes 1769480 | tf_op jit(solution)/shard_map/ppermute | solution.py:780
  38.1 38.8 %collective-permute-start.5 = (bf16[96,6144]{1,0:T(8,128)(2,1)S(1)}, bf16[96,6144]{1,0:T(8,128)(2,1)}, u32[]{:S(2)}, u32[]{:S(2)}) collective-permute-start(bf16[96,6144]{1,0:T(8,128)(2,1)S(1)} %slice_dynamic-update-slice_fusion.refs_5_), channel_id=1, source_target_pairs={{0,2},{1,5},{2,0},{3,7},{4,6},{5,1},{6,4},{7,3},{8,10},{9,13},{10,... | collective-permute-start | bytes 3538952 | tf_op jit(solution)/shard_map/ppermute | solution.py:780
  54.3 16.5 %collective-permute-start.12 = (bf16[96,3072]{1,0:T(8,128)(2,1)}, bf16[96,3072]{1,0:T(8,128)(2,1)S(1)}, u32[]{:S(2)}, u32[]{:S(2)}) collective-permute-start(bf16[96,3072]{1,0:T(8,128)(2,1)} %collective-permute-done.6.refs_5_.refs_8_.refs_7_), channel_id=1, source_target_pairs={{0,4},{1,3},{2,6},{3,1},{4,0},{5,7},{6,2},{7,5},{8,12},{9,11},{10,... | collective-permute-start | bytes 1769480 | tf_op jit(solution)/shard_map/ppermute | solution.py:780
  56.0 41.0 %collective-permute-start.17 = (bf16[96,6144]{1,0:T(8,128)(2,1)S(1)}, bf16[96,6144]{1,0:T(8,128)(2,1)S(1)}, u32[]{:S(2)}, u32[]{:S(2)}) collective-permute-start(bf16[96,6144]{1,0:T(8,128)(2,1)S(1)} %copy-done.10), channel_id=1, source_target_pairs={{0,2},{1,5},{2,0},{3,7},{4,6},{5,1},{6,4},{7,3},{8,10},{9,13},{10,... | collective-permute-start | bytes 3538952 | tf_op jit(solution)/shard_map/ppermute | solution.py:780
  56.8 20.2 %collective-permute-start.13 = (bf16[96,3072]{1,0:T(8,128)(2,1)}, bf16[96,3072]{1,0:T(8,128)(2,1)S(1)}, u32[]{:S(2)}, u32[]{:S(2)}) collective-permute-start(bf16[96,3072]{1,0:T(8,128)(2,1)} %collective-permute-done.6.refs_5_.refs_8_.refs_7_), channel_id=1, source_target_pairs={{0,1},{1,0},{2,3},{3,2},{4,5},{5,4},{6,7},{7,6},{8,9},{9,8},{10,11... | collective-permute-start | bytes 1769480 | tf_op jit(solution)/shard_map/ppermute | solution.py:780
  56.8 20.2 %collective-permute-start.14 = (bf16[96,3072]{1,0:T(8,128)(2,1)}, bf16[96,3072]{1,0:T(8,128)(2,1)S(1)}, u32[]{:S(2)}, u32[]{:S(2)}) collective-permute-start(bf16[96,3072]{1,0:T(8,128)(2,1)} %collective-permute-done.7.refs_6_.refs_9_.refs_8_), channel_id=1, source_target_pairs={{0,1},{1,0},{2,3},{3,2},{4,5},{5,4},{6,7},{7,6},{8,9},{9,8},{10,11... | collective-permute-start | bytes 1769480 | tf_op jit(solution)/shard_map/ppermute | solution.py:780
  70.8 6.1 %collective-permute-start.15 = (bf16[96,3072]{1,0:T(8,128)(2,1)S(1)}, bf16[96,3072]{1,0:T(8,128)(2,1)S(1)}, u32[]{:S(2)}, u32[]{:S(2)}) collective-permute-start(bf16[96,3072]{1,0:T(8,128)(2,1)S(1)} %collective-permute-done.12.refs_7_.refs_10_.refs_9_), channel_id=1, source_target_pairs={{0,1},{1,0},{2,3},{3,2},{4,5},{5,4},{6,7},{7,6},{8,9},{9,8},{10,11... | collective-permute-start | bytes 1769480 | tf_op jit(solution)/shard_map/ppermute | solution.py:780
  77.9 19.6 %collective-permute-start.18 = (bf16[96,6144]{1,0:T(8,128)(2,1)}, bf16[96,6144]{1,0:T(8,128)(2,1)S(1)}, u32[]{:S(2)}, u32[]{:S(2)}) collective-permute-start(bf16[96,6144]{1,0:T(8,128)(2,1)} %collective-permute-done.5.refs_7_), channel_id=1, source_target_pairs={{0,1},{1,0},{2,3},{3,2},{4,5},{5,4},{6,7},{7,6},{8,9},{9,8},{10,11... | collective-permute-start | bytes 3538952 | tf_op jit(solution)/shard_map/ppermute | solution.py:780
  78.6 18.4 %collective-permute-start.16 = (bf16[96,6144]{1,0:T(8,128)(2,1)}, bf16[96,6144]{1,0:T(8,128)(2,1)}, u32[]{:S(2)}, u32[]{:S(2)}) collective-permute-start(bf16[96,6144]{1,0:T(8,128)(2,1)} %collective-permute-done.5.refs_7_), channel_id=1, source_target_pairs={{0,4},{1,3},{2,6},{3,1},{4,0},{5,7},{6,2},{7,5},{8,12},{9,11},{10,... | collective-permute-start | bytes 3538952 | tf_op jit(solution)/shard_map/ppermute | solution.py:780
  131.0 12.7 %collective-permute-start.21 = (bf16[8,48,3072]{2,1,0:T(8,128)(2,1)}, bf16[8,48,3072]{2,1,0:T(8,128)(2,1)}, u32[]{:S(2)}, u32[]{:S(2)}) collective-permute-start(bf16[8,48,3072]{2,1,0:T(8,128)(2,1)} %get-tuple-element.208), channel_id=1, source_target_pairs={{0,1},{1,0},{2,3},{3,2},{4,5},{5,4},{6,7},{7,6},{8,9},{9,8},{10,11... | collective-permute-start | bytes 7077896 | tf_op jit(solution)/shard_map/ppermute | solution.py:780
  145.9 17.4 %collective-permute-start.22 = (bf16[2,48,3072]{2,1,0:T(8,128)(2,1)S(1)}, bf16[2,48,3072]{2,1,0:T(8,128)(2,1)S(1)}, u32[]{:S(2)}, u32[]{:S(2)}) collective-permute-start(bf16[2,48,3072]{2,1,0:T(8,128)(2,1)S(1)} %get-tuple-element.214), channel_id=1, source_target_pairs={{0,2},{1,3},{2,0},{3,1},{4,6},{5,7},{6,4},{7,5},{8,10},{9,11},{10,... | collective-permute-start | bytes 1769480 | tf_op jit(solution)/shard_map/ppermute | solution.py:780
  147.1 16.3 %collective-permute-start.23 = (bf16[2,48,3072]{2,1,0:T(8,128)(2,1)S(1)}, bf16[2,48,3072]{2,1,0:T(8,128)(2,1)S(1)}, u32[]{:S(2)}, u32[]{:S(2)}) collective-permute-start(bf16[2,48,3072]{2,1,0:T(8,128)(2,1)S(1)} %get-tuple-element.215), channel_id=1, source_target_pairs={{0,4},{1,5},{2,6},{3,7},{4,0},{5,1},{6,2},{7,3},{8,12},{9,13},{10,... | collective-permute-start | bytes 1769480 | tf_op jit(solution)/shard_map/ppermute | solution.py:780
  165.5 23.5 %collective-permute-start.25 = (bf16[1,48,9216]{2,1,0:T(8,128)(2,1)S(1)}, bf16[1,48,9216]{2,1,0:T(8,128)(2,1)S(1)}, u32[]{:S(2)}, u32[]{:S(2)}) collective-permute-start(bf16[1,48,9216]{2,1,0:T(8,128)(2,1)S(1)} %pad_maximum_fusion.4), channel_id=1, source_target_pairs={{0,4},{1,5},{2,6},{3,7},{4,0},{5,1},{6,2},{7,3},{8,12},{9,13},{10,... | collective-permute-start | bytes 2654216 | tf_op jit(solution)/shard_map/ppermute | solution.py:780
  166.5 22.5 %collective-permute-start.26 = (bf16[1,48,9216]{2,1,0:T(8,128)(2,1)S(1)}, bf16[1,48,9216]{2,1,0:T(8,128)(2,1)S(1)}, u32[]{:S(2)}, u32[]{:S(2)}) collective-permute-start(bf16[1,48,9216]{2,1,0:T(8,128)(2,1)S(1)} %pad_maximum_fusion.3), channel_id=1, source_target_pairs={{0,2},{1,3},{2,0},{3,1},{4,6},{5,7},{6,4},{7,5},{8,10},{9,11},{10,... | collective-permute-start | bytes 2654216 | tf_op jit(solution)/shard_map/ppermute | solution.py:780
  188.9 17.8 %collective-permute-start.27 = (bf16[8,48,3072]{2,1,0:T(8,128)(2,1)S(1)}, bf16[8,48,3072]{2,1,0:T(8,128)(2,1)S(1)}, u32[]{:S(2)}, u32[]{:S(2)}) collective-permute-start(bf16[8,48,3072]{2,1,0:T(8,128)(2,1)S(1)} %get-tuple-element.232), channel_id=1, source_target_pairs={{0,1},{1,0},{2,3},{3,2},{4,5},{5,4},{6,7},{7,6},{8,9},{9,8},{10,11... | collective-permute-start | bytes 7077896 | tf_op jit(solution)/shard_map/ppermute | solution.py:780
  192.0 12.7 %collective-permute-start.28 = (bf16[48,3072]{1,0:T(8,128)(2,1)S(1)}, bf16[48,3072]{1,0:T(8,128)(2,1)S(1)}, u32[]{:S(2)}, u32[]{:S(2)}) collective-permute-start(bf16[48,3072]{1,0:T(8,128)(2,1)S(1)} %get-tuple-element.234), channel_id=1, source_target_pairs={{0,8},{1,9},{2,10},{3,11},{4,12},{5,13},{6,14},{7,15},{8,0},{9,1},... | collective-permute-start | bytes 884744 | tf_op jit(solution)/shard_map/ppermute | solution.py:865
  193.6 11.1 %collective-permute-start.29 = (bf16[1,48,3072]{2,1,0:T(8,128)(2,1)S(1)}, bf16[1,48,3072]{2,1,0:T(8,128)(2,1)S(1)}, u32[]{:S(2)}, u32[]{:S(2)}) collective-permute-start(bf16[1,48,3072]{2,1,0:T(8,128)(2,1)S(1)} %get-tuple-element.235), channel_id=1, source_target_pairs={{0,2},{1,3},{2,0},{3,1},{4,6},{5,7},{6,4},{7,5},{8,10},{9,11},{10,... | collective-permute-start | bytes 884744 | tf_op jit(solution)/shard_map/ppermute | solution.py:780
  194.2 10.6 %collective-permute-start.30 = (bf16[1,48,3072]{2,1,0:T(8,128)(2,1)S(1)}, bf16[1,48,3072]{2,1,0:T(8,128)(2,1)S(1)}, u32[]{:S(2)}, u32[]{:S(2)}) collective-permute-start(bf16[1,48,3072]{2,1,0:T(8,128)(2,1)S(1)} %get-tuple-element.236), channel_id=1, source_target_pairs={{0,4},{1,5},{2,6},{3,7},{4,0},{5,1},{6,2},{7,3},{8,12},{9,13},{10,... | collective-permute-start | bytes 884744 | tf_op jit(solution)/shard_map/ppermute | solution.py:780
  207.2 19.0 %collective-permute-start.32 = (bf16[48,3072]{1,0:T(8,128)(2,1)S(1)}, bf16[48,3072]{1,0:T(8,128)(2,1)S(1)}, u32[]{:S(2)}, u32[]{:S(2)}) collective-permute-start(bf16[48,3072]{1,0:T(8,128)(2,1)S(1)} %get-tuple-element.246), channel_id=1, source_target_pairs={{0,8},{1,9},{2,10},{3,11},{4,12},{5,13},{6,14},{7,15},{8,0},{9,1},... | collective-permute-start | bytes 884744 | tf_op jit(solution)/shard_map/ppermute | solution.py:865
  207.7 18.5 %collective-permute-start.31 = (bf16[48,3072]{1,0:T(8,128)(2,1)S(1)}, bf16[48,3072]{1,0:T(8,128)(2,1)S(1)}, u32[]{:S(2)}, u32[]{:S(2)}) collective-permute-start(bf16[48,3072]{1,0:T(8,128)(2,1)S(1)} %add_convert_fusion.21), channel_id=1, source_target_pairs={{0,16},{8,24},{16,0},{24,8},{1,17},{9,25},{17,1},{25,9},{2,18},{10... | collective-permute-start | bytes 884744 | tf_op jit(solution)/shard_map/ppermute | solution.py:869
  210.3 15.9 %collective-permute-start.33 = (bf16[2,48,3072]{2,1,0:T(8,128)(2,1)S(1)}, bf16[2,48,3072]{2,1,0:T(8,128)(2,1)S(1)}, u32[]{:S(2)}, u32[]{:S(2)}) collective-permute-start(bf16[2,48,3072]{2,1,0:T(8,128)(2,1)S(1)} %get-tuple-element.247), channel_id=1, source_target_pairs={{0,2},{1,3},{2,0},{3,1},{4,6},{5,7},{6,4},{7,5},{8,10},{9,11},{10,... | collective-permute-start | bytes 1769480 | tf_op jit(solution)/shard_map/ppermute | solution.py:780
  211.2 15.0 %collective-permute-start.34 = (bf16[2,48,3072]{2,1,0:T(8,128)(2,1)S(1)}, bf16[2,48,3072]{2,1,0:T(8,128)(2,1)S(1)}, u32[]{:S(2)}, u32[]{:S(2)}) collective-permute-start(bf16[2,48,3072]{2,1,0:T(8,128)(2,1)S(1)} %get-tuple-element.248), channel_id=1, source_target_pairs={{0,4},{1,5},{2,6},{3,7},{4,0},{5,1},{6,2},{7,3},{8,12},{9,13},{10,... | collective-permute-start | bytes 1769480 | tf_op jit(solution)/shard_map/ppermute | solution.py:780
  229.4 15.0 %collective-permute-start.38 = (bf16[48,3072]{1,0:T(8,128)(2,1)S(1)}, bf16[48,3072]{1,0:T(8,128)(2,1)S(1)}, u32[]{:S(2)}, u32[]{:S(2)}) collective-permute-start(bf16[48,3072]{1,0:T(8,128)(2,1)S(1)} %add_convert_fusion.18), channel_id=1, source_target_pairs={{0,8},{1,9},{2,10},{3,11},{4,12},{5,13},{6,14},{7,15},{8,0},{9,1},... | collective-permute-start | bytes 884744 | tf_op jit(solution)/shard_map/ppermute | solution.py:865
  231.0 16.0 %collective-permute-start.39 = (bf16[48,3072]{1,0:T(8,128)(2,1)S(1)}, bf16[48,3072]{1,0:T(8,128)(2,1)S(1)}, u32[]{:S(2)}, u32[]{:S(2)}) collective-permute-start(bf16[48,3072]{1,0:T(8,128)(2,1)S(1)} %add_convert_fusion.17), channel_id=1, source_target_pairs={{0,16},{8,24},{16,0},{24,8},{1,17},{9,25},{17,1},{25,9},{2,18},{10... | collective-permute-start | bytes 884744 | tf_op jit(solution)/shard_map/ppermute | solution.py:869
  231.3 15.7 %collective-permute-start.36 = (bf16[1,48,6144]{2,1,0:T(8,128)(2,1)S(1)}, bf16[1,48,6144]{2,1,0:T(8,128)(2,1)S(1)}, u32[]{:S(2)}, u32[]{:S(2)}) collective-permute-start(bf16[1,48,6144]{2,1,0:T(8,128)(2,1)S(1)} %pad_maximum_fusion.8), channel_id=1, source_target_pairs={{0,2},{1,3},{2,0},{3,1},{4,6},{5,7},{6,4},{7,5},{8,10},{9,11},{10,... | collective-permute-start | bytes 1769480 | tf_op jit(solution)/shard_map/ppermute | solution.py:780
  231.9 15.2 %collective-permute-start.37 = (bf16[1,48,6144]{2,1,0:T(8,128)(2,1)S(1)}, bf16[1,48,6144]{2,1,0:T(8,128)(2,1)S(1)}, u32[]{:S(2)}, u32[]{:S(2)}) collective-permute-start(bf16[1,48,6144]{2,1,0:T(8,128)(2,1)S(1)} %pad_maximum_fusion.9), channel_id=1, source_target_pairs={{0,4},{1,5},{2,6},{3,7},{4,0},{5,1},{6,2},{7,3},{8,12},{9,13},{10,... | collective-permute-start | bytes 1769480 | tf_op jit(solution)/shard_map/ppermute | solution.py:780
  248.7 11.6 %collective-permute-start.41 = (bf16[1,48,1536]{2,1,0:T(8,128)(2,1)S(1)}, bf16[1,48,1536]{2,1,0:T(8,128)(2,1)S(1)}, u32[]{:S(2)}, u32[]{:S(2)}) collective-permute-start(bf16[1,48,1536]{2,1,0:T(8,128)(2,1)S(1)} %get-tuple-element.279), channel_id=1, source_target_pairs={{0,2},{1,3},{2,0},{3,1},{4,6},{5,7},{6,4},{7,5},{8,10},{9,11},{10,... | collective-permute-start | bytes 442376 | tf_op jit(solution)/shard_map/ppermute | solution.py:780
  249.6 10.7 %collective-permute-start.42 = (bf16[1,48,1536]{2,1,0:T(8,128)(2,1)S(1)}, bf16[1,48,1536]{2,1,0:T(8,128)(2,1)S(1)}, u32[]{:S(2)}, u32[]{:S(2)}) collective-permute-start(bf16[1,48,1536]{2,1,0:T(8,128)(2,1)S(1)} %get-tuple-element.280), channel_id=1, source_target_pairs={{0,4},{1,5},{2,6},{3,7},{4,0},{5,1},{6,2},{7,3},{8,12},{9,13},{10,... | collective-permute-start | bytes 442376 | tf_op jit(solution)/shard_map/ppermute | solution.py:780
  250.4 9.9 %collective-permute-start.40 = (bf16[48,3072]{1,0:T(8,128)(2,1)S(1)}, bf16[48,3072]{1,0:T(8,128)(2,1)S(1)}, u32[]{:S(2)}, u32[]{:S(2)}) collective-permute-start(bf16[48,3072]{1,0:T(8,128)(2,1)S(1)} %get-tuple-element.278), channel_id=1, source_target_pairs={{0,8},{1,9},{2,10},{3,11},{4,12},{5,13},{6,14},{7,15},{8,0},{9,1},... | collective-permute-start | bytes 884744 | tf_op jit(solution)/shard_map/ppermute | solution.py:865
  265.3 10.4 %collective-permute-start.46 = (bf16[48,1536]{1,0:T(8,128)(2,1)S(1)}, bf16[48,1536]{1,0:T(8,128)(2,1)S(1)}, u32[]{:S(2)}, u32[]{:S(2)}) collective-permute-start(bf16[48,1536]{1,0:T(8,128)(2,1)S(1)} %get-tuple-element.332), channel_id=1, source_target_pairs={{0,8},{1,9},{2,10},{3,11},{4,12},{5,13},{6,14},{7,15},{8,0},{9,1},... | collective-permute-start | bytes 442376 | tf_op jit(solution)/shard_map/ppermute | solution.py:865
  267.3 18.8 %collective-permute-start.49 = (bf16[48,3072]{1,0:T(8,128)(2,1)S(1)}, bf16[48,3072]{1,0:T(8,128)(2,1)S(1)}, u32[]{:S(2)}, u32[]{:S(2)}) collective-permute-start(bf16[48,3072]{1,0:T(8,128)(2,1)S(1)} %add_convert_fusion.10), channel_id=1, source_target_pairs={{0,16},{8,24},{16,0},{24,8},{1,17},{9,25},{17,1},{25,9},{2,18},{10... | collective-permute-start | bytes 884744 | tf_op jit(solution)/shard_map/ppermute | solution.py:869
  269.7 37.1 %collective-permute-start.55 = (bf16[48,3072]{1,0:T(8,128)(2,1)S(1)}, bf16[48,3072]{1,0:T(8,128)(2,1)S(1)}, u32[]{:S(2)}, u32[]{:S(2)}) collective-permute-start(bf16[48,3072]{1,0:T(8,128)(2,1)S(1)} %add_convert_fusion.8), channel_id=1, source_target_pairs={{0,8},{1,9},{2,10},{3,11},{4,12},{5,13},{6,14},{7,15},{8,0},{9,1},... | collective-permute-start | bytes 884744 | tf_op jit(solution)/shard_map/ppermute | solution.py:865
  270.1 11.9 %collective-permute-start.44 = (bf16[2,48,2432]{2,1,0:T(8,128)(2,1)S(1)}, bf16[2,48,2432]{2,1,0:T(8,128)(2,1)S(1)}, u32[]{:S(2)}, u32[]{:S(2)}) collective-permute-start(bf16[2,48,2432]{2,1,0:T(8,128)(2,1)S(1)} %get-tuple-element.301), channel_id=1, source_target_pairs={{0,2},{1,3},{2,0},{3,1},{4,6},{5,7},{6,4},{7,5},{8,10},{9,11},{10,... | collective-permute-start | bytes 1400840 | tf_op jit(solution)/shard_map/ppermute | solution.py:780
  271.3 11.6 %collective-permute-start.45 = (bf16[2,48,2432]{2,1,0:T(8,128)(2,1)S(1)}, bf16[2,48,2432]{2,1,0:T(8,128)(2,1)S(1)}, u32[]{:S(2)}, u32[]{:S(2)}) collective-permute-start(bf16[2,48,2432]{2,1,0:T(8,128)(2,1)S(1)} %get-tuple-element.302), channel_id=1, source_target_pairs={{0,4},{1,5},{2,6},{3,7},{4,0},{5,1},{6,2},{7,3},{8,12},{9,13},{10,... | collective-permute-start | bytes 1400840 | tf_op jit(solution)/shard_map/ppermute | solution.py:780
  283.1 6.1 %collective-permute-start.47 = (bf16[1,48,2432]{2,1,0:T(8,128)(2,1)S(1)}, bf16[1,48,2432]{2,1,0:T(8,128)(2,1)S(1)}, u32[]{:S(2)}, u32[]{:S(2)}) collective-permute-start(bf16[1,48,2432]{2,1,0:T(8,128)(2,1)S(1)} %get-tuple-element.308), channel_id=1, source_target_pairs={{0,2},{1,3},{2,0},{3,1},{4,6},{5,7},{6,4},{7,5},{8,10},{9,11},{10,... | collective-permute-start | bytes 700424 | tf_op jit(solution)/shard_map/ppermute | solution.py:780
  285.7 7.9 %collective-permute-start.51 = (bf16[48,1536]{1,0:T(8,128)(2,1)S(1)}, bf16[48,1536]{1,0:T(8,128)(2,1)S(1)}, u32[]{:S(2)}, u32[]{:S(2)}) collective-permute-start(bf16[48,1536]{1,0:T(8,128)(2,1)S(1)} %fusion.6), channel_id=1, source_target_pairs={{0,16},{8,24},{16,0},{24,8},{1,17},{9,25},{17,1},{25,9},{2,18},{10... | collective-permute-start | bytes 442376 | tf_op jit(solution)/shard_map/ppermute | solution.py:869
  290.5 11.2 %collective-permute-start.50 = (bf16[48,2432]{1,0:T(8,128)(2,1)S(1)}, bf16[48,2432]{1,0:T(8,128)(2,1)S(1)}, u32[]{:S(2)}, u32[]{:S(2)}) collective-permute-start(bf16[48,2432]{1,0:T(8,128)(2,1)S(1)} %get-tuple-element.316), channel_id=1, source_target_pairs={{0,8},{1,9},{2,10},{3,11},{4,12},{5,13},{6,14},{7,15},{8,0},{9,1},... | collective-permute-start | bytes 700424 | tf_op jit(solution)/shard_map/ppermute | solution.py:865
  293.1 14.7 %collective-permute-start.54 = (bf16[48,3072]{1,0:T(8,128)(2,1)S(1)}, bf16[48,3072]{1,0:T(8,128)(2,1)S(1)}, u32[]{:S(2)}, u32[]{:S(2)}) collective-permute-start(bf16[48,3072]{1,0:T(8,128)(2,1)S(1)} %add_convert_fusion.9), channel_id=1, source_target_pairs={{0,8},{1,9},{2,10},{3,11},{4,12},{5,13},{6,14},{7,15},{8,0},{9,1},... | collective-permute-start | bytes 884744 | tf_op jit(solution)/shard_map/ppermute | solution.py:865
  301.9 8.2 %collective-permute-start.53 = (bf16[48,1536]{1,0:T(8,128)(2,1)S(1)}, bf16[48,1536]{1,0:T(8,128)(2,1)S(1)}, u32[]{:S(2)}, u32[]{:S(2)}) collective-permute-start(bf16[48,1536]{1,0:T(8,128)(2,1)S(1)} %add_convert_fusion.34), channel_id=1, source_target_pairs={{0,8},{1,9},{2,10},{3,11},{4,12},{5,13},{6,14},{7,15},{8,0},{9,1},... | collective-permute-start | bytes 442376 | tf_op jit(solution)/shard_map/ppermute | solution.py:865
  301.9 10.7 %collective-permute-start.52 = (bf16[48,2432]{1,0:T(8,128)(2,1)S(1)}, bf16[48,2432]{1,0:T(8,128)(2,1)S(1)}, u32[]{:S(2)}, u32[]{:S(2)}) collective-permute-start(bf16[48,2432]{1,0:T(8,128)(2,1)S(1)} %add_convert_fusion.29), channel_id=1, source_target_pairs={{0,16},{8,24},{16,0},{24,8},{1,17},{9,25},{17,1},{25,9},{2,18},{10... | collective-permute-start | bytes 700424 | tf_op jit(solution)/shard_map/ppermute | solution.py:869
  (73 other events, 467.6 us)

commit v9 on v8

--- a/solution.py
+++ b/solution.py
@@ -988,6 +988,8 @@
             sum_t.first(), got_s, got_e, sum_m.last_x, sum_m.last_y, gx, out
         )
         sum_t.cross(sent_t)
+        input_grad = unpack_rows(gx, clips)
+        input_grad, got_s, got_e, sum_m.last_x, sum_m.last_y = tie(input_grad, got_s, got_e, sum_m.last_x, sum_m.last_y)
         held_s, held_e = total(held_s, got_s), total(held_e, got_e)
         held_m, sent_m = split_groups(sum_m.finish(), even)
         got_s, got_m, got_e = across_pairs(held_s), swap_z(sent_m), swap_z(held_e)
@@ -995,13 +997,11 @@
         held_m, sent_t = tie(total(held_m, got_m), sum_t.second())
         sum_t.cross_again(sent_t)
         got_m = across_pairs(held_m)
-        sum_t.last_x, sum_t.last_y, got_s = tie(sum_t.last_x, sum_t.last_y, got_s)
         held_t, sent_t = split_groups(sum_t.finish(), even)
-        held_t, sent_t, held_s = tie(held_t, sent_t, total(held_s, got_s))
-        got_t, got_s = swap_z(sent_t), swap_z(held_s)
-        got_t, got_m = tie(got_t, got_m)
-        held_t, held_m = tie(total(held_t, got_t), total(held_m, got_m))
-        got_t, got_m = across_pairs(held_t), swap_z(held_m)
+        got_t = swap_z(sent_t)
+        got_t, got_m, got_s = tie(got_t, got_m, got_s)
+        held_t, held_m, held_s = tie(total(held_t, got_t), total(held_m, got_m), total(held_s, got_s))
+        got_t, got_m, got_s = across_pairs(held_t), swap_z(held_m), swap_z(held_s)
         got_t, got_m, got_s, got_e = tie(got_t, got_m, got_s, got_e)
         held_t = total(held_t, got_t)
         got_t = swap_z(held_t)
@@ -1022,10 +1022,11 @@
         rows = [sums_t[0:4], sums_s[0:3], sums_f[0:1], sums_t[4:5], norm_s[0:1], norm_f[0:1], sums_t[5:6], norm_s[1:2], norm_f[1:2]]
         cut = lax.dynamic_slice_in_dim(lax.psum(jnp.concatenate(rows, axis=0), BOTH), mine * part, part, axis=1)
         biases, gains, shifts = cut[0:8], cut[8:11], cut[11:14]
+        input_grad = unpack_rows(gx, clips)
         rows_hidden = lax.dynamic_slice_in_dim(lax.psum(ghb[0], BOTH), mine * hidden_bias.shape[0], hidden_bias.shape[0])
     return (
         (unpack_rows(out, clips) * flags)[:, None],
-        unpack_rows(gx, clips)[:, None],
+        input_grad[:, None],
         rt[:, : 3 * columns],
         rm[:, :columns],
         rm[:, columns:],

time: 327 us -> 336 us (1.028)
  waiting for transfers between devices: 66 us -> 71.7 us
    ppermute x5, waiting for transfers between devices: 5.26 us -> 15.3 us  [across_pairs(): return lax.ppermute(value, 'grp', [(z, z ^ 2) for z in range(4)])]
    ppermute x42, waiting for transfers between devices: 46.2 us -> 39.1 us  [permute(): return lax.ppermute(value, BOTH, pairs)]
    unnamed x136 -> x138, local copies, waits for them, and re-layouts: 15.4 us -> 16.3 us
  transfers between devices with their start and end apart: 57 -> 57, of which waited for: 19 -> 22; matrix products, arithmetic and copies ran while one was open for 12% -> 12% of each run, Pallas kernels for 34% -> 33%
where the time goes in v9:
time: 336 us; the launch traced here: 332 us
  Pallas kernels  139 us (41%)
  waiting for transfers between devices  71.7 us (21%)
  starting transfers between devices  54.2 us (16%)
  other arithmetic  40.9 us (12%)
  local copies, waits for them, and re-layouts  24.4 us (7%)
    pallas_call x10, Pallas kernels, call(): pl.pallas_call(kernel, out_shape=[jax.ShapeDtypeStruct(s, d) for s, d in...  139 us
    ppermute x42, waiting for transfers between devices, permute(): return lax.ppermute(value, BOTH, pairs)  39.1 us
    ppermute x42, starting transfers between devices, permute(): return lax.ppermute(value, BOTH, pairs)  34.7 us
    ppermute x10, waiting for transfers between devices, swap_z(): return lax.ppermute(value, BOTH, pairs)  17.3 us
    unnamed x138, local copies, waits for them, and re-layouts  16.3 us
    ppermute x5, waiting for transfers between devices, across_pairs(): return lax.ppermute(value, 'grp', [(z, z ^ 2) for z in range(4)])  15.3 us
    ppermute x5, starting transfers between devices, across_pairs(): return lax.ppermute(value, 'grp', [(z, z ^ 2) for z in range(4)])  11.1 us
    another operation x4, other arithmetic, pack_rows(): return jnp.stack(frames, axis=1).reshape(clips * FRAMES * BLOCK, columns)  10.3 us
  transfers between devices with their start and end apart: 57, of which 22 were waited for; matrix products, arithmetic and copies ran while one was open for 12% of the time, Pallas kernels for 33%

profile of v9, /device:TPU:0, one launch (start us, length us, event | category | flops | bytes accessed | tf_op | source)
XLA Modules:
  0.0 331.9 jit_solution(12188996994709602387)
XLA Ops:
  6.5 2.9 collective-permute-start.1
  10.2 3.6 %fusion.4 = (bf16[2,1,208,768]{3,0,2,1:T(2,128)(2,1)S(1)}, bf16[2,1,208,768]{3,0,2,1:T(2,128)(2,1)S(1)}) fusion(bf16[2,1,768]{2,0,1:T(2,128)(2,1)S(1)} %slice.491, bf16[2,196,768]{2,0,1:T(2,128)(2,1)S(1)} %get-tuple-element.372, bf16[208]{0:T(256)(128)(2,1)S(1)} %pad.62.clone, bf16[2,196,768]{2,0,1:T(2,128)(2,1)S(1)} %get-tuple-element.373), kind=kLoop, calls=%fused_computation.23 | loop fusion | flops 1277952 | bytes 2485664 | tf_op jit(solution)/shard_map/stack | solution.py:664
  13.8 1.8 pad_maximum_fusion
  16.8 2.4 collective-permute-done.1.refs_4_.refs_6_.refs_10_
  20.2 2.1 collective-permute-start.4
  22.2 9.7 %collective-permute-done.8.refs_5_.refs_7_.refs_11_ = bf16[96,3968]{1,0:T(8,128)(2,1)} collective-permute-done((bf16[96,3968]{1,0:T(8,128)(2,1)S(1)}, bf16[96,3968]{1,0:T(8,128)(2,1)}, u32[]{:S(2)}, u32[]{:S(2)}) %collective-permute-start.8) | collective-permute-done | bytes 761888 | tf_op jit(solution)/shard_map/ppermute | solution.py:780
  32.4 2.6 collective-permute-done.4.refs_6_.refs_8_.refs_12_
  36.0 2.0 collective-permute-start.6
  38.1 2.0 collective-permute-start.5
  40.1 14.1 %time_forward.1 = (bf16[832,768]{1,0:T(8,128)(2,1)}, bf16[832,2304]{1,0:T(8,128)(2,1)}, bf16[832,768]{1,0:T(8,128)(2,1)}, bf16[832,768]{1,0:T(8,128)(2,1)}, f32[...) custom-call(s32[16]{0:T(128)} %stack.76.refs_0_, bf16[832,768]{1,0:T(8,128)(2,1)} %bitcast.66, ...), custom_call_target="tpu_custom_call" | custom-call | flops 56000000000 | tf_op jit(solution)/shard_map/time_forward/pallas_call | solution.py:284
  57.3 2.4 bitcast_multiply_fusion
  60.5 10.3 %collective-permute-done.12.refs_7_.refs_10_.refs_9_ = bf16[96,3072]{1,0:T(8,128)(2,1)S(1)} collective-permute-done((bf16[96,3072]{1,0:T(8,128)(2,1)}, bf16[96,3072]{1,0:T(8,128)(2,1)S(1)}, u32[]{:S(2)}, u32[]{:S(2)}) %collective-permute-start.12) | collective-permute-done | bytes 589856 | tf_op jit(solution)/shard_map/ppermute | solution.py:780
  70.8 3.1 maximum_bitcast_fusion
  73.9 1.8 pad_maximum_fusion.1
  80.1 16.8 %space_forward.1 = (bf16[832,768]{1,0:T(8,128)(2,1)}, bf16[832,2304]{1,0:T(8,128)(2,1)}, bf16[48,208,208]{2,1,0:T(8,128)(2,1)}, bf16[832,768]{1,0:T(8,128)(2,1)}, f32[832,768]{1,0:T(8,128)}) custom-call(s32[16]{0:T(128)} %stack.76.refs_0_, f32[832,768]{1,0:T(8,128)} %get-tuple-element.192.refs_1_.refs_2_, ...), custom_call_target="tpu_custom_call" | custom-call | flops 64000000000 | tf_op jit(solution)/shard_map/space_forward/pallas_call | solution.py:284
  97.6 3.2 collective-permute-done.19.refs_11_
  102.8 28.1 %feed_out.1 = (bf16[832,768]{1,0:T(8,128)(2,1)}, bf16[832,768]{1,0:T(8,128)(2,1)}, bf16[832,3072]{1,0:T(8,128)(2,1)}, f32[8,768]{1,0:T(8,128)}, bf16[8,48,3072]{...) custom-call(s32[16]{0:T(128)} %stack.76.refs_0_, f32[832,768]{1,0:T(8,128)} %get-tuple-element.203.refs_1_.refs_2_, ...), custom_call_target="tpu_custom_call" | custom-call | flops 120000004096 | tf_op jit(solution)/shard_map/feed_out/pallas_call | solution.py:284
  131.2 2.4 copy-done.32
  134.9 7.8 %feed_in.1 = (f32[8,3072]{1,0:T(8,128)S(1)}, bf16[8,48,3072]{2,1,0:T(8,128)(2,1)S(1)}, bf16[8,48,3072]{2,1,0:T(8,128)(2,1)}) custom-call(s32[16]{0:T(128)S(1)} %copy-done.8, bf16[832,3072]{1,0:T(8,128)(2,1)S(1)} %copy-done.32, bf16[832,768]{1,0:T(8,128)(2,1)S(1)} %copy-done.41), custom_call_target="tpu_custom_call" | custom-call | flops 32000000000 | tf_op jit(solution)/shard_map/feed_in/pallas_call | solution.py:284
  143.7 2.1 add_convert_fusion.4
  150.4 2.4 copy-done.33
  152.8 1.7 copy-done.36
  154.6 8.7 %feed_norm.1 = (f32[832,768]{1,0:T(8,128)S(1)}, f32[8,768]{1,0:T(8,128)S(1)}) custom-call(s32[16]{0:T(128)S(1)} %copy-done.8, bf16[832,3072]{1,0:T(8,128)(2,1)S(1)} %copy-done.33, f32[832,768]{1,0:T(8,128)S(1)} %copy-done.36, bf16[832,768]{1,0:T(8,128)(2,1)S(1)} %bitcast.69, f32[32,768]{1,0:T(8,128)S(1)} %copy-done.48, bf16[96,6144]{1,0:T(8,128)(2,1)S(1)} %copy-done.7, ...), custom_call_target="tpu_custom_call" | custom-call | flops 40000000000 | tf_op jit(solution)/shard_map/feed_norm/pallas_call | solution.py:284
  163.4 1.9 add_convert_fusion.26
  168.1 20.8 %space_backward.1 = (bf16[832,2304]{1,0:T(8,128)(2,1)S(1)}, f32[8,768]{1,0:T(8,128)S(1)}, bf16[8,48,3072]{2,1,0:T(8,128)(2,1)S(1)}, bf16[8,48,3072]{2,1,0:T(8,128)(2,1)S(1)}) custom-call(s32[16]{0:T(128)S(1)} %copy-done.8, f32[832,768]{1,0:T(8,128)S(1)} %get-tuple-element.224.refs_1_.refs_3_, bf16[832,768]{1,0:T(8,128)(2,1)S(1)} %copy-done.44, ...), custom_call_target="tpu_custom_call" | custom-call | flops 80000000000 | tf_op jit(solution)/shard_map/space_backward/pallas_call | solution.py:284
  192.0 1.6 collective-permute-start.28
  195.3 1.7 copy-done.38
  197.0 7.7 %space_norm.1 = (f32[832,768]{1,0:T(8,128)S(1)}, f32[8,768]{1,0:T(8,128)S(1)}) custom-call(s32[16]{0:T(128)S(1)} %copy-done.8, bf16[832,2304]{1,0:T(8,128)(2,1)S(1)} %get-tuple-element.238.refs_1_, f32[832,768]{1,0:T(8,128)S(1)} %copy-done.38, f32[832,768]{1,0:T(8,128)S(1)} %get-tuple-element.224.refs_1_.refs_3_, f32[32,768]{1,0:T(8,128)S(1)} %copy-done.48, ...), custom_call_target="tpu_custom_call" | custom-call | flops 40000000000 | tf_op jit(solution)/shard_map/space_norm/pallas_call | solution.py:284
  204.8 1.9 select_bitcast_fusion.2
  207.7 2.6 collective-permute-start.31
  212.8 13.3 %mixer_backward.1 = (bf16[832,768]{1,0:T(8,128)(2,1)S(1)}, f32[8,768]{1,0:T(8,128)S(1)}, bf16[8,48,1536]{2,1,0:T(8,128)(2,1)S(1)}, bf16[8,48,1536]{2,1,0:T(8,128)(2,1)S(1)}) custom-call(s32[16]{0:T(128)S(1)} %copy-done.8, f32[832,768]{1,0:T(8,128)S(1)} %get-tuple-element.250.refs_1_.refs_5_, bf16[832,768]{1,0:T(8,128)(2,1)S(1)} %copy-done.39, ...), custom_call_target="tpu_custom_call" | custom-call | flops 32000000000 | tf_op jit(solution)/shard_map/mixer_backward/pallas_call | solution.py:284
  226.6 2.4 collective-permute-done.35
  233.0 11.4 %time_backward.1 = (bf16[832,2304]{1,0:T(8,128)(2,1)S(1)}, bf16[832,768]{1,0:T(8,128)(2,1)S(1)}, f32[8,768]{1,0:T(8,128)S(1)}) custom-call(s32[16]{0:T(128)S(1)} %copy-done.8, bf16[832,768]{1,0:T(8,128)(2,1)S(1)} %get-tuple-element.268.refs_1_, bf16[832,2304]{1,0:T(8,128)(2,1)S(1)} %copy-done.37, f32[1664,128]{1,0:T(8,128)S(1)} %copy-done.43, ...), custom_call_target="tpu_custom_call" | custom-call | flops 48000000000 | tf_op jit(solution)/shard_map/time_backward/pallas_call | solution.py:284
  244.4 2.6 collective-permute-done.39
  250.5 9.7 %time_weights.1 = (bf16[8,48,2432]{2,1,0:T(8,128)(2,1)S(1)}, bf16[8,48,2432]{2,1,0:T(8,128)(2,1)S(1)}) custom-call(s32[16]{0:T(128)S(1)} %copy-done.8, bf16[832,2304]{1,0:T(8,128)(2,1)S(1)} %get-tuple-element.282.refs_1_, bf16[832,768]{1,0:T(8,128)(2,1)S(1)} %copy-done.42, f32[8,768]{1,0:T(8,128)S(1)} %get-tuple-element.284.refs_3_, ...), custom_call_target="tpu_custom_call" | custom-call | flops 32000000000 | tf_op jit(solution)/shard_map/time_weights/pallas_call | solution.py:284
  261.7 2.5 collective-permute-done.43
  267.8 2.8 pad_maximum_fusion.2
  270.8 2.1 collective-permute-start.46
  272.9 3.5 %collective-permute-done.46 = bf16[48,1536]{1,0:T(8,128)(2,1)S(1)} collective-permute-done((bf16[48,1536]{1,0:T(8,128)(2,1)S(1)}, bf16[48,1536]{1,0:T(8,128)(2,1)S(1)}, u32[]{:S(2)}, u32[]{:S(2)}) %collective-permute-start.46) | collective-permute-done | bytes 147488 | tf_op jit(solution)/shard_map/ppermute | solution.py:865
  281.5 2.6 collective-permute-start.51
  286.7 2.1 collective-permute-start.49
  289.9 10.7 %collective-permute-done.51 = bf16[48,3072]{1,0:T(8,128)(2,1)S(1)} collective-permute-done((bf16[48,3072]{1,0:T(8,128)(2,1)S(1)}, bf16[48,3072]{1,0:T(8,128)(2,1)S(1)}, u32[]{:S(2)}, u32[]{:S(2)}) %collective-permute-start.51) | collective-permute-done | bytes 294944 | tf_op jit(solution)/shard_map/ppermute | solution.py:869
  300.6 2.0 collective-permute-done.50
  303.9 5.2 %collective-permute-start.52 = (bf16[48,2432]{1,0:T(8,128)(2,1)S(1)}, bf16[48,2432]{1,0:T(8,128)(2,1)S(1)}, u32[]{:S(2)}, u32[]{:S(2)}) collective-permute-start(bf16[48,2432]{1,0:T(8,128)(2,1)S(1)} %fusion.6), channel_id=1, source_target_pairs={{0,16},{8,24},{16,0},{24,8},{1,17},{9,25},{17,1},{25,9},{2,18},{10... | collective-permute-start | bytes 700424 | tf_op jit(solution)/shard_map/ppermute | solution.py:869
  309.1 2.8 maximum_multiply_fusion
  312.3 5.8 %collective-permute-done.53 = bf16[48,1536]{1,0:T(8,128)(2,1)S(1)} collective-permute-done((bf16[48,1536]{1,0:T(8,128)(2,1)S(1)}, bf16[48,1536]{1,0:T(8,128)(2,1)S(1)}, u32[]{:S(2)}, u32[]{:S(2)}) %collective-permute-start.53) | collective-permute-done | bytes 147488 | tf_op jit(solution)/shard_map/ppermute | solution.py:865
  318.1 3.6 %collective-permute-done.54 = bf16[48,3072]{1,0:T(8,128)(2,1)S(1)} collective-permute-done((bf16[48,3072]{1,0:T(8,128)(2,1)S(1)}, bf16[48,3072]{1,0:T(8,128)(2,1)S(1)}, u32[]{:S(2)}, u32[]{:S(2)}) %collective-permute-start.54) | collective-permute-done | bytes 294944 | tf_op jit(solution)/shard_map/ppermute | solution.py:865
  325.7 3.1 collective-permute-done.56
  (295 shorter events, 69.4 us)
Async XLA Ops:
  5.8 13.3 %collective-permute-start.3 = (bf16[96,6144]{1,0:T(8,128)(2,1)S(1)}, bf16[96,6144]{1,0:T(8,128)(2,1)S(1)}, u32[]{:S(2)}, u32[]{:S(2)}) collective-permute-start(bf16[96,6144]{1,0:T(8,128)(2,1)S(1)} %slice_dynamic-update-slice_fusion.refs_5_), channel_id=1, source_target_pairs={{0,1},{1,0},{2,3},{3,2},{4,5},{5,4},{6,7},{7,6},{8,9},{9,8},{10,11... | collective-permute-start | bytes 3538952 | tf_op jit(solution)/shard_map/ppermute | solution.py:780
  6.3 10.5 %collective-permute-start.2 = (bf16[96,3072]{1,0:T(8,128)(2,1)S(1)}, bf16[96,3072]{1,0:T(8,128)(2,1)}, u32[]{:S(2)}, u32[]{:S(2)}) collective-permute-start(bf16[96,3072]{1,0:T(8,128)(2,1)S(1)} %pad_maximum_fusion.8.refs_3_.refs_6_.refs_5_), channel_id=1, source_target_pairs={{0,1},{1,0},{2,3},{3,2},{4,5},{5,4},{6,7},{7,6},{8,9},{9,8},{10,11... | collective-permute-start | bytes 1769480 | tf_op jit(solution)/shard_map/ppermute | solution.py:780
  6.5 12.7 %collective-permute-start.1 = (bf16[96,3968]{1,0:T(8,128)(2,1)S(1)}, bf16[96,3968]{1,0:T(8,128)(2,1)}, u32[]{:S(2)}, u32[]{:S(2)}) collective-permute-start(bf16[96,3968]{1,0:T(8,128)(2,1)S(1)} %fusion.1.refs_2_.refs_4_.refs_8_), channel_id=1, source_target_pairs={{0,2},{1,5},{2,0},{3,7},{4,6},{5,1},{6,4},{7,3},{8,10},{9,13},{10,... | collective-permute-start | bytes 2285576 | tf_op jit(solution)/shard_map/ppermute | solution.py:780
  9.4 22.5 %collective-permute-start.8 = (bf16[96,3968]{1,0:T(8,128)(2,1)S(1)}, bf16[96,3968]{1,0:T(8,128)(2,1)}, u32[]{:S(2)}, u32[]{:S(2)}) collective-permute-start(bf16[96,3968]{1,0:T(8,128)(2,1)S(1)} %collective-permute-done.refs_3_.refs_5_.refs_9_), channel_id=1, source_target_pairs={{0,2},{1,5},{2,0},{3,7},{4,6},{5,1},{6,4},{7,3},{8,10},{9,13},{10,... | collective-permute-start | bytes 2285576 | tf_op jit(solution)/shard_map/ppermute | solution.py:780
  20.2 14.8 %collective-permute-start.4 = (bf16[96,3968]{1,0:T(8,128)(2,1)}, bf16[96,3968]{1,0:T(8,128)(2,1)}, u32[]{:S(2)}, u32[]{:S(2)}) collective-permute-start(bf16[96,3968]{1,0:T(8,128)(2,1)} %collective-permute-done.1.refs_4_.refs_6_.refs_10_), channel_id=1, source_target_pairs={{0,4},{1,3},{2,6},{3,1},{4,0},{5,7},{6,2},{7,5},{8,12},{9,11},{10,... | collective-permute-start | bytes 2285576 | tf_op jit(solution)/shard_map/ppermute | solution.py:780
  31.9 6.2 %collective-permute-start.10 = (bf16[96,3968]{1,0:T(8,128)(2,1)}, bf16[96,3968]{1,0:T(8,128)(2,1)S(1)}, u32[]{:S(2)}, u32[]{:S(2)}) collective-permute-start(bf16[96,3968]{1,0:T(8,128)(2,1)} %collective-permute-done.8.refs_5_.refs_7_.refs_11_), channel_id=1, source_target_pairs={{0,1},{1,0},{2,3},{3,2},{4,5},{5,4},{6,7},{7,6},{8,9},{9,8},{10,11... | collective-permute-start | bytes 2285576 | tf_op jit(solution)/shard_map/ppermute | solution.py:780
  31.9 8.2 %collective-permute-start.9 = (bf16[96,3968]{1,0:T(8,128)(2,1)}, bf16[96,3968]{1,0:T(8,128)(2,1)}, u32[]{:S(2)}, u32[]{:S(2)}) collective-permute-start(bf16[96,3968]{1,0:T(8,128)(2,1)} %collective-permute-done.1.refs_4_.refs_6_.refs_10_), channel_id=1, source_target_pairs={{0,1},{1,0},{2,3},{3,2},{4,5},{5,4},{6,7},{7,6},{8,9},{9,8},{10,11... | collective-permute-start | bytes 2285576 | tf_op jit(solution)/shard_map/ppermute | solution.py:780
  36.0 18.2 %collective-permute-start.6 = (bf16[96,3072]{1,0:T(8,128)(2,1)S(1)}, bf16[96,3072]{1,0:T(8,128)(2,1)}, u32[]{:S(2)}, u32[]{:S(2)}) collective-permute-start(bf16[96,3072]{1,0:T(8,128)(2,1)S(1)} %pad_maximum_fusion.8.refs_3_.refs_6_.refs_5_), channel_id=1, source_target_pairs={{0,2},{1,5},{2,0},{3,7},{4,6},{5,1},{6,4},{7,3},{8,10},{9,13},{10,... | collective-permute-start | bytes 1769480 | tf_op jit(solution)/shard_map/ppermute | solution.py:780
  38.0 16.2 %collective-permute-start.7 = (bf16[96,3072]{1,0:T(8,128)(2,1)}, bf16[96,3072]{1,0:T(8,128)(2,1)}, u32[]{:S(2)}, u32[]{:S(2)}) collective-permute-start(bf16[96,3072]{1,0:T(8,128)(2,1)} %collective-permute-done.2.refs_4_.refs_7_.refs_6_), channel_id=1, source_target_pairs={{0,2},{1,5},{2,0},{3,7},{4,6},{5,1},{6,4},{7,3},{8,10},{9,13},{10,... | collective-permute-start | bytes 1769480 | tf_op jit(solution)/shard_map/ppermute | solution.py:780
  38.1 38.8 %collective-permute-start.5 = (bf16[96,6144]{1,0:T(8,128)(2,1)S(1)}, bf16[96,6144]{1,0:T(8,128)(2,1)}, u32[]{:S(2)}, u32[]{:S(2)}) collective-permute-start(bf16[96,6144]{1,0:T(8,128)(2,1)S(1)} %slice_dynamic-update-slice_fusion.refs_5_), channel_id=1, source_target_pairs={{0,2},{1,5},{2,0},{3,7},{4,6},{5,1},{6,4},{7,3},{8,10},{9,13},{10,... | collective-permute-start | bytes 3538952 | tf_op jit(solution)/shard_map/ppermute | solution.py:780
  54.3 16.5 %collective-permute-start.12 = (bf16[96,3072]{1,0:T(8,128)(2,1)}, bf16[96,3072]{1,0:T(8,128)(2,1)S(1)}, u32[]{:S(2)}, u32[]{:S(2)}) collective-permute-start(bf16[96,3072]{1,0:T(8,128)(2,1)} %collective-permute-done.6.refs_5_.refs_8_.refs_7_), channel_id=1, source_target_pairs={{0,4},{1,3},{2,6},{3,1},{4,0},{5,7},{6,2},{7,5},{8,12},{9,11},{10,... | collective-permute-start | bytes 1769480 | tf_op jit(solution)/shard_map/ppermute | solution.py:780
  55.9 41.0 %collective-permute-start.17 = (bf16[96,6144]{1,0:T(8,128)(2,1)S(1)}, bf16[96,6144]{1,0:T(8,128)(2,1)S(1)}, u32[]{:S(2)}, u32[]{:S(2)}) collective-permute-start(bf16[96,6144]{1,0:T(8,128)(2,1)S(1)} %copy-done.10), channel_id=1, source_target_pairs={{0,2},{1,5},{2,0},{3,7},{4,6},{5,1},{6,4},{7,3},{8,10},{9,13},{10,... | collective-permute-start | bytes 3538952 | tf_op jit(solution)/shard_map/ppermute | solution.py:780
  56.8 20.2 %collective-permute-start.13 = (bf16[96,3072]{1,0:T(8,128)(2,1)}, bf16[96,3072]{1,0:T(8,128)(2,1)S(1)}, u32[]{:S(2)}, u32[]{:S(2)}) collective-permute-start(bf16[96,3072]{1,0:T(8,128)(2,1)} %collective-permute-done.6.refs_5_.refs_8_.refs_7_), channel_id=1, source_target_pairs={{0,1},{1,0},{2,3},{3,2},{4,5},{5,4},{6,7},{7,6},{8,9},{9,8},{10,11... | collective-permute-start | bytes 1769480 | tf_op jit(solution)/shard_map/ppermute | solution.py:780
  56.8 20.2 %collective-permute-start.14 = (bf16[96,3072]{1,0:T(8,128)(2,1)}, bf16[96,3072]{1,0:T(8,128)(2,1)S(1)}, u32[]{:S(2)}, u32[]{:S(2)}) collective-permute-start(bf16[96,3072]{1,0:T(8,128)(2,1)} %collective-permute-done.7.refs_6_.refs_9_.refs_8_), channel_id=1, source_target_pairs={{0,1},{1,0},{2,3},{3,2},{4,5},{5,4},{6,7},{7,6},{8,9},{9,8},{10,11... | collective-permute-start | bytes 1769480 | tf_op jit(solution)/shard_map/ppermute | solution.py:780
  70.8 6.1 %collective-permute-start.15 = (bf16[96,3072]{1,0:T(8,128)(2,1)S(1)}, bf16[96,3072]{1,0:T(8,128)(2,1)S(1)}, u32[]{:S(2)}, u32[]{:S(2)}) collective-permute-start(bf16[96,3072]{1,0:T(8,128)(2,1)S(1)} %collective-permute-done.12.refs_7_.refs_10_.refs_9_), channel_id=1, source_target_pairs={{0,1},{1,0},{2,3},{3,2},{4,5},{5,4},{6,7},{7,6},{8,9},{9,8},{10,11... | collective-permute-start | bytes 1769480 | tf_op jit(solution)/shard_map/ppermute | solution.py:780
  78.0 19.6 %collective-permute-start.18 = (bf16[96,6144]{1,0:T(8,128)(2,1)}, bf16[96,6144]{1,0:T(8,128)(2,1)S(1)}, u32[]{:S(2)}, u32[]{:S(2)}) collective-permute-start(bf16[96,6144]{1,0:T(8,128)(2,1)} %collective-permute-done.5.refs_7_), channel_id=1, source_target_pairs={{0,1},{1,0},{2,3},{3,2},{4,5},{5,4},{6,7},{7,6},{8,9},{9,8},{10,11... | collective-permute-start | bytes 3538952 | tf_op jit(solution)/shard_map/ppermute | solution.py:780
  78.6 18.4 %collective-permute-start.16 = (bf16[96,6144]{1,0:T(8,128)(2,1)}, bf16[96,6144]{1,0:T(8,128)(2,1)}, u32[]{:S(2)}, u32[]{:S(2)}) collective-permute-start(bf16[96,6144]{1,0:T(8,128)(2,1)} %collective-permute-done.5.refs_7_), channel_id=1, source_target_pairs={{0,4},{1,3},{2,6},{3,1},{4,0},{5,7},{6,2},{7,5},{8,12},{9,11},{10,... | collective-permute-start | bytes 3538952 | tf_op jit(solution)/shard_map/ppermute | solution.py:780
  131.0 12.7 %collective-permute-start.21 = (bf16[8,48,3072]{2,1,0:T(8,128)(2,1)}, bf16[8,48,3072]{2,1,0:T(8,128)(2,1)}, u32[]{:S(2)}, u32[]{:S(2)}) collective-permute-start(bf16[8,48,3072]{2,1,0:T(8,128)(2,1)} %get-tuple-element.209), channel_id=1, source_target_pairs={{0,1},{1,0},{2,3},{3,2},{4,5},{5,4},{6,7},{7,6},{8,9},{9,8},{10,11... | collective-permute-start | bytes 7077896 | tf_op jit(solution)/shard_map/ppermute | solution.py:780
  145.9 17.4 %collective-permute-start.22 = (bf16[2,48,3072]{2,1,0:T(8,128)(2,1)S(1)}, bf16[2,48,3072]{2,1,0:T(8,128)(2,1)S(1)}, u32[]{:S(2)}, u32[]{:S(2)}) collective-permute-start(bf16[2,48,3072]{2,1,0:T(8,128)(2,1)S(1)} %get-tuple-element.215), channel_id=1, source_target_pairs={{0,2},{1,3},{2,0},{3,1},{4,6},{5,7},{6,4},{7,5},{8,10},{9,11},{10,... | collective-permute-start | bytes 1769480 | tf_op jit(solution)/shard_map/ppermute | solution.py:780
  147.1 16.3 %collective-permute-start.23 = (bf16[2,48,3072]{2,1,0:T(8,128)(2,1)S(1)}, bf16[2,48,3072]{2,1,0:T(8,128)(2,1)S(1)}, u32[]{:S(2)}, u32[]{:S(2)}) collective-permute-start(bf16[2,48,3072]{2,1,0:T(8,128)(2,1)S(1)} %get-tuple-element.216), channel_id=1, source_target_pairs={{0,4},{1,5},{2,6},{3,7},{4,0},{5,1},{6,2},{7,3},{8,12},{9,13},{10,... | collective-permute-start | bytes 1769480 | tf_op jit(solution)/shard_map/ppermute | solution.py:780
  165.5 23.5 %collective-permute-start.25 = (bf16[1,48,9216]{2,1,0:T(8,128)(2,1)S(1)}, bf16[1,48,9216]{2,1,0:T(8,128)(2,1)S(1)}, u32[]{:S(2)}, u32[]{:S(2)}) collective-permute-start(bf16[1,48,9216]{2,1,0:T(8,128)(2,1)S(1)} %pad_maximum_fusion.5), channel_id=1, source_target_pairs={{0,4},{1,5},{2,6},{3,7},{4,0},{5,1},{6,2},{7,3},{8,12},{9,13},{10,... | collective-permute-start | bytes 2654216 | tf_op jit(solution)/shard_map/ppermute | solution.py:780
  166.5 22.5 %collective-permute-start.26 = (bf16[1,48,9216]{2,1,0:T(8,128)(2,1)S(1)}, bf16[1,48,9216]{2,1,0:T(8,128)(2,1)S(1)}, u32[]{:S(2)}, u32[]{:S(2)}) collective-permute-start(bf16[1,48,9216]{2,1,0:T(8,128)(2,1)S(1)} %pad_maximum_fusion.4), channel_id=1, source_target_pairs={{0,2},{1,3},{2,0},{3,1},{4,6},{5,7},{6,4},{7,5},{8,10},{9,11},{10,... | collective-permute-start | bytes 2654216 | tf_op jit(solution)/shard_map/ppermute | solution.py:780
  188.9 17.8 %collective-permute-start.27 = (bf16[8,48,3072]{2,1,0:T(8,128)(2,1)S(1)}, bf16[8,48,3072]{2,1,0:T(8,128)(2,1)S(1)}, u32[]{:S(2)}, u32[]{:S(2)}) collective-permute-start(bf16[8,48,3072]{2,1,0:T(8,128)(2,1)S(1)} %get-tuple-element.233), channel_id=1, source_target_pairs={{0,1},{1,0},{2,3},{3,2},{4,5},{5,4},{6,7},{7,6},{8,9},{9,8},{10,11... | collective-permute-start | bytes 7077896 | tf_op jit(solution)/shard_map/ppermute | solution.py:780
  192.0 12.7 %collective-permute-start.28 = (bf16[48,3072]{1,0:T(8,128)(2,1)S(1)}, bf16[48,3072]{1,0:T(8,128)(2,1)S(1)}, u32[]{:S(2)}, u32[]{:S(2)}) collective-permute-start(bf16[48,3072]{1,0:T(8,128)(2,1)S(1)} %get-tuple-element.235), channel_id=1, source_target_pairs={{0,8},{1,9},{2,10},{3,11},{4,12},{5,13},{6,14},{7,15},{8,0},{9,1},... | collective-permute-start | bytes 884744 | tf_op jit(solution)/shard_map/ppermute | solution.py:865
  193.6 11.1 %collective-permute-start.29 = (bf16[1,48,3072]{2,1,0:T(8,128)(2,1)S(1)}, bf16[1,48,3072]{2,1,0:T(8,128)(2,1)S(1)}, u32[]{:S(2)}, u32[]{:S(2)}) collective-permute-start(bf16[1,48,3072]{2,1,0:T(8,128)(2,1)S(1)} %get-tuple-element.236), channel_id=1, source_target_pairs={{0,2},{1,3},{2,0},{3,1},{4,6},{5,7},{6,4},{7,5},{8,10},{9,11},{10,... | collective-permute-start | bytes 884744 | tf_op jit(solution)/shard_map/ppermute | solution.py:780
  194.2 10.6 %collective-permute-start.30 = (bf16[1,48,3072]{2,1,0:T(8,128)(2,1)S(1)}, bf16[1,48,3072]{2,1,0:T(8,128)(2,1)S(1)}, u32[]{:S(2)}, u32[]{:S(2)}) collective-permute-start(bf16[1,48,3072]{2,1,0:T(8,128)(2,1)S(1)} %get-tuple-element.237), channel_id=1, source_target_pairs={{0,4},{1,5},{2,6},{3,7},{4,0},{5,1},{6,2},{7,3},{8,12},{9,13},{10,... | collective-permute-start | bytes 884744 | tf_op jit(solution)/shard_map/ppermute | solution.py:780
  207.2 19.0 %collective-permute-start.32 = (bf16[48,3072]{1,0:T(8,128)(2,1)S(1)}, bf16[48,3072]{1,0:T(8,128)(2,1)S(1)}, u32[]{:S(2)}, u32[]{:S(2)}) collective-permute-start(bf16[48,3072]{1,0:T(8,128)(2,1)S(1)} %get-tuple-element.247), channel_id=1, source_target_pairs={{0,8},{1,9},{2,10},{3,11},{4,12},{5,13},{6,14},{7,15},{8,0},{9,1},... | collective-permute-start | bytes 884744 | tf_op jit(solution)/shard_map/ppermute | solution.py:865
  207.7 18.5 %collective-permute-start.31 = (bf16[48,3072]{1,0:T(8,128)(2,1)S(1)}, bf16[48,3072]{1,0:T(8,128)(2,1)S(1)}, u32[]{:S(2)}, u32[]{:S(2)}) collective-permute-start(bf16[48,3072]{1,0:T(8,128)(2,1)S(1)} %add_convert_fusion.21), channel_id=1, source_target_pairs={{0,16},{8,24},{16,0},{24,8},{1,17},{9,25},{17,1},{25,9},{2,18},{10... | collective-permute-start | bytes 884744 | tf_op jit(solution)/shard_map/ppermute | solution.py:869
  210.3 15.9 %collective-permute-start.33 = (bf16[2,48,3072]{2,1,0:T(8,128)(2,1)S(1)}, bf16[2,48,3072]{2,1,0:T(8,128)(2,1)S(1)}, u32[]{:S(2)}, u32[]{:S(2)}) collective-permute-start(bf16[2,48,3072]{2,1,0:T(8,128)(2,1)S(1)} %get-tuple-element.248), channel_id=1, source_target_pairs={{0,2},{1,3},{2,0},{3,1},{4,6},{5,7},{6,4},{7,5},{8,10},{9,11},{10,... | collective-permute-start | bytes 1769480 | tf_op jit(solution)/shard_map/ppermute | solution.py:780
  211.2 15.0 %collective-permute-start.34 = (bf16[2,48,3072]{2,1,0:T(8,128)(2,1)S(1)}, bf16[2,48,3072]{2,1,0:T(8,128)(2,1)S(1)}, u32[]{:S(2)}, u32[]{:S(2)}) collective-permute-start(bf16[2,48,3072]{2,1,0:T(8,128)(2,1)S(1)} %get-tuple-element.249), channel_id=1, source_target_pairs={{0,4},{1,5},{2,6},{3,7},{4,0},{5,1},{6,2},{7,3},{8,12},{9,13},{10,... | collective-permute-start | bytes 1769480 | tf_op jit(solution)/shard_map/ppermute | solution.py:780
  229.3 15.0 %collective-permute-start.38 = (bf16[48,3072]{1,0:T(8,128)(2,1)S(1)}, bf16[48,3072]{1,0:T(8,128)(2,1)S(1)}, u32[]{:S(2)}, u32[]{:S(2)}) collective-permute-start(bf16[48,3072]{1,0:T(8,128)(2,1)S(1)} %add_convert_fusion.18), channel_id=1, source_target_pairs={{0,8},{1,9},{2,10},{3,11},{4,12},{5,13},{6,14},{7,15},{8,0},{9,1},... | collective-permute-start | bytes 884744 | tf_op jit(solution)/shard_map/ppermute | solution.py:865
  231.0 16.0 %collective-permute-start.39 = (bf16[48,3072]{1,0:T(8,128)(2,1)S(1)}, bf16[48,3072]{1,0:T(8,128)(2,1)S(1)}, u32[]{:S(2)}, u32[]{:S(2)}) collective-permute-start(bf16[48,3072]{1,0:T(8,128)(2,1)S(1)} %add_convert_fusion.17), channel_id=1, source_target_pairs={{0,16},{8,24},{16,0},{24,8},{1,17},{9,25},{17,1},{25,9},{2,18},{10... | collective-permute-start | bytes 884744 | tf_op jit(solution)/shard_map/ppermute | solution.py:869
  231.3 15.7 %collective-permute-start.36 = (bf16[1,48,6144]{2,1,0:T(8,128)(2,1)S(1)}, bf16[1,48,6144]{2,1,0:T(8,128)(2,1)S(1)}, u32[]{:S(2)}, u32[]{:S(2)}) collective-permute-start(bf16[1,48,6144]{2,1,0:T(8,128)(2,1)S(1)} %pad_maximum_fusion.9), channel_id=1, source_target_pairs={{0,2},{1,3},{2,0},{3,1},{4,6},{5,7},{6,4},{7,5},{8,10},{9,11},{10,... | collective-permute-start | bytes 1769480 | tf_op jit(solution)/shard_map/ppermute | solution.py:780
  231.9 15.2 %collective-permute-start.37 = (bf16[1,48,6144]{2,1,0:T(8,128)(2,1)S(1)}, bf16[1,48,6144]{2,1,0:T(8,128)(2,1)S(1)}, u32[]{:S(2)}, u32[]{:S(2)}) collective-permute-start(bf16[1,48,6144]{2,1,0:T(8,128)(2,1)S(1)} %pad_maximum_fusion.10), channel_id=1, source_target_pairs={{0,4},{1,5},{2,6},{3,7},{4,0},{5,1},{6,2},{7,3},{8,12},{9,13},{10,... | collective-permute-start | bytes 1769480 | tf_op jit(solution)/shard_map/ppermute | solution.py:780
  248.6 11.6 %collective-permute-start.41 = (bf16[1,48,1536]{2,1,0:T(8,128)(2,1)S(1)}, bf16[1,48,1536]{2,1,0:T(8,128)(2,1)S(1)}, u32[]{:S(2)}, u32[]{:S(2)}) collective-permute-start(bf16[1,48,1536]{2,1,0:T(8,128)(2,1)S(1)} %get-tuple-element.280), channel_id=1, source_target_pairs={{0,2},{1,3},{2,0},{3,1},{4,6},{5,7},{6,4},{7,5},{8,10},{9,11},{10,... | collective-permute-start | bytes 442376 | tf_op jit(solution)/shard_map/ppermute | solution.py:780
  249.6 10.7 %collective-permute-start.42 = (bf16[1,48,1536]{2,1,0:T(8,128)(2,1)S(1)}, bf16[1,48,1536]{2,1,0:T(8,128)(2,1)S(1)}, u32[]{:S(2)}, u32[]{:S(2)}) collective-permute-start(bf16[1,48,1536]{2,1,0:T(8,128)(2,1)S(1)} %get-tuple-element.281), channel_id=1, source_target_pairs={{0,4},{1,5},{2,6},{3,7},{4,0},{5,1},{6,2},{7,3},{8,12},{9,13},{10,... | collective-permute-start | bytes 442376 | tf_op jit(solution)/shard_map/ppermute | solution.py:780
  250.4 9.9 %collective-permute-start.40 = (bf16[48,3072]{1,0:T(8,128)(2,1)S(1)}, bf16[48,3072]{1,0:T(8,128)(2,1)S(1)}, u32[]{:S(2)}, u32[]{:S(2)}) collective-permute-start(bf16[48,3072]{1,0:T(8,128)(2,1)S(1)} %get-tuple-element.279), channel_id=1, source_target_pairs={{0,8},{1,9},{2,10},{3,11},{4,12},{5,13},{6,14},{7,15},{8,0},{9,1},... | collective-permute-start | bytes 884744 | tf_op jit(solution)/shard_map/ppermute | solution.py:865
  265.0 12.8 %collective-permute-start.44 = (bf16[2,48,2432]{2,1,0:T(8,128)(2,1)S(1)}, bf16[2,48,2432]{2,1,0:T(8,128)(2,1)S(1)}, u32[]{:S(2)}, u32[]{:S(2)}) collective-permute-start(bf16[2,48,2432]{2,1,0:T(8,128)(2,1)S(1)} %get-tuple-element.307), channel_id=1, source_target_pairs={{0,2},{1,3},{2,0},{3,1},{4,6},{5,7},{6,4},{7,5},{8,10},{9,11},{10,... | collective-permute-start | bytes 1400840 | tf_op jit(solution)/shard_map/ppermute | solution.py:780
  266.2 12.5 %collective-permute-start.45 = (bf16[2,48,2432]{2,1,0:T(8,128)(2,1)S(1)}, bf16[2,48,2432]{2,1,0:T(8,128)(2,1)S(1)}, u32[]{:S(2)}, u32[]{:S(2)}) collective-permute-start(bf16[2,48,2432]{2,1,0:T(8,128)(2,1)S(1)} %get-tuple-element.308), channel_id=1, source_target_pairs={{0,4},{1,5},{2,6},{3,7},{4,0},{5,1},{6,2},{7,3},{8,12},{9,13},{10,... | collective-permute-start | bytes 1400840 | tf_op jit(solution)/shard_map/ppermute | solution.py:780
  278.9 6.6 %collective-permute-start.47 = (bf16[1,48,2432]{2,1,0:T(8,128)(2,1)S(1)}, bf16[1,48,2432]{2,1,0:T(8,128)(2,1)S(1)}, u32[]{:S(2)}, u32[]{:S(2)}) collective-permute-start(bf16[1,48,2432]{2,1,0:T(8,128)(2,1)S(1)} %get-tuple-element.314), channel_id=1, source_target_pairs={{0,4},{1,5},{2,6},{3,7},{4,0},{5,1},{6,2},{7,3},{8,12},{9,13},{10,... | collective-permute-start | bytes 700424 | tf_op jit(solution)/shard_map/ppermute | solution.py:780
  280.1 6.3 %collective-permute-start.48 = (bf16[1,48,2432]{2,1,0:T(8,128)(2,1)S(1)}, bf16[1,48,2432]{2,1,0:T(8,128)(2,1)S(1)}, u32[]{:S(2)}, u32[]{:S(2)}) collective-permute-start(bf16[1,48,2432]{2,1,0:T(8,128)(2,1)S(1)} %get-tuple-element.315), channel_id=1, source_target_pairs={{0,2},{1,3},{2,0},{3,1},{4,6},{5,7},{6,4},{7,5},{8,10},{9,11},{10,... | collective-permute-start | bytes 700424 | tf_op jit(solution)/shard_map/ppermute | solution.py:780
  281.5 19.1 %collective-permute-start.51 = (bf16[48,3072]{1,0:T(8,128)(2,1)S(1)}, bf16[48,3072]{1,0:T(8,128)(2,1)S(1)}, u32[]{:S(2)}, u32[]{:S(2)}) collective-permute-start(bf16[48,3072]{1,0:T(8,128)(2,1)S(1)} %add_convert_fusion.10), channel_id=1, source_target_pairs={{0,16},{8,24},{16,0},{24,8},{1,17},{9,25},{17,1},{25,9},{2,18},{10... | collective-permute-start | bytes 884744 | tf_op jit(solution)/shard_map/ppermute | solution.py:869
  284.2 18.4 %collective-permute-start.50 = (bf16[48,1536]{1,0:T(8,128)(2,1)S(1)}, bf16[48,1536]{1,0:T(8,128)(2,1)S(1)}, u32[]{:S(2)}, u32[]{:S(2)}) collective-permute-start(bf16[48,1536]{1,0:T(8,128)(2,1)S(1)} %fusion.7), channel_id=1, source_target_pairs={{0,16},{8,24},{16,0},{24,8},{1,17},{9,25},{17,1},{25,9},{2,18},{10... | collective-permute-start | bytes 442376 | tf_op jit(solution)/shard_map/ppermute | solution.py:869
  286.7 16.9 %collective-permute-start.49 = (bf16[48,2432]{1,0:T(8,128)(2,1)S(1)}, bf16[48,2432]{1,0:T(8,128)(2,1)S(1)}, u32[]{:S(2)}, u32[]{:S(2)}) collective-permute-start(bf16[48,2432]{1,0:T(8,128)(2,1)S(1)} %get-tuple-element.331), channel_id=1, source_target_pairs={{0,8},{1,9},{2,10},{3,11},{4,12},{5,13},{6,14},{7,15},{8,0},{9,1},... | collective-permute-start | bytes 700424 | tf_op jit(solution)/shard_map/ppermute | solution.py:865
  289.8 22.5 %collective-permute-start.55 = (bf16[48,3072]{1,0:T(8,128)(2,1)S(1)}, bf16[48,3072]{1,0:T(8,128)(2,1)S(1)}, u32[]{:S(2)}, u32[]{:S(2)}) collective-permute-start(bf16[48,3072]{1,0:T(8,128)(2,1)S(1)} %add_convert_fusion.8), channel_id=1, source_target_pairs={{0,8},{1,9},{2,10},{3,11},{4,12},{5,13},{6,14},{7,15},{8,0},{9,1},... | collective-permute-start | bytes 884744 | tf_op jit(solution)/shard_map/ppermute | solution.py:865
  303.8 14.3 %collective-permute-start.53 = (bf16[48,1536]{1,0:T(8,128)(2,1)S(1)}, bf16[48,1536]{1,0:T(8,128)(2,1)S(1)}, u32[]{:S(2)}, u32[]{:S(2)}) collective-permute-start(bf16[48,1536]{1,0:T(8,128)(2,1)S(1)} %add_convert_fusion.33), channel_id=1, source_target_pairs={{0,8},{1,9},{2,10},{3,11},{4,12},{5,13},{6,14},{7,15},{8,0},{9,1},... | collective-permute-start | bytes 442376 | tf_op jit(solution)/shard_map/ppermute | solution.py:865
  303.9 14.2 %collective-permute-start.52 = (bf16[48,2432]{1,0:T(8,128)(2,1)S(1)}, bf16[48,2432]{1,0:T(8,128)(2,1)S(1)}, u32[]{:S(2)}, u32[]{:S(2)}) collective-permute-start(bf16[48,2432]{1,0:T(8,128)(2,1)S(1)} %fusion.6), channel_id=1, source_target_pairs={{0,16},{8,24},{16,0},{24,8},{1,17},{9,25},{17,1},{25,9},{2,18},{10... | collective-permute-start | bytes 700424 | tf_op jit(solution)/shard_map/ppermute | solution.py:869
  309.0 12.6 %collective-permute-start.54 = (bf16[48,3072]{1,0:T(8,128)(2,1)S(1)}, bf16[48,3072]{1,0:T(8,128)(2,1)S(1)}, u32[]{:S(2)}, u32[]{:S(2)}) collective-permute-start(bf16[48,3072]{1,0:T(8,128)(2,1)S(1)} %add_convert_fusion.9), channel_id=1, source_target_pairs={{0,8},{1,9},{2,10},{3,11},{4,12},{5,13},{6,14},{7,15},{8,0},{9,1},... | collective-permute-start | bytes 884744 | tf_op jit(solution)/shard_map/ppermute | solution.py:865
  (73 other events, 479.1 us)
